TPU v7x, 32 devices: a whole 2x2x4 slice. The times are simulated.
32 devices in a mesh: groups: 2 (over y), inst: 4 (over z), feat: 4 (over x, core).
Axes of the slice: x: 2, y: 2, z: 4, core: 2. Of those that a mesh axis runs over, the one named last changes fastest.
Arguments:
- tiles: bfloat16 [8, 4, 64, 128, 128], P(('groups', 'inst'), 'feat'), parts along dimension 0, may hold values from -0.25 to 0.25
- tile_rows: int32 [8, 4, 64], P(('groups', 'inst'), 'feat'), parts along dimension 0, may hold values from 0 to 7, as said below
- tile_cols: int32 [8, 4, 64], P(('groups', 'inst'), 'feat'), parts along dimension 0, may hold values from 0 to 2047, as said below
- tile_count: int32 [8, 4], P(('groups', 'inst'), 'feat'), parts along dimension 0, may hold values from 16 to 64, as said below
- sample_ids: int32 [8, 512], P(('groups', 'inst')), parts along dimension 0, may hold values from 0 to 1023, as said below
- labels: int32 [8, 1024], P(('groups', 'inst')), parts along dimension 0, may hold values 0 or 1
- weights: float32 [8, 262144], P(('groups', 'feat')), parts along dimension 0, may hold values from -8 to 8
Outputs:
- newton_step: float32 [8, 262144], P(('groups', 'feat'), 'inst'), parts along dimension 0
- residual: float32 [8, 262144], P(('groups', 'feat'), 'inst'), parts along dimension 0
There are 2 independent parts, one for each index of `groups`. A program takes and returns all parts, laid end to end along the dimension named above; each array names one. Nothing has to cross between parts.
Inputs may be any that keep to these rules, and one draw needn't show every extreme that they name: `tile_rows`: the (row, column) pairs of one device's slots are distinct. `tile_cols`: the (row, column) pairs of one device's slots are distinct; over all 64 slots of one device, at most 17 lie in one aligned run of 512 column blocks, and every device has a run with exactly 17. `tile_count`: slots at and beyond the count hold unused values; some device has exactly 64 live slots. `sample_ids`: distinct impressions of the instance block, numbered within it.
All inputs are finite; a program needn't handle non-finite values. No bound on the sum of `labels` on one device may be relied on, other than what follows from the above.
Results may differ from a plain program's by a relative error of at most 0.0003.
Values sent between devices are 32-bit elements; how exact they have to be, the bound alone decides.
No kernel may reach another device: no remote copies, remote signals or barrier semaphores. Data moves between devices by JAX's collectives and lax.ppermute only.
A program may use at most 64 MiB of HBM per device.

v0:
```python
import jax
import jax.numpy as jnp
from jax import lax
from jax.sharding import PartitionSpec as P

ITERS = 3


LAMBDA = 0.02


def body(tiles, tile_rows, tile_cols, tile_count, sample_ids, labels, weights):
    slots = tiles.shape[2]
    edge = tiles.shape[3]
    blocks = tiles.reshape(slots, edge, edge).astype(jnp.float32)
    tile_row = tile_rows.reshape(slots)
    tile_col = tile_cols.reshape(slots)
    filled = tile_count.reshape(())
    row_total = labels.shape[1]
    row_blocks = row_total // edge
    feat_len = weights.shape[1]
    col_blocks = feat_len // edge
    inst_size = lax.axis_size("inst")
    own_len = feat_len // inst_size
    offset = lax.axis_index("inst") * own_len
    active = (jnp.arange(slots) < filled).astype(jnp.float32)
    onehot = (tile_row[None, :] == jnp.arange(row_blocks)[:, None]).astype(jnp.float32) * active[
        None, :
    ]

    def forward_picked(picked):
        product = jnp.einsum("tij,tj->ti", blocks, picked, precision=lax.Precision.HIGHEST)
        return jnp.dot(onehot, product, precision=lax.Precision.HIGHEST).reshape(-1)

    def forward(vector):
        return forward_picked(vector.reshape(col_blocks, edge)[tile_col])

    def backward_slots(rowvec):
        spread = jnp.dot(
            onehot.T, rowvec.reshape(row_blocks, edge), precision=lax.Precision.HIGHEST
        )
        return jnp.einsum("tij,ti->tj", blocks, spread, precision=lax.Precision.HIGHEST)

    def backward(rowvec):
        return jax.ops.segment_sum(
            backward_slots(rowvec), tile_col, num_segments=col_blocks
        ).reshape(-1)

    chosen = sample_ids.reshape(-1)
    sampled = jnp.any(chosen[:, None] == jnp.arange(row_total)[None, :], axis=0).astype(jnp.float32)
    weight_vec = weights.reshape(-1)
    margin = lax.psum(forward(weight_vec), "feat")
    chance = jax.nn.sigmoid(margin)
    curv_weight = float(row_total) / float(chosen.shape[0]) * sampled * chance * (1.0 - chance)
    target = labels.reshape(-1).astype(jnp.float32)
    weight_own = lax.dynamic_slice_in_dim(weight_vec, offset, own_len)
    grad_own = (
        lax.psum_scatter(backward(chance - target), "inst", scatter_dimension=0, tiled=True)
        + LAMBDA * weight_own
    )
    residual = -grad_own
    newton_step = jnp.zeros_like(residual)
    direction = residual
    own_res = residual
    norm_now = lax.psum(jnp.sum(own_res * own_res), ("inst", "feat"))
    for iteration in range(ITERS):
        whole = lax.all_gather(direction, "inst", axis=0, tiled=True)
        partial_value = lax.psum(forward(whole), "feat")
        image = (
            lax.psum_scatter(
                backward(curv_weight * partial_value), "inst", scatter_dimension=0, tiled=True
            )
            + LAMBDA * direction
        )
        own_dir = direction
        curvature = lax.psum(jnp.sum(own_dir * image), ("inst", "feat"))
        step_len = norm_now / curvature
        newton_step = newton_step + step_len * direction
        residual = residual - step_len * image
        own_res = residual
        norm_next = lax.psum(jnp.sum(own_res * own_res), ("inst", "feat"))
        direction = residual + norm_next / norm_now * direction
        norm_now = norm_next
    return (newton_step.reshape(1, own_len), residual.reshape(1, own_len))


def solution(mesh):
    return jax.shard_map(
        body,
        mesh=mesh,
        in_specs=(
            P(("groups", "inst"), "feat", None, None, None),
            P(("groups", "inst"), "feat", None),
            P(("groups", "inst"), "feat", None),
            P(("groups", "inst"), "feat"),
            P(("groups", "inst"), None),
            P(("groups", "inst"), None),
            P(("groups", "feat"), None),
        ),
        out_specs=(P(("groups", "feat"), "inst"), P(("groups", "feat"), "inst")),
        check_vma=False,
    )
```

profile of v0, /device:TPU:0, one launch (start us, length us, event | category | flops | bytes accessed | tf_op | source)
XLA Modules:
  0.0 543.1 jit_solution(4272441471484433466)
XLA Ops:
  7.2 0.0 all-reduce.10.cloned.1.call-start
  8.0 0.7 fusion.70
  8.7 0.7 convert_element_type.17
  9.4 1.8 gather_fusion
  11.2 3.3 fusion.14
  14.6 0.1 convolution_bitcast_fusion.3
  14.7 8.3 %psum.70 = f32[1024]{0:T(1024)S(1)} all-reduce(f32[1024]{0:T(1024)S(1)} %convolution_bitcast_fusion.3), channel_id=1, replica_groups=mesh['groups'=2,'inst'=4,'feat'=4] {'feat'}, use_global_device_ids=true, to_apply=%region_0.0 | all-reduce | flops 1024 | bytes 8192 | tf_op jit(solution)/shard_map/psum | solution.py:52
  23.0 0.2 fusion.35
  23.3 1.7 fusion.12
  25.0 2.0 scatter_custom_fusion
  27.0 0.0 all-reduce.10.cloned.1.call-update
  27.0 0.0 all-gather.4.cloned.1.call-start
  27.1 1.2 dynamic-slice_multiply_fusion
  28.3 0.6 dynamic-slice.1
  29.6 49.8 %all-reduce.10.cloned.1.call-done = f32[262144]{0:T(1024)} async-done(((f32[262144]{0:T(1024)}), f32[262144]{0:T(1024)}) %all-reduce.10.cloned.1.call-update) | async-done | bytes 1048592
  79.3 2.3 multiply_reduce_fusion.5
  81.6 0.0 all-gather.4.cloned.1.call-update
  81.6 0.0 all-reduce.12.cloned.1.call-start
  81.7 0.4 fusion.16
  82.0 27.1 %all-gather.4.cloned.1.call-done = f32[262144]{0:T(1024)} async-done(((f32[65536]{0:T(1024)}), f32[262144]{0:T(1024)}) %all-gather.4.cloned.1.call-update) | async-done | bytes 1048592 | tf_op jit(solution)/shard_map/all_gather | solution.py:67
  109.1 1.8 gather_fusion.1
  110.9 3.3 fusion.10
  114.3 0.1 convolution_bitcast_fusion.2
  114.4 6.4 %psum.72 = f32[1024]{0:T(1024)S(1)} all-reduce(f32[1024]{0:T(1024)S(1)} %convolution_bitcast_fusion.2), channel_id=1, replica_groups=mesh['groups'=2,'inst'=4,'feat'=4] {'feat'}, use_global_device_ids=true, to_apply=%region_6.0 | all-reduce | flops 1024 | bytes 8192 | tf_op jit(solution)/shard_map/psum | solution.py:68
  120.8 0.2 fusion.32
  121.1 1.7 fusion.8
  122.8 2.0 scatter_custom_fusion.1
  124.8 0.0 all-gather.6.cloned.1.call-start
  124.9 50.9 %all-reduce.12.cloned.1.call-done = f32[262144]{0:T(1024)} async-done(((f32[262144]{0:T(1024)}), f32[262144]{0:T(1024)}) %all-reduce.12.cloned.1.call-update) | async-done | bytes 1048592
  175.8 1.6 multiply_reduce_fusion.4
  177.5 32.4 %all-reduce.4 = (f32[]{:T(128)}, f32[]{:T(128)}) all-reduce(f32[]{:T(128)} %get-tuple-element.6, f32[]{:T(128)} %multiply_reduce_fusion.4), channel_id=1, replica_groups=mesh['groups'=2,'inst'=4,'feat'=4] {'inst','feat'}, use_global_device_ids=true, to_apply=%region_4.0 | all-reduce | flops 2 | bytes 16 | tf_op jit(solution)/shard_map/psum | solution.py:65
  211.2 1.6 multiply_reduce_fusion.3
  212.8 30.1 %psum.74 = f32[]{:T(128)} all-reduce(f32[]{:T(128)} %multiply_reduce_fusion.3), channel_id=1, replica_groups=mesh['groups'=2,'inst'=4,'feat'=4] {'inst','feat'}, use_global_device_ids=true, to_apply=%region_12.0 | all-reduce | flops 1 | bytes 8 | tf_op jit(solution)/shard_map/psum | solution.py:81
  244.1 1.7 multiply_add_fusion.2
  245.9 0.0 all-gather.6.cloned.1.call-update
  245.9 0.0 all-reduce.14.cloned.1.call-start
  245.9 25.3 %all-gather.6.cloned.1.call-done = f32[262144]{0:T(1024)} async-done(((f32[65536]{0:T(1024)}), f32[262144]{0:T(1024)}) %all-gather.6.cloned.1.call-update) | async-done | bytes 1048592 | tf_op jit(solution)/shard_map/all_gather | solution.py:67
  271.2 1.8 gather_fusion.2
  273.0 3.3 fusion.6
  276.4 0.1 convolution_bitcast_fusion.1
  276.5 6.4 %psum.75 = f32[1024]{0:T(1024)S(1)} all-reduce(f32[1024]{0:T(1024)S(1)} %convolution_bitcast_fusion.1), channel_id=1, replica_groups=mesh['groups'=2,'inst'=4,'feat'=4] {'feat'}, use_global_device_ids=true, to_apply=%region_13.0 | all-reduce | flops 1024 | bytes 8192 | tf_op jit(solution)/shard_map/psum | solution.py:68
  282.9 0.2 fusion.29
  283.2 1.7 fusion.4
  284.9 1.9 scatter_custom_fusion.2
  286.9 0.0 all-gather.8.cloned.1.call-start
  286.9 51.0 %all-reduce.14.cloned.1.call-done = f32[262144]{0:T(1024)} async-done(((f32[262144]{0:T(1024)}), f32[262144]{0:T(1024)}) %all-reduce.14.cloned.1.call-update) | async-done | bytes 1048592
  337.9 1.6 multiply_reduce_fusion.2
  339.5 32.4 %psum.76 = f32[]{:T(128)} all-reduce(f32[]{:T(128)} %multiply_reduce_fusion.2), channel_id=1, replica_groups=mesh['groups'=2,'inst'=4,'feat'=4] {'inst','feat'}, use_global_device_ids=true, to_apply=%region_17.0 | all-reduce | flops 1 | bytes 8 | tf_op jit(solution)/shard_map/psum | solution.py:76
  373.2 1.8 multiply_reduce_fusion.1
  374.9 30.1 %psum.77 = f32[]{:T(128)} all-reduce(f32[]{:T(128)} %get-tuple-element.4), channel_id=1, replica_groups=mesh['groups'=2,'inst'=4,'feat'=4] {'inst','feat'}, use_global_device_ids=true, to_apply=%region_19.0 | all-reduce | flops 1 | bytes 8 | tf_op jit(solution)/shard_map/psum | solution.py:81
  406.3 0.7 multiply_add_fusion.1
  407.0 0.0 all-reduce.16.cloned.1.call-start
  407.1 25.3 %all-gather.8.cloned.1.call-done = f32[262144]{0:T(1024)} async-done(((f32[65536]{0:T(1024)}), f32[262144]{0:T(1024)}) %all-gather.8.cloned.1.call-update) | async-done | bytes 1048592 | tf_op jit(solution)/shard_map/all_gather | solution.py:67
  432.3 1.8 gather_fusion.3
  434.2 3.3 fusion.2
  437.5 0.1 convolution_bitcast_fusion
  437.6 6.4 %psum.78 = f32[1024]{0:T(1024)S(1)} all-reduce(f32[1024]{0:T(1024)S(1)} %convolution_bitcast_fusion), channel_id=1, replica_groups=mesh['groups'=2,'inst'=4,'feat'=4] {'feat'}, use_global_device_ids=true, to_apply=%region_20.0 | all-reduce | flops 1024 | bytes 8192 | tf_op jit(solution)/shard_map/psum | solution.py:68
  444.1 0.2 fusion.26
  444.3 1.7 fusion
  446.1 2.0 scatter_custom_fusion.3
  448.1 51.0 %all-reduce.16.cloned.1.call-done = f32[262144]{0:T(1024)} async-done(((f32[262144]{0:T(1024)}), f32[262144]{0:T(1024)}) %all-reduce.16.cloned.1.call-update) | async-done | bytes 1048592
  499.1 1.6 multiply_reduce_fusion
  500.7 32.4 %psum.79 = f32[]{:T(128)} all-reduce(f32[]{:T(128)} %multiply_reduce_fusion), channel_id=1, replica_groups=mesh['groups'=2,'inst'=4,'feat'=4] {'inst','feat'}, use_global_device_ids=true, to_apply=%region_24.0 | all-reduce | flops 1 | bytes 8 | tf_op jit(solution)/shard_map/psum | solution.py:76
  534.4 1.9 multiply_subtract_fusion
  (20 shorter events, 0.1 us)
Async XLA Ops:
  7.2 4.0 copy-start
  7.2 7.4 %copy-start.4 = (s32[1,1,64]{2,1,0:T(1,128)S(1)}, s32[1,1,64]{2,1,0:T(1,128)}, u32[]{:S(2)}) copy-start(s32[1,1,64]{2,1,0:T(1,128)} %param.8) | copy-start | bytes 772
  7.2 72.1 %all-reduce.10.cloned.1.call-start = ((), (), s32[]{:S(2)}) async-start(), calls=%async_computation.3 | async-start | bytes 2097152
  23.3 5.0 copy-start.6
  25.0 56.7 %copy-start.5 = (s32[1,512]{1,0:T(1,128)S(1)}, s32[1,512]{1,0:T(1,128)}, u32[]{:S(2)}) copy-start(s32[1,512]{1,0:T(1,128)} %param.11) | copy-start | bytes 6148
  27.0 82.1 %all-gather.4.cloned.1.call-start = ((), (), s32[]{:S(2)}) async-start(), calls=%async_computation | async-start | bytes 1310720 | tf_op jit(solution)/shard_map/all_gather | solution.py:67
  81.6 94.2 %all-reduce.12.cloned.1.call-start = ((), (), s32[]{:S(2)}) async-start(), calls=%async_computation.4 | async-start | bytes 2097152
  121.1 54.8 %copy-start.1 = (f32[65536]{0:T(1024)S(1)}, f32[65536]{0:T(1024)}, u32[]{:S(2)}) copy-start(f32[65536]{0:T(1024)} %get-tuple-element.7) | copy-start | bytes 786436
  124.8 146.4 %all-gather.6.cloned.1.call-start = ((), (), s32[]{:S(2)}) async-start(), calls=%async_computation.1 | async-start | bytes 1310720 | tf_op jit(solution)/shard_map/all_gather | solution.py:67
  245.9 92.0 %all-reduce.14.cloned.1.call-start = ((), (), s32[]{:S(2)}) async-start(), calls=%async_computation.5 | async-start | bytes 2097152
  283.2 54.7 %copy-start.2 = (f32[65536]{0:T(1024)S(1)}, f32[65536]{0:T(1024)}, u32[]{:S(2)}) copy-start(f32[65536]{0:T(1024)} %multiply_add_fusion.2) | copy-start | bytes 786436
  286.9 145.5 %all-gather.8.cloned.1.call-start = ((), (), s32[]{:S(2)}) async-start(), calls=%async_computation.2 | async-start | bytes 1310720 | tf_op jit(solution)/shard_map/all_gather | solution.py:67
  407.0 92.0 %all-reduce.16.cloned.1.call-start = ((), (), s32[]{:S(2)}) async-start(), calls=%async_computation.6 | async-start | bytes 2097152
  444.3 54.8 %copy-start.3 = (f32[65536]{0:T(1024)S(1)}, f32[65536]{0:T(1024)}, u32[]{:S(2)}) copy-start(f32[65536]{0:T(1024)} %multiply_add_fusion.1) | copy-start | bytes 786436
Sparse Core Ops, SparseCore 0:
  27.2 52.1 all-reduce.9
  81.7 27.3 all-gather.3
  124.9 50.8 all-reduce.11
  246.0 25.1 all-gather.5
  287.0 50.8 all-reduce.13
  407.1 25.1 all-gather.7
  448.2 50.8 all-reduce.15
where the time goes:
time: 544 us; the launch traced here: 543 us
  waiting for transfers between devices  280 us (51%)
  blocking collectives  185 us (34%)
  other arithmetic  25.8 us (5%)
  between operations  22.1 us (4%)
  matrix products  21.8 us (4%)
  local copies, waits for them, and re-layouts  7.91 us (1%)
    unnamed x11, waiting for transfers between devices  203 us
    all_gather x3, waiting for transfers between devices, body(): whole = lax.all_gather(direction, 'inst', axis=0, tiled=True)  77.6 us
    psum x2, blocking collectives, body(): curvature = lax.psum(jnp.sum(own_dir * image), ('inst', 'feat'))  64.8 us
    psum x2, blocking collectives, body(): norm_next = lax.psum(jnp.sum(own_res * own_res), ('inst', 'feat'))  60.2 us
    psum x1, blocking collectives, body(): norm_now = lax.psum(jnp.sum(own_res * own_res), ('inst', 'feat'))  32.4 us
    psum x3, blocking collectives, body(): partial_value = lax.psum(forward(whole), 'feat')  19.2 us
    dot_general x4, matrix products, forward_picked(): jnp.einsum('tij,tj->ti', blocks, picked, precision=lax.Precision.HIGHEST)  13.3 us
  transfers between devices with their start and end apart: 7, of which 7 were waited for; matrix products, arithmetic and copies ran while one was open for 0% of the time, Pallas kernels for 0%

commit v1 on v0

v1 whole, which is shorter than its diff:
```python
import functools

import jax
import jax.numpy as jnp
from jax import lax
from jax.experimental import pallas as pl
from jax.experimental.pallas import tpu as pltpu
from jax.sharding import PartitionSpec as P

ITERS = 3
LAMBDA = 0.02

F32, BF16, I32 = jnp.float32, jnp.bfloat16, jnp.int32
LANES, SUB = 128, 8
TAIL = 8
COLS_ROW = 3


VM = pl.BlockSpec(memory_space=pltpu.VMEM)
SM = pl.BlockSpec(memory_space=pltpu.SMEM)
ANY = pl.BlockSpec(memory_space=pl.ANY)


def call(kernel, ins, in_specs, outs, out_specs=None, scratch=(), flops=1 << 21):
    return pl.pallas_call(
        kernel,
        in_specs=in_specs,
        out_shape=outs,
        out_specs=out_specs or [VM] * len(outs),
        scratch_shapes=list(scratch),
        compiler_params=pltpu.CompilerParams(vmem_limit_bytes=24 << 20),
        cost_estimate=pl.CostEstimate(flops=flops, bytes_accessed=1 << 20, transcendentals=0),
    )(*ins)


def f32(*shape):
    return jax.ShapeDtypeStruct(shape, F32)


def iota(shape, dim):
    return lax.broadcasted_iota(I32, shape, dim)


def total(x):
    return jnp.sum(x, axis=(0, 1), keepdims=True)


def split3(x):
    hi = x.astype(BF16)
    rest = x - hi.astype(F32)
    mid = rest.astype(BF16)
    low = (rest - mid.astype(F32)).astype(BF16)
    return jnp.concatenate([hi, mid, low], axis=1)


def exact_pick(pick, values):
    wide = values.shape[1]
    out = jnp.dot(pick, split3(values), preferred_element_type=F32)
    return out[:, :wide] + out[:, wide : 2 * wide] + out[:, 2 * wide :]


def by_rows(tiles, order, start, row_of, row_blocks):
    lane = iota((SUB, LANES), 1)
    groups = LANES // SUB
    out = jnp.zeros((SUB, LANES), F32)
    for block in range(row_blocks):

        def step(n, acc):
            slot = order[n]
            return acc + tiles[slot].astype(F32) * row_of(slot)

        acc = lax.fori_loop(start[block], start[block + 1], step, jnp.zeros((LANES, LANES), F32))
        for g in range(groups):
            sums = jnp.sum(acc[g * SUB : (g + 1) * SUB], axis=1, keepdims=True)
            out = jnp.where(lane == block * groups + g, sums, out)
    return out


def by_cols(tiles, rows, count, vec, spread, msg):
    slots = tiles.shape[0]
    groups = LANES // SUB
    for k in range(spread.shape[0] // SUB):
        spread[k * SUB : (k + 1) * SUB, :] = jnp.broadcast_to(vec[:, k : k + 1], (SUB, LANES))
    msg[0:slots, :] = jnp.zeros((slots, LANES), F32)

    def chunk(c, carry):
        base = pl.multiple_of(c * SUB, SUB)
        lines = []
        for s in range(SUB):
            slot = base + s
            at = pl.multiple_of(rows[slot] * LANES, LANES)
            prod = tiles[slot].astype(F32) * spread[pl.ds(at, LANES), :]
            part = jnp.sum(prod.reshape(groups, SUB, LANES), axis=0)
            line = jnp.sum(part, axis=0, keepdims=True)
            lines.append(jnp.where(slot < count, line, 0.0))
        msg[pl.ds(base, SUB), :] = jnp.concatenate(lines, axis=0)
        return carry

    lax.fori_loop(0, (count + SUB - 1) // SUB, chunk, 0)


def start_kernel(row_blocks, rows, cols, count, tiles_hbm, w_hbm, part, tiles, w, order, start, sems):
    slots = tiles.shape[0]
    w_copy = pltpu.make_async_copy(w_hbm, w, sems.at[0])
    t_copy = pltpu.make_async_copy(tiles_hbm, tiles, sems.at[1])
    w_copy.start()
    t_copy.start()
    live = count[0]
    for b in range(row_blocks + 1):
        start[b] = 0

    def tally(t, carry):
        start[rows[t] + 1] += 1
        return carry

    lax.fori_loop(0, live, tally, 0)
    for b in range(row_blocks):
        start[b + 1] += start[b]

    def place(t, carry):
        r = rows[t]
        at = start[r]
        order[at] = t
        start[r] = at + 1
        return carry

    lax.fori_loop(0, live, place, 0)
    for b in range(row_blocks, 0, -1):
        start[b] = start[b - 1]
    start[0] = 0
    w_copy.wait()
    squares = jnp.zeros((SUB, LANES), F32)
    rows_w = w.shape[0]
    step_rows = min(rows_w, 512)
    for b in range(0, rows_w, step_rows):
        block = w[b : b + step_rows, :]
        squares = squares + jnp.sum((block * block).reshape(step_rows // SUB, SUB, LANES), axis=0)
    part[SUB : 2 * SUB, :] = squares
    t_copy.wait()
    part[0:SUB, :] = by_rows(tiles, order, start, lambda s: w[pl.ds(cols[s], 1), :], row_blocks)


def prep_kernel(labels, ids, cols_line, count, mask_out, label_out, cols_out, own_out):
    def to_grid(index, value):
        n = index.shape[1]
        left = jnp.where((index & (SUB - 1)) == iota((SUB, n), 0), value, 0.0).astype(BF16)
        right = ((index >> 3) == iota((LANES, n), 0)).astype(F32).astype(BF16)
        return lax.dot_general(left, right, (((1,), (1,)), ((), ())), preferred_element_type=F32)

    row_total, slots = labels.shape[1], cols_line.shape[1]
    label_out[...] = to_grid(iota((1, row_total), 1), labels[...].astype(F32))
    mask_out[...] = jnp.minimum(to_grid(ids[...], jnp.ones(ids.shape, F32)), 1.0)
    line = jnp.where(iota((1, slots), 1) < count[0], cols_line[...], -1).astype(F32)
    twice = jnp.concatenate([line, line], axis=1)
    cols_out[...] = jnp.broadcast_to(twice, (SUB, LANES))
    wide = jnp.broadcast_to(twice, (slots, LANES))
    own = jnp.where(iota((slots, LANES), 0) == iota((slots, LANES), 1), wide, 0.0)
    own_out[...] = jnp.broadcast_to(jnp.sum(own, axis=1, keepdims=True), (slots, LANES))


def feat_sum(refs, first=0):
    out = None
    for ref, height in refs:
        for at in range(0, ref.shape[0], height):
            piece = ref[at + first : at + first + SUB, :]
            out = piece if out is None else out + piece
    return out


def parts_of(refs, slots):
    height = slots + TAIL
    return [(ref, at) for ref in refs for at in range(0, ref.shape[0], height)]


def summed(refs, slots, row):
    line = None
    for ref, at in parts_of(refs, slots):
        piece = ref[at + slots + row : at + slots + row + 1, :]
        line = piece if line is None else line + piece
    return total(line)


def slot_cols(refs, slots):
    parts = parts_of(refs, slots)
    low = iota((1, LANES), 1) < slots
    lines = []
    for a, b in zip(parts[::2], parts[1::2], strict=True):
        first, second = (r[at + slots + COLS_ROW : at + slots + COLS_ROW + 1, :] for r, at in (a, b))
        lines.append(jnp.where(low, first, second))
    return jnp.concatenate(lines, axis=1)


def slot_values(refs, slots):
    return jnp.concatenate([ref[at : at + slots, :] for ref, at in parts_of(refs, slots)], axis=0)


def write_tail(msg, slots, lines):
    pad = jnp.zeros((TAIL - len(lines), LANES), F32)
    msg[slots : slots + TAIL, :] = jnp.concatenate([*lines, pad], axis=0)


def line_of(x):
    return jnp.sum(x, axis=0, keepdims=True)


def margin_kernel(n_f, scale, rows, count, tiles, mask, label, cols, *refs):
    got, (msg, m_out, c_out, e_out, ww_out, spread) = refs[:n_f], refs[n_f:]
    slots = tiles.shape[0]
    pieces = [(ref, 2 * SUB) for ref in got]
    m = feat_sum(pieces)
    ww_out[...] = feat_sum(pieces, SUB)
    chance = jax.nn.sigmoid(m)
    c_out[...] = scale * mask[...] * chance * (1.0 - chance)
    e = chance - label[...]
    m_out[...] = m
    e_out[...] = e
    by_cols(tiles, rows, count[0], e, spread, msg)
    zero = jnp.zeros((1, LANES), F32)
    write_tail(msg, slots, [zero, zero, zero, cols[0:1, :]])


def match_kernel(n_i, own, *refs):
    got, (match,) = refs[:n_i], refs[n_i:]
    slots = own.shape[0]
    line = slot_cols(got, slots)
    for at in range(0, line.shape[1], LANES):
        same = own[...] == line[:, at : at + LANES]
        match[:, at : at + LANES] = same.astype(F32).astype(BF16)


def forward_kernel(n_i, row_blocks, order, start, tiles, match, *refs):
    got, (out, picked) = refs[:n_i], refs[n_i:]
    slots = tiles.shape[0]
    picked[...] = exact_pick(match[...], slot_values(got, slots))
    out[...] = by_rows(tiles, order, start, lambda s: picked[pl.ds(s, 1), :], row_blocks)


def first_kernel(n_f, rows, count, tiles, m, c, e, *refs):
    got, (msg, v_out, spread) = refs[:n_f], refs[n_f:]
    slots = tiles.shape[0]
    v = -(LAMBDA * m[...] + feat_sum([(ref, SUB) for ref in got]))
    v_out[...] = v
    u = c[...] * v
    by_cols(tiles, rows, count[0], u, spread, msg)
    s = -e[...]
    write_tail(msg, slots, [line_of(-LAMBDA * m[...] * s + s * v), line_of(u * v)])


def next_kernel(n_f, n_i, first, rows, count, tiles, m, c, ww, *refs):
    got, msgs = refs[:n_f], refs[n_f : n_f + n_i]
    vec, num, msg, vec_out, num_out, spread = refs[n_f + n_i :]
    slots = tiles.shape[0]
    mm, cc = m[...], c[...]

    def at(ref, k):
        return ref[k * SUB : (k + 1) * SUB, :]

    gram_r = feat_sum([(ref, SUB) for ref in got])
    rr_new = summed(msgs, slots, 0)
    cur_r = summed(msgs, slots, 1)
    if first:
        e, v = vec[0], vec[1]
        v_r, s_r = v[...], -e[...]
        v_d, s_d, gram_d = v_r, s_r, gram_r
        a_r = a_d = jnp.full((1, 1), -LAMBDA, F32)
        rr = dd = a_r * a_r * total(ww[...]) + rr_new
        cur = cur_r
    else:
        (old,) = vec
        v_r, v_d, s_r, s_d = (at(old, k) for k in range(4))
        numbers = num[0]
        rr_old, dd, cur, a_r, a_d = (numbers[k : k + 1, 0:1] for k in range(5))
        rr = a_r * a_r * total(ww[...]) + rr_new
        beta = rr / rr_old
        dd = rr + beta * beta * dd
        cur = cur_r + 2.0 * beta * summed(msgs, slots, 2) + beta * beta * cur
        a_d = a_r + beta * a_d
        v_d = v_r + beta * v_d
        s_d = s_r + beta * s_d
        gram_d = gram_r + beta * at(old, 4)
    alpha = rr / (cur + LAMBDA * dd)
    v_r = v_r - alpha * (gram_d + LAMBDA * v_d)
    s_r = s_r - alpha * (cc * v_d + LAMBDA * s_d)
    a_r = a_r - alpha * (LAMBDA * a_d)
    u = cc * v_r
    by_cols(tiles, rows, count[0], u, spread, msg)
    write_tail(
        msg, slots, [line_of(a_r * mm * s_r + s_r * v_r), line_of(u * v_r), line_of(u * v_d)]
    )
    for k, value in enumerate((v_r, v_d, s_r, s_d, gram_d)):
        vec_out[k * SUB : (k + 1) * SUB, :] = value
    beta_out = jnp.zeros((1, 1), F32) if first else beta
    lines = [rr, dd, cur, a_r, a_d, alpha, beta_out, jnp.zeros((1, 1), F32)]
    num_out[...] = jnp.concatenate([jnp.broadcast_to(x, (1, LANES)) for x in lines], axis=0)


def last_kernel(n_i, slots, ww, w, index, *refs):
    iters = ITERS
    msgs = [refs[k * n_i : (k + 1) * n_i] for k in range(iters + 1)]
    nums = refs[(iters + 1) * n_i : (iters + 1) * n_i + iters - 1]
    step_out, res_out = refs[-2:]
    own_blocks = step_out.shape[0]
    basis = iters + 2
    zero, one = jnp.zeros((1, 1), F32), jnp.ones((1, 1), F32)

    def unit(k):
        return [one if j == k else zero for j in range(basis)]

    def plus(x, factor, y):
        return [a + factor * b for a, b in zip(x, y, strict=True)]

    res = [-LAMBDA * one, -one] + [zero] * iters
    step, direction, curved = [zero] * basis, res, unit(2)
    for k in range(iters):
        if k < iters - 1:
            rr, dd, cur, alpha, beta = (nums[k][j : j + 1, 0:1] for j in (0, 1, 2, 5, 6))
            a_r = nums[k][3:4, 0:1]
        else:
            rr_old, dd_old, cur_old = rr, dd, cur
            rr = a_r * a_r * total(ww[...]) + summed(msgs[k + 1], slots, 0)
            beta = rr / rr_old
            dd = rr + beta * beta * dd_old
            cur = summed(msgs[k + 1], slots, 1) + beta * beta * cur_old
            cur = cur + 2.0 * beta * summed(msgs[k + 1], slots, 2)
            alpha = rr / (cur + LAMBDA * dd)
        if k:
            direction = plus(res, beta, direction)
            curved = plus(unit(2 + k), beta, curved)
        step = plus(step, alpha, direction)
        res = plus(res, -alpha, plus(curved, LAMBDA, direction))

    values = [slot_values(group, slots) for group in msgs]
    mixed = []
    for weights_of in (step, res):
        mix = weights_of[1] * values[0]
        for k in range(1, iters + 1):
            mix = mix + weights_of[1 + k] * values[k]
        mixed.append(mix)
    line = slot_cols(msgs[0], slots)
    offset = index[0] * own_blocks
    own = (iota((own_blocks, LANES), 0) + offset).astype(F32)
    pick = jnp.concatenate(
        [(own == line[:, a : a + LANES]).astype(F32).astype(BF16) for a in range(0, line.shape[1], LANES)],
        axis=1,
    )
    mine = w[pl.ds(pl.multiple_of(offset, own_blocks), own_blocks), :]
    for out, mix, factor in ((step_out, mixed[0], step[0]), (res_out, mixed[1], res[0])):
        out[...] = factor * mine + exact_pick(pick, mix)


def exchange(x, axis):
    size = lax.axis_size(axis)
    if size & (size - 1) or size > 8:
        return [lax.all_gather(x, axis, axis=0, tiled=True)]
    return [x] + [
        lax.ppermute(x, axis, [(i, i ^ k) for i in range(size)]) for k in range(size - 1, 0, -1)
    ]


def body(tiles, tile_rows, tile_cols, tile_count, sample_ids, labels, weights):
    slots, edge = tiles.shape[2], tiles.shape[3]
    row_total, feat_len = labels.shape[1], weights.shape[1]
    row_blocks, col_blocks = row_total // edge, feat_len // edge
    own_len = feat_len // lax.axis_size("inst")
    own_blocks = own_len // edge
    tiles = tiles.reshape(slots, edge, edge)
    rows, cols = tile_rows.reshape(slots), tile_cols.reshape(slots)
    count = tile_count.reshape(1)
    scale = float(row_total) / float(sample_ids.shape[1])
    index = lax.axis_index("inst").astype(I32).reshape(1)
    spread = pltpu.VMEM((row_total, LANES), F32)
    grid = f32(SUB, LANES)
    msg_shape = f32(slots + TAIL, LANES)

    part, tiles, w, order, start = call(
        functools.partial(start_kernel, row_blocks),
        (rows, cols, count, tiles, weights.reshape(col_blocks, edge)),
        [SM, SM, SM, ANY, ANY],
        [
            f32(2 * SUB, LANES),
            jax.ShapeDtypeStruct((slots, edge, edge), BF16),
            f32(col_blocks, edge),
            jax.ShapeDtypeStruct((slots,), I32),
            jax.ShapeDtypeStruct((row_blocks + 1,), I32),
        ],
        [VM, VM, VM, SM, SM],
        [pltpu.SemaphoreType.DMA((2,))],
    )
    mask, label, cols_line, own = call(
        prep_kernel,
        (labels, sample_ids, cols.reshape(1, slots), count),
        [VM, VM, VM, SM],
        [grid, grid, grid, f32(slots, LANES)],
    )
    got = exchange(part, "feat")
    n_f = len(got)
    msg, m, c, e, ww = call(
        functools.partial(margin_kernel, n_f, scale),
        (rows, count, tiles, mask, label, cols_line, *got),
        [SM, SM] + [VM] * (4 + n_f),
        [msg_shape, grid, grid, grid, grid],
        scratch=[spread],
    )
    msgs = exchange(msg, "inst")
    n_i = len(msgs)
    (match,) = call(
        functools.partial(match_kernel, n_i),
        (own, *msgs),
        [VM] * (1 + n_i),
        [jax.ShapeDtypeStruct((slots, slots * lax.axis_size("inst")), BF16)],
    )

    def forward(msgs):
        (out,) = call(
            functools.partial(forward_kernel, n_i, row_blocks),
            (order, start, tiles, match, *msgs),
            [SM, SM] + [VM] * (2 + n_i),
            [grid],
            scratch=[pltpu.VMEM((slots, LANES), F32)],
        )
        return exchange(out, "feat")

    history = [msgs]
    got = forward(msgs)
    msg, v = call(
        functools.partial(first_kernel, n_f),
        (rows, count, tiles, m, c, e, *got),
        [SM, SM] + [VM] * (4 + n_f),
        [msg_shape, grid],
        scratch=[spread],
    )
    history.append(exchange(msg, "inst"))
    state, nums = [e, v], []
    for k in range(ITERS - 1):
        got = forward(history[-1])
        if k == 0:
            kernel = functools.partial(wrapped_first, n_f, n_i)
            extra = state
        else:
            kernel = functools.partial(wrapped_next, n_f, n_i)
            extra = state + [nums[-1]]
        msg, vec, num = call(
            kernel,
            (rows, count, tiles, m, c, ww, *got, *history[-1], *extra),
            [SM, SM] + [VM] * (4 + n_f + n_i + len(extra)),
            [msg_shape, f32(5 * SUB, LANES), grid],
            scratch=[spread],
        )
        history.append(exchange(msg, "inst"))
        state = [vec]
        nums.append(num)
    step, res = call(
        functools.partial(last_kernel, n_i, slots),
        (ww, w, index, *(ref for group in history for ref in group), *nums),
        [VM, VM, SM] + [VM] * (n_i * (ITERS + 1) + len(nums)),
        [f32(own_blocks, edge), f32(own_blocks, edge)],
    )
    return step.reshape(1, own_len), res.reshape(1, own_len)


def wrapped_first(n_f, n_i, *refs):
    base = 6 + n_f + n_i
    next_kernel(n_f, n_i, True, *refs[:base], refs[base : base + 2], (), *refs[base + 2 :])


def wrapped_next(n_f, n_i, *refs):
    base = 6 + n_f + n_i
    next_kernel(
        n_f, n_i, False, *refs[:base], refs[base : base + 1], refs[base + 1 : base + 2], *refs[base + 2 :]
    )


def solution(mesh):
    return jax.shard_map(
        body,
        mesh=mesh,
        in_specs=(
            P(("groups", "inst"), "feat", None, None, None),
            P(("groups", "inst"), "feat", None),
            P(("groups", "inst"), "feat", None),
            P(("groups", "inst"), "feat"),
            P(("groups", "inst"), None),
            P(("groups", "inst"), None),
            P(("groups", "feat"), None),
        ),
        out_specs=(P(("groups", "feat"), "inst"), P(("groups", "feat"), "inst")),
        check_vma=False,
    )
```

time: 544 us -> 71.5 us (0.13)
  waiting for transfers between devices: 280 us -> 22.4 us
  blocking collectives: 185 us -> 0 us
  starting transfers between devices: 0.29 us -> 26.5 us
  other arithmetic: 25.8 us -> 0 us
  matrix products: 21.8 us -> 0 us
  between operations: 22.1 us -> 1.45 us
  Pallas kernels: 0 us -> 17.3 us
    unnamed x11 -> x0, waiting for transfers between devices: 203 us -> none
    psum x9 -> x0, blocking collectives: 185 us -> none  [the longest x2 64.8 us: body(): curvature = lax.psum(jnp.sum(own_dir * image), ('inst', 'feat'))]
    all_gather x3 -> x0, waiting for transfers between devices: 77.6 us -> none  [body(): whole = lax.all_gather(direction, 'inst', axis=0, tiled=True)]
    ppermute x0 -> x24, starting transfers between devices: none -> 26.5 us  [exchange(): lax.ppermute(x, axis, [(i, i ^ k) for i in range(size)])]
    ppermute x0 -> x24, waiting for transfers between devices: none -> 22.4 us  [exchange(): lax.ppermute(x, axis, [(i, i ^ k) for i in range(size)])]
    dot_general x16 -> x0, matrix products: 21.8 us -> none  [the longest x4 13.3 us: forward_picked(): jnp.einsum('tij,tj->ti', blocks, picked, precision=lax.Precision.HIGHEST)]
    pallas_call x0 -> x11, Pallas kernels: none -> 17.3 us  [call(): pl.pallas_call(kernel, in_specs=in_specs, out_shape=outs, out_specs=out_s...]
    reduce_sum x6 -> x0, other arithmetic: 10.6 us -> none  [the longest x3 4.95 us: body(): curvature = lax.psum(jnp.sum(own_dir * image), ('inst', 'feat'))]
  transfers between devices with their start and end apart: 7 -> 24, of which waited for: 7 -> 17; matrix products, arithmetic and copies ran while one was open for 0% -> 0% of each run, Pallas kernels for 0% -> 0%
where the time goes in v1:
time: 71.5 us; the launch traced here: 71.8 us
  starting transfers between devices  26.5 us (37%)
  waiting for transfers between devices  22.4 us (31%)
  Pallas kernels  17.3 us (24%)
  local copies, waits for them, and re-layouts  4.13 us (6%)
  between operations  1.45 us (2%)
    ppermute x24, starting transfers between devices, exchange(): lax.ppermute(x, axis, [(i, i ^ k) for i in range(size)])  26.5 us
    ppermute x24, waiting for transfers between devices, exchange(): lax.ppermute(x, axis, [(i, i ^ k) for i in range(size)])  22.4 us
    pallas_call x11, Pallas kernels, call(): pl.pallas_call(kernel, in_specs=in_specs, out_shape=outs, out_specs=out_s...  17.3 us
    unnamed x16, local copies, waits for them, and re-layouts  4.13 us
  transfers between devices with their start and end apart: 24, of which 17 were waited for; matrix products, arithmetic and copies ran while one was open for 0% of the time, Pallas kernels for 0%

profile of v1, /device:TPU:0, one launch (start us, length us, event | category | flops | bytes accessed | tf_op | source)
XLA Modules:
  0.0 71.8 jit_solution(15660068731057483665)
XLA Ops:
  0.6 0.0 copy-start.3
  0.6 0.0 copy-start.5
  1.4 1.6 %copy-done = bf16[1,1,64,128,128]{4,3,2,1,0:T(8,128)(2,1)S(1)} copy-done((bf16[1,1,64,128,128]{4,3,2,1,0:T(8,128)(2,1)S(1)}, bf16[1,1,64,128,128]{4,3,2,1,0:T(8,128)(2,1)}, u32[]{:S(2)}) %copy-start) | copy-done | bytes 2097176
  2.9 1.2 %copy-done.1 = f32[1,262144]{1,0:T(1,128)S(1)} copy-done((f32[1,262144]{1,0:T(1,128)S(1)}, f32[1,262144]{1,0:T(1,128)}, u32[]{:S(2)}) %copy-start.1) | copy-done | bytes 1048600
  4.2 0.7 copy-done.2
  4.8 0.7 copy-done.4
  5.5 3.7 %shard_map.86 = (f32[16,128]{1,0:T(8,128)S(1)}, bf16[64,128,128]{2,1,0:T(8,128)(2,1)S(1)}, f32[2048,128]{1,0:T(8,128)S(1)}, s32[64]{0:T(128)S(1)}, s32[9]{0:T(128)S(1)}) custom-call(s32[64]{0:T(128)S(1)} %bitcast.17, s32[64]{0:T(128)S(1)} %bitcast.22, s32[1]{0:T(128)} %bitcast.9.count, bf16[64,128,128]{2,1,0:T(8,128)(2,1)S(1)} %bitcast.15, ...), custom_call_target="tpu_custom_call" | custom-call | flops 2097152 | bytes 1048576 | tf_op jit(solution)/shard_map/pallas_call | solution.py:25
  9.2 2.8 %collective-permute-start = (f32[16,128]{1,0:T(8,128)S(1)}, f32[16,128]{1,0:T(8,128)S(1)}, u32[]{:S(2)}, u32[]{:S(2)}) collective-permute-start(f32[16,128]{1,0:T(8,128)S(1)} %get-tuple-element.29.refs_0_), channel_id=1, source_target_pairs={{0,3},{1,2},{2,1},{3,0},{4,7},{5,6},{6,5},{7,4},{8,11},{9,10},{10,... | collective-permute-start | bytes 24584 | tf_op jit(solution)/shard_map/ppermute | solution.py:356
  12.0 0.0 collective-permute-start.1
  12.0 0.2 collective-permute-start.2
  12.2 0.2 shard_map.87
  12.4 0.9 %collective-permute-done.refs_1_ = f32[16,128]{1,0:T(8,128)S(1)} collective-permute-done((f32[16,128]{1,0:T(8,128)S(1)}, f32[16,128]{1,0:T(8,128)S(1)}, u32[]{:S(2)}, u32[]{:S(2)}) %collective-permute-start) | collective-permute-done | bytes 8224 | tf_op jit(solution)/shard_map/ppermute | solution.py:356
  13.4 2.3 %collective-permute-done.1.refs_2_ = f32[16,128]{1,0:T(8,128)S(1)} collective-permute-done((f32[16,128]{1,0:T(8,128)S(1)}, f32[16,128]{1,0:T(8,128)S(1)}, u32[]{:S(2)}, u32[]{:S(2)}) %collective-permute-start.1) | collective-permute-done | bytes 8224 | tf_op jit(solution)/shard_map/ppermute | solution.py:356
  15.7 0.0 collective-permute-done.2.refs_3_
  15.7 1.3 %shard_map.88 = (f32[72,128]{1,0:T(8,128)S(1)}, f32[8,128]{1,0:T(8,128)S(1)}, f32[8,128]{1,0:T(8,128)S(1)}, f32[8,128]{1,0:T(8,128)S(1)}, f32[8,128]{1,0:T(8,128)S(1)}) custom-call(s32[64]{0:T(128)S(1)} %bitcast.18, s32[1]{0:T(128)} %bitcast.11.count, bf16[64,128,128]{2,1,0:T(8,128)(2,1)S(1)} %get-tuple-element.25.tiles.refs_2_, ...), custom_call_target="tpu_custom_call" | custom-call | flops 2097152 | bytes 1048576 | tf_op jit(solution)/shard_map/pallas_call | solution.py:25
  16.9 3.7 %collective-permute-start.3 = (f32[72,128]{1,0:T(8,128)S(1)}, f32[72,128]{1,0:T(8,128)S(1)}, u32[]{:S(2)}, u32[]{:S(2)}) collective-permute-start(f32[72,128]{1,0:T(8,128)S(1)} %get-tuple-element.32.refs_0_), channel_id=1, source_target_pairs={{0,12},{4,8},{8,4},{12,0},{1,13},{5,9},{9,5},{13,1},{2,14},{6,10},... | collective-permute-start | bytes 110600 | tf_op jit(solution)/shard_map/ppermute | solution.py:356
  20.6 0.0 collective-permute-start.4
  20.6 0.8 %collective-permute-start.5 = (f32[72,128]{1,0:T(8,128)S(1)}, f32[72,128]{1,0:T(8,128)S(1)}, u32[]{:S(2)}, u32[]{:S(2)}) collective-permute-start(f32[72,128]{1,0:T(8,128)S(1)} %get-tuple-element.32.refs_0_), channel_id=1, source_target_pairs={{0,4},{4,0},{8,12},{12,8},{1,5},{5,1},{9,13},{13,9},{2,6},{6,2},{1... | collective-permute-start | bytes 110600 | tf_op jit(solution)/shard_map/ppermute | solution.py:356
  21.4 1.5 %collective-permute-done.3.refs_1_ = f32[72,128]{1,0:T(8,128)S(1)} collective-permute-done((f32[72,128]{1,0:T(8,128)S(1)}, f32[72,128]{1,0:T(8,128)S(1)}, u32[]{:S(2)}, u32[]{:S(2)}) %collective-permute-start.3) | collective-permute-done | bytes 36896 | tf_op jit(solution)/shard_map/ppermute | solution.py:356
  22.9 2.6 %collective-permute-done.4.refs_2_ = f32[72,128]{1,0:T(8,128)S(1)} collective-permute-done((f32[72,128]{1,0:T(8,128)S(1)}, f32[72,128]{1,0:T(8,128)S(1)}, u32[]{:S(2)}, u32[]{:S(2)}) %collective-permute-start.4) | collective-permute-done | bytes 36896 | tf_op jit(solution)/shard_map/ppermute | solution.py:356
  25.5 0.0 collective-permute-done.5.refs_3_
  25.5 2.0 %shard_map.90.refs_0_ = f32[8,128]{1,0:T(8,128)S(1)} custom-call(s32[64]{0:T(128)S(1)} %get-tuple-element.36.order, s32[9]{0:T(128)S(1)} %get-tuple-element.37.start, bf16[64,128,128]{2,1,0:T(8,128)(2,1)S(1)} %get-tuple-element.25.tiles.refs_2_, bf16[64,256]{1,0:T(8,128)(2,1)S(1)} %shard_map.89.match, f32[72,128]{1,0:T(8,128)S(1)} %get-tuple-element.32.refs_0_, ...), custom_call_target="tpu_custom_call" | custom-call | flops 2097152 | bytes 1048576 | tf_op jit(solution)/shard_map/pallas_call | solution.py:25
  27.5 0.1 collective-permute-start.6
  27.6 0.1 collective-permute-start.7
  27.7 1.8 %collective-permute-start.8 = (f32[8,128]{1,0:T(8,128)S(1)}, f32[8,128]{1,0:T(8,128)S(1)}, u32[]{:S(2)}, u32[]{:S(2)}) collective-permute-start(f32[8,128]{1,0:T(8,128)S(1)} %shard_map.90.refs_0_), channel_id=1, source_target_pairs={{0,1},{1,0},{2,3},{3,2},{4,5},{5,4},{6,7},{7,6},{8,9},{9,8},{10,11... | collective-permute-start | bytes 12296 | tf_op jit(solution)/shard_map/ppermute | solution.py:356
  29.4 1.2 %collective-permute-done.6.refs_1_ = f32[8,128]{1,0:T(8,128)S(1)} collective-permute-done((f32[8,128]{1,0:T(8,128)S(1)}, f32[8,128]{1,0:T(8,128)S(1)}, u32[]{:S(2)}, u32[]{:S(2)}) %collective-permute-start.6) | collective-permute-done | bytes 4128 | tf_op jit(solution)/shard_map/ppermute | solution.py:356
  30.6 0.7 collective-permute-done.7.refs_2_
  31.3 0.0 collective-permute-done.8.refs_3_
  31.3 1.3 %shard_map.91 = (f32[72,128]{1,0:T(8,128)S(1)}, f32[8,128]{1,0:T(8,128)S(1)}) custom-call(s32[64]{0:T(128)S(1)} %bitcast.19, s32[1]{0:T(128)} %bitcast.12.count, bf16[64,128,128]{2,1,0:T(8,128)(2,1)S(1)} %get-tuple-element.25.tiles.refs_2_, f32[8,128]{1,0:T(8,128)S(1)} %get-tuple-element.33.m.refs_3_, f32[8,128]{1,0:T(8,128)S(1)} %get-tuple-element.34.c.refs_4_, ...), custom_call_target="tpu_custom_call" | custom-call | flops 2097152 | bytes 1048576 | tf_op jit(solution)/shard_map/pallas_call | solution.py:25
  32.5 1.9 %collective-permute-start.10 = (f32[72,128]{1,0:T(8,128)S(1)}, f32[72,128]{1,0:T(8,128)S(1)}, u32[]{:S(2)}, u32[]{:S(2)}) collective-permute-start(f32[72,128]{1,0:T(8,128)S(1)} %get-tuple-element.39.refs_0_.refs_10_.refs_4_), channel_id=1, source_target_pairs={{0,8},{4,12},{8,0},{12,4},{1,9},{5,13},{9,1},{13,5},{2,10},{6,14},... | collective-permute-start | bytes 110600 | tf_op jit(solution)/shard_map/ppermute | solution.py:356
  34.4 0.5 collective-permute-start.11
  34.9 2.1 %collective-permute-start.9 = (f32[72,128]{1,0:T(8,128)S(1)}, f32[72,128]{1,0:T(8,128)S(1)}, u32[]{:S(2)}, u32[]{:S(2)}) collective-permute-start(f32[72,128]{1,0:T(8,128)S(1)} %get-tuple-element.39.refs_0_.refs_10_.refs_4_), channel_id=1, source_target_pairs={{0,12},{4,8},{8,4},{12,0},{1,13},{5,9},{9,5},{13,1},{2,14},{6,10},... | collective-permute-start | bytes 110600 | tf_op jit(solution)/shard_map/ppermute | solution.py:356
  37.0 0.5 collective-permute-done.10.refs_2_.refs_12_.refs_6_
  37.4 1.3 %collective-permute-done.11.refs_3_.refs_13_.refs_7_ = f32[72,128]{1,0:T(8,128)S(1)} collective-permute-done((f32[72,128]{1,0:T(8,128)S(1)}, f32[72,128]{1,0:T(8,128)S(1)}, u32[]{:S(2)}, u32[]{:S(2)}) %collective-permute-start.11) | collective-permute-done | bytes 36896 | tf_op jit(solution)/shard_map/ppermute | solution.py:356
  38.8 1.9 %collective-permute-done.9.refs_1_.refs_11_.refs_5_ = f32[72,128]{1,0:T(8,128)S(1)} collective-permute-done((f32[72,128]{1,0:T(8,128)S(1)}, f32[72,128]{1,0:T(8,128)S(1)}, u32[]{:S(2)}, u32[]{:S(2)}) %collective-permute-start.9) | collective-permute-done | bytes 36896 | tf_op jit(solution)/shard_map/ppermute | solution.py:356
  40.6 2.0 %shard_map.92.refs_6_ = f32[8,128]{1,0:T(8,128)S(1)} custom-call(s32[64]{0:T(128)S(1)} %get-tuple-element.36.order, s32[9]{0:T(128)S(1)} %get-tuple-element.37.start, bf16[64,128,128]{2,1,0:T(8,128)(2,1)S(1)} %get-tuple-element.25.tiles.refs_2_, bf16[64,256]{1,0:T(8,128)(2,1)S(1)} %shard_map.89.match, ...), custom_call_target="tpu_custom_call" | custom-call | flops 2097152 | bytes 1048576 | tf_op jit(solution)/shard_map/pallas_call | solution.py:25
  42.7 0.1 collective-permute-start.12
  42.7 0.1 collective-permute-start.13
  42.8 1.8 %collective-permute-start.14 = (f32[8,128]{1,0:T(8,128)S(1)}, f32[8,128]{1,0:T(8,128)S(1)}, u32[]{:S(2)}, u32[]{:S(2)}) collective-permute-start(f32[8,128]{1,0:T(8,128)S(1)} %shard_map.92.refs_6_), channel_id=1, source_target_pairs={{0,1},{1,0},{2,3},{3,2},{4,5},{5,4},{6,7},{7,6},{8,9},{9,8},{10,11... | collective-permute-start | bytes 12296 | tf_op jit(solution)/shard_map/ppermute | solution.py:356
  44.6 1.2 %collective-permute-done.12.refs_7_ = f32[8,128]{1,0:T(8,128)S(1)} collective-permute-done((f32[8,128]{1,0:T(8,128)S(1)}, f32[8,128]{1,0:T(8,128)S(1)}, u32[]{:S(2)}, u32[]{:S(2)}) %collective-permute-start.12) | collective-permute-done | bytes 4128 | tf_op jit(solution)/shard_map/ppermute | solution.py:356
  45.8 0.7 collective-permute-done.13.refs_8_
  46.4 0.0 collective-permute-done.14.refs_9_
  46.4 1.4 %shard_map.93 = (f32[72,128]{1,0:T(8,128)S(1)}, f32[40,128]{1,0:T(8,128)S(1)}, f32[8,128]{1,0:T(8,128)S(1)}) custom-call(s32[64]{0:T(128)S(1)} %bitcast.20, s32[1]{0:T(128)} %bitcast.13.refs_1_, bf16[64,128,128]{2,1,0:T(8,128)(2,1)S(1)} %get-tuple-element.25.tiles.refs_2_, f32[8,128]{1,0:T(8,128)S(1)} %get-tuple-element.33.m.refs_3_, ...), custom_call_target="tpu_custom_call" | custom-call | flops 2097152 | bytes 1048576 | tf_op jit(solution)/shard_map/pallas_call | solution.py:25
  47.8 2.4 %collective-permute-start.15 = (f32[72,128]{1,0:T(8,128)S(1)}, f32[72,128]{1,0:T(8,128)S(1)}, u32[]{:S(2)}, u32[]{:S(2)}) collective-permute-start(f32[72,128]{1,0:T(8,128)S(1)} %get-tuple-element.41.refs_0_.refs_10_.refs_8_), channel_id=1, source_target_pairs={{0,12},{4,8},{8,4},{12,0},{1,13},{5,9},{9,5},{13,1},{2,14},{6,10},... | collective-permute-start | bytes 110600 | tf_op jit(solution)/shard_map/ppermute | solution.py:356
  50.3 0.0 collective-permute-start.16
  50.3 2.0 %collective-permute-start.17 = (f32[72,128]{1,0:T(8,128)S(1)}, f32[72,128]{1,0:T(8,128)S(1)}, u32[]{:S(2)}, u32[]{:S(2)}) collective-permute-start(f32[72,128]{1,0:T(8,128)S(1)} %get-tuple-element.41.refs_0_.refs_10_.refs_8_), channel_id=1, source_target_pairs={{0,4},{4,0},{8,12},{12,8},{1,5},{5,1},{9,13},{13,9},{2,6},{6,2},{1... | collective-permute-start | bytes 110600 | tf_op jit(solution)/shard_map/ppermute | solution.py:356
  52.3 1.4 %collective-permute-done.15.refs_1_.refs_11_.refs_9_ = f32[72,128]{1,0:T(8,128)S(1)} collective-permute-done((f32[72,128]{1,0:T(8,128)S(1)}, f32[72,128]{1,0:T(8,128)S(1)}, u32[]{:S(2)}, u32[]{:S(2)}) %collective-permute-start.15) | collective-permute-done | bytes 36896 | tf_op jit(solution)/shard_map/ppermute | solution.py:356
  53.7 1.5 %collective-permute-done.16.refs_2_.refs_12_.refs_10_ = f32[72,128]{1,0:T(8,128)S(1)} collective-permute-done((f32[72,128]{1,0:T(8,128)S(1)}, f32[72,128]{1,0:T(8,128)S(1)}, u32[]{:S(2)}, u32[]{:S(2)}) %collective-permute-start.16) | collective-permute-done | bytes 36896 | tf_op jit(solution)/shard_map/ppermute | solution.py:356
  55.1 0.0 collective-permute-done.17.refs_3_.refs_13_.refs_11_
  55.1 2.0 %shard_map.94.refs_6_ = f32[8,128]{1,0:T(8,128)S(1)} custom-call(s32[64]{0:T(128)S(1)} %get-tuple-element.36.order, s32[9]{0:T(128)S(1)} %get-tuple-element.37.start, bf16[64,128,128]{2,1,0:T(8,128)(2,1)S(1)} %get-tuple-element.25.tiles.refs_2_, bf16[64,256]{1,0:T(8,128)(2,1)S(1)} %shard_map.89.match, ...), custom_call_target="tpu_custom_call" | custom-call | flops 2097152 | bytes 1048576 | tf_op jit(solution)/shard_map/pallas_call | solution.py:25
  57.2 0.3 collective-permute-start.18
  57.5 0.0 collective-permute-start.19
  57.5 1.6 %collective-permute-start.20 = (f32[8,128]{1,0:T(8,128)S(1)}, f32[8,128]{1,0:T(8,128)S(1)}, u32[]{:S(2)}, u32[]{:S(2)}) collective-permute-start(f32[8,128]{1,0:T(8,128)S(1)} %shard_map.94.refs_6_), channel_id=1, source_target_pairs={{0,1},{1,0},{2,3},{3,2},{4,5},{5,4},{6,7},{7,6},{8,9},{9,8},{10,11... | collective-permute-start | bytes 12296 | tf_op jit(solution)/shard_map/ppermute | solution.py:356
  59.1 1.2 %collective-permute-done.18.refs_7_ = f32[8,128]{1,0:T(8,128)S(1)} collective-permute-done((f32[8,128]{1,0:T(8,128)S(1)}, f32[8,128]{1,0:T(8,128)S(1)}, u32[]{:S(2)}, u32[]{:S(2)}) %collective-permute-start.18) | collective-permute-done | bytes 4128 | tf_op jit(solution)/shard_map/ppermute | solution.py:356
  60.3 0.8 %collective-permute-done.19.refs_8_ = f32[8,128]{1,0:T(8,128)S(1)} collective-permute-done((f32[8,128]{1,0:T(8,128)S(1)}, f32[8,128]{1,0:T(8,128)S(1)}, u32[]{:S(2)}, u32[]{:S(2)}) %collective-permute-start.19) | collective-permute-done | bytes 4128 | tf_op jit(solution)/shard_map/ppermute | solution.py:356
  61.1 0.0 collective-permute-done.20.refs_9_
  61.1 2.1 %shard_map.95 = (f32[72,128]{1,0:T(8,128)S(1)}, f32[40,128]{1,0:T(8,128)}, f32[8,128]{1,0:T(8,128)S(1)}) custom-call(s32[64]{0:T(128)S(1)} %bitcast.21, s32[1]{0:T(128)} %bitcast.14.refs_1_, bf16[64,128,128]{2,1,0:T(8,128)(2,1)S(1)} %get-tuple-element.25.tiles.refs_2_, f32[8,128]{1,0:T(8,128)S(1)} %get-tuple-element.33.m.refs_3_, ...), custom_call_target="tpu_custom_call" | custom-call | flops 2097152 | bytes 1048576 | tf_op jit(solution)/shard_map/pallas_call | solution.py:25
  63.1 2.5 %collective-permute-start.21 = (f32[72,128]{1,0:T(8,128)S(1)}, f32[72,128]{1,0:T(8,128)S(1)}, u32[]{:S(2)}, u32[]{:S(2)}) collective-permute-start(f32[72,128]{1,0:T(8,128)S(1)} %get-tuple-element.44.refs_12_), channel_id=1, source_target_pairs={{0,12},{4,8},{8,4},{12,0},{1,13},{5,9},{9,5},{13,1},{2,14},{6,10},... | collective-permute-start | bytes 110600 | tf_op jit(solution)/shard_map/ppermute | solution.py:356
  65.6 0.0 collective-permute-start.22
  65.6 1.9 %collective-permute-start.23 = (f32[72,128]{1,0:T(8,128)S(1)}, f32[72,128]{1,0:T(8,128)S(1)}, u32[]{:S(2)}, u32[]{:S(2)}) collective-permute-start(f32[72,128]{1,0:T(8,128)S(1)} %get-tuple-element.44.refs_12_), channel_id=1, source_target_pairs={{0,4},{4,0},{8,12},{12,8},{1,5},{5,1},{9,13},{13,9},{2,6},{6,2},{1... | collective-permute-start | bytes 110600 | tf_op jit(solution)/shard_map/ppermute | solution.py:356
  67.5 1.4 %collective-permute-done.21.refs_13_ = f32[72,128]{1,0:T(8,128)S(1)} collective-permute-done((f32[72,128]{1,0:T(8,128)S(1)}, f32[72,128]{1,0:T(8,128)S(1)}, u32[]{:S(2)}, u32[]{:S(2)}) %collective-permute-start.21) | collective-permute-done | bytes 36896 | tf_op jit(solution)/shard_map/ppermute | solution.py:356
  68.9 1.6 %collective-permute-done.22.refs_14_ = f32[72,128]{1,0:T(8,128)S(1)} collective-permute-done((f32[72,128]{1,0:T(8,128)S(1)}, f32[72,128]{1,0:T(8,128)S(1)}, u32[]{:S(2)}, u32[]{:S(2)}) %collective-permute-start.22) | collective-permute-done | bytes 36896 | tf_op jit(solution)/shard_map/ppermute | solution.py:356
  70.4 0.0 collective-permute-done.23.refs_15_
  70.4 1.4 %shard_map.96 = (f32[512,128]{1,0:T(8,128)}, f32[512,128]{1,0:T(8,128)}) custom-call(f32[8,128]{1,0:T(8,128)S(1)} %get-tuple-element.30.refs_5_.ww, f32[2048,128]{1,0:T(8,128)S(1)} %get-tuple-element.31.w, s32[1]{0:T(128)} %bitcast.6.index, f32[72,128]{1,0:T(8,128)S(1)} %get-tuple-element.32.refs_0_, f32[72,128]{1,0:T(8,128)S(1)} %collective-permute-done.3.refs_1_, ...), custom_call_target="tpu_custom_call" | custom-call | flops 2097152 | bytes 1048576 | tf_op jit(solution)/shard_map/pallas_call | solution.py:25
  (11 shorter events, 0.0 us)
Async XLA Ops:
  0.6 15.0 %copy-start.3 = (s32[1,1,64]{2,1,0:T(1,128)S(1)}, s32[1,1,64]{2,1,0:T(1,128)}, u32[]{:S(2)}) copy-start(s32[1,1,64]{2,1,0:T(1,128)} %param.8) | copy-start | bytes 772
  0.6 11.6 %copy-start.5 = (s32[1,1,64]{2,1,0:T(1,128)S(1)}, s32[1,1,64]{2,1,0:T(1,128)}, u32[]{:S(2)}) copy-start(s32[1,1,64]{2,1,0:T(1,128)} %param.9) | copy-start | bytes 772
  0.7 11.6 %copy-start.7 = (s32[1,512]{1,0:T(1,128)S(1)}, s32[1,512]{1,0:T(1,128)}, u32[]{:S(2)}) copy-start(s32[1,512]{1,0:T(1,128)} %ids.1) | copy-start | bytes 6148
  0.7 11.6 %copy-start.6 = (s32[1,1024]{1,0:T(1,128)S(1)}, s32[1,1024]{1,0:T(1,128)}, u32[]{:S(2)}) copy-start(s32[1,1024]{1,0:T(1,128)} %labels.1) | copy-start | bytes 12292
  1.3 1.6 %copy-start = (bf16[1,1,64,128,128]{4,3,2,1,0:T(8,128)(2,1)S(1)}, bf16[1,1,64,128,128]{4,3,2,1,0:T(8,128)(2,1)}, u32[]{:S(2)}) copy-start(bf16[1,1,64,128,128]{4,3,2,1,0:T(8,128)(2,1)} %param.7) | copy-start | bytes 6291460
  2.9 1.2 %copy-start.1 = (f32[1,262144]{1,0:T(1,128)S(1)}, f32[1,262144]{1,0:T(1,128)}, u32[]{:S(2)}) copy-start(f32[1,262144]{1,0:T(1,128)} %param.13) | copy-start | bytes 3145732
  4.2 0.7 copy-start.2
  4.8 0.7 copy-start.4
  9.2 4.2 %collective-permute-start = (f32[16,128]{1,0:T(8,128)S(1)}, f32[16,128]{1,0:T(8,128)S(1)}, u32[]{:S(2)}, u32[]{:S(2)}) collective-permute-start(f32[16,128]{1,0:T(8,128)S(1)} %get-tuple-element.29.refs_0_), channel_id=1, source_target_pairs={{0,3},{1,2},{2,1},{3,0},{4,7},{5,6},{6,5},{7,4},{8,11},{9,10},{10,... | collective-permute-start | bytes 24584 | tf_op jit(solution)/shard_map/ppermute | solution.py:356
  12.0 3.7 %collective-permute-start.1 = (f32[16,128]{1,0:T(8,128)S(1)}, f32[16,128]{1,0:T(8,128)S(1)}, u32[]{:S(2)}, u32[]{:S(2)}) collective-permute-start(f32[16,128]{1,0:T(8,128)S(1)} %get-tuple-element.29.refs_0_), channel_id=1, source_target_pairs={{0,2},{1,3},{2,0},{3,1},{4,6},{5,7},{6,4},{7,5},{8,10},{9,11},{10,... | collective-permute-start | bytes 24584 | tf_op jit(solution)/shard_map/ppermute | solution.py:356
  12.0 3.7 %collective-permute-start.2 = (f32[16,128]{1,0:T(8,128)S(1)}, f32[16,128]{1,0:T(8,128)S(1)}, u32[]{:S(2)}, u32[]{:S(2)}) collective-permute-start(f32[16,128]{1,0:T(8,128)S(1)} %get-tuple-element.29.refs_0_), channel_id=1, source_target_pairs={{0,1},{1,0},{2,3},{3,2},{4,5},{5,4},{6,7},{7,6},{8,9},{9,8},{10,11... | collective-permute-start | bytes 24584 | tf_op jit(solution)/shard_map/ppermute | solution.py:356
  16.9 5.9 %collective-permute-start.3 = (f32[72,128]{1,0:T(8,128)S(1)}, f32[72,128]{1,0:T(8,128)S(1)}, u32[]{:S(2)}, u32[]{:S(2)}) collective-permute-start(f32[72,128]{1,0:T(8,128)S(1)} %get-tuple-element.32.refs_0_), channel_id=1, source_target_pairs={{0,12},{4,8},{8,4},{12,0},{1,13},{5,9},{9,5},{13,1},{2,14},{6,10},... | collective-permute-start | bytes 110600 | tf_op jit(solution)/shard_map/ppermute | solution.py:356
  20.6 4.9 %collective-permute-start.4 = (f32[72,128]{1,0:T(8,128)S(1)}, f32[72,128]{1,0:T(8,128)S(1)}, u32[]{:S(2)}, u32[]{:S(2)}) collective-permute-start(f32[72,128]{1,0:T(8,128)S(1)} %get-tuple-element.32.refs_0_), channel_id=1, source_target_pairs={{0,8},{4,12},{8,0},{12,4},{1,9},{5,13},{9,1},{13,5},{2,10},{6,14},... | collective-permute-start | bytes 110600 | tf_op jit(solution)/shard_map/ppermute | solution.py:356
  20.6 4.9 %collective-permute-start.5 = (f32[72,128]{1,0:T(8,128)S(1)}, f32[72,128]{1,0:T(8,128)S(1)}, u32[]{:S(2)}, u32[]{:S(2)}) collective-permute-start(f32[72,128]{1,0:T(8,128)S(1)} %get-tuple-element.32.refs_0_), channel_id=1, source_target_pairs={{0,4},{4,0},{8,12},{12,8},{1,5},{5,1},{9,13},{13,9},{2,6},{6,2},{1... | collective-permute-start | bytes 110600 | tf_op jit(solution)/shard_map/ppermute | solution.py:356
  27.5 3.1 %collective-permute-start.6 = (f32[8,128]{1,0:T(8,128)S(1)}, f32[8,128]{1,0:T(8,128)S(1)}, u32[]{:S(2)}, u32[]{:S(2)}) collective-permute-start(f32[8,128]{1,0:T(8,128)S(1)} %shard_map.90.refs_0_), channel_id=1, source_target_pairs={{0,3},{1,2},{2,1},{3,0},{4,7},{5,6},{6,5},{7,4},{8,11},{9,10},{10,... | collective-permute-start | bytes 12296 | tf_op jit(solution)/shard_map/ppermute | solution.py:356
  27.6 3.7 %collective-permute-start.7 = (f32[8,128]{1,0:T(8,128)S(1)}, f32[8,128]{1,0:T(8,128)S(1)}, u32[]{:S(2)}, u32[]{:S(2)}) collective-permute-start(f32[8,128]{1,0:T(8,128)S(1)} %shard_map.90.refs_0_), channel_id=1, source_target_pairs={{0,2},{1,3},{2,0},{3,1},{4,6},{5,7},{6,4},{7,5},{8,10},{9,11},{10,... | collective-permute-start | bytes 12296 | tf_op jit(solution)/shard_map/ppermute | solution.py:356
  27.7 3.6 %collective-permute-start.8 = (f32[8,128]{1,0:T(8,128)S(1)}, f32[8,128]{1,0:T(8,128)S(1)}, u32[]{:S(2)}, u32[]{:S(2)}) collective-permute-start(f32[8,128]{1,0:T(8,128)S(1)} %shard_map.90.refs_0_), channel_id=1, source_target_pairs={{0,1},{1,0},{2,3},{3,2},{4,5},{5,4},{6,7},{7,6},{8,9},{9,8},{10,11... | collective-permute-start | bytes 12296 | tf_op jit(solution)/shard_map/ppermute | solution.py:356
  32.5 4.9 %collective-permute-start.10 = (f32[72,128]{1,0:T(8,128)S(1)}, f32[72,128]{1,0:T(8,128)S(1)}, u32[]{:S(2)}, u32[]{:S(2)}) collective-permute-start(f32[72,128]{1,0:T(8,128)S(1)} %get-tuple-element.39.refs_0_.refs_10_.refs_4_), channel_id=1, source_target_pairs={{0,8},{4,12},{8,0},{12,4},{1,9},{5,13},{9,1},{13,5},{2,10},{6,14},... | collective-permute-start | bytes 110600 | tf_op jit(solution)/shard_map/ppermute | solution.py:356
  34.4 4.4 %collective-permute-start.11 = (f32[72,128]{1,0:T(8,128)S(1)}, f32[72,128]{1,0:T(8,128)S(1)}, u32[]{:S(2)}, u32[]{:S(2)}) collective-permute-start(f32[72,128]{1,0:T(8,128)S(1)} %get-tuple-element.39.refs_0_.refs_10_.refs_4_), channel_id=1, source_target_pairs={{0,4},{4,0},{8,12},{12,8},{1,5},{5,1},{9,13},{13,9},{2,6},{6,2},{1... | collective-permute-start | bytes 110600 | tf_op jit(solution)/shard_map/ppermute | solution.py:356
  34.9 5.8 %collective-permute-start.9 = (f32[72,128]{1,0:T(8,128)S(1)}, f32[72,128]{1,0:T(8,128)S(1)}, u32[]{:S(2)}, u32[]{:S(2)}) collective-permute-start(f32[72,128]{1,0:T(8,128)S(1)} %get-tuple-element.39.refs_0_.refs_10_.refs_4_), channel_id=1, source_target_pairs={{0,12},{4,8},{8,4},{12,0},{1,13},{5,9},{9,5},{13,1},{2,14},{6,10},... | collective-permute-start | bytes 110600 | tf_op jit(solution)/shard_map/ppermute | solution.py:356
  42.7 3.1 %collective-permute-start.12 = (f32[8,128]{1,0:T(8,128)S(1)}, f32[8,128]{1,0:T(8,128)S(1)}, u32[]{:S(2)}, u32[]{:S(2)}) collective-permute-start(f32[8,128]{1,0:T(8,128)S(1)} %shard_map.92.refs_6_), channel_id=1, source_target_pairs={{0,3},{1,2},{2,1},{3,0},{4,7},{5,6},{6,5},{7,4},{8,11},{9,10},{10,... | collective-permute-start | bytes 12296 | tf_op jit(solution)/shard_map/ppermute | solution.py:356
  42.7 3.7 %collective-permute-start.13 = (f32[8,128]{1,0:T(8,128)S(1)}, f32[8,128]{1,0:T(8,128)S(1)}, u32[]{:S(2)}, u32[]{:S(2)}) collective-permute-start(f32[8,128]{1,0:T(8,128)S(1)} %shard_map.92.refs_6_), channel_id=1, source_target_pairs={{0,2},{1,3},{2,0},{3,1},{4,6},{5,7},{6,4},{7,5},{8,10},{9,11},{10,... | collective-permute-start | bytes 12296 | tf_op jit(solution)/shard_map/ppermute | solution.py:356
  42.8 3.6 %collective-permute-start.14 = (f32[8,128]{1,0:T(8,128)S(1)}, f32[8,128]{1,0:T(8,128)S(1)}, u32[]{:S(2)}, u32[]{:S(2)}) collective-permute-start(f32[8,128]{1,0:T(8,128)S(1)} %shard_map.92.refs_6_), channel_id=1, source_target_pairs={{0,1},{1,0},{2,3},{3,2},{4,5},{5,4},{6,7},{7,6},{8,9},{9,8},{10,11... | collective-permute-start | bytes 12296 | tf_op jit(solution)/shard_map/ppermute | solution.py:356
  47.8 5.8 %collective-permute-start.15 = (f32[72,128]{1,0:T(8,128)S(1)}, f32[72,128]{1,0:T(8,128)S(1)}, u32[]{:S(2)}, u32[]{:S(2)}) collective-permute-start(f32[72,128]{1,0:T(8,128)S(1)} %get-tuple-element.41.refs_0_.refs_10_.refs_8_), channel_id=1, source_target_pairs={{0,12},{4,8},{8,4},{12,0},{1,13},{5,9},{9,5},{13,1},{2,14},{6,10},... | collective-permute-start | bytes 110600 | tf_op jit(solution)/shard_map/ppermute | solution.py:356
  50.3 4.9 %collective-permute-start.16 = (f32[72,128]{1,0:T(8,128)S(1)}, f32[72,128]{1,0:T(8,128)S(1)}, u32[]{:S(2)}, u32[]{:S(2)}) collective-permute-start(f32[72,128]{1,0:T(8,128)S(1)} %get-tuple-element.41.refs_0_.refs_10_.refs_8_), channel_id=1, source_target_pairs={{0,8},{4,12},{8,0},{12,4},{1,9},{5,13},{9,1},{13,5},{2,10},{6,14},... | collective-permute-start | bytes 110600 | tf_op jit(solution)/shard_map/ppermute | solution.py:356
  50.3 4.9 %collective-permute-start.17 = (f32[72,128]{1,0:T(8,128)S(1)}, f32[72,128]{1,0:T(8,128)S(1)}, u32[]{:S(2)}, u32[]{:S(2)}) collective-permute-start(f32[72,128]{1,0:T(8,128)S(1)} %get-tuple-element.41.refs_0_.refs_10_.refs_8_), channel_id=1, source_target_pairs={{0,4},{4,0},{8,12},{12,8},{1,5},{5,1},{9,13},{13,9},{2,6},{6,2},{1... | collective-permute-start | bytes 110600 | tf_op jit(solution)/shard_map/ppermute | solution.py:356
  57.2 3.1 %collective-permute-start.18 = (f32[8,128]{1,0:T(8,128)S(1)}, f32[8,128]{1,0:T(8,128)S(1)}, u32[]{:S(2)}, u32[]{:S(2)}) collective-permute-start(f32[8,128]{1,0:T(8,128)S(1)} %shard_map.94.refs_6_), channel_id=1, source_target_pairs={{0,3},{1,2},{2,1},{3,0},{4,7},{5,6},{6,5},{7,4},{8,11},{9,10},{10,... | collective-permute-start | bytes 12296 | tf_op jit(solution)/shard_map/ppermute | solution.py:356
  57.5 3.6 %collective-permute-start.19 = (f32[8,128]{1,0:T(8,128)S(1)}, f32[8,128]{1,0:T(8,128)S(1)}, u32[]{:S(2)}, u32[]{:S(2)}) collective-permute-start(f32[8,128]{1,0:T(8,128)S(1)} %shard_map.94.refs_6_), channel_id=1, source_target_pairs={{0,2},{1,3},{2,0},{3,1},{4,6},{5,7},{6,4},{7,5},{8,10},{9,11},{10,... | collective-permute-start | bytes 12296 | tf_op jit(solution)/shard_map/ppermute | solution.py:356
  57.5 3.6 %collective-permute-start.20 = (f32[8,128]{1,0:T(8,128)S(1)}, f32[8,128]{1,0:T(8,128)S(1)}, u32[]{:S(2)}, u32[]{:S(2)}) collective-permute-start(f32[8,128]{1,0:T(8,128)S(1)} %shard_map.94.refs_6_), channel_id=1, source_target_pairs={{0,1},{1,0},{2,3},{3,2},{4,5},{5,4},{6,7},{7,6},{8,9},{9,8},{10,11... | collective-permute-start | bytes 12296 | tf_op jit(solution)/shard_map/ppermute | solution.py:356
  63.1 5.8 %collective-permute-start.21 = (f32[72,128]{1,0:T(8,128)S(1)}, f32[72,128]{1,0:T(8,128)S(1)}, u32[]{:S(2)}, u32[]{:S(2)}) collective-permute-start(f32[72,128]{1,0:T(8,128)S(1)} %get-tuple-element.44.refs_12_), channel_id=1, source_target_pairs={{0,12},{4,8},{8,4},{12,0},{1,13},{5,9},{9,5},{13,1},{2,14},{6,10},... | collective-permute-start | bytes 110600 | tf_op jit(solution)/shard_map/ppermute | solution.py:356
  65.6 4.9 %collective-permute-start.22 = (f32[72,128]{1,0:T(8,128)S(1)}, f32[72,128]{1,0:T(8,128)S(1)}, u32[]{:S(2)}, u32[]{:S(2)}) collective-permute-start(f32[72,128]{1,0:T(8,128)S(1)} %get-tuple-element.44.refs_12_), channel_id=1, source_target_pairs={{0,8},{4,12},{8,0},{12,4},{1,9},{5,13},{9,1},{13,5},{2,10},{6,14},... | collective-permute-start | bytes 110600 | tf_op jit(solution)/shard_map/ppermute | solution.py:356
  65.6 4.9 %collective-permute-start.23 = (f32[72,128]{1,0:T(8,128)S(1)}, f32[72,128]{1,0:T(8,128)S(1)}, u32[]{:S(2)}, u32[]{:S(2)}) collective-permute-start(f32[72,128]{1,0:T(8,128)S(1)} %get-tuple-element.44.refs_12_), channel_id=1, source_target_pairs={{0,4},{4,0},{8,12},{12,8},{1,5},{5,1},{9,13},{13,9},{2,6},{6,2},{1... | collective-permute-start | bytes 110600 | tf_op jit(solution)/shard_map/ppermute | solution.py:356

commit v2 on v0

v2 whole, which is shorter than its diff:
```python
import functools

import jax
import jax.numpy as jnp
from jax import lax
from jax.experimental import pallas as pl
from jax.experimental.pallas import tpu as pltpu
from jax.sharding import PartitionSpec as P

ITERS = 3
LAMBDA = 0.02

F32, BF16, I32 = jnp.float32, jnp.bfloat16, jnp.int32
LANES, SUB = 128, 8
TAIL = 8
COLS_ROW = 3


VM = pl.BlockSpec(memory_space=pltpu.VMEM)
SM = pl.BlockSpec(memory_space=pltpu.SMEM)
ANY = pl.BlockSpec(memory_space=pl.ANY)
HBM = pl.BlockSpec(memory_space=pltpu.HBM)


def call(kernel, ins, in_specs, outs, out_specs=None, scratch=(), flops=1 << 21):
    return pl.pallas_call(
        kernel,
        in_specs=in_specs,
        out_shape=outs,
        out_specs=out_specs or [VM] * len(outs),
        scratch_shapes=list(scratch),
        compiler_params=pltpu.CompilerParams(vmem_limit_bytes=24 << 20),
        cost_estimate=pl.CostEstimate(flops=flops, bytes_accessed=1 << 20, transcendentals=0),
    )(*ins)


def f32(*shape):
    return jax.ShapeDtypeStruct(shape, F32)


def iota(shape, dim):
    return lax.broadcasted_iota(I32, shape, dim)


def total(x):
    return jnp.sum(x, axis=(0, 1), keepdims=True)


def split3(x):
    hi = x.astype(BF16).astype(F32)
    rest = x - hi
    mid = rest.astype(BF16).astype(F32)
    return hi, mid, (rest - mid).astype(BF16).astype(F32)


def exact_pick(pick, values):
    wide = values.shape[1]
    pieces = jnp.concatenate(split3(values), axis=1).astype(BF16)
    out = jnp.dot(pick, pieces, preferred_element_type=F32)
    return out[:, :wide] + out[:, wide : 2 * wide] + out[:, 2 * wide :]


def left_of(pieces):
    return jnp.concatenate([*pieces, jnp.zeros((SUB, LANES), F32)], axis=0).astype(BF16)


def fold3(acc, at=0):
    return acc[at : at + SUB] + acc[at + SUB : at + 2 * SUB] + acc[at + 2 * SUB : at + 3 * SUB]


def save_pieces(x, pieces):
    slots = x.shape[0]
    for p, piece in enumerate(split3(x)):
        pieces[p * slots : (p + 1) * slots, :] = piece


def masked_line(pieces, slots, slot, mask):
    return [
        mask * jnp.broadcast_to(pieces[p * slots + slot : p * slots + slot + 1, :], (SUB, LANES))
        for p in range(3)
    ]


def by_rows(turned, pieces, row_mask):
    slots = turned.shape[0]
    acc = jnp.zeros((4 * SUB, LANES), F32)
    for s in range(0, slots, 2):
        left = [
            left_of(masked_line(pieces, slots, t, row_mask[t * SUB : (t + 1) * SUB, :]))
            for t in (s, s + 1)
        ]
        right = jnp.concatenate([turned[s], turned[s + 1]], axis=0)
        acc = acc + jnp.dot(
            jnp.concatenate(left, axis=1), right, preferred_element_type=F32
        )
    return fold3(acc)


def by_cols(tiles, row_pick, vec, msg):
    slots = tiles.shape[0]
    pieces = jnp.concatenate(split3(vec), axis=1)
    pad = jnp.zeros((LANES - SUB, 3 * LANES), F32)
    stacked = jnp.concatenate([pieces, pad], axis=0).astype(BF16)
    lines = jnp.dot(row_pick[...], stacked, preferred_element_type=F32)
    sub = iota((SUB, LANES), 0)
    for g in range(0, slots, SUB):
        group = [lines[g : g + SUB, p * LANES : (p + 1) * LANES] for p in range(3)]
        acc = jnp.zeros((4 * SUB, LANES), F32)
        for s in range(0, SUB, 2):
            left = [left_of([jnp.where(sub == t, piece, 0.0) for piece in group]) for t in (s, s + 1)]
            right = jnp.concatenate([tiles[g + s], tiles[g + s + 1]], axis=0)
            acc = acc + jnp.dot(jnp.concatenate(left, axis=1), right, preferred_element_type=F32)
        msg[g : g + SUB, :] = fold3(acc)


CHUNKS = 4


def start_kernel(
    rows_hbm, cols_hbm, count_hbm, tiles_hbm, w_hbm,
    part, tiles, w, row_mask,
    rows, cols, count, picked, pieces, sems,
):
    slots = tiles.shape[0]
    each = slots // CHUNKS
    small = [
        pltpu.make_async_copy(src, dst, sems.at[k])
        for k, (src, dst) in enumerate(((cols_hbm, cols), (rows_hbm, rows), (count_hbm, count)))
    ]
    w_copy = pltpu.make_async_copy(w_hbm, w, sems.at[3])
    t_copies = [
        pltpu.make_async_copy(
            tiles_hbm.at[pl.ds(k * each, each)], tiles.at[pl.ds(k * each, each)], sems.at[4 + k]
        )
        for k in range(CHUNKS)
    ]
    for copy in [*small, w_copy, *t_copies]:
        copy.start()
    for copy in small:
        copy.wait()
    live = count[0]
    sub = iota((SUB, LANES), 0)
    for t in range(slots):
        row = jnp.where(t < live, rows[t], -1)
        row_mask[t * SUB : (t + 1) * SUB, :] = (sub == row).astype(F32)
    w_copy.wait()
    for t in range(slots):
        col = jnp.where(t < live, cols[t], 0)
        picked[t : t + 1, :] = w[pl.ds(col, 1), :]
    save_pieces(picked[...], pieces)
    squares = jnp.zeros((SUB, LANES), F32)
    rows_w = w.shape[0]
    step_rows = min(rows_w, 256)
    for b in range(0, rows_w, step_rows):
        block = w[b : b + step_rows, :]
        squares = squares + jnp.sum((block * block).reshape(step_rows // SUB, SUB, LANES), axis=0)
    part[SUB : 2 * SUB, :] = squares
    acc = jnp.zeros((6 * SUB, 2 * LANES), F32)
    for s in range(0, slots, 4):
        if s % each == 0:
            t_copies[s // each].wait()
        a, b, c, d = (
            masked_line(pieces, slots, t, row_mask[t * SUB : (t + 1) * SUB, :]) for t in range(s, s + 4)
        )
        left = [jnp.concatenate([*x, *y], axis=0).astype(BF16) for x, y in ((a, c), (b, d))]
        right = [jnp.concatenate([tiles[t], tiles[t + 1]], axis=1) for t in (s, s + 2)]
        acc = acc + lax.dot_general(
            jnp.concatenate(left, axis=1),
            jnp.concatenate(right, axis=0),
            (((1,), (1,)), ((), ())),
            preferred_element_type=F32,
        )
    part[0:SUB, :] = fold3(acc[:, :LANES]) + fold3(acc[:, LANES:], 3 * SUB)


def turn_kernel(tiles, turned):
    for t in range(tiles.shape[0]):
        turned[t] = tiles[t].T


def prep_kernel(ids, rows_line, cols_line, count, mask_out, pick_out, cols_out, own_out):
    slots = cols_line.shape[1]
    n = ids.shape[1]
    left = ((ids[...] >> 7) == iota((SUB, n), 0)).astype(F32).astype(BF16)
    right = ((ids[...] & (LANES - 1)) == iota((LANES, n), 0)).astype(F32).astype(BF16)
    hits = lax.dot_general(left, right, (((1,), (1,)), ((), ())), preferred_element_type=F32)
    mask_out[...] = jnp.minimum(hits, 1.0)
    live = iota((1, slots), 1) < count[...]

    def both(line):
        line = jnp.where(live, line, -1).astype(F32)
        line = jnp.concatenate([line, line], axis=1)
        wide = jnp.broadcast_to(line, (slots, LANES))
        own = jnp.where(iota((slots, LANES), 0) == iota((slots, LANES), 1), wide, 0.0)
        return line, jnp.broadcast_to(jnp.sum(own, axis=1, keepdims=True), (slots, LANES))

    line, own = both(cols_line[...])
    cols_out[...] = jnp.broadcast_to(line, (SUB, LANES))
    own_out[...] = own
    _, own = both(rows_line[...])
    pick_out[...] = (own == iota((slots, LANES), 1).astype(F32)).astype(F32).astype(BF16)


def feat_sum(refs, first=0):
    out = None
    for ref, height in refs:
        for at in range(0, ref.shape[0], height):
            piece = ref[at + first : at + first + SUB, :]
            out = piece if out is None else out + piece
    return out


def parts_of(refs, slots):
    height = slots + TAIL
    return [(ref, at) for ref in refs for at in range(0, ref.shape[0], height)]


def summed(refs, slots, row):
    line = None
    for ref, at in parts_of(refs, slots):
        piece = ref[at + slots + row : at + slots + row + 1, :]
        line = piece if line is None else line + piece
    return total(line)


def slot_cols(refs, slots):
    parts = parts_of(refs, slots)
    low = iota((1, LANES), 1) < slots
    lines = []
    for a, b in zip(parts[::2], parts[1::2], strict=True):
        first, second = (r[at + slots + COLS_ROW : at + slots + COLS_ROW + 1, :] for r, at in (a, b))
        lines.append(jnp.where(low, first, second))
    return jnp.concatenate(lines, axis=1)


def slot_values(refs, slots):
    return jnp.concatenate([ref[at : at + slots, :] for ref, at in parts_of(refs, slots)], axis=0)


def write_tail(msg, slots, lines):
    pad = jnp.zeros((TAIL - len(lines), LANES), F32)
    msg[slots : slots + TAIL, :] = jnp.concatenate([*lines, pad], axis=0)


def line_of(x):
    return jnp.sum(x, axis=0, keepdims=True)


def margin_kernel(n_f, scale, tiles, row_pick, mask, labels, cols, *refs):
    got, (msg, m_out, c_out, e_out, ww_out) = refs[:n_f], refs[n_f:]
    slots = tiles.shape[0]
    pieces = [(ref, 2 * SUB) for ref in got]
    m = feat_sum(pieces)
    chance = jax.nn.sigmoid(m)
    e = chance - labels[...].astype(F32)
    by_cols(tiles, row_pick, e, msg)
    zero = jnp.zeros((1, LANES), F32)
    write_tail(msg, slots, [zero, zero, zero, cols[0:1, :]])
    ww_out[...] = feat_sum(pieces, SUB)
    c_out[...] = scale * mask[...] * chance * (1.0 - chance)
    m_out[...] = m
    e_out[...] = e


def match_kernel(n_i, own, *refs):
    got, (match,) = refs[:n_i], refs[n_i:]
    slots = own.shape[0]
    line = slot_cols(got, slots)
    for at in range(0, line.shape[1], LANES):
        same = own[...] == line[:, at : at + LANES]
        match[:, at : at + LANES] = same.astype(F32).astype(BF16)


def forward_kernel(n_i, turned, row_mask, match, *refs):
    got, (out, pieces) = refs[:n_i], refs[n_i:]
    slots = turned.shape[0]
    save_pieces(exact_pick(match[...], slot_values(got, slots)), pieces)
    out[...] = by_rows(turned, pieces, row_mask)


def first_kernel(n_f, tiles, row_pick, m, c, e, *refs):
    got, (msg, v_out) = refs[:n_f], refs[n_f:]
    slots = tiles.shape[0]
    v = -(LAMBDA * m[...] + feat_sum([(ref, SUB) for ref in got]))
    v_out[...] = v
    u = c[...] * v
    by_cols(tiles, row_pick, u, msg)
    s = -e[...]
    write_tail(msg, slots, [line_of(-LAMBDA * m[...] * s + s * v), line_of(u * v)])


NUMBERS = ("rr", "dd", "cur", "a_r", "a_d", "alpha", "beta")


def numbers_of(num):
    return {name: num[k : k + 1, 0:1] for k, name in enumerate(NUMBERS)}


def save_numbers(num, values):
    lines = [jnp.broadcast_to(values[name], (1, LANES)) for name in NUMBERS]
    num[...] = jnp.concatenate([*lines, jnp.zeros((1, LANES), F32)], axis=0)


def advance(msgs, slots, ww, old):
    rr_new, cur_r = summed(msgs, slots, 0), summed(msgs, slots, 1)
    if old is None:
        a_r = a_d = jnp.full((1, 1), -LAMBDA, F32)
        rr = a_r * a_r * total(ww[...]) + rr_new
        dd, cur, beta = rr, cur_r, jnp.zeros((1, 1), F32)
    else:
        cross = summed(msgs, slots, 2)
        rr = old["a_r"] * old["a_r"] * total(ww[...]) + rr_new
        beta = rr / old["rr"]
        a_d = old["a_r"] + beta * old["a_d"]
        dd = rr + beta * beta * old["dd"]
        cur = cur_r + 2.0 * beta * cross + beta * beta * old["cur"]
        a_r = old["a_r"]
    alpha = rr / (cur + LAMBDA * dd)
    a_r = a_r - alpha * (LAMBDA * a_d)
    return {"rr": rr, "dd": dd, "cur": cur, "a_r": a_r, "a_d": a_d, "alpha": alpha, "beta": beta}


def at(ref, k):
    return ref[k * SUB : (k + 1) * SUB, :]


def save_all(ref, values):
    for k, value in enumerate(values):
        ref[k * SUB : (k + 1) * SUB, :] = value


def numbers_kernel(n_i, slots, first, m, c, ww, *refs):
    msgs = refs[:n_i]
    vec_out, num_out = refs[-2:]
    if first:
        e, v = refs[n_i:-2]
        new = advance(msgs, slots, ww, None)
        v_r, s_r = v[...], -e[...]
        v_d, s_d, gram = v_r, s_r, jnp.zeros((SUB, LANES), F32)
    else:
        v, gram_d, vec, num = refs[n_i:-2]
        new = advance(msgs, slots, ww, numbers_of(num))
        v_r, s_r = v[...], at(vec, 2)
        v_d = v_r + new["beta"] * at(vec, 1)
        s_d = s_r + new["beta"] * at(vec, 3)
        gram = new["beta"] * gram_d[...]
    v_r = v_r - new["alpha"] * (gram + LAMBDA * v_d)
    s_r = s_r - new["alpha"] * (c[...] * v_d + LAMBDA * s_d)
    save_all(vec_out, (v_r, v_d, s_r, s_d, new["a_r"] * m[...] * s_r, gram))
    save_numbers(num_out, new)


def next_kernel(n_f, tiles, row_pick, c, vec, num, *refs):
    got, (msg, *kept) = refs[:n_f], refs[n_f:]
    slots = tiles.shape[0]
    gram = feat_sum([(ref, SUB) for ref in got])
    v = at(vec, 0) - numbers_of(num)["alpha"] * gram
    u = c[...] * v
    by_cols(tiles, row_pick, u, msg)
    write_tail(
        msg, slots, [line_of(at(vec, 4) + at(vec, 2) * v), line_of(u * v), line_of(u * at(vec, 1))]
    )
    for out, value in zip(kept, (v, gram + at(vec, 5))):
        out[...] = value


def dense_kernel(n_i, slots, iters, w, index, *refs):
    msgs = [refs[k * n_i : (k + 1) * n_i] for k in range(iters)]
    nums = [numbers_of(num) for num in refs[iters * n_i : iters * n_i + iters - 1]]
    res_out, dir_out, step_out, curved_out, pick_out = refs[-5:]
    own_blocks = res_out.shape[0]
    line = slot_cols(msgs[0], slots)
    offset = index[0] * own_blocks
    own = (iota((own_blocks, LANES), 0) + offset).astype(F32)
    for a in range(0, line.shape[1], LANES):
        pick_out[:, a : a + LANES] = (own == line[:, a : a + LANES]).astype(F32).astype(BF16)
    mine = w[pl.ds(pl.multiple_of(offset, own_blocks), own_blocks), :]
    res = -LAMBDA * mine - exact_pick(pick_out[...], slot_values(msgs[0], slots))
    step = jnp.zeros_like(res)
    for k in range(iters - 1):
        image = exact_pick(pick_out[...], slot_values(msgs[k + 1], slots))
        if k == 0:
            direction, curved = res, image
        else:
            direction = res + nums[k]["beta"] * direction
            curved = image + nums[k]["beta"] * curved
        step = step + nums[k]["alpha"] * direction
        res = res - nums[k]["alpha"] * (curved + LAMBDA * direction)
    res_out[...] = res
    dir_out[...] = direction
    step_out[...] = step
    curved_out[...] = curved


def last_kernel(n_i, slots, ww, num, res, direction, step, curved, pick, *refs):
    msgs, (step_out, res_out) = refs[:n_i], refs[n_i:]
    image = exact_pick(pick[...], slot_values(msgs, slots))
    new = advance(msgs, slots, ww, numbers_of(num))
    last = res[...] + new["beta"] * direction[...]
    step_out[...] = step[...] + new["alpha"] * last
    image = image + new["beta"] * curved[...] + LAMBDA * last
    res_out[...] = res[...] - new["alpha"] * image


def exchange(x, axis):
    size = lax.axis_size(axis)
    if size & (size - 1) or size > 8:
        return [lax.all_gather(x, axis, axis=0, tiled=True)]
    return [x] + [
        lax.ppermute(x, axis, [(i, i ^ k) for i in range(size)]) for k in range(size - 1, 0, -1)
    ]


def in_hbm(x):
    return pltpu.with_memory_space_constraint(x, pltpu.HBM)


def body(tiles, tile_rows, tile_cols, tile_count, sample_ids, labels, weights):
    slots, edge = tiles.shape[2], tiles.shape[3]
    row_total, feat_len = labels.shape[1], weights.shape[1]
    row_blocks, col_blocks = row_total // edge, feat_len // edge
    assert row_blocks == SUB and edge == LANES and 2 * slots == LANES
    inst = lax.axis_size("inst")
    own_len = feat_len // inst
    own_blocks = own_len // edge
    tiles = tiles.reshape(slots, edge, edge)
    scale = float(row_total) / float(sample_ids.shape[1])
    index = lax.axis_index("inst").astype(I32).reshape(1)
    grid, msg_shape = f32(SUB, LANES), f32(slots + TAIL, LANES)
    tile_shape = jax.ShapeDtypeStruct((slots, edge, edge), BF16)
    picks = jax.ShapeDtypeStruct

    part, tiles, w, row_mask = call(
        start_kernel,
        (
            in_hbm(tile_rows.reshape(slots)),
            in_hbm(tile_cols.reshape(slots)),
            tile_count.reshape(1),
            in_hbm(tiles),
            in_hbm(weights.reshape(col_blocks, edge)),
        ),
        [HBM] * 2 + [ANY] + [HBM] * 2,
        [f32(2 * SUB, LANES), tile_shape, f32(col_blocks, edge), f32(slots * SUB, LANES)],
        scratch=[
            pltpu.SMEM((slots,), I32),
            pltpu.SMEM((slots,), I32),
            pltpu.SMEM((1,), I32),
            pltpu.VMEM((slots, LANES), F32),
            pltpu.VMEM((3 * slots, LANES), F32),
            pltpu.SemaphoreType.DMA((4 + CHUNKS,)),
        ],
    )
    mask, row_pick, cols_line, own = call(
        prep_kernel,
        (
            sample_ids,
            tile_rows.reshape(1, slots),
            tile_cols.reshape(1, slots),
            tile_count.reshape(1, 1),
        ),
        [VM] * 4,
        [grid, picks((slots, LANES), BF16), grid, f32(slots, LANES)],
    )
    (turned,) = call(turn_kernel, (tiles,), [VM], [tile_shape])
    got = exchange(part, "feat")
    n_f = len(got)
    msg, m, c, e, ww = call(
        functools.partial(margin_kernel, n_f, scale),
        (tiles, row_pick, mask, labels.reshape(SUB, LANES), cols_line, *got),
        [VM] * (5 + n_f),
        [msg_shape, grid, grid, grid, grid],
    )
    msgs = exchange(msg, "inst")
    n_i = len(msgs)
    (match,) = call(
        functools.partial(match_kernel, n_i),
        (own, *msgs),
        [VM] * (1 + n_i),
        [picks((slots, slots * inst), BF16)],
    )

    def forward(msgs):
        (out,) = call(
            functools.partial(forward_kernel, n_i),
            (turned, row_mask, match, *msgs),
            [VM] * (3 + n_i),
            [grid],
            scratch=[pltpu.VMEM((3 * slots, LANES), F32)],
        )
        return exchange(out, "feat")

    got = forward(msgs)
    msg, v = call(
        functools.partial(first_kernel, n_f),
        (tiles, row_pick, m, c, e, *got),
        [VM] * (5 + n_f),
        [msg_shape, grid],
    )
    history = [msgs, exchange(msg, "inst")]
    state, nums = (e, v), []
    for k in range(ITERS - 1):
        got = forward(history[-1])
        vec, num = call(
            functools.partial(numbers_kernel, n_i, slots, k == 0),
            (m, c, ww, *history[-1], *state),
            [VM] * (3 + n_i + len(state)),
            [f32(6 * SUB, LANES), grid],
        )
        msg, *kept = call(
            functools.partial(next_kernel, n_f),
            (tiles, row_pick, c, vec, num, *got),
            [VM] * (5 + n_f),
            [msg_shape] + [grid, grid] * (k < ITERS - 2),
        )
        history.append(exchange(msg, "inst"))
        state = (*kept, vec, num)
        nums.append(num)
    block = f32(own_blocks, edge)
    *dense, pick = call(
        functools.partial(dense_kernel, n_i, slots, ITERS),
        (w, index, *(ref for group in history[:ITERS] for ref in group), *nums),
        [VM, SM] + [VM] * (n_i * ITERS + len(nums)),
        [block, block, block, block, picks((own_blocks, slots * inst), BF16)],
    )
    step, res = call(
        functools.partial(last_kernel, n_i, slots),
        (ww, nums[-1], *dense, pick, *history[-1]),
        [VM] * (7 + n_i),
        [block, block],
    )
    return step.reshape(1, own_len), res.reshape(1, own_len)


def solution(mesh):
    return jax.shard_map(
        body,
        mesh=mesh,
        in_specs=(
            P(("groups", "inst"), "feat", None, None, None),
            P(("groups", "inst"), "feat", None),
            P(("groups", "inst"), "feat", None),
            P(("groups", "inst"), "feat"),
            P(("groups", "inst"), None),
            P(("groups", "inst"), None),
            P(("groups", "feat"), None),
        ),
        out_specs=(P(("groups", "feat"), "inst"), P(("groups", "feat"), "inst")),
        check_vma=False,
    )
```

time: 544 us -> 57.9 us (0.11)
  waiting for transfers between devices: 280 us -> 19.8 us
  blocking collectives: 185 us -> 0 us
  starting transfers between devices: 0.29 us -> 26.7 us
  other arithmetic: 25.8 us -> 0 us
  matrix products: 21.8 us -> 0 us
  between operations: 22.1 us -> 1.45 us
  Pallas kernels: 0 us -> 9.78 us
  local copies, waits for them, and re-layouts: 7.91 us -> 0.02 us
    unnamed x11 -> x0, waiting for transfers between devices: 203 us -> none
    psum x9 -> x0, blocking collectives: 185 us -> none  [the longest x2 64.8 us: body(): curvature = lax.psum(jnp.sum(own_dir * image), ('inst', 'feat'))]
    all_gather x3 -> x0, waiting for transfers between devices: 77.6 us -> none  [body(): whole = lax.all_gather(direction, 'inst', axis=0, tiled=True)]
    ppermute x0 -> x24, starting transfers between devices: none -> 26.7 us  [exchange(): lax.ppermute(x, axis, [(i, i ^ k) for i in range(size)])]
    dot_general x16 -> x0, matrix products: 21.8 us -> none  [the longest x4 13.3 us: forward_picked(): jnp.einsum('tij,tj->ti', blocks, picked, precision=lax.Precision.HIGHEST)]
    ppermute x0 -> x24, waiting for transfers between devices: none -> 19.8 us  [exchange(): lax.ppermute(x, axis, [(i, i ^ k) for i in range(size)])]
    reduce_sum x6 -> x0, other arithmetic: 10.6 us -> none  [the longest x3 4.95 us: body(): curvature = lax.psum(jnp.sum(own_dir * image), ('inst', 'feat'))]
    pallas_call x0 -> x15, Pallas kernels: none -> 9.78 us  [call(): pl.pallas_call(kernel, in_specs=in_specs, out_shape=outs, out_specs=out_s...]
  transfers between devices with their start and end apart: 7 -> 24, of which waited for: 7 -> 17; matrix products, arithmetic and copies ran while one was open for 0% -> 0% of each run, Pallas kernels for 0% -> 3%
where the time goes in v2:
time: 57.9 us; the launch traced here: 57.8 us
  starting transfers between devices  26.7 us (46%)
  waiting for transfers between devices  19.8 us (34%)
  Pallas kernels  9.78 us (17%)
  between operations  1.45 us (3%)
    ppermute x24, starting transfers between devices, exchange(): lax.ppermute(x, axis, [(i, i ^ k) for i in range(size)])  26.7 us
    ppermute x24, waiting for transfers between devices, exchange(): lax.ppermute(x, axis, [(i, i ^ k) for i in range(size)])  19.8 us
    pallas_call x15, Pallas kernels, call(): pl.pallas_call(kernel, in_specs=in_specs, out_shape=outs, out_specs=out_s...  9.78 us
  transfers between devices with their start and end apart: 24, of which 17 were waited for; matrix products, arithmetic and copies ran while one was open for 0% of the time, Pallas kernels for 3%

profile of v2, /device:TPU:0, one launch (start us, length us, event | category | flops | bytes accessed | tf_op | source)
XLA Modules:
  0.0 57.8 jit_solution(9066755549478178965)
XLA Ops:
  0.6 0.0 copy-start.1
  0.6 0.0 copy-start.2
  1.3 3.0 %shard_map.86 = (f32[16,128]{1,0:T(8,128)S(1)}, bf16[64,128,128]{2,1,0:T(8,128)(2,1)S(1)}, f32[2048,128]{1,0:T(8,128)S(1)}, f32[512,128]{1,0:T(8,128)S(1)}) custom-call(s32[64]{0:T(128)} %bitcast.13, s32[64]{0:T(128)} %bitcast.15, s32[1]{0:T(128)} %bitcast.11.count_hbm, bf16[64,128,128]{2,1,0:T(8,128)(2,1)} %bitcast.17, f32[2048,128]{1,0:T(8,128)} %bitcast.18), custom_call_target="tpu_custom_call" | custom-call | flops 2097152 | bytes 1048576 | tf_op jit(solution)/shard_map/pallas_call | solution.py:26
  4.4 2.4 %collective-permute-start = (f32[16,128]{1,0:T(8,128)S(1)}, f32[16,128]{1,0:T(8,128)S(1)}, u32[]{:S(2)}, u32[]{:S(2)}) collective-permute-start(f32[16,128]{1,0:T(8,128)S(1)} %get-tuple-element.35.refs_0_), channel_id=1, source_target_pairs={{0,3},{1,2},{2,1},{3,0},{4,7},{5,6},{6,5},{7,4},{8,11},{9,10},{10,... | collective-permute-start | bytes 24584 | tf_op jit(solution)/shard_map/ppermute | solution.py:410
  6.8 0.6 %collective-permute-start.1 = (f32[16,128]{1,0:T(8,128)S(1)}, f32[16,128]{1,0:T(8,128)S(1)}, u32[]{:S(2)}, u32[]{:S(2)}) collective-permute-start(f32[16,128]{1,0:T(8,128)S(1)} %get-tuple-element.35.refs_0_), channel_id=1, source_target_pairs={{0,2},{1,3},{2,0},{3,1},{4,6},{5,7},{6,4},{7,5},{8,10},{9,11},{10,... | collective-permute-start | bytes 24584 | tf_op jit(solution)/shard_map/ppermute | solution.py:410
  7.5 0.0 collective-permute-start.2
  7.5 0.2 shard_map.87
  7.8 0.4 collective-permute-done.refs_1_
  8.2 2.3 %collective-permute-done.1.refs_2_ = f32[16,128]{1,0:T(8,128)S(1)} collective-permute-done((f32[16,128]{1,0:T(8,128)S(1)}, f32[16,128]{1,0:T(8,128)S(1)}, u32[]{:S(2)}, u32[]{:S(2)}) %collective-permute-start.1) | collective-permute-done | bytes 8224 | tf_op jit(solution)/shard_map/ppermute | solution.py:410
  10.5 0.0 collective-permute-done.2.refs_3_
  10.5 0.5 shard_map.88
  11.0 3.7 %collective-permute-start.3 = (f32[72,128]{1,0:T(8,128)S(1)}, f32[72,128]{1,0:T(8,128)S(1)}, u32[]{:S(2)}, u32[]{:S(2)}) collective-permute-start(f32[72,128]{1,0:T(8,128)S(1)} %get-tuple-element.42.refs_0_), channel_id=1, source_target_pairs={{0,12},{4,8},{8,4},{12,0},{1,13},{5,9},{9,5},{13,1},{2,14},{6,10},... | collective-permute-start | bytes 110600 | tf_op jit(solution)/shard_map/ppermute | solution.py:410
  14.7 0.0 collective-permute-start.4
  14.7 0.8 %collective-permute-start.5 = (f32[72,128]{1,0:T(8,128)S(1)}, f32[72,128]{1,0:T(8,128)S(1)}, u32[]{:S(2)}, u32[]{:S(2)}) collective-permute-start(f32[72,128]{1,0:T(8,128)S(1)} %get-tuple-element.42.refs_0_), channel_id=1, source_target_pairs={{0,4},{4,0},{8,12},{12,8},{1,5},{5,1},{9,13},{13,9},{2,6},{6,2},{1... | collective-permute-start | bytes 110600 | tf_op jit(solution)/shard_map/ppermute | solution.py:410
  15.5 0.6 %shard_map.89.turned = bf16[64,128,128]{2,1,0:T(8,128)(2,1)S(1)} custom-call(bf16[64,128,128]{2,1,0:T(8,128)(2,1)S(1)} %get-tuple-element.31.tiles), custom_call_target="tpu_custom_call" | custom-call | flops 2097152 | bytes 1048576 | tf_op jit(solution)/shard_map/pallas_call | solution.py:26
  16.1 1.2 %collective-permute-done.3.refs_1_ = f32[72,128]{1,0:T(8,128)S(1)} collective-permute-done((f32[72,128]{1,0:T(8,128)S(1)}, f32[72,128]{1,0:T(8,128)S(1)}, u32[]{:S(2)}, u32[]{:S(2)}) %collective-permute-start.3) | collective-permute-done | bytes 36896 | tf_op jit(solution)/shard_map/ppermute | solution.py:410
  17.3 2.3 %collective-permute-done.4.refs_2_ = f32[72,128]{1,0:T(8,128)S(1)} collective-permute-done((f32[72,128]{1,0:T(8,128)S(1)}, f32[72,128]{1,0:T(8,128)S(1)}, u32[]{:S(2)}, u32[]{:S(2)}) %collective-permute-start.4) | collective-permute-done | bytes 36896 | tf_op jit(solution)/shard_map/ppermute | solution.py:410
  19.5 0.0 collective-permute-done.5.refs_3_
  19.6 0.6 %shard_map.91.refs_0_ = f32[8,128]{1,0:T(8,128)S(1)} custom-call(bf16[64,128,128]{2,1,0:T(8,128)(2,1)S(1)} %shard_map.89.turned, f32[512,128]{1,0:T(8,128)S(1)} %get-tuple-element.40.row_mask, bf16[64,256]{1,0:T(8,128)(2,1)S(1)} %shard_map.90.match, f32[72,128]{1,0:T(8,128)S(1)} %get-tuple-element.42.refs_0_, f32[72,128]{1,0:T(8,128)S(1)} %collective-permute-done.3.refs_1_, ...), custom_call_target="tpu_custom_call" | custom-call | flops 2097152 | bytes 1048576 | tf_op jit(solution)/shard_map/pallas_call | solution.py:26
  20.1 0.1 collective-permute-start.6
  20.2 0.7 %collective-permute-start.7 = (f32[8,128]{1,0:T(8,128)S(1)}, f32[8,128]{1,0:T(8,128)S(1)}, u32[]{:S(2)}, u32[]{:S(2)}) collective-permute-start(f32[8,128]{1,0:T(8,128)S(1)} %shard_map.91.refs_0_), channel_id=1, source_target_pairs={{0,2},{1,3},{2,0},{3,1},{4,6},{5,7},{6,4},{7,5},{8,10},{9,11},{10,... | collective-permute-start | bytes 12296 | tf_op jit(solution)/shard_map/ppermute | solution.py:410
  20.9 1.1 %collective-permute-start.8 = (f32[8,128]{1,0:T(8,128)S(1)}, f32[8,128]{1,0:T(8,128)S(1)}, u32[]{:S(2)}, u32[]{:S(2)}) collective-permute-start(f32[8,128]{1,0:T(8,128)S(1)} %shard_map.91.refs_0_), channel_id=1, source_target_pairs={{0,1},{1,0},{2,3},{3,2},{4,5},{5,4},{6,7},{7,6},{8,9},{9,8},{10,11... | collective-permute-start | bytes 12296 | tf_op jit(solution)/shard_map/ppermute | solution.py:410
  22.1 1.2 %collective-permute-done.6.refs_1_ = f32[8,128]{1,0:T(8,128)S(1)} collective-permute-done((f32[8,128]{1,0:T(8,128)S(1)}, f32[8,128]{1,0:T(8,128)S(1)}, u32[]{:S(2)}, u32[]{:S(2)}) %collective-permute-start.6) | collective-permute-done | bytes 4128 | tf_op jit(solution)/shard_map/ppermute | solution.py:410
  23.2 0.7 %collective-permute-done.7.refs_2_ = f32[8,128]{1,0:T(8,128)S(1)} collective-permute-done((f32[8,128]{1,0:T(8,128)S(1)}, f32[8,128]{1,0:T(8,128)S(1)}, u32[]{:S(2)}, u32[]{:S(2)}) %collective-permute-start.7) | collective-permute-done | bytes 4128 | tf_op jit(solution)/shard_map/ppermute | solution.py:410
  23.9 0.0 collective-permute-done.8.refs_3_
  23.9 0.5 shard_map.92
  24.4 2.1 %collective-permute-start.10 = (f32[72,128]{1,0:T(8,128)S(1)}, f32[72,128]{1,0:T(8,128)S(1)}, u32[]{:S(2)}, u32[]{:S(2)}) collective-permute-start(f32[72,128]{1,0:T(8,128)S(1)} %get-tuple-element.43.refs_0_.refs_4_), channel_id=1, source_target_pairs={{0,8},{4,12},{8,0},{12,4},{1,9},{5,13},{9,1},{13,5},{2,10},{6,14},... | collective-permute-start | bytes 110600 | tf_op jit(solution)/shard_map/ppermute | solution.py:410
  26.5 0.0 collective-permute-start.11
  26.5 2.4 %collective-permute-start.9 = (f32[72,128]{1,0:T(8,128)S(1)}, f32[72,128]{1,0:T(8,128)S(1)}, u32[]{:S(2)}, u32[]{:S(2)}) collective-permute-start(f32[72,128]{1,0:T(8,128)S(1)} %get-tuple-element.43.refs_0_.refs_4_), channel_id=1, source_target_pairs={{0,12},{4,8},{8,4},{12,0},{1,13},{5,9},{9,5},{13,1},{2,14},{6,10},... | collective-permute-start | bytes 110600 | tf_op jit(solution)/shard_map/ppermute | solution.py:410
  28.9 0.5 collective-permute-done.10.refs_2_.refs_6_
  29.4 1.5 %collective-permute-done.11.refs_3_.refs_7_ = f32[72,128]{1,0:T(8,128)S(1)} collective-permute-done((f32[72,128]{1,0:T(8,128)S(1)}, f32[72,128]{1,0:T(8,128)S(1)}, u32[]{:S(2)}, u32[]{:S(2)}) %collective-permute-start.11) | collective-permute-done | bytes 36896 | tf_op jit(solution)/shard_map/ppermute | solution.py:410
  30.9 1.5 %collective-permute-done.9.refs_1_.refs_5_ = f32[72,128]{1,0:T(8,128)S(1)} collective-permute-done((f32[72,128]{1,0:T(8,128)S(1)}, f32[72,128]{1,0:T(8,128)S(1)}, u32[]{:S(2)}, u32[]{:S(2)}) %collective-permute-start.9) | collective-permute-done | bytes 36896 | tf_op jit(solution)/shard_map/ppermute | solution.py:410
  32.3 0.6 %shard_map.94.refs_0_ = f32[8,128]{1,0:T(8,128)S(1)} custom-call(bf16[64,128,128]{2,1,0:T(8,128)(2,1)S(1)} %shard_map.89.turned, f32[512,128]{1,0:T(8,128)S(1)} %get-tuple-element.40.row_mask, bf16[64,256]{1,0:T(8,128)(2,1)S(1)} %shard_map.90.match, f32[72,128]{1,0:T(8,128)S(1)} %get-tuple-element.43.refs_0_.refs_4_, ...), custom_call_target="tpu_custom_call" | custom-call | flops 2097152 | bytes 1048576 | tf_op jit(solution)/shard_map/pallas_call | solution.py:26
  32.9 0.1 collective-permute-start.12
  33.0 0.7 %collective-permute-start.13 = (f32[8,128]{1,0:T(8,128)S(1)}, f32[8,128]{1,0:T(8,128)S(1)}, u32[]{:S(2)}, u32[]{:S(2)}) collective-permute-start(f32[8,128]{1,0:T(8,128)S(1)} %shard_map.94.refs_0_), channel_id=1, source_target_pairs={{0,2},{1,3},{2,0},{3,1},{4,6},{5,7},{6,4},{7,5},{8,10},{9,11},{10,... | collective-permute-start | bytes 12296 | tf_op jit(solution)/shard_map/ppermute | solution.py:410
  33.7 1.1 %collective-permute-start.14 = (f32[8,128]{1,0:T(8,128)S(1)}, f32[8,128]{1,0:T(8,128)S(1)}, u32[]{:S(2)}, u32[]{:S(2)}) collective-permute-start(f32[8,128]{1,0:T(8,128)S(1)} %shard_map.94.refs_0_), channel_id=1, source_target_pairs={{0,1},{1,0},{2,3},{3,2},{4,5},{5,4},{6,7},{7,6},{8,9},{9,8},{10,11... | collective-permute-start | bytes 12296 | tf_op jit(solution)/shard_map/ppermute | solution.py:410
  34.8 0.1 shard_map.93
  35.0 1.0 %collective-permute-done.12.refs_1_ = f32[8,128]{1,0:T(8,128)S(1)} collective-permute-done((f32[8,128]{1,0:T(8,128)S(1)}, f32[8,128]{1,0:T(8,128)S(1)}, u32[]{:S(2)}, u32[]{:S(2)}) %collective-permute-start.12) | collective-permute-done | bytes 4128 | tf_op jit(solution)/shard_map/ppermute | solution.py:410
  36.0 0.7 %collective-permute-done.13.refs_2_ = f32[8,128]{1,0:T(8,128)S(1)} collective-permute-done((f32[8,128]{1,0:T(8,128)S(1)}, f32[8,128]{1,0:T(8,128)S(1)}, u32[]{:S(2)}, u32[]{:S(2)}) %collective-permute-start.13) | collective-permute-done | bytes 4128 | tf_op jit(solution)/shard_map/ppermute | solution.py:410
  36.7 0.0 collective-permute-done.14.refs_3_
  36.7 0.6 shard_map.95
  37.2 2.4 %collective-permute-start.15 = (f32[72,128]{1,0:T(8,128)S(1)}, f32[72,128]{1,0:T(8,128)S(1)}, u32[]{:S(2)}, u32[]{:S(2)}) collective-permute-start(f32[72,128]{1,0:T(8,128)S(1)} %get-tuple-element.47.refs_0_.refs_8_), channel_id=1, source_target_pairs={{0,12},{4,8},{8,4},{12,0},{1,13},{5,9},{9,5},{13,1},{2,14},{6,10},... | collective-permute-start | bytes 110600 | tf_op jit(solution)/shard_map/ppermute | solution.py:410
  39.6 0.0 collective-permute-start.16
  39.6 2.1 %collective-permute-start.17 = (f32[72,128]{1,0:T(8,128)S(1)}, f32[72,128]{1,0:T(8,128)S(1)}, u32[]{:S(2)}, u32[]{:S(2)}) collective-permute-start(f32[72,128]{1,0:T(8,128)S(1)} %get-tuple-element.47.refs_0_.refs_8_), channel_id=1, source_target_pairs={{0,4},{4,0},{8,12},{12,8},{1,5},{5,1},{9,13},{13,9},{2,6},{6,2},{1... | collective-permute-start | bytes 110600 | tf_op jit(solution)/shard_map/ppermute | solution.py:410
  41.7 1.4 %collective-permute-done.15.refs_1_.refs_9_ = f32[72,128]{1,0:T(8,128)S(1)} collective-permute-done((f32[72,128]{1,0:T(8,128)S(1)}, f32[72,128]{1,0:T(8,128)S(1)}, u32[]{:S(2)}, u32[]{:S(2)}) %collective-permute-start.15) | collective-permute-done | bytes 36896 | tf_op jit(solution)/shard_map/ppermute | solution.py:410
  43.1 1.3 %collective-permute-done.16.refs_2_.refs_10_ = f32[72,128]{1,0:T(8,128)S(1)} collective-permute-done((f32[72,128]{1,0:T(8,128)S(1)}, f32[72,128]{1,0:T(8,128)S(1)}, u32[]{:S(2)}, u32[]{:S(2)}) %collective-permute-start.16) | collective-permute-done | bytes 36896 | tf_op jit(solution)/shard_map/ppermute | solution.py:410
  44.5 0.0 collective-permute-done.17.refs_3_.refs_11_
  44.5 0.6 %shard_map.98.refs_0_ = f32[8,128]{1,0:T(8,128)S(1)} custom-call(bf16[64,128,128]{2,1,0:T(8,128)(2,1)S(1)} %shard_map.89.turned, f32[512,128]{1,0:T(8,128)S(1)} %get-tuple-element.40.row_mask, bf16[64,256]{1,0:T(8,128)(2,1)S(1)} %shard_map.90.match, f32[72,128]{1,0:T(8,128)S(1)} %get-tuple-element.47.refs_0_.refs_8_, ...), custom_call_target="tpu_custom_call" | custom-call | flops 2097152 | bytes 1048576 | tf_op jit(solution)/shard_map/pallas_call | solution.py:26
  45.0 0.1 collective-permute-start.18
  45.1 0.7 %collective-permute-start.19 = (f32[8,128]{1,0:T(8,128)S(1)}, f32[8,128]{1,0:T(8,128)S(1)}, u32[]{:S(2)}, u32[]{:S(2)}) collective-permute-start(f32[8,128]{1,0:T(8,128)S(1)} %shard_map.98.refs_0_), channel_id=1, source_target_pairs={{0,2},{1,3},{2,0},{3,1},{4,6},{5,7},{6,4},{7,5},{8,10},{9,11},{10,... | collective-permute-start | bytes 12296 | tf_op jit(solution)/shard_map/ppermute | solution.py:410
  45.8 1.1 %collective-permute-start.20 = (f32[8,128]{1,0:T(8,128)S(1)}, f32[8,128]{1,0:T(8,128)S(1)}, u32[]{:S(2)}, u32[]{:S(2)}) collective-permute-start(f32[8,128]{1,0:T(8,128)S(1)} %shard_map.98.refs_0_), channel_id=1, source_target_pairs={{0,1},{1,0},{2,3},{3,2},{4,5},{5,4},{6,7},{7,6},{8,9},{9,8},{10,11... | collective-permute-start | bytes 12296 | tf_op jit(solution)/shard_map/ppermute | solution.py:410
  47.0 0.2 shard_map.96
  47.2 0.9 %collective-permute-done.18.refs_1_ = f32[8,128]{1,0:T(8,128)S(1)} collective-permute-done((f32[8,128]{1,0:T(8,128)S(1)}, f32[8,128]{1,0:T(8,128)S(1)}, u32[]{:S(2)}, u32[]{:S(2)}) %collective-permute-start.18) | collective-permute-done | bytes 4128 | tf_op jit(solution)/shard_map/ppermute | solution.py:410
  48.1 0.7 %collective-permute-done.19.refs_2_ = f32[8,128]{1,0:T(8,128)S(1)} collective-permute-done((f32[8,128]{1,0:T(8,128)S(1)}, f32[8,128]{1,0:T(8,128)S(1)}, u32[]{:S(2)}, u32[]{:S(2)}) %collective-permute-start.19) | collective-permute-done | bytes 4128 | tf_op jit(solution)/shard_map/ppermute | solution.py:410
  48.8 0.0 collective-permute-done.20.refs_3_
  48.8 0.6 shard_map.99.refs_0_
  49.4 2.4 %collective-permute-start.21 = (f32[72,128]{1,0:T(8,128)S(1)}, f32[72,128]{1,0:T(8,128)S(1)}, u32[]{:S(2)}, u32[]{:S(2)}) collective-permute-start(f32[72,128]{1,0:T(8,128)S(1)} %shard_map.99.refs_0_), channel_id=1, source_target_pairs={{0,12},{4,8},{8,4},{12,0},{1,13},{5,9},{9,5},{13,1},{2,14},{6,10},... | collective-permute-start | bytes 110600 | tf_op jit(solution)/shard_map/ppermute | solution.py:410
  51.8 0.3 collective-permute-start.22
  52.1 1.7 %collective-permute-start.23 = (f32[72,128]{1,0:T(8,128)S(1)}, f32[72,128]{1,0:T(8,128)S(1)}, u32[]{:S(2)}, u32[]{:S(2)}) collective-permute-start(f32[72,128]{1,0:T(8,128)S(1)} %shard_map.99.refs_0_), channel_id=1, source_target_pairs={{0,4},{4,0},{8,12},{12,8},{1,5},{5,1},{9,13},{13,9},{2,6},{6,2},{1... | collective-permute-start | bytes 110600 | tf_op jit(solution)/shard_map/ppermute | solution.py:410
  53.8 0.6 %shard_map.97 = (f32[512,128]{1,0:T(8,128)S(1)}, f32[512,128]{1,0:T(8,128)S(1)}, f32[512,128]{1,0:T(8,128)S(1)}, f32[512,128]{1,0:T(8,128)S(1)}, bf16[512,256]{1,0:T(8,128)(2,1)S(1)}) custom-call(f32[2048,128]{1,0:T(8,128)S(1)} %get-tuple-element.51.w, s32[1]{0:T(128)} %bitcast.8.index, f32[72,128]{1,0:T(8,128)S(1)} %get-tuple-element.42.refs_0_, ...), custom_call_target="tpu_custom_call" | custom-call | flops 2097152 | bytes 1048576 | tf_op jit(solution)/shard_map/pallas_call | solution.py:26
  54.4 0.8 %collective-permute-done.21.refs_1_ = f32[72,128]{1,0:T(8,128)S(1)} collective-permute-done((f32[72,128]{1,0:T(8,128)S(1)}, f32[72,128]{1,0:T(8,128)S(1)}, u32[]{:S(2)}, u32[]{:S(2)}) %collective-permute-start.21) | collective-permute-done | bytes 36896 | tf_op jit(solution)/shard_map/ppermute | solution.py:410
  55.2 1.5 %collective-permute-done.22.refs_2_ = f32[72,128]{1,0:T(8,128)S(1)} collective-permute-done((f32[72,128]{1,0:T(8,128)S(1)}, f32[72,128]{1,0:T(8,128)S(1)}, u32[]{:S(2)}, u32[]{:S(2)}) %collective-permute-start.22) | collective-permute-done | bytes 36896 | tf_op jit(solution)/shard_map/ppermute | solution.py:410
  56.7 0.0 collective-permute-done.23.refs_3_
  56.7 1.0 %shard_map.100 = (f32[512,128]{1,0:T(8,128)}, f32[512,128]{1,0:T(8,128)}) custom-call(f32[8,128]{1,0:T(8,128)S(1)} %get-tuple-element.36.ww, f32[8,128]{1,0:T(8,128)S(1)} %get-tuple-element.50.refs_13_.num, f32[512,128]{1,0:T(8,128)S(1)} %get-tuple-element.52.res, f32[512,128]{1,0:T(8,128)S(1)} %get-tuple-element.53.direction, ...), custom_call_target="tpu_custom_call" | custom-call | flops 2097152 | bytes 1048576 | tf_op jit(solution)/shard_map/pallas_call | solution.py:26
  (7 shorter events, 0.0 us)
Async XLA Ops:
  0.6 6.9 %copy-start.1 = (s32[1,1,64]{2,1,0:T(1,128)S(1)}, s32[1,1,64]{2,1,0:T(1,128)}, u32[]{:S(2)}) copy-start(s32[1,1,64]{2,1,0:T(1,128)} %param.8) | copy-start | bytes 772
  0.6 6.9 %copy-start.2 = (s32[1,1,64]{2,1,0:T(1,128)S(1)}, s32[1,1,64]{2,1,0:T(1,128)}, u32[]{:S(2)}) copy-start(s32[1,1,64]{2,1,0:T(1,128)} %param.9) | copy-start | bytes 772
  0.7 6.9 %copy-start.3 = (s32[1,512]{1,0:T(1,128)S(1)}, s32[1,512]{1,0:T(1,128)}, u32[]{:S(2)}) copy-start(s32[1,512]{1,0:T(1,128)} %ids.1) | copy-start | bytes 6148
  0.7 9.8 %copy-start = (s32[1,1024]{1,0:T(1,128)S(1)}, s32[1,1024]{1,0:T(1,128)}, u32[]{:S(2)}) copy-start(s32[1,1024]{1,0:T(1,128)} %param.12) | copy-start | bytes 12292
  4.4 3.8 %collective-permute-start = (f32[16,128]{1,0:T(8,128)S(1)}, f32[16,128]{1,0:T(8,128)S(1)}, u32[]{:S(2)}, u32[]{:S(2)}) collective-permute-start(f32[16,128]{1,0:T(8,128)S(1)} %get-tuple-element.35.refs_0_), channel_id=1, source_target_pairs={{0,3},{1,2},{2,1},{3,0},{4,7},{5,6},{6,5},{7,4},{8,11},{9,10},{10,... | collective-permute-start | bytes 24584 | tf_op jit(solution)/shard_map/ppermute | solution.py:410
  6.8 3.7 %collective-permute-start.1 = (f32[16,128]{1,0:T(8,128)S(1)}, f32[16,128]{1,0:T(8,128)S(1)}, u32[]{:S(2)}, u32[]{:S(2)}) collective-permute-start(f32[16,128]{1,0:T(8,128)S(1)} %get-tuple-element.35.refs_0_), channel_id=1, source_target_pairs={{0,2},{1,3},{2,0},{3,1},{4,6},{5,7},{6,4},{7,5},{8,10},{9,11},{10,... | collective-permute-start | bytes 24584 | tf_op jit(solution)/shard_map/ppermute | solution.py:410
  7.5 3.0 %collective-permute-start.2 = (f32[16,128]{1,0:T(8,128)S(1)}, f32[16,128]{1,0:T(8,128)S(1)}, u32[]{:S(2)}, u32[]{:S(2)}) collective-permute-start(f32[16,128]{1,0:T(8,128)S(1)} %get-tuple-element.35.refs_0_), channel_id=1, source_target_pairs={{0,1},{1,0},{2,3},{3,2},{4,5},{5,4},{6,7},{7,6},{8,9},{9,8},{10,11... | collective-permute-start | bytes 24584 | tf_op jit(solution)/shard_map/ppermute | solution.py:410
  11.0 6.3 %collective-permute-start.3 = (f32[72,128]{1,0:T(8,128)S(1)}, f32[72,128]{1,0:T(8,128)S(1)}, u32[]{:S(2)}, u32[]{:S(2)}) collective-permute-start(f32[72,128]{1,0:T(8,128)S(1)} %get-tuple-element.42.refs_0_), channel_id=1, source_target_pairs={{0,12},{4,8},{8,4},{12,0},{1,13},{5,9},{9,5},{13,1},{2,14},{6,10},... | collective-permute-start | bytes 110600 | tf_op jit(solution)/shard_map/ppermute | solution.py:410
  14.7 4.9 %collective-permute-start.4 = (f32[72,128]{1,0:T(8,128)S(1)}, f32[72,128]{1,0:T(8,128)S(1)}, u32[]{:S(2)}, u32[]{:S(2)}) collective-permute-start(f32[72,128]{1,0:T(8,128)S(1)} %get-tuple-element.42.refs_0_), channel_id=1, source_target_pairs={{0,8},{4,12},{8,0},{12,4},{1,9},{5,13},{9,1},{13,5},{2,10},{6,14},... | collective-permute-start | bytes 110600 | tf_op jit(solution)/shard_map/ppermute | solution.py:410
  14.7 4.9 %collective-permute-start.5 = (f32[72,128]{1,0:T(8,128)S(1)}, f32[72,128]{1,0:T(8,128)S(1)}, u32[]{:S(2)}, u32[]{:S(2)}) collective-permute-start(f32[72,128]{1,0:T(8,128)S(1)} %get-tuple-element.42.refs_0_), channel_id=1, source_target_pairs={{0,4},{4,0},{8,12},{12,8},{1,5},{5,1},{9,13},{13,9},{2,6},{6,2},{1... | collective-permute-start | bytes 110600 | tf_op jit(solution)/shard_map/ppermute | solution.py:410
  20.1 3.1 %collective-permute-start.6 = (f32[8,128]{1,0:T(8,128)S(1)}, f32[8,128]{1,0:T(8,128)S(1)}, u32[]{:S(2)}, u32[]{:S(2)}) collective-permute-start(f32[8,128]{1,0:T(8,128)S(1)} %shard_map.91.refs_0_), channel_id=1, source_target_pairs={{0,3},{1,2},{2,1},{3,0},{4,7},{5,6},{6,5},{7,4},{8,11},{9,10},{10,... | collective-permute-start | bytes 12296 | tf_op jit(solution)/shard_map/ppermute | solution.py:410
  20.2 3.7 %collective-permute-start.7 = (f32[8,128]{1,0:T(8,128)S(1)}, f32[8,128]{1,0:T(8,128)S(1)}, u32[]{:S(2)}, u32[]{:S(2)}) collective-permute-start(f32[8,128]{1,0:T(8,128)S(1)} %shard_map.91.refs_0_), channel_id=1, source_target_pairs={{0,2},{1,3},{2,0},{3,1},{4,6},{5,7},{6,4},{7,5},{8,10},{9,11},{10,... | collective-permute-start | bytes 12296 | tf_op jit(solution)/shard_map/ppermute | solution.py:410
  20.9 3.0 %collective-permute-start.8 = (f32[8,128]{1,0:T(8,128)S(1)}, f32[8,128]{1,0:T(8,128)S(1)}, u32[]{:S(2)}, u32[]{:S(2)}) collective-permute-start(f32[8,128]{1,0:T(8,128)S(1)} %shard_map.91.refs_0_), channel_id=1, source_target_pairs={{0,1},{1,0},{2,3},{3,2},{4,5},{5,4},{6,7},{7,6},{8,9},{9,8},{10,11... | collective-permute-start | bytes 12296 | tf_op jit(solution)/shard_map/ppermute | solution.py:410
  24.4 4.9 %collective-permute-start.10 = (f32[72,128]{1,0:T(8,128)S(1)}, f32[72,128]{1,0:T(8,128)S(1)}, u32[]{:S(2)}, u32[]{:S(2)}) collective-permute-start(f32[72,128]{1,0:T(8,128)S(1)} %get-tuple-element.43.refs_0_.refs_4_), channel_id=1, source_target_pairs={{0,8},{4,12},{8,0},{12,4},{1,9},{5,13},{9,1},{13,5},{2,10},{6,14},... | collective-permute-start | bytes 110600 | tf_op jit(solution)/shard_map/ppermute | solution.py:410
  26.5 4.4 %collective-permute-start.11 = (f32[72,128]{1,0:T(8,128)S(1)}, f32[72,128]{1,0:T(8,128)S(1)}, u32[]{:S(2)}, u32[]{:S(2)}) collective-permute-start(f32[72,128]{1,0:T(8,128)S(1)} %get-tuple-element.43.refs_0_.refs_4_), channel_id=1, source_target_pairs={{0,4},{4,0},{8,12},{12,8},{1,5},{5,1},{9,13},{13,9},{2,6},{6,2},{1... | collective-permute-start | bytes 110600 | tf_op jit(solution)/shard_map/ppermute | solution.py:410
  26.5 5.8 %collective-permute-start.9 = (f32[72,128]{1,0:T(8,128)S(1)}, f32[72,128]{1,0:T(8,128)S(1)}, u32[]{:S(2)}, u32[]{:S(2)}) collective-permute-start(f32[72,128]{1,0:T(8,128)S(1)} %get-tuple-element.43.refs_0_.refs_4_), channel_id=1, source_target_pairs={{0,12},{4,8},{8,4},{12,0},{1,13},{5,9},{9,5},{13,1},{2,14},{6,10},... | collective-permute-start | bytes 110600 | tf_op jit(solution)/shard_map/ppermute | solution.py:410
  32.9 3.1 %collective-permute-start.12 = (f32[8,128]{1,0:T(8,128)S(1)}, f32[8,128]{1,0:T(8,128)S(1)}, u32[]{:S(2)}, u32[]{:S(2)}) collective-permute-start(f32[8,128]{1,0:T(8,128)S(1)} %shard_map.94.refs_0_), channel_id=1, source_target_pairs={{0,3},{1,2},{2,1},{3,0},{4,7},{5,6},{6,5},{7,4},{8,11},{9,10},{10,... | collective-permute-start | bytes 12296 | tf_op jit(solution)/shard_map/ppermute | solution.py:410
  33.0 3.7 %collective-permute-start.13 = (f32[8,128]{1,0:T(8,128)S(1)}, f32[8,128]{1,0:T(8,128)S(1)}, u32[]{:S(2)}, u32[]{:S(2)}) collective-permute-start(f32[8,128]{1,0:T(8,128)S(1)} %shard_map.94.refs_0_), channel_id=1, source_target_pairs={{0,2},{1,3},{2,0},{3,1},{4,6},{5,7},{6,4},{7,5},{8,10},{9,11},{10,... | collective-permute-start | bytes 12296 | tf_op jit(solution)/shard_map/ppermute | solution.py:410
  33.7 3.0 %collective-permute-start.14 = (f32[8,128]{1,0:T(8,128)S(1)}, f32[8,128]{1,0:T(8,128)S(1)}, u32[]{:S(2)}, u32[]{:S(2)}) collective-permute-start(f32[8,128]{1,0:T(8,128)S(1)} %shard_map.94.refs_0_), channel_id=1, source_target_pairs={{0,1},{1,0},{2,3},{3,2},{4,5},{5,4},{6,7},{7,6},{8,9},{9,8},{10,11... | collective-permute-start | bytes 12296 | tf_op jit(solution)/shard_map/ppermute | solution.py:410
  37.2 5.9 %collective-permute-start.15 = (f32[72,128]{1,0:T(8,128)S(1)}, f32[72,128]{1,0:T(8,128)S(1)}, u32[]{:S(2)}, u32[]{:S(2)}) collective-permute-start(f32[72,128]{1,0:T(8,128)S(1)} %get-tuple-element.47.refs_0_.refs_8_), channel_id=1, source_target_pairs={{0,12},{4,8},{8,4},{12,0},{1,13},{5,9},{9,5},{13,1},{2,14},{6,10},... | collective-permute-start | bytes 110600 | tf_op jit(solution)/shard_map/ppermute | solution.py:410
  39.6 4.9 %collective-permute-start.16 = (f32[72,128]{1,0:T(8,128)S(1)}, f32[72,128]{1,0:T(8,128)S(1)}, u32[]{:S(2)}, u32[]{:S(2)}) collective-permute-start(f32[72,128]{1,0:T(8,128)S(1)} %get-tuple-element.47.refs_0_.refs_8_), channel_id=1, source_target_pairs={{0,8},{4,12},{8,0},{12,4},{1,9},{5,13},{9,1},{13,5},{2,10},{6,14},... | collective-permute-start | bytes 110600 | tf_op jit(solution)/shard_map/ppermute | solution.py:410
  39.6 4.9 %collective-permute-start.17 = (f32[72,128]{1,0:T(8,128)S(1)}, f32[72,128]{1,0:T(8,128)S(1)}, u32[]{:S(2)}, u32[]{:S(2)}) collective-permute-start(f32[72,128]{1,0:T(8,128)S(1)} %get-tuple-element.47.refs_0_.refs_8_), channel_id=1, source_target_pairs={{0,4},{4,0},{8,12},{12,8},{1,5},{5,1},{9,13},{13,9},{2,6},{6,2},{1... | collective-permute-start | bytes 110600 | tf_op jit(solution)/shard_map/ppermute | solution.py:410
  45.0 3.1 %collective-permute-start.18 = (f32[8,128]{1,0:T(8,128)S(1)}, f32[8,128]{1,0:T(8,128)S(1)}, u32[]{:S(2)}, u32[]{:S(2)}) collective-permute-start(f32[8,128]{1,0:T(8,128)S(1)} %shard_map.98.refs_0_), channel_id=1, source_target_pairs={{0,3},{1,2},{2,1},{3,0},{4,7},{5,6},{6,5},{7,4},{8,11},{9,10},{10,... | collective-permute-start | bytes 12296 | tf_op jit(solution)/shard_map/ppermute | solution.py:410
  45.1 3.7 %collective-permute-start.19 = (f32[8,128]{1,0:T(8,128)S(1)}, f32[8,128]{1,0:T(8,128)S(1)}, u32[]{:S(2)}, u32[]{:S(2)}) collective-permute-start(f32[8,128]{1,0:T(8,128)S(1)} %shard_map.98.refs_0_), channel_id=1, source_target_pairs={{0,2},{1,3},{2,0},{3,1},{4,6},{5,7},{6,4},{7,5},{8,10},{9,11},{10,... | collective-permute-start | bytes 12296 | tf_op jit(solution)/shard_map/ppermute | solution.py:410
  45.8 3.0 %collective-permute-start.20 = (f32[8,128]{1,0:T(8,128)S(1)}, f32[8,128]{1,0:T(8,128)S(1)}, u32[]{:S(2)}, u32[]{:S(2)}) collective-permute-start(f32[8,128]{1,0:T(8,128)S(1)} %shard_map.98.refs_0_), channel_id=1, source_target_pairs={{0,1},{1,0},{2,3},{3,2},{4,5},{5,4},{6,7},{7,6},{8,9},{9,8},{10,11... | collective-permute-start | bytes 12296 | tf_op jit(solution)/shard_map/ppermute | solution.py:410
  49.4 5.8 %collective-permute-start.21 = (f32[72,128]{1,0:T(8,128)S(1)}, f32[72,128]{1,0:T(8,128)S(1)}, u32[]{:S(2)}, u32[]{:S(2)}) collective-permute-start(f32[72,128]{1,0:T(8,128)S(1)} %shard_map.99.refs_0_), channel_id=1, source_target_pairs={{0,12},{4,8},{8,4},{12,0},{1,13},{5,9},{9,5},{13,1},{2,14},{6,10},... | collective-permute-start | bytes 110600 | tf_op jit(solution)/shard_map/ppermute | solution.py:410
  51.8 4.9 %collective-permute-start.22 = (f32[72,128]{1,0:T(8,128)S(1)}, f32[72,128]{1,0:T(8,128)S(1)}, u32[]{:S(2)}, u32[]{:S(2)}) collective-permute-start(f32[72,128]{1,0:T(8,128)S(1)} %shard_map.99.refs_0_), channel_id=1, source_target_pairs={{0,8},{4,12},{8,0},{12,4},{1,9},{5,13},{9,1},{13,5},{2,10},{6,14},... | collective-permute-start | bytes 110600 | tf_op jit(solution)/shard_map/ppermute | solution.py:410
  52.1 4.6 %collective-permute-start.23 = (f32[72,128]{1,0:T(8,128)S(1)}, f32[72,128]{1,0:T(8,128)S(1)}, u32[]{:S(2)}, u32[]{:S(2)}) collective-permute-start(f32[72,128]{1,0:T(8,128)S(1)} %shard_map.99.refs_0_), channel_id=1, source_target_pairs={{0,4},{4,0},{8,12},{12,8},{1,5},{5,1},{9,13},{13,9},{2,6},{6,2},{1... | collective-permute-start | bytes 110600 | tf_op jit(solution)/shard_map/ppermute | solution.py:410

commit v3 on v2

--- a/solution.py
+++ b/solution.py
@@ -9,6 +9,7 @@
 
 ITERS = 3
 LAMBDA = 0.02
+ORDERS = ((3, 2, 1), (1, 3, 2)) + ((3, 2, 1),) * (ITERS - 1)
 
 F32, BF16, I32 = jnp.float32, jnp.bfloat16, jnp.int32
 LANES, SUB = 128, 8
@@ -113,32 +114,23 @@
         msg[g : g + SUB, :] = fold3(acc)
 
 
-CHUNKS = 4
-
-
 def start_kernel(
-    rows_hbm, cols_hbm, count_hbm, tiles_hbm, w_hbm,
+    count, rows_hbm, cols_hbm, tiles_hbm, w_hbm,
     part, tiles, w, row_mask,
-    rows, cols, count, picked, pieces, sems,
+    rows, cols, picked, pieces, sems,
 ):
     slots = tiles.shape[0]
-    each = slots // CHUNKS
     small = [
         pltpu.make_async_copy(src, dst, sems.at[k])
-        for k, (src, dst) in enumerate(((cols_hbm, cols), (rows_hbm, rows), (count_hbm, count)))
+        for k, (src, dst) in enumerate(((cols_hbm, cols), (rows_hbm, rows)))
     ]
     w_copy = pltpu.make_async_copy(w_hbm, w, sems.at[3])
-    t_copies = [
-        pltpu.make_async_copy(
-            tiles_hbm.at[pl.ds(k * each, each)], tiles.at[pl.ds(k * each, each)], sems.at[4 + k]
-        )
-        for k in range(CHUNKS)
-    ]
-    for copy in [*small, w_copy, *t_copies]:
+    t_copy = pltpu.make_async_copy(tiles_hbm, tiles, sems.at[2])
+    for copy in [*small, w_copy, t_copy]:
         copy.start()
     for copy in small:
         copy.wait()
-    live = count[0]
+    live = count[0, 0]
     sub = iota((SUB, LANES), 0)
     for t in range(slots):
         row = jnp.where(t < live, rows[t], -1)
@@ -156,9 +148,8 @@
         squares = squares + jnp.sum((block * block).reshape(step_rows // SUB, SUB, LANES), axis=0)
     part[SUB : 2 * SUB, :] = squares
     acc = jnp.zeros((6 * SUB, 2 * LANES), F32)
+    t_copy.wait()
     for s in range(0, slots, 4):
-        if s % each == 0:
-            t_copies[s // each].wait()
         a, b, c, d = (
             masked_line(pieces, slots, t, row_mask[t * SUB : (t + 1) * SUB, :]) for t in range(s, s + 4)
         )
@@ -185,7 +176,7 @@
     right = ((ids[...] & (LANES - 1)) == iota((LANES, n), 0)).astype(F32).astype(BF16)
     hits = lax.dot_general(left, right, (((1,), (1,)), ((), ())), preferred_element_type=F32)
     mask_out[...] = jnp.minimum(hits, 1.0)
-    live = iota((1, slots), 1) < count[...]
+    live = iota((1, slots), 1) < count[0, 0]
 
     def both(line):
         line = jnp.where(live, line, -1).astype(F32)
@@ -271,8 +262,8 @@
         match[:, at : at + LANES] = same.astype(F32).astype(BF16)
 
 
-def forward_kernel(n_i, turned, row_mask, match, *refs):
-    got, (out, pieces) = refs[:n_i], refs[n_i:]
+def forward_kernel(n_i, order, turned, row_mask, match, *refs):
+    got, (out, pieces) = sorted_as(order, refs[:n_i]), refs[n_i:]
     slots = turned.shape[0]
     save_pieces(exact_pick(match[...], slot_values(got, slots)), pieces)
     out[...] = by_rows(turned, pieces, row_mask)
@@ -364,8 +355,8 @@
         out[...] = value
 
 
-def dense_kernel(n_i, slots, iters, w, index, *refs):
-    msgs = [refs[k * n_i : (k + 1) * n_i] for k in range(iters)]
+def dense_kernel(n_i, orders, slots, iters, w, index, *refs):
+    msgs = [sorted_as(orders[k], refs[k * n_i : (k + 1) * n_i]) for k in range(iters)]
     nums = [numbers_of(num) for num in refs[iters * n_i : iters * n_i + iters - 1]]
     res_out, dir_out, step_out, curved_out, pick_out = refs[-5:]
     own_blocks = res_out.shape[0]
@@ -392,8 +383,8 @@
     curved_out[...] = curved
 
 
-def last_kernel(n_i, slots, ww, num, res, direction, step, curved, pick, *refs):
-    msgs, (step_out, res_out) = refs[:n_i], refs[n_i:]
+def last_kernel(n_i, order, slots, ww, num, res, direction, step, curved, pick, *refs):
+    msgs, (step_out, res_out) = sorted_as(order, refs[:n_i]), refs[n_i:]
     image = exact_pick(pick[...], slot_values(msgs, slots))
     new = advance(msgs, slots, ww, numbers_of(num))
     last = res[...] + new["beta"] * direction[...]
@@ -402,13 +393,17 @@
     res_out[...] = res[...] - new["alpha"] * image
 
 
-def exchange(x, axis):
+def exchange(x, axis, order=(3, 2, 1)):
     size = lax.axis_size(axis)
-    if size & (size - 1) or size > 8:
+    if size != 4:
         return [lax.all_gather(x, axis, axis=0, tiled=True)]
-    return [x] + [
-        lax.ppermute(x, axis, [(i, i ^ k) for i in range(size)]) for k in range(size - 1, 0, -1)
-    ]
+    return [x] + [lax.ppermute(x, axis, [(i, i ^ k) for i in range(size)]) for k in order]
+
+
+def sorted_as(order, refs):
+    if len(refs) == 1:
+        return refs
+    return [refs[0]] + [refs[1 + order.index(k)] for k in (3, 2, 1)]
 
 
 def in_hbm(x):
@@ -433,21 +428,20 @@
     part, tiles, w, row_mask = call(
         start_kernel,
         (
+            tile_count,
             in_hbm(tile_rows.reshape(slots)),
             in_hbm(tile_cols.reshape(slots)),
-            tile_count.reshape(1),
             in_hbm(tiles),
             in_hbm(weights.reshape(col_blocks, edge)),
         ),
-        [HBM] * 2 + [ANY] + [HBM] * 2,
+        [SM] + [HBM] * 4,
         [f32(2 * SUB, LANES), tile_shape, f32(col_blocks, edge), f32(slots * SUB, LANES)],
         scratch=[
             pltpu.SMEM((slots,), I32),
             pltpu.SMEM((slots,), I32),
-            pltpu.SMEM((1,), I32),
             pltpu.VMEM((slots, LANES), F32),
             pltpu.VMEM((3 * slots, LANES), F32),
-            pltpu.SemaphoreType.DMA((4 + CHUNKS,)),
+            pltpu.SemaphoreType.DMA((4,)),
         ],
     )
     mask, row_pick, cols_line, own = call(
@@ -456,9 +450,9 @@
             sample_ids,
             tile_rows.reshape(1, slots),
             tile_cols.reshape(1, slots),
-            tile_count.reshape(1, 1),
+            tile_count,
         ),
-        [VM] * 4,
+        [VM] * 3 + [SM],
         [grid, picks((slots, LANES), BF16), grid, f32(slots, LANES)],
     )
     (turned,) = call(turn_kernel, (tiles,), [VM], [tile_shape])
@@ -470,7 +464,7 @@
         [VM] * (5 + n_f),
         [msg_shape, grid, grid, grid, grid],
     )
-    msgs = exchange(msg, "inst")
+    msgs = exchange(msg, "inst", ORDERS[0])
     n_i = len(msgs)
     (match,) = call(
         functools.partial(match_kernel, n_i),
@@ -479,9 +473,9 @@
         [picks((slots, slots * inst), BF16)],
     )
 
-    def forward(msgs):
+    def forward(msgs, order):
         (out,) = call(
-            functools.partial(forward_kernel, n_i),
+            functools.partial(forward_kernel, n_i, order),
             (turned, row_mask, match, *msgs),
             [VM] * (3 + n_i),
             [grid],
@@ -489,17 +483,17 @@
         )
         return exchange(out, "feat")
 
-    got = forward(msgs)
+    got = forward(msgs, ORDERS[0])
     msg, v = call(
         functools.partial(first_kernel, n_f),
         (tiles, row_pick, m, c, e, *got),
         [VM] * (5 + n_f),
         [msg_shape, grid],
     )
-    history = [msgs, exchange(msg, "inst")]
+    history = [msgs, exchange(msg, "inst", ORDERS[1])]
     state, nums = (e, v), []
     for k in range(ITERS - 1):
-        got = forward(history[-1])
+        got = forward(history[-1], ORDERS[k + 1])
         vec, num = call(
             functools.partial(numbers_kernel, n_i, slots, k == 0),
             (m, c, ww, *history[-1], *state),
@@ -512,18 +506,18 @@
             [VM] * (5 + n_f),
             [msg_shape] + [grid, grid] * (k < ITERS - 2),
         )
-        history.append(exchange(msg, "inst"))
+        history.append(exchange(msg, "inst", ORDERS[k + 2]))
         state = (*kept, vec, num)
         nums.append(num)
     block = f32(own_blocks, edge)
     *dense, pick = call(
-        functools.partial(dense_kernel, n_i, slots, ITERS),
+        functools.partial(dense_kernel, n_i, ORDERS, slots, ITERS),
         (w, index, *(ref for group in history[:ITERS] for ref in group), *nums),
         [VM, SM] + [VM] * (n_i * ITERS + len(nums)),
         [block, block, block, block, picks((own_blocks, slots * inst), BF16)],
     )
     step, res = call(
-        functools.partial(last_kernel, n_i, slots),
+        functools.partial(last_kernel, n_i, ORDERS[ITERS], slots),
         (ww, nums[-1], *dense, pick, *history[-1]),
         [VM] * (7 + n_i),
         [block, block],

time: 57.9 us -> 56.7 us (0.979)
  waiting for transfers between devices: 19.8 us -> 19 us
    ppermute x24, waiting for transfers between devices: 19.8 us -> 19 us  [exchange(): lax.ppermute(x, axis, [(i, i ^ k) for i in range(size)])]
  transfers between devices with their start and end apart: 24 -> 24, of which waited for: 17 -> 18; matrix products, arithmetic and copies ran while one was open for 0% -> 0% of each run, Pallas kernels for 3% -> 3%
where the time goes in v3:
time: 56.7 us; the launch traced here: 56.6 us
  starting transfers between devices  26.7 us (47%)
  waiting for transfers between devices  19 us (34%)
  Pallas kernels  9.4 us (17%)
  between operations  1.44 us (3%)
    ppermute x24, starting transfers between devices, exchange(): lax.ppermute(x, axis, [(i, i ^ k) for i in range(size)])  26.7 us
    ppermute x24, waiting for transfers between devices, exchange(): lax.ppermute(x, axis, [(i, i ^ k) for i in range(size)])  19 us
    pallas_call x15, Pallas kernels, call(): pl.pallas_call(kernel, in_specs=in_specs, out_shape=outs, out_specs=out_s...  9.4 us
  transfers between devices with their start and end apart: 24, of which 18 were waited for; matrix products, arithmetic and copies ran while one was open for 0% of the time, Pallas kernels for 3%

profile of v3, /device:TPU:0, one launch (start us, length us, event | category | flops | bytes accessed | tf_op | source)
XLA Modules:
  0.0 56.6 jit_solution(12454353525013354697)
XLA Ops:
  1.3 2.7 %shard_map.86 = (f32[16,128]{1,0:T(8,128)S(1)}, bf16[64,128,128]{2,1,0:T(8,128)(2,1)S(1)}, f32[2048,128]{1,0:T(8,128)S(1)}, f32[512,128]{1,0:T(8,128)S(1)}) custom-call(s32[1,1]{1,0:T(1,128)S(6)} %copy.9.count, s32[64]{0:T(128)} %bitcast.11, s32[64]{0:T(128)} %bitcast.13, bf16[64,128,128]{2,1,0:T(8,128)(2,1)} %bitcast.15, f32[2048,128]{1,0:T(8,128)} %bitcast.16), custom_call_target="tpu_custom_call" | custom-call | flops 2097152 | bytes 1048576 | tf_op jit(solution)/shard_map/pallas_call | solution.py:27
  4.1 2.4 %collective-permute-start = (f32[16,128]{1,0:T(8,128)S(1)}, f32[16,128]{1,0:T(8,128)S(1)}, u32[]{:S(2)}, u32[]{:S(2)}) collective-permute-start(f32[16,128]{1,0:T(8,128)S(1)} %get-tuple-element.35.refs_0_), channel_id=1, source_target_pairs={{0,3},{1,2},{2,1},{3,0},{4,7},{5,6},{6,5},{7,4},{8,11},{9,10},{10,... | collective-permute-start | bytes 24584 | tf_op jit(solution)/shard_map/ppermute | solution.py:400
  6.5 0.6 %collective-permute-start.1 = (f32[16,128]{1,0:T(8,128)S(1)}, f32[16,128]{1,0:T(8,128)S(1)}, u32[]{:S(2)}, u32[]{:S(2)}) collective-permute-start(f32[16,128]{1,0:T(8,128)S(1)} %get-tuple-element.35.refs_0_), channel_id=1, source_target_pairs={{0,2},{1,3},{2,0},{3,1},{4,6},{5,7},{6,4},{7,5},{8,10},{9,11},{10,... | collective-permute-start | bytes 24584 | tf_op jit(solution)/shard_map/ppermute | solution.py:400
  7.1 0.0 collective-permute-start.2
  7.2 0.0 copy-done.3
  7.2 0.2 shard_map.87
  7.4 0.5 collective-permute-done.refs_1_
  7.9 2.3 %collective-permute-done.1.refs_2_ = f32[16,128]{1,0:T(8,128)S(1)} collective-permute-done((f32[16,128]{1,0:T(8,128)S(1)}, f32[16,128]{1,0:T(8,128)S(1)}, u32[]{:S(2)}, u32[]{:S(2)}) %collective-permute-start.1) | collective-permute-done | bytes 8224 | tf_op jit(solution)/shard_map/ppermute | solution.py:400
  10.2 0.0 collective-permute-done.2.refs_3_
  10.2 0.0 copy-done
  10.2 0.5 shard_map.88
  10.7 3.7 %collective-permute-start.3 = (f32[72,128]{1,0:T(8,128)S(1)}, f32[72,128]{1,0:T(8,128)S(1)}, u32[]{:S(2)}, u32[]{:S(2)}) collective-permute-start(f32[72,128]{1,0:T(8,128)S(1)} %get-tuple-element.42.refs_0_), channel_id=1, source_target_pairs={{0,12},{4,8},{8,4},{12,0},{1,13},{5,9},{9,5},{13,1},{2,14},{6,10},... | collective-permute-start | bytes 110600 | tf_op jit(solution)/shard_map/ppermute | solution.py:400
  14.4 0.0 collective-permute-start.4
  14.4 0.8 %collective-permute-start.5 = (f32[72,128]{1,0:T(8,128)S(1)}, f32[72,128]{1,0:T(8,128)S(1)}, u32[]{:S(2)}, u32[]{:S(2)}) collective-permute-start(f32[72,128]{1,0:T(8,128)S(1)} %get-tuple-element.42.refs_0_), channel_id=1, source_target_pairs={{0,4},{4,0},{8,12},{12,8},{1,5},{5,1},{9,13},{13,9},{2,6},{6,2},{1... | collective-permute-start | bytes 110600 | tf_op jit(solution)/shard_map/ppermute | solution.py:400
  15.1 0.6 %shard_map.89.turned = bf16[64,128,128]{2,1,0:T(8,128)(2,1)S(1)} custom-call(bf16[64,128,128]{2,1,0:T(8,128)(2,1)S(1)} %get-tuple-element.31.tiles), custom_call_target="tpu_custom_call" | custom-call | flops 2097152 | bytes 1048576 | tf_op jit(solution)/shard_map/pallas_call | solution.py:27
  15.7 1.2 %collective-permute-done.3.refs_1_ = f32[72,128]{1,0:T(8,128)S(1)} collective-permute-done((f32[72,128]{1,0:T(8,128)S(1)}, f32[72,128]{1,0:T(8,128)S(1)}, u32[]{:S(2)}, u32[]{:S(2)}) %collective-permute-start.3) | collective-permute-done | bytes 36896 | tf_op jit(solution)/shard_map/ppermute | solution.py:400
  16.9 2.3 %collective-permute-done.4.refs_2_ = f32[72,128]{1,0:T(8,128)S(1)} collective-permute-done((f32[72,128]{1,0:T(8,128)S(1)}, f32[72,128]{1,0:T(8,128)S(1)}, u32[]{:S(2)}, u32[]{:S(2)}) %collective-permute-start.4) | collective-permute-done | bytes 36896 | tf_op jit(solution)/shard_map/ppermute | solution.py:400
  19.2 0.0 collective-permute-done.5.refs_3_
  19.2 0.6 %shard_map.91.refs_0_ = f32[8,128]{1,0:T(8,128)S(1)} custom-call(bf16[64,128,128]{2,1,0:T(8,128)(2,1)S(1)} %shard_map.89.turned, f32[512,128]{1,0:T(8,128)S(1)} %get-tuple-element.40.row_mask, bf16[64,256]{1,0:T(8,128)(2,1)S(1)} %shard_map.90.match, f32[72,128]{1,0:T(8,128)S(1)} %get-tuple-element.42.refs_0_, f32[72,128]{1,0:T(8,128)S(1)} %collective-permute-done.3.refs_1_, ...), custom_call_target="tpu_custom_call" | custom-call | flops 2097152 | bytes 1048576 | tf_op jit(solution)/shard_map/pallas_call | solution.py:27
  19.8 0.1 collective-permute-start.6
  19.9 0.7 %collective-permute-start.7 = (f32[8,128]{1,0:T(8,128)S(1)}, f32[8,128]{1,0:T(8,128)S(1)}, u32[]{:S(2)}, u32[]{:S(2)}) collective-permute-start(f32[8,128]{1,0:T(8,128)S(1)} %shard_map.91.refs_0_), channel_id=1, source_target_pairs={{0,2},{1,3},{2,0},{3,1},{4,6},{5,7},{6,4},{7,5},{8,10},{9,11},{10,... | collective-permute-start | bytes 12296 | tf_op jit(solution)/shard_map/ppermute | solution.py:400
  20.6 1.1 %collective-permute-start.8 = (f32[8,128]{1,0:T(8,128)S(1)}, f32[8,128]{1,0:T(8,128)S(1)}, u32[]{:S(2)}, u32[]{:S(2)}) collective-permute-start(f32[8,128]{1,0:T(8,128)S(1)} %shard_map.91.refs_0_), channel_id=1, source_target_pairs={{0,1},{1,0},{2,3},{3,2},{4,5},{5,4},{6,7},{7,6},{8,9},{9,8},{10,11... | collective-permute-start | bytes 12296 | tf_op jit(solution)/shard_map/ppermute | solution.py:400
  21.8 1.2 %collective-permute-done.6.refs_1_ = f32[8,128]{1,0:T(8,128)S(1)} collective-permute-done((f32[8,128]{1,0:T(8,128)S(1)}, f32[8,128]{1,0:T(8,128)S(1)}, u32[]{:S(2)}, u32[]{:S(2)}) %collective-permute-start.6) | collective-permute-done | bytes 4128 | tf_op jit(solution)/shard_map/ppermute | solution.py:400
  22.9 0.7 %collective-permute-done.7.refs_2_ = f32[8,128]{1,0:T(8,128)S(1)} collective-permute-done((f32[8,128]{1,0:T(8,128)S(1)}, f32[8,128]{1,0:T(8,128)S(1)}, u32[]{:S(2)}, u32[]{:S(2)}) %collective-permute-start.7) | collective-permute-done | bytes 4128 | tf_op jit(solution)/shard_map/ppermute | solution.py:400
  23.6 0.0 collective-permute-done.8.refs_3_
  23.6 0.5 shard_map.92
  24.1 1.5 %collective-permute-start.10 = (f32[72,128]{1,0:T(8,128)S(1)}, f32[72,128]{1,0:T(8,128)S(1)}, u32[]{:S(2)}, u32[]{:S(2)}) collective-permute-start(f32[72,128]{1,0:T(8,128)S(1)} %get-tuple-element.43.refs_0_.refs_4_), channel_id=1, source_target_pairs={{0,12},{4,8},{8,4},{12,0},{1,13},{5,9},{9,5},{13,1},{2,14},{6,10},... | collective-permute-start | bytes 110600 | tf_op jit(solution)/shard_map/ppermute | solution.py:400
  25.6 0.6 %collective-permute-start.11 = (f32[72,128]{1,0:T(8,128)S(1)}, f32[72,128]{1,0:T(8,128)S(1)}, u32[]{:S(2)}, u32[]{:S(2)}) collective-permute-start(f32[72,128]{1,0:T(8,128)S(1)} %get-tuple-element.43.refs_0_.refs_4_), channel_id=1, source_target_pairs={{0,8},{4,12},{8,0},{12,4},{1,9},{5,13},{9,1},{13,5},{2,10},{6,14},... | collective-permute-start | bytes 110600 | tf_op jit(solution)/shard_map/ppermute | solution.py:400
  26.3 2.3 %collective-permute-start.9 = (f32[72,128]{1,0:T(8,128)S(1)}, f32[72,128]{1,0:T(8,128)S(1)}, u32[]{:S(2)}, u32[]{:S(2)}) collective-permute-start(f32[72,128]{1,0:T(8,128)S(1)} %get-tuple-element.43.refs_0_.refs_4_), channel_id=1, source_target_pairs={{0,4},{4,0},{8,12},{12,8},{1,5},{5,1},{9,13},{13,9},{2,6},{6,2},{1... | collective-permute-start | bytes 110600 | tf_op jit(solution)/shard_map/ppermute | solution.py:400
  28.6 1.8 %collective-permute-done.10.refs_2_.refs_6_ = f32[72,128]{1,0:T(8,128)S(1)} collective-permute-done((f32[72,128]{1,0:T(8,128)S(1)}, f32[72,128]{1,0:T(8,128)S(1)}, u32[]{:S(2)}, u32[]{:S(2)}) %collective-permute-start.10) | collective-permute-done | bytes 36896 | tf_op jit(solution)/shard_map/ppermute | solution.py:400
  30.3 0.3 collective-permute-done.11.refs_3_.refs_7_
  30.6 0.3 collective-permute-done.9.refs_1_.refs_5_
  31.0 0.6 %shard_map.94.refs_0_ = f32[8,128]{1,0:T(8,128)S(1)} custom-call(bf16[64,128,128]{2,1,0:T(8,128)(2,1)S(1)} %shard_map.89.turned, f32[512,128]{1,0:T(8,128)S(1)} %get-tuple-element.40.row_mask, bf16[64,256]{1,0:T(8,128)(2,1)S(1)} %shard_map.90.match, f32[72,128]{1,0:T(8,128)S(1)} %get-tuple-element.43.refs_0_.refs_4_, ...), custom_call_target="tpu_custom_call" | custom-call | flops 2097152 | bytes 1048576 | tf_op jit(solution)/shard_map/pallas_call | solution.py:27
  31.6 0.3 collective-permute-start.12
  31.9 0.7 %collective-permute-start.13 = (f32[8,128]{1,0:T(8,128)S(1)}, f32[8,128]{1,0:T(8,128)S(1)}, u32[]{:S(2)}, u32[]{:S(2)}) collective-permute-start(f32[8,128]{1,0:T(8,128)S(1)} %shard_map.94.refs_0_), channel_id=1, source_target_pairs={{0,2},{1,3},{2,0},{3,1},{4,6},{5,7},{6,4},{7,5},{8,10},{9,11},{10,... | collective-permute-start | bytes 12296 | tf_op jit(solution)/shard_map/ppermute | solution.py:400
  32.6 0.9 %collective-permute-start.14 = (f32[8,128]{1,0:T(8,128)S(1)}, f32[8,128]{1,0:T(8,128)S(1)}, u32[]{:S(2)}, u32[]{:S(2)}) collective-permute-start(f32[8,128]{1,0:T(8,128)S(1)} %shard_map.94.refs_0_), channel_id=1, source_target_pairs={{0,1},{1,0},{2,3},{3,2},{4,5},{5,4},{6,7},{7,6},{8,9},{9,8},{10,11... | collective-permute-start | bytes 12296 | tf_op jit(solution)/shard_map/ppermute | solution.py:400
  33.5 0.1 shard_map.93
  33.6 1.0 %collective-permute-done.12.refs_1_ = f32[8,128]{1,0:T(8,128)S(1)} collective-permute-done((f32[8,128]{1,0:T(8,128)S(1)}, f32[8,128]{1,0:T(8,128)S(1)}, u32[]{:S(2)}, u32[]{:S(2)}) %collective-permute-start.12) | collective-permute-done | bytes 4128 | tf_op jit(solution)/shard_map/ppermute | solution.py:400
  34.7 0.8 %collective-permute-done.13.refs_2_ = f32[8,128]{1,0:T(8,128)S(1)} collective-permute-done((f32[8,128]{1,0:T(8,128)S(1)}, f32[8,128]{1,0:T(8,128)S(1)}, u32[]{:S(2)}, u32[]{:S(2)}) %collective-permute-start.13) | collective-permute-done | bytes 4128 | tf_op jit(solution)/shard_map/ppermute | solution.py:400
  35.5 0.0 collective-permute-done.14.refs_3_
  35.5 0.6 shard_map.95
  36.1 2.1 %collective-permute-start.15 = (f32[72,128]{1,0:T(8,128)S(1)}, f32[72,128]{1,0:T(8,128)S(1)}, u32[]{:S(2)}, u32[]{:S(2)}) collective-permute-start(f32[72,128]{1,0:T(8,128)S(1)} %get-tuple-element.47.refs_0_.refs_8_), channel_id=1, source_target_pairs={{0,12},{4,8},{8,4},{12,0},{1,13},{5,9},{9,5},{13,1},{2,14},{6,10},... | collective-permute-start | bytes 110600 | tf_op jit(solution)/shard_map/ppermute | solution.py:400
  38.2 0.7 %collective-permute-start.16 = (f32[72,128]{1,0:T(8,128)S(1)}, f32[72,128]{1,0:T(8,128)S(1)}, u32[]{:S(2)}, u32[]{:S(2)}) collective-permute-start(f32[72,128]{1,0:T(8,128)S(1)} %get-tuple-element.47.refs_0_.refs_8_), channel_id=1, source_target_pairs={{0,8},{4,12},{8,0},{12,4},{1,9},{5,13},{9,1},{13,5},{2,10},{6,14},... | collective-permute-start | bytes 110600 | tf_op jit(solution)/shard_map/ppermute | solution.py:400
  38.9 1.6 %collective-permute-start.17 = (f32[72,128]{1,0:T(8,128)S(1)}, f32[72,128]{1,0:T(8,128)S(1)}, u32[]{:S(2)}, u32[]{:S(2)}) collective-permute-start(f32[72,128]{1,0:T(8,128)S(1)} %get-tuple-element.47.refs_0_.refs_8_), channel_id=1, source_target_pairs={{0,4},{4,0},{8,12},{12,8},{1,5},{5,1},{9,13},{13,9},{2,6},{6,2},{1... | collective-permute-start | bytes 110600 | tf_op jit(solution)/shard_map/ppermute | solution.py:400
  40.5 1.4 %collective-permute-done.15.refs_1_.refs_9_ = f32[72,128]{1,0:T(8,128)S(1)} collective-permute-done((f32[72,128]{1,0:T(8,128)S(1)}, f32[72,128]{1,0:T(8,128)S(1)}, u32[]{:S(2)}, u32[]{:S(2)}) %collective-permute-start.15) | collective-permute-done | bytes 36896 | tf_op jit(solution)/shard_map/ppermute | solution.py:400
  41.9 1.2 %collective-permute-done.16.refs_2_.refs_10_ = f32[72,128]{1,0:T(8,128)S(1)} collective-permute-done((f32[72,128]{1,0:T(8,128)S(1)}, f32[72,128]{1,0:T(8,128)S(1)}, u32[]{:S(2)}, u32[]{:S(2)}) %collective-permute-start.16) | collective-permute-done | bytes 36896 | tf_op jit(solution)/shard_map/ppermute | solution.py:400
  43.1 0.3 collective-permute-done.17.refs_3_.refs_11_
  43.5 0.6 %shard_map.98.refs_0_ = f32[8,128]{1,0:T(8,128)S(1)} custom-call(bf16[64,128,128]{2,1,0:T(8,128)(2,1)S(1)} %shard_map.89.turned, f32[512,128]{1,0:T(8,128)S(1)} %get-tuple-element.40.row_mask, bf16[64,256]{1,0:T(8,128)(2,1)S(1)} %shard_map.90.match, f32[72,128]{1,0:T(8,128)S(1)} %get-tuple-element.47.refs_0_.refs_8_, ...), custom_call_target="tpu_custom_call" | custom-call | flops 2097152 | bytes 1048576 | tf_op jit(solution)/shard_map/pallas_call | solution.py:27
  44.1 0.1 collective-permute-start.18
  44.1 0.9 %collective-permute-start.19 = (f32[8,128]{1,0:T(8,128)S(1)}, f32[8,128]{1,0:T(8,128)S(1)}, u32[]{:S(2)}, u32[]{:S(2)}) collective-permute-start(f32[8,128]{1,0:T(8,128)S(1)} %shard_map.98.refs_0_), channel_id=1, source_target_pairs={{0,2},{1,3},{2,0},{3,1},{4,6},{5,7},{6,4},{7,5},{8,10},{9,11},{10,... | collective-permute-start | bytes 12296 | tf_op jit(solution)/shard_map/ppermute | solution.py:400
  45.0 1.0 %collective-permute-start.20 = (f32[8,128]{1,0:T(8,128)S(1)}, f32[8,128]{1,0:T(8,128)S(1)}, u32[]{:S(2)}, u32[]{:S(2)}) collective-permute-start(f32[8,128]{1,0:T(8,128)S(1)} %shard_map.98.refs_0_), channel_id=1, source_target_pairs={{0,1},{1,0},{2,3},{3,2},{4,5},{5,4},{6,7},{7,6},{8,9},{9,8},{10,11... | collective-permute-start | bytes 12296 | tf_op jit(solution)/shard_map/ppermute | solution.py:400
  46.0 0.2 shard_map.96
  46.2 0.9 %collective-permute-done.18.refs_1_ = f32[8,128]{1,0:T(8,128)S(1)} collective-permute-done((f32[8,128]{1,0:T(8,128)S(1)}, f32[8,128]{1,0:T(8,128)S(1)}, u32[]{:S(2)}, u32[]{:S(2)}) %collective-permute-start.18) | collective-permute-done | bytes 4128 | tf_op jit(solution)/shard_map/ppermute | solution.py:400
  47.2 0.7 %collective-permute-done.19.refs_2_ = f32[8,128]{1,0:T(8,128)S(1)} collective-permute-done((f32[8,128]{1,0:T(8,128)S(1)}, f32[8,128]{1,0:T(8,128)S(1)}, u32[]{:S(2)}, u32[]{:S(2)}) %collective-permute-start.19) | collective-permute-done | bytes 4128 | tf_op jit(solution)/shard_map/ppermute | solution.py:400
  47.8 0.0 collective-permute-done.20.refs_3_
  47.8 0.6 shard_map.99.refs_0_
  48.4 2.1 %collective-permute-start.21 = (f32[72,128]{1,0:T(8,128)S(1)}, f32[72,128]{1,0:T(8,128)S(1)}, u32[]{:S(2)}, u32[]{:S(2)}) collective-permute-start(f32[72,128]{1,0:T(8,128)S(1)} %shard_map.99.refs_0_), channel_id=1, source_target_pairs={{0,12},{4,8},{8,4},{12,0},{1,13},{5,9},{9,5},{13,1},{2,14},{6,10},... | collective-permute-start | bytes 110600 | tf_op jit(solution)/shard_map/ppermute | solution.py:400
  50.5 0.5 collective-permute-start.22
  50.9 1.9 %collective-permute-start.23 = (f32[72,128]{1,0:T(8,128)S(1)}, f32[72,128]{1,0:T(8,128)S(1)}, u32[]{:S(2)}, u32[]{:S(2)}) collective-permute-start(f32[72,128]{1,0:T(8,128)S(1)} %shard_map.99.refs_0_), channel_id=1, source_target_pairs={{0,4},{4,0},{8,12},{12,8},{1,5},{5,1},{9,13},{13,9},{2,6},{6,2},{1... | collective-permute-start | bytes 110600 | tf_op jit(solution)/shard_map/ppermute | solution.py:400
  52.8 0.6 %shard_map.97 = (f32[512,128]{1,0:T(8,128)S(1)}, f32[512,128]{1,0:T(8,128)S(1)}, f32[512,128]{1,0:T(8,128)S(1)}, f32[512,128]{1,0:T(8,128)S(1)}, bf16[512,256]{1,0:T(8,128)(2,1)S(1)}) custom-call(f32[2048,128]{1,0:T(8,128)S(1)} %get-tuple-element.51.w, s32[1]{0:T(128)} %bitcast.7.index, f32[72,128]{1,0:T(8,128)S(1)} %get-tuple-element.42.refs_0_, ...), custom_call_target="tpu_custom_call" | custom-call | flops 2097152 | bytes 1048576 | tf_op jit(solution)/shard_map/pallas_call | solution.py:27
  53.5 0.7 %collective-permute-done.21.refs_1_ = f32[72,128]{1,0:T(8,128)S(1)} collective-permute-done((f32[72,128]{1,0:T(8,128)S(1)}, f32[72,128]{1,0:T(8,128)S(1)}, u32[]{:S(2)}, u32[]{:S(2)}) %collective-permute-start.21) | collective-permute-done | bytes 36896 | tf_op jit(solution)/shard_map/ppermute | solution.py:400
  54.2 1.3 %collective-permute-done.22.refs_2_ = f32[72,128]{1,0:T(8,128)S(1)} collective-permute-done((f32[72,128]{1,0:T(8,128)S(1)}, f32[72,128]{1,0:T(8,128)S(1)}, u32[]{:S(2)}, u32[]{:S(2)}) %collective-permute-start.22) | collective-permute-done | bytes 36896 | tf_op jit(solution)/shard_map/ppermute | solution.py:400
  55.5 0.0 collective-permute-done.23.refs_3_
  55.5 1.0 %shard_map.100 = (f32[512,128]{1,0:T(8,128)}, f32[512,128]{1,0:T(8,128)}) custom-call(f32[8,128]{1,0:T(8,128)S(1)} %get-tuple-element.36.ww, f32[8,128]{1,0:T(8,128)S(1)} %get-tuple-element.50.refs_13_.num, f32[512,128]{1,0:T(8,128)S(1)} %get-tuple-element.52.res, f32[512,128]{1,0:T(8,128)S(1)} %get-tuple-element.53.direction, ...), custom_call_target="tpu_custom_call" | custom-call | flops 2097152 | bytes 1048576 | tf_op jit(solution)/shard_map/pallas_call | solution.py:27
  (7 shorter events, 0.0 us)
Async XLA Ops:
  0.6 6.5 %copy-start.1 = (s32[1,1,64]{2,1,0:T(1,128)S(1)}, s32[1,1,64]{2,1,0:T(1,128)}, u32[]{:S(2)}) copy-start(s32[1,1,64]{2,1,0:T(1,128)} %param.8) | copy-start | bytes 772
  0.6 6.5 %copy-start.2 = (s32[1,1,64]{2,1,0:T(1,128)S(1)}, s32[1,1,64]{2,1,0:T(1,128)}, u32[]{:S(2)}) copy-start(s32[1,1,64]{2,1,0:T(1,128)} %param.9) | copy-start | bytes 772
  0.7 6.5 %copy-start.3 = (s32[1,512]{1,0:T(1,128)S(1)}, s32[1,512]{1,0:T(1,128)}, u32[]{:S(2)}) copy-start(s32[1,512]{1,0:T(1,128)} %ids.1) | copy-start | bytes 6148
  0.7 9.5 %copy-start = (s32[1,1024]{1,0:T(1,128)S(1)}, s32[1,1024]{1,0:T(1,128)}, u32[]{:S(2)}) copy-start(s32[1,1024]{1,0:T(1,128)} %param.12) | copy-start | bytes 12292
  4.1 3.8 %collective-permute-start = (f32[16,128]{1,0:T(8,128)S(1)}, f32[16,128]{1,0:T(8,128)S(1)}, u32[]{:S(2)}, u32[]{:S(2)}) collective-permute-start(f32[16,128]{1,0:T(8,128)S(1)} %get-tuple-element.35.refs_0_), channel_id=1, source_target_pairs={{0,3},{1,2},{2,1},{3,0},{4,7},{5,6},{6,5},{7,4},{8,11},{9,10},{10,... | collective-permute-start | bytes 24584 | tf_op jit(solution)/shard_map/ppermute | solution.py:400
  6.5 3.7 %collective-permute-start.1 = (f32[16,128]{1,0:T(8,128)S(1)}, f32[16,128]{1,0:T(8,128)S(1)}, u32[]{:S(2)}, u32[]{:S(2)}) collective-permute-start(f32[16,128]{1,0:T(8,128)S(1)} %get-tuple-element.35.refs_0_), channel_id=1, source_target_pairs={{0,2},{1,3},{2,0},{3,1},{4,6},{5,7},{6,4},{7,5},{8,10},{9,11},{10,... | collective-permute-start | bytes 24584 | tf_op jit(solution)/shard_map/ppermute | solution.py:400
  7.1 3.0 %collective-permute-start.2 = (f32[16,128]{1,0:T(8,128)S(1)}, f32[16,128]{1,0:T(8,128)S(1)}, u32[]{:S(2)}, u32[]{:S(2)}) collective-permute-start(f32[16,128]{1,0:T(8,128)S(1)} %get-tuple-element.35.refs_0_), channel_id=1, source_target_pairs={{0,1},{1,0},{2,3},{3,2},{4,5},{5,4},{6,7},{7,6},{8,9},{9,8},{10,11... | collective-permute-start | bytes 24584 | tf_op jit(solution)/shard_map/ppermute | solution.py:400
  10.7 6.3 %collective-permute-start.3 = (f32[72,128]{1,0:T(8,128)S(1)}, f32[72,128]{1,0:T(8,128)S(1)}, u32[]{:S(2)}, u32[]{:S(2)}) collective-permute-start(f32[72,128]{1,0:T(8,128)S(1)} %get-tuple-element.42.refs_0_), channel_id=1, source_target_pairs={{0,12},{4,8},{8,4},{12,0},{1,13},{5,9},{9,5},{13,1},{2,14},{6,10},... | collective-permute-start | bytes 110600 | tf_op jit(solution)/shard_map/ppermute | solution.py:400
  14.4 4.9 %collective-permute-start.4 = (f32[72,128]{1,0:T(8,128)S(1)}, f32[72,128]{1,0:T(8,128)S(1)}, u32[]{:S(2)}, u32[]{:S(2)}) collective-permute-start(f32[72,128]{1,0:T(8,128)S(1)} %get-tuple-element.42.refs_0_), channel_id=1, source_target_pairs={{0,8},{4,12},{8,0},{12,4},{1,9},{5,13},{9,1},{13,5},{2,10},{6,14},... | collective-permute-start | bytes 110600 | tf_op jit(solution)/shard_map/ppermute | solution.py:400
  14.4 4.9 %collective-permute-start.5 = (f32[72,128]{1,0:T(8,128)S(1)}, f32[72,128]{1,0:T(8,128)S(1)}, u32[]{:S(2)}, u32[]{:S(2)}) collective-permute-start(f32[72,128]{1,0:T(8,128)S(1)} %get-tuple-element.42.refs_0_), channel_id=1, source_target_pairs={{0,4},{4,0},{8,12},{12,8},{1,5},{5,1},{9,13},{13,9},{2,6},{6,2},{1... | collective-permute-start | bytes 110600 | tf_op jit(solution)/shard_map/ppermute | solution.py:400
  19.8 3.1 %collective-permute-start.6 = (f32[8,128]{1,0:T(8,128)S(1)}, f32[8,128]{1,0:T(8,128)S(1)}, u32[]{:S(2)}, u32[]{:S(2)}) collective-permute-start(f32[8,128]{1,0:T(8,128)S(1)} %shard_map.91.refs_0_), channel_id=1, source_target_pairs={{0,3},{1,2},{2,1},{3,0},{4,7},{5,6},{6,5},{7,4},{8,11},{9,10},{10,... | collective-permute-start | bytes 12296 | tf_op jit(solution)/shard_map/ppermute | solution.py:400
  19.9 3.7 %collective-permute-start.7 = (f32[8,128]{1,0:T(8,128)S(1)}, f32[8,128]{1,0:T(8,128)S(1)}, u32[]{:S(2)}, u32[]{:S(2)}) collective-permute-start(f32[8,128]{1,0:T(8,128)S(1)} %shard_map.91.refs_0_), channel_id=1, source_target_pairs={{0,2},{1,3},{2,0},{3,1},{4,6},{5,7},{6,4},{7,5},{8,10},{9,11},{10,... | collective-permute-start | bytes 12296 | tf_op jit(solution)/shard_map/ppermute | solution.py:400
  20.6 3.0 %collective-permute-start.8 = (f32[8,128]{1,0:T(8,128)S(1)}, f32[8,128]{1,0:T(8,128)S(1)}, u32[]{:S(2)}, u32[]{:S(2)}) collective-permute-start(f32[8,128]{1,0:T(8,128)S(1)} %shard_map.91.refs_0_), channel_id=1, source_target_pairs={{0,1},{1,0},{2,3},{3,2},{4,5},{5,4},{6,7},{7,6},{8,9},{9,8},{10,11... | collective-permute-start | bytes 12296 | tf_op jit(solution)/shard_map/ppermute | solution.py:400
  24.1 6.2 %collective-permute-start.10 = (f32[72,128]{1,0:T(8,128)S(1)}, f32[72,128]{1,0:T(8,128)S(1)}, u32[]{:S(2)}, u32[]{:S(2)}) collective-permute-start(f32[72,128]{1,0:T(8,128)S(1)} %get-tuple-element.43.refs_0_.refs_4_), channel_id=1, source_target_pairs={{0,12},{4,8},{8,4},{12,0},{1,13},{5,9},{9,5},{13,1},{2,14},{6,10},... | collective-permute-start | bytes 110600 | tf_op jit(solution)/shard_map/ppermute | solution.py:400
  25.6 5.0 %collective-permute-start.11 = (f32[72,128]{1,0:T(8,128)S(1)}, f32[72,128]{1,0:T(8,128)S(1)}, u32[]{:S(2)}, u32[]{:S(2)}) collective-permute-start(f32[72,128]{1,0:T(8,128)S(1)} %get-tuple-element.43.refs_0_.refs_4_), channel_id=1, source_target_pairs={{0,8},{4,12},{8,0},{12,4},{1,9},{5,13},{9,1},{13,5},{2,10},{6,14},... | collective-permute-start | bytes 110600 | tf_op jit(solution)/shard_map/ppermute | solution.py:400
  26.3 4.7 %collective-permute-start.9 = (f32[72,128]{1,0:T(8,128)S(1)}, f32[72,128]{1,0:T(8,128)S(1)}, u32[]{:S(2)}, u32[]{:S(2)}) collective-permute-start(f32[72,128]{1,0:T(8,128)S(1)} %get-tuple-element.43.refs_0_.refs_4_), channel_id=1, source_target_pairs={{0,4},{4,0},{8,12},{12,8},{1,5},{5,1},{9,13},{13,9},{2,6},{6,2},{1... | collective-permute-start | bytes 110600 | tf_op jit(solution)/shard_map/ppermute | solution.py:400
  31.6 3.1 %collective-permute-start.12 = (f32[8,128]{1,0:T(8,128)S(1)}, f32[8,128]{1,0:T(8,128)S(1)}, u32[]{:S(2)}, u32[]{:S(2)}) collective-permute-start(f32[8,128]{1,0:T(8,128)S(1)} %shard_map.94.refs_0_), channel_id=1, source_target_pairs={{0,3},{1,2},{2,1},{3,0},{4,7},{5,6},{6,5},{7,4},{8,11},{9,10},{10,... | collective-permute-start | bytes 12296 | tf_op jit(solution)/shard_map/ppermute | solution.py:400
  31.9 3.6 %collective-permute-start.13 = (f32[8,128]{1,0:T(8,128)S(1)}, f32[8,128]{1,0:T(8,128)S(1)}, u32[]{:S(2)}, u32[]{:S(2)}) collective-permute-start(f32[8,128]{1,0:T(8,128)S(1)} %shard_map.94.refs_0_), channel_id=1, source_target_pairs={{0,2},{1,3},{2,0},{3,1},{4,6},{5,7},{6,4},{7,5},{8,10},{9,11},{10,... | collective-permute-start | bytes 12296 | tf_op jit(solution)/shard_map/ppermute | solution.py:400
  32.6 2.9 %collective-permute-start.14 = (f32[8,128]{1,0:T(8,128)S(1)}, f32[8,128]{1,0:T(8,128)S(1)}, u32[]{:S(2)}, u32[]{:S(2)}) collective-permute-start(f32[8,128]{1,0:T(8,128)S(1)} %shard_map.94.refs_0_), channel_id=1, source_target_pairs={{0,1},{1,0},{2,3},{3,2},{4,5},{5,4},{6,7},{7,6},{8,9},{9,8},{10,11... | collective-permute-start | bytes 12296 | tf_op jit(solution)/shard_map/ppermute | solution.py:400
  36.1 5.9 %collective-permute-start.15 = (f32[72,128]{1,0:T(8,128)S(1)}, f32[72,128]{1,0:T(8,128)S(1)}, u32[]{:S(2)}, u32[]{:S(2)}) collective-permute-start(f32[72,128]{1,0:T(8,128)S(1)} %get-tuple-element.47.refs_0_.refs_8_), channel_id=1, source_target_pairs={{0,12},{4,8},{8,4},{12,0},{1,13},{5,9},{9,5},{13,1},{2,14},{6,10},... | collective-permute-start | bytes 110600 | tf_op jit(solution)/shard_map/ppermute | solution.py:400
  38.2 4.9 %collective-permute-start.16 = (f32[72,128]{1,0:T(8,128)S(1)}, f32[72,128]{1,0:T(8,128)S(1)}, u32[]{:S(2)}, u32[]{:S(2)}) collective-permute-start(f32[72,128]{1,0:T(8,128)S(1)} %get-tuple-element.47.refs_0_.refs_8_), channel_id=1, source_target_pairs={{0,8},{4,12},{8,0},{12,4},{1,9},{5,13},{9,1},{13,5},{2,10},{6,14},... | collective-permute-start | bytes 110600 | tf_op jit(solution)/shard_map/ppermute | solution.py:400
  38.9 4.5 %collective-permute-start.17 = (f32[72,128]{1,0:T(8,128)S(1)}, f32[72,128]{1,0:T(8,128)S(1)}, u32[]{:S(2)}, u32[]{:S(2)}) collective-permute-start(f32[72,128]{1,0:T(8,128)S(1)} %get-tuple-element.47.refs_0_.refs_8_), channel_id=1, source_target_pairs={{0,4},{4,0},{8,12},{12,8},{1,5},{5,1},{9,13},{13,9},{2,6},{6,2},{1... | collective-permute-start | bytes 110600 | tf_op jit(solution)/shard_map/ppermute | solution.py:400
  44.1 3.1 %collective-permute-start.18 = (f32[8,128]{1,0:T(8,128)S(1)}, f32[8,128]{1,0:T(8,128)S(1)}, u32[]{:S(2)}, u32[]{:S(2)}) collective-permute-start(f32[8,128]{1,0:T(8,128)S(1)} %shard_map.98.refs_0_), channel_id=1, source_target_pairs={{0,3},{1,2},{2,1},{3,0},{4,7},{5,6},{6,5},{7,4},{8,11},{9,10},{10,... | collective-permute-start | bytes 12296 | tf_op jit(solution)/shard_map/ppermute | solution.py:400
  44.1 3.7 %collective-permute-start.19 = (f32[8,128]{1,0:T(8,128)S(1)}, f32[8,128]{1,0:T(8,128)S(1)}, u32[]{:S(2)}, u32[]{:S(2)}) collective-permute-start(f32[8,128]{1,0:T(8,128)S(1)} %shard_map.98.refs_0_), channel_id=1, source_target_pairs={{0,2},{1,3},{2,0},{3,1},{4,6},{5,7},{6,4},{7,5},{8,10},{9,11},{10,... | collective-permute-start | bytes 12296 | tf_op jit(solution)/shard_map/ppermute | solution.py:400
  45.0 2.8 %collective-permute-start.20 = (f32[8,128]{1,0:T(8,128)S(1)}, f32[8,128]{1,0:T(8,128)S(1)}, u32[]{:S(2)}, u32[]{:S(2)}) collective-permute-start(f32[8,128]{1,0:T(8,128)S(1)} %shard_map.98.refs_0_), channel_id=1, source_target_pairs={{0,1},{1,0},{2,3},{3,2},{4,5},{5,4},{6,7},{7,6},{8,9},{9,8},{10,11... | collective-permute-start | bytes 12296 | tf_op jit(solution)/shard_map/ppermute | solution.py:400
  48.4 5.8 %collective-permute-start.21 = (f32[72,128]{1,0:T(8,128)S(1)}, f32[72,128]{1,0:T(8,128)S(1)}, u32[]{:S(2)}, u32[]{:S(2)}) collective-permute-start(f32[72,128]{1,0:T(8,128)S(1)} %shard_map.99.refs_0_), channel_id=1, source_target_pairs={{0,12},{4,8},{8,4},{12,0},{1,13},{5,9},{9,5},{13,1},{2,14},{6,10},... | collective-permute-start | bytes 110600 | tf_op jit(solution)/shard_map/ppermute | solution.py:400
  50.5 5.1 %collective-permute-start.22 = (f32[72,128]{1,0:T(8,128)S(1)}, f32[72,128]{1,0:T(8,128)S(1)}, u32[]{:S(2)}, u32[]{:S(2)}) collective-permute-start(f32[72,128]{1,0:T(8,128)S(1)} %shard_map.99.refs_0_), channel_id=1, source_target_pairs={{0,8},{4,12},{8,0},{12,4},{1,9},{5,13},{9,1},{13,5},{2,10},{6,14},... | collective-permute-start | bytes 110600 | tf_op jit(solution)/shard_map/ppermute | solution.py:400
  50.9 4.6 %collective-permute-start.23 = (f32[72,128]{1,0:T(8,128)S(1)}, f32[72,128]{1,0:T(8,128)S(1)}, u32[]{:S(2)}, u32[]{:S(2)}) collective-permute-start(f32[72,128]{1,0:T(8,128)S(1)} %shard_map.99.refs_0_), channel_id=1, source_target_pairs={{0,4},{4,0},{8,12},{12,8},{1,5},{5,1},{9,13},{13,9},{2,6},{6,2},{1... | collective-permute-start | bytes 110600 | tf_op jit(solution)/shard_map/ppermute | solution.py:400

commit v4 on v3

--- a/solution.py
+++ b/solution.py
@@ -9,12 +9,15 @@
 
 ITERS = 3
 LAMBDA = 0.02
-ORDERS = ((3, 2, 1), (1, 3, 2)) + ((3, 2, 1),) * (ITERS - 1)
+ORDERS = ((1, 2, 3),) * ITERS + ((3, 2, 1),)
+FEAT_ORDER = (1, 2, 3)
 
 F32, BF16, I32 = jnp.float32, jnp.bfloat16, jnp.int32
 LANES, SUB = 128, 8
 TAIL = 8
 COLS_ROW = 3
+CAP, CAP_RUN = 17, 512
+SHORT, SHORT_PAD = 24, 32
 
 
 VM = pl.BlockSpec(memory_space=pltpu.VMEM)
@@ -169,7 +172,25 @@
         turned[t] = tiles[t].T
 
 
-def prep_kernel(ids, rows_line, cols_line, count, mask_out, pick_out, cols_out, own_out):
+def ranks(line, column, parts):
+    shift = CAP_RUN.bit_length() - 1
+    run, run_column = line.astype(I32) >> shift, column.astype(I32) >> shift
+    sub, lane = iota(column.shape, 0), iota(column.shape, 1)
+    same = (run == run_column) & (sub < lane)
+    if parts == 2:
+        same = same & ((sub < LANES // 2) == (lane < LANES // 2))
+    return run, jnp.sum(same.astype(F32), axis=0, keepdims=True).astype(I32)
+
+
+def column_of(line, rows):
+    wide = jnp.broadcast_to(line, (rows, LANES))
+    own = jnp.where(iota((rows, LANES), 0) == iota((rows, LANES), 1), wide, 0.0)
+    return jnp.broadcast_to(jnp.sum(own, axis=1, keepdims=True), (rows, LANES))
+
+
+def prep_kernel(
+    ids, rows_line, cols_line, count, index, mask_out, pick_out, cols_out, own_out, *send_out
+):
     slots = cols_line.shape[1]
     n = ids.shape[1]
     left = ((ids[...] >> 7) == iota((SUB, n), 0)).astype(F32).astype(BF16)
@@ -181,13 +202,17 @@
     def both(line):
         line = jnp.where(live, line, -1).astype(F32)
         line = jnp.concatenate([line, line], axis=1)
-        wide = jnp.broadcast_to(line, (slots, LANES))
-        own = jnp.where(iota((slots, LANES), 0) == iota((slots, LANES), 1), wide, 0.0)
-        return line, jnp.broadcast_to(jnp.sum(own, axis=1, keepdims=True), (slots, LANES))
+        return line, column_of(line, slots)
 
     line, own = both(cols_line[...])
     cols_out[...] = jnp.broadcast_to(line, (SUB, LANES))
     own_out[...] = own
+    for out in send_out:
+        run, rank = ranks(line, own, 1)
+        row = iota((SHORT, LANES), 0)
+        for j, k in enumerate((0, 3, 2, 1)):
+            sent = (row == rank) & (run == (index[0] ^ k))
+            out[j * SHORT : (j + 1) * SHORT, :] = sent.astype(F32)[:, :slots].astype(BF16)
     _, own = both(rows_line[...])
     pick_out[...] = (own == iota((slots, LANES), 1).astype(F32)).astype(F32).astype(BF16)
 
@@ -253,8 +278,8 @@
     e_out[...] = e
 
 
-def match_kernel(n_i, own, *refs):
-    got, (match,) = refs[:n_i], refs[n_i:]
+def match_kernel(n_i, order, own, *refs):
+    got, (match,) = sorted_as(order, refs[:n_i]), refs[n_i:]
     slots = own.shape[0]
     line = slot_cols(got, slots)
     for at in range(0, line.shape[1], LANES):
@@ -292,14 +317,14 @@
     num[...] = jnp.concatenate([*lines, jnp.zeros((1, LANES), F32)], axis=0)
 
 
-def advance(msgs, slots, ww, old):
-    rr_new, cur_r = summed(msgs, slots, 0), summed(msgs, slots, 1)
+def advance(msgs, slots, ww, old, shift=0):
+    rr_new, cur_r = summed(msgs, slots, shift), summed(msgs, slots, shift + 1)
     if old is None:
         a_r = a_d = jnp.full((1, 1), -LAMBDA, F32)
         rr = a_r * a_r * total(ww[...]) + rr_new
         dd, cur, beta = rr, cur_r, jnp.zeros((1, 1), F32)
     else:
-        cross = summed(msgs, slots, 2)
+        cross = summed(msgs, slots, shift + 2)
         rr = old["a_r"] * old["a_r"] * total(ww[...]) + rr_new
         beta = rr / old["rr"]
         a_d = old["a_r"] + beta * old["a_d"]
@@ -341,24 +366,35 @@
     save_numbers(num_out, new)
 
 
-def next_kernel(n_f, tiles, row_pick, c, vec, num, *refs):
+def next_kernel(n_f, short, tiles, row_pick, c, vec, num, *refs):
     got, (msg, *kept) = refs[:n_f], refs[n_f:]
     slots = tiles.shape[0]
+    if short:
+        send, *outs, msg = refs[n_f:]
     gram = feat_sum([(ref, SUB) for ref in got])
     v = at(vec, 0) - numbers_of(num)["alpha"] * gram
     u = c[...] * v
     by_cols(tiles, row_pick, u, msg)
-    write_tail(
-        msg, slots, [line_of(at(vec, 4) + at(vec, 2) * v), line_of(u * v), line_of(u * at(vec, 1))]
-    )
+    lines = [line_of(at(vec, 4) + at(vec, 2) * v), line_of(u * v), line_of(u * at(vec, 1))]
+    if short:
+        chosen = exact_pick(send[...], msg[...])
+        pad = [jnp.zeros((n, LANES), F32) for n in (CAP, SHORT - CAP - len(lines))]
+        tail = jnp.concatenate([pad[0], *lines, pad[1]], axis=0)
+        for j, out in enumerate(outs):
+            slots_rows = chosen[j * SHORT : (j + 1) * SHORT]
+            out[...] = jnp.where(iota((SHORT, LANES), 0) < CAP, slots_rows, tail)
+        return
+    write_tail(msg, slots, lines)
     for out, value in zip(kept, (v, gram + at(vec, 5))):
         out[...] = value
 
 
-def dense_kernel(n_i, orders, slots, iters, w, index, *refs):
+def dense_kernel(n_i, short, orders, slots, iters, w, index, *refs):
     msgs = [sorted_as(orders[k], refs[k * n_i : (k + 1) * n_i]) for k in range(iters)]
     nums = [numbers_of(num) for num in refs[iters * n_i : iters * n_i + iters - 1]]
-    res_out, dir_out, step_out, curved_out, pick_out = refs[-5:]
+    res_out, dir_out, step_out, curved_out, pick_out = refs[iters * n_i + iters - 1 :][:5]
+    if short:
+        short_out, pick_out = refs[-2:]
     own_blocks = res_out.shape[0]
     line = slot_cols(msgs[0], slots)
     offset = index[0] * own_blocks
@@ -377,27 +413,57 @@
             curved = image + nums[k]["beta"] * curved
         step = step + nums[k]["alpha"] * direction
         res = res - nums[k]["alpha"] * (curved + LAMBDA * direction)
+    if short:
+        blocks = []
+        for a in range(0, line.shape[1], LANES):
+            pair = line[:, a : a + LANES]
+            run, rank = ranks(pair, column_of(pair, LANES), 2)
+            first = a // slots * SHORT_PAD
+            second = iota((1, LANES), 1) >= slots
+            want = rank + jnp.where(second, first + SHORT_PAD, first)
+            row = iota((LANES, LANES), 0)
+            blocks.append(((row == want) & (run == index[0])).astype(F32).astype(BF16))
+        short_out[...] = lax.dot_general(
+            pick_out[...],
+            jnp.concatenate(blocks, axis=1),
+            (((1,), (1,)), ((), ())),
+            preferred_element_type=F32,
+        ).astype(BF16)
     res_out[...] = res
     dir_out[...] = direction
     step_out[...] = step
     curved_out[...] = curved
 
 
-def last_kernel(n_i, order, slots, ww, num, res, direction, step, curved, pick, *refs):
+def last_kernel(n_i, short, order, slots, ww, num, res, direction, step, curved, pick, *refs):
     msgs, (step_out, res_out) = sorted_as(order, refs[:n_i]), refs[n_i:]
-    image = exact_pick(pick[...], slot_values(msgs, slots))
-    new = advance(msgs, slots, ww, numbers_of(num))
+    if short:
+        pad = jnp.zeros((SHORT_PAD - SHORT, LANES), F32)
+        values = jnp.concatenate([piece for msg in msgs for piece in (msg[...], pad)], axis=0)
+        new = advance(msgs, SHORT - TAIL, ww, numbers_of(num), CAP - (SHORT - TAIL))
+    else:
+        values = slot_values(msgs, slots)
+        new = advance(msgs, slots, ww, numbers_of(num))
+    image = exact_pick(pick[...], values)
     last = res[...] + new["beta"] * direction[...]
     step_out[...] = step[...] + new["alpha"] * last
     image = image + new["beta"] * curved[...] + LAMBDA * last
     res_out[...] = res[...] - new["alpha"] * image
 
 
-def exchange(x, axis, order=(3, 2, 1)):
+def exchange(x, axis, order=FEAT_ORDER):
     size = lax.axis_size(axis)
     if size != 4:
         return [lax.all_gather(x, axis, axis=0, tiled=True)]
     return [x] + [lax.ppermute(x, axis, [(i, i ^ k) for i in range(size)]) for k in order]
+
+
+def exchange_each(arrays, axis):
+    keys = (3, 2, 1)
+    return [arrays[0]] + [
+        lax.ppermute(x, axis, [(i, i ^ k) for i in range(4)])
+        for k, x in zip(keys, arrays[1:], strict=True)
+    ]
 
 
 def sorted_as(order, refs):
@@ -422,6 +488,7 @@
     scale = float(row_total) / float(sample_ids.shape[1])
     index = lax.axis_index("inst").astype(I32).reshape(1)
     grid, msg_shape = f32(SUB, LANES), f32(slots + TAIL, LANES)
+    short = inst == 4 and own_blocks == CAP_RUN
     tile_shape = jax.ShapeDtypeStruct((slots, edge, edge), BF16)
     picks = jax.ShapeDtypeStruct
 
@@ -444,16 +511,18 @@
             pltpu.SemaphoreType.DMA((4,)),
         ],
     )
-    mask, row_pick, cols_line, own = call(
+    mask, row_pick, cols_line, own, *send = call(
         prep_kernel,
         (
             sample_ids,
             tile_rows.reshape(1, slots),
             tile_cols.reshape(1, slots),
             tile_count,
+            index,
         ),
-        [VM] * 3 + [SM],
-        [grid, picks((slots, LANES), BF16), grid, f32(slots, LANES)],
+        [VM] * 3 + [SM] * 2,
+        [grid, picks((slots, LANES), BF16), grid, f32(slots, LANES)]
+        + [picks((4 * SHORT, slots), BF16)] * short,
     )
     (turned,) = call(turn_kernel, (tiles,), [VM], [tile_shape])
     got = exchange(part, "feat")
@@ -467,7 +536,7 @@
     msgs = exchange(msg, "inst", ORDERS[0])
     n_i = len(msgs)
     (match,) = call(
-        functools.partial(match_kernel, n_i),
+        functools.partial(match_kernel, n_i, ORDERS[0]),
         (own, *msgs),
         [VM] * (1 + n_i),
         [picks((slots, slots * inst), BF16)],
@@ -500,8 +569,19 @@
             [VM] * (3 + n_i + len(state)),
             [f32(6 * SUB, LANES), grid],
         )
+        if short and k == ITERS - 2:
+            to_each = call(
+                functools.partial(next_kernel, n_f, True),
+                (tiles, row_pick, c, vec, num, *got, *send),
+                [VM] * (6 + n_f),
+                [f32(SHORT, LANES)] * 4,
+                scratch=[pltpu.VMEM((slots, LANES), F32)],
+            )
+            history.append(exchange_each(to_each, "inst"))
+            nums.append(num)
+            break
         msg, *kept = call(
-            functools.partial(next_kernel, n_f),
+            functools.partial(next_kernel, n_f, False),
             (tiles, row_pick, c, vec, num, *got),
             [VM] * (5 + n_f),
             [msg_shape] + [grid, grid] * (k < ITERS - 2),
@@ -511,13 +591,14 @@
         nums.append(num)
     block = f32(own_blocks, edge)
     *dense, pick = call(
-        functools.partial(dense_kernel, n_i, ORDERS, slots, ITERS),
+        functools.partial(dense_kernel, n_i, short, ORDERS, slots, ITERS),
         (w, index, *(ref for group in history[:ITERS] for ref in group), *nums),
         [VM, SM] + [VM] * (n_i * ITERS + len(nums)),
-        [block, block, block, block, picks((own_blocks, slots * inst), BF16)],
+        [block] * 4 + [picks((own_blocks, LANES if short else slots * inst), BF16)],
+        scratch=[pltpu.VMEM((own_blocks, slots * inst), BF16)] * short,
     )
     step, res = call(
-        functools.partial(last_kernel, n_i, ORDERS[ITERS], slots),
+        functools.partial(last_kernel, n_i, short, ORDERS[ITERS], slots),
         (ww, nums[-1], *dense, pick, *history[-1]),
         [VM] * (7 + n_i),
         [block, block],

time: 56.7 us -> 56.5 us (level)
  waiting for transfers between devices: 19 us -> 18.4 us
    ppermute x24 -> x21, starting transfers between devices: 26.7 us -> 22.2 us  [exchange(): lax.ppermute(x, axis, [(i, i ^ k) for i in range(size)])]
    ppermute x0 -> x3, starting transfers between devices: none -> 4.45 us  [exchange_each(): lax.ppermute(x, axis, [(i, i ^ k) for i in range(4)])]
    ppermute x24 -> x21, waiting for transfers between devices: 19 us -> 16.9 us  [exchange(): lax.ppermute(x, axis, [(i, i ^ k) for i in range(size)])]
    ppermute x0 -> x3, waiting for transfers between devices: none -> 1.48 us  [exchange_each(): lax.ppermute(x, axis, [(i, i ^ k) for i in range(4)])]
where the time goes in v4:
time: 56.5 us; the launch traced here: 56.3 us
  starting transfers between devices  26.7 us (47%)
  waiting for transfers between devices  18.4 us (33%)
  Pallas kernels  9.77 us (17%)
  between operations  1.44 us (3%)
    ppermute x21, starting transfers between devices, exchange(): lax.ppermute(x, axis, [(i, i ^ k) for i in range(size)])  22.2 us
    ppermute x21, waiting for transfers between devices, exchange(): lax.ppermute(x, axis, [(i, i ^ k) for i in range(size)])  16.9 us
    pallas_call x15, Pallas kernels, call(): pl.pallas_call(kernel, in_specs=in_specs, out_shape=outs, out_specs=out_s...  9.77 us
    ppermute x3, starting transfers between devices, exchange_each(): lax.ppermute(x, axis, [(i, i ^ k) for i in range(4)])  4.45 us
    ppermute x3, waiting for transfers between devices, exchange_each(): lax.ppermute(x, axis, [(i, i ^ k) for i in range(4)])  1.48 us
  transfers between devices with their start and end apart: 24, of which 18 were waited for; matrix products, arithmetic and copies ran while one was open for 0% of the time, Pallas kernels for 3%

profile of v4, /device:TPU:0, one launch (start us, length us, event | category | flops | bytes accessed | tf_op | source)
XLA Modules:
  0.0 56.3 jit_solution(10315357983070102736)
XLA Ops:
  0.6 0.0 copy-start.1
  1.3 2.7 %shard_map.86 = (f32[16,128]{1,0:T(8,128)S(1)}, bf16[64,128,128]{2,1,0:T(8,128)(2,1)S(1)}, f32[2048,128]{1,0:T(8,128)S(1)}, f32[512,128]{1,0:T(8,128)S(1)}) custom-call(s32[1,1]{1,0:T(1,128)S(6)} %copy.9.count, s32[64]{0:T(128)} %bitcast.11, s32[64]{0:T(128)} %bitcast.13, bf16[64,128,128]{2,1,0:T(8,128)(2,1)} %bitcast.15, f32[2048,128]{1,0:T(8,128)} %bitcast.16), custom_call_target="tpu_custom_call" | custom-call | flops 2097152 | bytes 1048576 | tf_op jit(solution)/shard_map/pallas_call | solution.py:30
  4.0 2.4 %collective-permute-start.2 = (f32[16,128]{1,0:T(8,128)S(1)}, f32[16,128]{1,0:T(8,128)S(1)}, u32[]{:S(2)}, u32[]{:S(2)}) collective-permute-start(f32[16,128]{1,0:T(8,128)S(1)} %get-tuple-element.40.refs_0_), channel_id=1, source_target_pairs={{0,3},{1,2},{2,1},{3,0},{4,7},{5,6},{6,5},{7,4},{8,11},{9,10},{10,... | collective-permute-start | bytes 24584 | tf_op jit(solution)/shard_map/ppermute | solution.py:458
  6.5 0.6 %collective-permute-start.1 = (f32[16,128]{1,0:T(8,128)S(1)}, f32[16,128]{1,0:T(8,128)S(1)}, u32[]{:S(2)}, u32[]{:S(2)}) collective-permute-start(f32[16,128]{1,0:T(8,128)S(1)} %get-tuple-element.40.refs_0_), channel_id=1, source_target_pairs={{0,2},{1,3},{2,0},{3,1},{4,6},{5,7},{6,4},{7,5},{8,10},{9,11},{10,... | collective-permute-start | bytes 24584 | tf_op jit(solution)/shard_map/ppermute | solution.py:458
  7.1 0.0 collective-permute-start
  7.2 0.0 copy-done.2
  7.2 0.2 shard_map.87
  7.4 0.5 collective-permute-done.2.refs_3_
  7.9 2.3 %collective-permute-done.1.refs_2_ = f32[16,128]{1,0:T(8,128)S(1)} collective-permute-done((f32[16,128]{1,0:T(8,128)S(1)}, f32[16,128]{1,0:T(8,128)S(1)}, u32[]{:S(2)}, u32[]{:S(2)}) %collective-permute-start.1) | collective-permute-done | bytes 8224 | tf_op jit(solution)/shard_map/ppermute | solution.py:458
  10.1 0.0 collective-permute-done.refs_1_
  10.2 0.5 shard_map.88
  10.7 3.7 %collective-permute-start.5 = (f32[72,128]{1,0:T(8,128)S(1)}, f32[72,128]{1,0:T(8,128)S(1)}, u32[]{:S(2)}, u32[]{:S(2)}) collective-permute-start(f32[72,128]{1,0:T(8,128)S(1)} %get-tuple-element.47.refs_0_), channel_id=1, source_target_pairs={{0,12},{4,8},{8,4},{12,0},{1,13},{5,9},{9,5},{13,1},{2,14},{6,10},... | collective-permute-start | bytes 110600 | tf_op jit(solution)/shard_map/ppermute | solution.py:458
  14.4 0.0 collective-permute-start.4
  14.4 0.8 %collective-permute-start.3 = (f32[72,128]{1,0:T(8,128)S(1)}, f32[72,128]{1,0:T(8,128)S(1)}, u32[]{:S(2)}, u32[]{:S(2)}) collective-permute-start(f32[72,128]{1,0:T(8,128)S(1)} %get-tuple-element.47.refs_0_), channel_id=1, source_target_pairs={{0,4},{4,0},{8,12},{12,8},{1,5},{5,1},{9,13},{13,9},{2,6},{6,2},{1... | collective-permute-start | bytes 110600 | tf_op jit(solution)/shard_map/ppermute | solution.py:458
  15.1 0.6 %shard_map.89.turned = bf16[64,128,128]{2,1,0:T(8,128)(2,1)S(1)} custom-call(bf16[64,128,128]{2,1,0:T(8,128)(2,1)S(1)} %get-tuple-element.36.tiles), custom_call_target="tpu_custom_call" | custom-call | flops 2097152 | bytes 1048576 | tf_op jit(solution)/shard_map/pallas_call | solution.py:30
  15.7 1.2 %collective-permute-done.5.refs_3_ = f32[72,128]{1,0:T(8,128)S(1)} collective-permute-done((f32[72,128]{1,0:T(8,128)S(1)}, f32[72,128]{1,0:T(8,128)S(1)}, u32[]{:S(2)}, u32[]{:S(2)}) %collective-permute-start.5) | collective-permute-done | bytes 36896 | tf_op jit(solution)/shard_map/ppermute | solution.py:458
  16.9 2.3 %collective-permute-done.4.refs_2_ = f32[72,128]{1,0:T(8,128)S(1)} collective-permute-done((f32[72,128]{1,0:T(8,128)S(1)}, f32[72,128]{1,0:T(8,128)S(1)}, u32[]{:S(2)}, u32[]{:S(2)}) %collective-permute-start.4) | collective-permute-done | bytes 36896 | tf_op jit(solution)/shard_map/ppermute | solution.py:458
  19.2 0.0 collective-permute-done.3.refs_1_
  19.2 0.6 %shard_map.91.refs_0_ = f32[8,128]{1,0:T(8,128)S(1)} custom-call(bf16[64,128,128]{2,1,0:T(8,128)(2,1)S(1)} %shard_map.89.turned, f32[512,128]{1,0:T(8,128)S(1)} %get-tuple-element.45.row_mask, bf16[64,256]{1,0:T(8,128)(2,1)S(1)} %shard_map.90.match, f32[72,128]{1,0:T(8,128)S(1)} %get-tuple-element.47.refs_0_, f32[72,128]{1,0:T(8,128)S(1)} %collective-permute-done.3.refs_1_, ...), custom_call_target="tpu_custom_call" | custom-call | flops 2097152 | bytes 1048576 | tf_op jit(solution)/shard_map/pallas_call | solution.py:30
  19.8 0.1 collective-permute-start.8
  19.9 0.7 %collective-permute-start.7 = (f32[8,128]{1,0:T(8,128)S(1)}, f32[8,128]{1,0:T(8,128)S(1)}, u32[]{:S(2)}, u32[]{:S(2)}) collective-permute-start(f32[8,128]{1,0:T(8,128)S(1)} %shard_map.91.refs_0_), channel_id=1, source_target_pairs={{0,2},{1,3},{2,0},{3,1},{4,6},{5,7},{6,4},{7,5},{8,10},{9,11},{10,... | collective-permute-start | bytes 12296 | tf_op jit(solution)/shard_map/ppermute | solution.py:458
  20.6 1.1 %collective-permute-start.6 = (f32[8,128]{1,0:T(8,128)S(1)}, f32[8,128]{1,0:T(8,128)S(1)}, u32[]{:S(2)}, u32[]{:S(2)}) collective-permute-start(f32[8,128]{1,0:T(8,128)S(1)} %shard_map.91.refs_0_), channel_id=1, source_target_pairs={{0,1},{1,0},{2,3},{3,2},{4,5},{5,4},{6,7},{7,6},{8,9},{9,8},{10,11... | collective-permute-start | bytes 12296 | tf_op jit(solution)/shard_map/ppermute | solution.py:458
  21.8 1.2 %collective-permute-done.8.refs_3_ = f32[8,128]{1,0:T(8,128)S(1)} collective-permute-done((f32[8,128]{1,0:T(8,128)S(1)}, f32[8,128]{1,0:T(8,128)S(1)}, u32[]{:S(2)}, u32[]{:S(2)}) %collective-permute-start.8) | collective-permute-done | bytes 4128 | tf_op jit(solution)/shard_map/ppermute | solution.py:458
  22.9 0.7 %collective-permute-done.7.refs_2_ = f32[8,128]{1,0:T(8,128)S(1)} collective-permute-done((f32[8,128]{1,0:T(8,128)S(1)}, f32[8,128]{1,0:T(8,128)S(1)}, u32[]{:S(2)}, u32[]{:S(2)}) %collective-permute-start.7) | collective-permute-done | bytes 4128 | tf_op jit(solution)/shard_map/ppermute | solution.py:458
  23.6 0.0 collective-permute-done.6.refs_1_
  23.6 0.5 shard_map.92
  24.1 1.5 %collective-permute-start.11 = (f32[72,128]{1,0:T(8,128)S(1)}, f32[72,128]{1,0:T(8,128)S(1)}, u32[]{:S(2)}, u32[]{:S(2)}) collective-permute-start(f32[72,128]{1,0:T(8,128)S(1)} %get-tuple-element.48.refs_0_.refs_4_), channel_id=1, source_target_pairs={{0,12},{4,8},{8,4},{12,0},{1,13},{5,9},{9,5},{13,1},{2,14},{6,10},... | collective-permute-start | bytes 110600 | tf_op jit(solution)/shard_map/ppermute | solution.py:458
  25.6 0.6 %collective-permute-start.10 = (f32[72,128]{1,0:T(8,128)S(1)}, f32[72,128]{1,0:T(8,128)S(1)}, u32[]{:S(2)}, u32[]{:S(2)}) collective-permute-start(f32[72,128]{1,0:T(8,128)S(1)} %get-tuple-element.48.refs_0_.refs_4_), channel_id=1, source_target_pairs={{0,8},{4,12},{8,0},{12,4},{1,9},{5,13},{9,1},{13,5},{2,10},{6,14},... | collective-permute-start | bytes 110600 | tf_op jit(solution)/shard_map/ppermute | solution.py:458
  26.3 2.3 %collective-permute-start.9 = (f32[72,128]{1,0:T(8,128)S(1)}, f32[72,128]{1,0:T(8,128)S(1)}, u32[]{:S(2)}, u32[]{:S(2)}) collective-permute-start(f32[72,128]{1,0:T(8,128)S(1)} %get-tuple-element.48.refs_0_.refs_4_), channel_id=1, source_target_pairs={{0,4},{4,0},{8,12},{12,8},{1,5},{5,1},{9,13},{13,9},{2,6},{6,2},{1... | collective-permute-start | bytes 110600 | tf_op jit(solution)/shard_map/ppermute | solution.py:458
  28.6 1.8 %collective-permute-done.11.refs_3_.refs_7_ = f32[72,128]{1,0:T(8,128)S(1)} collective-permute-done((f32[72,128]{1,0:T(8,128)S(1)}, f32[72,128]{1,0:T(8,128)S(1)}, u32[]{:S(2)}, u32[]{:S(2)}) %collective-permute-start.11) | collective-permute-done | bytes 36896 | tf_op jit(solution)/shard_map/ppermute | solution.py:458
  30.3 0.3 collective-permute-done.10.refs_2_.refs_6_
  30.7 0.3 collective-permute-done.9.refs_1_.refs_5_
  31.0 0.6 %shard_map.94.refs_0_ = f32[8,128]{1,0:T(8,128)S(1)} custom-call(bf16[64,128,128]{2,1,0:T(8,128)(2,1)S(1)} %shard_map.89.turned, f32[512,128]{1,0:T(8,128)S(1)} %get-tuple-element.45.row_mask, bf16[64,256]{1,0:T(8,128)(2,1)S(1)} %shard_map.90.match, f32[72,128]{1,0:T(8,128)S(1)} %get-tuple-element.48.refs_0_.refs_4_, ...), custom_call_target="tpu_custom_call" | custom-call | flops 2097152 | bytes 1048576 | tf_op jit(solution)/shard_map/pallas_call | solution.py:30
  31.6 0.3 collective-permute-start.14
  31.9 0.7 %collective-permute-start.13 = (f32[8,128]{1,0:T(8,128)S(1)}, f32[8,128]{1,0:T(8,128)S(1)}, u32[]{:S(2)}, u32[]{:S(2)}) collective-permute-start(f32[8,128]{1,0:T(8,128)S(1)} %shard_map.94.refs_0_), channel_id=1, source_target_pairs={{0,2},{1,3},{2,0},{3,1},{4,6},{5,7},{6,4},{7,5},{8,10},{9,11},{10,... | collective-permute-start | bytes 12296 | tf_op jit(solution)/shard_map/ppermute | solution.py:458
  32.6 0.9 %collective-permute-start.12 = (f32[8,128]{1,0:T(8,128)S(1)}, f32[8,128]{1,0:T(8,128)S(1)}, u32[]{:S(2)}, u32[]{:S(2)}) collective-permute-start(f32[8,128]{1,0:T(8,128)S(1)} %shard_map.94.refs_0_), channel_id=1, source_target_pairs={{0,1},{1,0},{2,3},{3,2},{4,5},{5,4},{6,7},{7,6},{8,9},{9,8},{10,11... | collective-permute-start | bytes 12296 | tf_op jit(solution)/shard_map/ppermute | solution.py:458
  33.5 0.1 shard_map.93
  33.7 1.0 %collective-permute-done.14.refs_3_ = f32[8,128]{1,0:T(8,128)S(1)} collective-permute-done((f32[8,128]{1,0:T(8,128)S(1)}, f32[8,128]{1,0:T(8,128)S(1)}, u32[]{:S(2)}, u32[]{:S(2)}) %collective-permute-start.14) | collective-permute-done | bytes 4128 | tf_op jit(solution)/shard_map/ppermute | solution.py:458
  34.7 0.8 %collective-permute-done.13.refs_2_ = f32[8,128]{1,0:T(8,128)S(1)} collective-permute-done((f32[8,128]{1,0:T(8,128)S(1)}, f32[8,128]{1,0:T(8,128)S(1)}, u32[]{:S(2)}, u32[]{:S(2)}) %collective-permute-start.13) | collective-permute-done | bytes 4128 | tf_op jit(solution)/shard_map/ppermute | solution.py:458
  35.5 0.0 collective-permute-done.12.refs_1_
  35.5 0.6 shard_map.95
  36.1 2.1 %collective-permute-start.17 = (f32[72,128]{1,0:T(8,128)S(1)}, f32[72,128]{1,0:T(8,128)S(1)}, u32[]{:S(2)}, u32[]{:S(2)}) collective-permute-start(f32[72,128]{1,0:T(8,128)S(1)} %get-tuple-element.52.refs_0_.refs_8_), channel_id=1, source_target_pairs={{0,12},{4,8},{8,4},{12,0},{1,13},{5,9},{9,5},{13,1},{2,14},{6,10},... | collective-permute-start | bytes 110600 | tf_op jit(solution)/shard_map/ppermute | solution.py:458
  38.2 0.7 %collective-permute-start.16 = (f32[72,128]{1,0:T(8,128)S(1)}, f32[72,128]{1,0:T(8,128)S(1)}, u32[]{:S(2)}, u32[]{:S(2)}) collective-permute-start(f32[72,128]{1,0:T(8,128)S(1)} %get-tuple-element.52.refs_0_.refs_8_), channel_id=1, source_target_pairs={{0,8},{4,12},{8,0},{12,4},{1,9},{5,13},{9,1},{13,5},{2,10},{6,14},... | collective-permute-start | bytes 110600 | tf_op jit(solution)/shard_map/ppermute | solution.py:458
  39.0 1.6 %collective-permute-start.15 = (f32[72,128]{1,0:T(8,128)S(1)}, f32[72,128]{1,0:T(8,128)S(1)}, u32[]{:S(2)}, u32[]{:S(2)}) collective-permute-start(f32[72,128]{1,0:T(8,128)S(1)} %get-tuple-element.52.refs_0_.refs_8_), channel_id=1, source_target_pairs={{0,4},{4,0},{8,12},{12,8},{1,5},{5,1},{9,13},{13,9},{2,6},{6,2},{1... | collective-permute-start | bytes 110600 | tf_op jit(solution)/shard_map/ppermute | solution.py:458
  40.6 1.4 %collective-permute-done.17.refs_3_.refs_11_ = f32[72,128]{1,0:T(8,128)S(1)} collective-permute-done((f32[72,128]{1,0:T(8,128)S(1)}, f32[72,128]{1,0:T(8,128)S(1)}, u32[]{:S(2)}, u32[]{:S(2)}) %collective-permute-start.17) | collective-permute-done | bytes 36896 | tf_op jit(solution)/shard_map/ppermute | solution.py:458
  42.0 1.2 %collective-permute-done.16.refs_2_.refs_10_ = f32[72,128]{1,0:T(8,128)S(1)} collective-permute-done((f32[72,128]{1,0:T(8,128)S(1)}, f32[72,128]{1,0:T(8,128)S(1)}, u32[]{:S(2)}, u32[]{:S(2)}) %collective-permute-start.16) | collective-permute-done | bytes 36896 | tf_op jit(solution)/shard_map/ppermute | solution.py:458
  43.2 0.3 collective-permute-done.15.refs_1_.refs_9_
  43.5 0.6 %shard_map.98.refs_0_ = f32[8,128]{1,0:T(8,128)S(1)} custom-call(bf16[64,128,128]{2,1,0:T(8,128)(2,1)S(1)} %shard_map.89.turned, f32[512,128]{1,0:T(8,128)S(1)} %get-tuple-element.45.row_mask, bf16[64,256]{1,0:T(8,128)(2,1)S(1)} %shard_map.90.match, f32[72,128]{1,0:T(8,128)S(1)} %get-tuple-element.52.refs_0_.refs_8_, ...), custom_call_target="tpu_custom_call" | custom-call | flops 2097152 | bytes 1048576 | tf_op jit(solution)/shard_map/pallas_call | solution.py:30
  44.1 0.1 collective-permute-start.20
  44.2 0.9 %collective-permute-start.19 = (f32[8,128]{1,0:T(8,128)S(1)}, f32[8,128]{1,0:T(8,128)S(1)}, u32[]{:S(2)}, u32[]{:S(2)}) collective-permute-start(f32[8,128]{1,0:T(8,128)S(1)} %shard_map.98.refs_0_), channel_id=1, source_target_pairs={{0,2},{1,3},{2,0},{3,1},{4,6},{5,7},{6,4},{7,5},{8,10},{9,11},{10,... | collective-permute-start | bytes 12296 | tf_op jit(solution)/shard_map/ppermute | solution.py:458
  45.0 1.0 %collective-permute-start.18 = (f32[8,128]{1,0:T(8,128)S(1)}, f32[8,128]{1,0:T(8,128)S(1)}, u32[]{:S(2)}, u32[]{:S(2)}) collective-permute-start(f32[8,128]{1,0:T(8,128)S(1)} %shard_map.98.refs_0_), channel_id=1, source_target_pairs={{0,1},{1,0},{2,3},{3,2},{4,5},{5,4},{6,7},{7,6},{8,9},{9,8},{10,11... | collective-permute-start | bytes 12296 | tf_op jit(solution)/shard_map/ppermute | solution.py:458
  46.0 0.2 shard_map.96
  46.2 0.9 %collective-permute-done.20.refs_3_ = f32[8,128]{1,0:T(8,128)S(1)} collective-permute-done((f32[8,128]{1,0:T(8,128)S(1)}, f32[8,128]{1,0:T(8,128)S(1)}, u32[]{:S(2)}, u32[]{:S(2)}) %collective-permute-start.20) | collective-permute-done | bytes 4128 | tf_op jit(solution)/shard_map/ppermute | solution.py:458
  47.2 0.7 %collective-permute-done.19.refs_2_ = f32[8,128]{1,0:T(8,128)S(1)} collective-permute-done((f32[8,128]{1,0:T(8,128)S(1)}, f32[8,128]{1,0:T(8,128)S(1)}, u32[]{:S(2)}, u32[]{:S(2)}) %collective-permute-start.19) | collective-permute-done | bytes 4128 | tf_op jit(solution)/shard_map/ppermute | solution.py:458
  47.9 0.0 collective-permute-done.18.refs_1_
  47.9 0.7 %shard_map.99 = (f32[24,128]{1,0:T(8,128)S(1)}, f32[24,128]{1,0:T(8,128)S(1)}, f32[24,128]{1,0:T(8,128)S(1)}, f32[24,128]{1,0:T(8,128)S(1)}) custom-call(bf16[64,128,128]{2,1,0:T(8,128)(2,1)S(1)} %get-tuple-element.36.tiles, bf16[64,128]{1,0:T(8,128)(2,1)S(1)} %get-tuple-element.37.row_pick, f32[8,128]{1,0:T(8,128)S(1)} %get-tuple-element.43.c, ...), custom_call_target="tpu_custom_call" | custom-call | flops 2097152 | bytes 1048576 | tf_op jit(solution)/shard_map/pallas_call | solution.py:30
  48.6 2.1 %collective-permute-start.21 = (f32[24,128]{1,0:T(8,128)S(1)}, f32[24,128]{1,0:T(8,128)S(1)}, u32[]{:S(2)}, u32[]{:S(2)}) collective-permute-start(f32[24,128]{1,0:T(8,128)S(1)} %get-tuple-element.65), channel_id=1, source_target_pairs={{0,12},{4,8},{8,4},{12,0},{1,13},{5,9},{9,5},{13,1},{2,14},{6,10},... | collective-permute-start | bytes 36872 | tf_op jit(solution)/shard_map/ppermute | solution.py:464
  50.6 0.5 collective-permute-start.22
  51.1 1.9 %collective-permute-start.23 = (f32[24,128]{1,0:T(8,128)S(1)}, f32[24,128]{1,0:T(8,128)S(1)}, u32[]{:S(2)}, u32[]{:S(2)}) collective-permute-start(f32[24,128]{1,0:T(8,128)S(1)} %get-tuple-element.67), channel_id=1, source_target_pairs={{0,4},{4,0},{8,12},{12,8},{1,5},{5,1},{9,13},{13,9},{2,6},{6,2},{1... | collective-permute-start | bytes 36872 | tf_op jit(solution)/shard_map/ppermute | solution.py:464
  53.0 0.7 %shard_map.97 = (f32[512,128]{1,0:T(8,128)S(1)}, f32[512,128]{1,0:T(8,128)S(1)}, f32[512,128]{1,0:T(8,128)S(1)}, f32[512,128]{1,0:T(8,128)S(1)}, bf16[512,128]{1,0:T(8,128)(2,1)S(1)}) custom-call(f32[2048,128]{1,0:T(8,128)S(1)} %get-tuple-element.56.w, s32[1]{0:T(128)} %bitcast.6.index, f32[72,128]{1,0:T(8,128)S(1)} %get-tuple-element.47.refs_0_, ...), custom_call_target="tpu_custom_call" | custom-call | flops 2097152 | bytes 1048576 | tf_op jit(solution)/shard_map/pallas_call | solution.py:30
  53.8 0.4 collective-permute-done.21.refs_1_
  54.1 1.1 %collective-permute-done.22.refs_2_ = f32[24,128]{1,0:T(8,128)S(1)} collective-permute-done((f32[24,128]{1,0:T(8,128)S(1)}, f32[24,128]{1,0:T(8,128)S(1)}, u32[]{:S(2)}, u32[]{:S(2)}) %collective-permute-start.22) | collective-permute-done | bytes 12320 | tf_op jit(solution)/shard_map/ppermute | solution.py:464
  55.2 0.0 collective-permute-done.23.refs_3_
  55.2 1.1 %shard_map.100 = (f32[512,128]{1,0:T(8,128)}, f32[512,128]{1,0:T(8,128)}) custom-call(f32[8,128]{1,0:T(8,128)S(1)} %get-tuple-element.41.ww, f32[8,128]{1,0:T(8,128)S(1)} %get-tuple-element.55.refs_13_.num, f32[512,128]{1,0:T(8,128)S(1)} %get-tuple-element.57.res, f32[512,128]{1,0:T(8,128)S(1)} %get-tuple-element.58.direction, ...), custom_call_target="tpu_custom_call" | custom-call | flops 2097152 | bytes 1048576 | tf_op jit(solution)/shard_map/pallas_call | solution.py:30
  (7 shorter events, 0.0 us)
Async XLA Ops:
  0.6 6.5 %copy-start.1 = (s32[1,1,64]{2,1,0:T(1,128)S(1)}, s32[1,1,64]{2,1,0:T(1,128)}, u32[]{:S(2)}) copy-start(s32[1,1,64]{2,1,0:T(1,128)} %param.8) | copy-start | bytes 772
  0.6 6.5 %copy-start.2 = (s32[1,1,64]{2,1,0:T(1,128)S(1)}, s32[1,1,64]{2,1,0:T(1,128)}, u32[]{:S(2)}) copy-start(s32[1,1,64]{2,1,0:T(1,128)} %param.9) | copy-start | bytes 772
  0.7 6.5 %copy-start.3 = (s32[1,512]{1,0:T(1,128)S(1)}, s32[1,512]{1,0:T(1,128)}, u32[]{:S(2)}) copy-start(s32[1,512]{1,0:T(1,128)} %ids.1) | copy-start | bytes 6148
  0.7 9.5 %copy-start = (s32[1,1024]{1,0:T(1,128)S(1)}, s32[1,1024]{1,0:T(1,128)}, u32[]{:S(2)}) copy-start(s32[1,1024]{1,0:T(1,128)} %param.12) | copy-start | bytes 12292
  4.0 3.8 %collective-permute-start.2 = (f32[16,128]{1,0:T(8,128)S(1)}, f32[16,128]{1,0:T(8,128)S(1)}, u32[]{:S(2)}, u32[]{:S(2)}) collective-permute-start(f32[16,128]{1,0:T(8,128)S(1)} %get-tuple-element.40.refs_0_), channel_id=1, source_target_pairs={{0,3},{1,2},{2,1},{3,0},{4,7},{5,6},{6,5},{7,4},{8,11},{9,10},{10,... | collective-permute-start | bytes 24584 | tf_op jit(solution)/shard_map/ppermute | solution.py:458
  6.5 3.7 %collective-permute-start.1 = (f32[16,128]{1,0:T(8,128)S(1)}, f32[16,128]{1,0:T(8,128)S(1)}, u32[]{:S(2)}, u32[]{:S(2)}) collective-permute-start(f32[16,128]{1,0:T(8,128)S(1)} %get-tuple-element.40.refs_0_), channel_id=1, source_target_pairs={{0,2},{1,3},{2,0},{3,1},{4,6},{5,7},{6,4},{7,5},{8,10},{9,11},{10,... | collective-permute-start | bytes 24584 | tf_op jit(solution)/shard_map/ppermute | solution.py:458
  7.1 3.0 %collective-permute-start = (f32[16,128]{1,0:T(8,128)S(1)}, f32[16,128]{1,0:T(8,128)S(1)}, u32[]{:S(2)}, u32[]{:S(2)}) collective-permute-start(f32[16,128]{1,0:T(8,128)S(1)} %get-tuple-element.40.refs_0_), channel_id=1, source_target_pairs={{0,1},{1,0},{2,3},{3,2},{4,5},{5,4},{6,7},{7,6},{8,9},{9,8},{10,11... | collective-permute-start | bytes 24584 | tf_op jit(solution)/shard_map/ppermute | solution.py:458
  10.7 6.3 %collective-permute-start.5 = (f32[72,128]{1,0:T(8,128)S(1)}, f32[72,128]{1,0:T(8,128)S(1)}, u32[]{:S(2)}, u32[]{:S(2)}) collective-permute-start(f32[72,128]{1,0:T(8,128)S(1)} %get-tuple-element.47.refs_0_), channel_id=1, source_target_pairs={{0,12},{4,8},{8,4},{12,0},{1,13},{5,9},{9,5},{13,1},{2,14},{6,10},... | collective-permute-start | bytes 110600 | tf_op jit(solution)/shard_map/ppermute | solution.py:458
  14.4 4.9 %collective-permute-start.4 = (f32[72,128]{1,0:T(8,128)S(1)}, f32[72,128]{1,0:T(8,128)S(1)}, u32[]{:S(2)}, u32[]{:S(2)}) collective-permute-start(f32[72,128]{1,0:T(8,128)S(1)} %get-tuple-element.47.refs_0_), channel_id=1, source_target_pairs={{0,8},{4,12},{8,0},{12,4},{1,9},{5,13},{9,1},{13,5},{2,10},{6,14},... | collective-permute-start | bytes 110600 | tf_op jit(solution)/shard_map/ppermute | solution.py:458
  14.4 4.9 %collective-permute-start.3 = (f32[72,128]{1,0:T(8,128)S(1)}, f32[72,128]{1,0:T(8,128)S(1)}, u32[]{:S(2)}, u32[]{:S(2)}) collective-permute-start(f32[72,128]{1,0:T(8,128)S(1)} %get-tuple-element.47.refs_0_), channel_id=1, source_target_pairs={{0,4},{4,0},{8,12},{12,8},{1,5},{5,1},{9,13},{13,9},{2,6},{6,2},{1... | collective-permute-start | bytes 110600 | tf_op jit(solution)/shard_map/ppermute | solution.py:458
  19.8 3.1 %collective-permute-start.8 = (f32[8,128]{1,0:T(8,128)S(1)}, f32[8,128]{1,0:T(8,128)S(1)}, u32[]{:S(2)}, u32[]{:S(2)}) collective-permute-start(f32[8,128]{1,0:T(8,128)S(1)} %shard_map.91.refs_0_), channel_id=1, source_target_pairs={{0,3},{1,2},{2,1},{3,0},{4,7},{5,6},{6,5},{7,4},{8,11},{9,10},{10,... | collective-permute-start | bytes 12296 | tf_op jit(solution)/shard_map/ppermute | solution.py:458
  19.9 3.7 %collective-permute-start.7 = (f32[8,128]{1,0:T(8,128)S(1)}, f32[8,128]{1,0:T(8,128)S(1)}, u32[]{:S(2)}, u32[]{:S(2)}) collective-permute-start(f32[8,128]{1,0:T(8,128)S(1)} %shard_map.91.refs_0_), channel_id=1, source_target_pairs={{0,2},{1,3},{2,0},{3,1},{4,6},{5,7},{6,4},{7,5},{8,10},{9,11},{10,... | collective-permute-start | bytes 12296 | tf_op jit(solution)/shard_map/ppermute | solution.py:458
  20.6 3.0 %collective-permute-start.6 = (f32[8,128]{1,0:T(8,128)S(1)}, f32[8,128]{1,0:T(8,128)S(1)}, u32[]{:S(2)}, u32[]{:S(2)}) collective-permute-start(f32[8,128]{1,0:T(8,128)S(1)} %shard_map.91.refs_0_), channel_id=1, source_target_pairs={{0,1},{1,0},{2,3},{3,2},{4,5},{5,4},{6,7},{7,6},{8,9},{9,8},{10,11... | collective-permute-start | bytes 12296 | tf_op jit(solution)/shard_map/ppermute | solution.py:458
  24.1 6.2 %collective-permute-start.11 = (f32[72,128]{1,0:T(8,128)S(1)}, f32[72,128]{1,0:T(8,128)S(1)}, u32[]{:S(2)}, u32[]{:S(2)}) collective-permute-start(f32[72,128]{1,0:T(8,128)S(1)} %get-tuple-element.48.refs_0_.refs_4_), channel_id=1, source_target_pairs={{0,12},{4,8},{8,4},{12,0},{1,13},{5,9},{9,5},{13,1},{2,14},{6,10},... | collective-permute-start | bytes 110600 | tf_op jit(solution)/shard_map/ppermute | solution.py:458
  25.6 5.0 %collective-permute-start.10 = (f32[72,128]{1,0:T(8,128)S(1)}, f32[72,128]{1,0:T(8,128)S(1)}, u32[]{:S(2)}, u32[]{:S(2)}) collective-permute-start(f32[72,128]{1,0:T(8,128)S(1)} %get-tuple-element.48.refs_0_.refs_4_), channel_id=1, source_target_pairs={{0,8},{4,12},{8,0},{12,4},{1,9},{5,13},{9,1},{13,5},{2,10},{6,14},... | collective-permute-start | bytes 110600 | tf_op jit(solution)/shard_map/ppermute | solution.py:458
  26.3 4.7 %collective-permute-start.9 = (f32[72,128]{1,0:T(8,128)S(1)}, f32[72,128]{1,0:T(8,128)S(1)}, u32[]{:S(2)}, u32[]{:S(2)}) collective-permute-start(f32[72,128]{1,0:T(8,128)S(1)} %get-tuple-element.48.refs_0_.refs_4_), channel_id=1, source_target_pairs={{0,4},{4,0},{8,12},{12,8},{1,5},{5,1},{9,13},{13,9},{2,6},{6,2},{1... | collective-permute-start | bytes 110600 | tf_op jit(solution)/shard_map/ppermute | solution.py:458
  31.6 3.1 %collective-permute-start.14 = (f32[8,128]{1,0:T(8,128)S(1)}, f32[8,128]{1,0:T(8,128)S(1)}, u32[]{:S(2)}, u32[]{:S(2)}) collective-permute-start(f32[8,128]{1,0:T(8,128)S(1)} %shard_map.94.refs_0_), channel_id=1, source_target_pairs={{0,3},{1,2},{2,1},{3,0},{4,7},{5,6},{6,5},{7,4},{8,11},{9,10},{10,... | collective-permute-start | bytes 12296 | tf_op jit(solution)/shard_map/ppermute | solution.py:458
  31.9 3.6 %collective-permute-start.13 = (f32[8,128]{1,0:T(8,128)S(1)}, f32[8,128]{1,0:T(8,128)S(1)}, u32[]{:S(2)}, u32[]{:S(2)}) collective-permute-start(f32[8,128]{1,0:T(8,128)S(1)} %shard_map.94.refs_0_), channel_id=1, source_target_pairs={{0,2},{1,3},{2,0},{3,1},{4,6},{5,7},{6,4},{7,5},{8,10},{9,11},{10,... | collective-permute-start | bytes 12296 | tf_op jit(solution)/shard_map/ppermute | solution.py:458
  32.6 2.9 %collective-permute-start.12 = (f32[8,128]{1,0:T(8,128)S(1)}, f32[8,128]{1,0:T(8,128)S(1)}, u32[]{:S(2)}, u32[]{:S(2)}) collective-permute-start(f32[8,128]{1,0:T(8,128)S(1)} %shard_map.94.refs_0_), channel_id=1, source_target_pairs={{0,1},{1,0},{2,3},{3,2},{4,5},{5,4},{6,7},{7,6},{8,9},{9,8},{10,11... | collective-permute-start | bytes 12296 | tf_op jit(solution)/shard_map/ppermute | solution.py:458
  36.1 5.9 %collective-permute-start.17 = (f32[72,128]{1,0:T(8,128)S(1)}, f32[72,128]{1,0:T(8,128)S(1)}, u32[]{:S(2)}, u32[]{:S(2)}) collective-permute-start(f32[72,128]{1,0:T(8,128)S(1)} %get-tuple-element.52.refs_0_.refs_8_), channel_id=1, source_target_pairs={{0,12},{4,8},{8,4},{12,0},{1,13},{5,9},{9,5},{13,1},{2,14},{6,10},... | collective-permute-start | bytes 110600 | tf_op jit(solution)/shard_map/ppermute | solution.py:458
  38.2 4.9 %collective-permute-start.16 = (f32[72,128]{1,0:T(8,128)S(1)}, f32[72,128]{1,0:T(8,128)S(1)}, u32[]{:S(2)}, u32[]{:S(2)}) collective-permute-start(f32[72,128]{1,0:T(8,128)S(1)} %get-tuple-element.52.refs_0_.refs_8_), channel_id=1, source_target_pairs={{0,8},{4,12},{8,0},{12,4},{1,9},{5,13},{9,1},{13,5},{2,10},{6,14},... | collective-permute-start | bytes 110600 | tf_op jit(solution)/shard_map/ppermute | solution.py:458
  39.0 4.5 %collective-permute-start.15 = (f32[72,128]{1,0:T(8,128)S(1)}, f32[72,128]{1,0:T(8,128)S(1)}, u32[]{:S(2)}, u32[]{:S(2)}) collective-permute-start(f32[72,128]{1,0:T(8,128)S(1)} %get-tuple-element.52.refs_0_.refs_8_), channel_id=1, source_target_pairs={{0,4},{4,0},{8,12},{12,8},{1,5},{5,1},{9,13},{13,9},{2,6},{6,2},{1... | collective-permute-start | bytes 110600 | tf_op jit(solution)/shard_map/ppermute | solution.py:458
  44.1 3.1 %collective-permute-start.20 = (f32[8,128]{1,0:T(8,128)S(1)}, f32[8,128]{1,0:T(8,128)S(1)}, u32[]{:S(2)}, u32[]{:S(2)}) collective-permute-start(f32[8,128]{1,0:T(8,128)S(1)} %shard_map.98.refs_0_), channel_id=1, source_target_pairs={{0,3},{1,2},{2,1},{3,0},{4,7},{5,6},{6,5},{7,4},{8,11},{9,10},{10,... | collective-permute-start | bytes 12296 | tf_op jit(solution)/shard_map/ppermute | solution.py:458
  44.2 3.7 %collective-permute-start.19 = (f32[8,128]{1,0:T(8,128)S(1)}, f32[8,128]{1,0:T(8,128)S(1)}, u32[]{:S(2)}, u32[]{:S(2)}) collective-permute-start(f32[8,128]{1,0:T(8,128)S(1)} %shard_map.98.refs_0_), channel_id=1, source_target_pairs={{0,2},{1,3},{2,0},{3,1},{4,6},{5,7},{6,4},{7,5},{8,10},{9,11},{10,... | collective-permute-start | bytes 12296 | tf_op jit(solution)/shard_map/ppermute | solution.py:458
  45.0 2.8 %collective-permute-start.18 = (f32[8,128]{1,0:T(8,128)S(1)}, f32[8,128]{1,0:T(8,128)S(1)}, u32[]{:S(2)}, u32[]{:S(2)}) collective-permute-start(f32[8,128]{1,0:T(8,128)S(1)} %shard_map.98.refs_0_), channel_id=1, source_target_pairs={{0,1},{1,0},{2,3},{3,2},{4,5},{5,4},{6,7},{7,6},{8,9},{9,8},{10,11... | collective-permute-start | bytes 12296 | tf_op jit(solution)/shard_map/ppermute | solution.py:458
  48.6 5.6 %collective-permute-start.21 = (f32[24,128]{1,0:T(8,128)S(1)}, f32[24,128]{1,0:T(8,128)S(1)}, u32[]{:S(2)}, u32[]{:S(2)}) collective-permute-start(f32[24,128]{1,0:T(8,128)S(1)} %get-tuple-element.65), channel_id=1, source_target_pairs={{0,12},{4,8},{8,4},{12,0},{1,13},{5,9},{9,5},{13,1},{2,14},{6,10},... | collective-permute-start | bytes 36872 | tf_op jit(solution)/shard_map/ppermute | solution.py:464
  50.6 4.6 %collective-permute-start.22 = (f32[24,128]{1,0:T(8,128)S(1)}, f32[24,128]{1,0:T(8,128)S(1)}, u32[]{:S(2)}, u32[]{:S(2)}) collective-permute-start(f32[24,128]{1,0:T(8,128)S(1)} %get-tuple-element.66), channel_id=1, source_target_pairs={{0,8},{4,12},{8,0},{12,4},{1,9},{5,13},{9,1},{13,5},{2,10},{6,14},... | collective-permute-start | bytes 36872 | tf_op jit(solution)/shard_map/ppermute | solution.py:464
  51.1 4.1 %collective-permute-start.23 = (f32[24,128]{1,0:T(8,128)S(1)}, f32[24,128]{1,0:T(8,128)S(1)}, u32[]{:S(2)}, u32[]{:S(2)}) collective-permute-start(f32[24,128]{1,0:T(8,128)S(1)} %get-tuple-element.67), channel_id=1, source_target_pairs={{0,4},{4,0},{8,12},{12,8},{1,5},{5,1},{9,13},{13,9},{2,6},{6,2},{1... | collective-permute-start | bytes 36872 | tf_op jit(solution)/shard_map/ppermute | solution.py:464

commit v5 on v4

--- a/solution.py
+++ b/solution.py
@@ -117,31 +117,26 @@
         msg[g : g + SUB, :] = fold3(acc)
 
 
-def start_kernel(
-    count, rows_hbm, cols_hbm, tiles_hbm, w_hbm,
-    part, tiles, w, row_mask,
-    rows, cols, picked, pieces, sems,
-):
+def first_look_kernel(rows_hbm, cols_hbm, rows_out, slot_out, cols_out, rows_line, sems):
+    pairs = ((rows_hbm, rows_line), (cols_hbm, cols_out))
+    copies = [pltpu.make_async_copy(src, dst, sems.at[k]) for k, (src, dst) in enumerate(pairs)]
+    for copy in copies:
+        copy.start()
+    slots = rows_line.shape[1]
+    slot_out[...] = iota((slots, LANES), 0)
+    copies[0].wait()
+    line = rows_line[...].astype(F32)
+    rows_out[...] = column_of(jnp.concatenate([line, line], axis=1), slots)
+    copies[1].wait()
+
+
+def start_kernel(cols, rows, tiles, w, part, row_mask, picked, pieces):
     slots = tiles.shape[0]
-    small = [
-        pltpu.make_async_copy(src, dst, sems.at[k])
-        for k, (src, dst) in enumerate(((cols_hbm, cols), (rows_hbm, rows)))
-    ]
-    w_copy = pltpu.make_async_copy(w_hbm, w, sems.at[3])
-    t_copy = pltpu.make_async_copy(tiles_hbm, tiles, sems.at[2])
-    for copy in [*small, w_copy, t_copy]:
-        copy.start()
-    for copy in small:
-        copy.wait()
-    live = count[0, 0]
-    sub = iota((SUB, LANES), 0)
+    sub = iota((SUB, LANES), 0).astype(F32)
     for t in range(slots):
-        row = jnp.where(t < live, rows[t], -1)
-        row_mask[t * SUB : (t + 1) * SUB, :] = (sub == row).astype(F32)
-    w_copy.wait()
+        row_mask[t * SUB : (t + 1) * SUB, :] = (sub == rows[t : t + 1, :]).astype(F32)
     for t in range(slots):
-        col = jnp.where(t < live, cols[t], 0)
-        picked[t : t + 1, :] = w[pl.ds(col, 1), :]
+        picked[t : t + 1, :] = w[pl.ds(cols[0, t], 1), :]
     save_pieces(picked[...], pieces)
     squares = jnp.zeros((SUB, LANES), F32)
     rows_w = w.shape[0]
@@ -151,7 +146,6 @@
         squares = squares + jnp.sum((block * block).reshape(step_rows // SUB, SUB, LANES), axis=0)
     part[SUB : 2 * SUB, :] = squares
     acc = jnp.zeros((6 * SUB, 2 * LANES), F32)
-    t_copy.wait()
     for s in range(0, slots, 4):
         a, b, c, d = (
             masked_line(pieces, slots, t, row_mask[t * SUB : (t + 1) * SUB, :]) for t in range(s, s + 4)
@@ -188,33 +182,27 @@
     return jnp.broadcast_to(jnp.sum(own, axis=1, keepdims=True), (rows, LANES))
 
 
-def prep_kernel(
-    ids, rows_line, cols_line, count, index, mask_out, pick_out, cols_out, own_out, *send_out
-):
-    slots = cols_line.shape[1]
+def prep_kernel(ids, rows, cols_line, index, mask_out, pick_out, cols_out, own_out, *send_out):
     n = ids.shape[1]
     left = ((ids[...] >> 7) == iota((SUB, n), 0)).astype(F32).astype(BF16)
     right = ((ids[...] & (LANES - 1)) == iota((LANES, n), 0)).astype(F32).astype(BF16)
     hits = lax.dot_general(left, right, (((1,), (1,)), ((), ())), preferred_element_type=F32)
     mask_out[...] = jnp.minimum(hits, 1.0)
-    live = iota((1, slots), 1) < count[0, 0]
-
-    def both(line):
-        line = jnp.where(live, line, -1).astype(F32)
-        line = jnp.concatenate([line, line], axis=1)
-        return line, column_of(line, slots)
-
-    line, own = both(cols_line[...])
+    slots = rows.shape[0]
+    sub, lane = iota((slots, LANES), 0), iota((slots, LANES), 1)
+    line = cols_line[...].astype(F32)
+    line = jnp.concatenate([line, line], axis=1)
+    own = jnp.where(rows[...] >= 0.0, column_of(line, slots), -1.0)
+    line = jnp.sum(jnp.where(sub == (lane & (slots - 1)), own, 0.0), axis=0, keepdims=True)
     cols_out[...] = jnp.broadcast_to(line, (SUB, LANES))
     own_out[...] = own
+    pick_out[...] = (rows[...] == lane.astype(F32)).astype(F32).astype(BF16)
     for out in send_out:
         run, rank = ranks(line, own, 1)
         row = iota((SHORT, LANES), 0)
         for j, k in enumerate((0, 3, 2, 1)):
             sent = (row == rank) & (run == (index[0] ^ k))
             out[j * SHORT : (j + 1) * SHORT, :] = sent.astype(F32)[:, :slots].astype(BF16)
-    _, own = both(rows_line[...])
-    pick_out[...] = (own == iota((slots, LANES), 1).astype(F32)).astype(F32).astype(BF16)
 
 
 def feat_sum(refs, first=0):
@@ -492,35 +480,28 @@
     tile_shape = jax.ShapeDtypeStruct((slots, edge, edge), BF16)
     picks = jax.ShapeDtypeStruct
 
-    part, tiles, w, row_mask = call(
+    w = weights.reshape(col_blocks, edge)
+    rows, slot, cols = call(
+        first_look_kernel,
+        (in_hbm(tile_rows.reshape(1, slots)), in_hbm(tile_cols.reshape(1, slots))),
+        [HBM] * 2,
+        [f32(slots, LANES), picks((slots, LANES), I32), pltpu.SMEM((1, slots), I32)],
+        [VM, VM, SM],
+        scratch=[pltpu.VMEM((1, slots), I32), pltpu.SemaphoreType.DMA((2,))],
+        flops=1 << 30,
+    )
+    rows = jnp.where(slot < tile_count, rows, -1.0)
+    part, row_mask = call(
         start_kernel,
-        (
-            tile_count,
-            in_hbm(tile_rows.reshape(slots)),
-            in_hbm(tile_cols.reshape(slots)),
-            in_hbm(tiles),
-            in_hbm(weights.reshape(col_blocks, edge)),
-        ),
-        [SM] + [HBM] * 4,
-        [f32(2 * SUB, LANES), tile_shape, f32(col_blocks, edge), f32(slots * SUB, LANES)],
-        scratch=[
-            pltpu.SMEM((slots,), I32),
-            pltpu.SMEM((slots,), I32),
-            pltpu.VMEM((slots, LANES), F32),
-            pltpu.VMEM((3 * slots, LANES), F32),
-            pltpu.SemaphoreType.DMA((4,)),
-        ],
+        (cols, rows, tiles, w),
+        [SM, VM, VM, VM],
+        [f32(2 * SUB, LANES), f32(slots * SUB, LANES)],
+        scratch=[pltpu.VMEM((slots, LANES), F32), pltpu.VMEM((3 * slots, LANES), F32)],
     )
     mask, row_pick, cols_line, own, *send = call(
         prep_kernel,
-        (
-            sample_ids,
-            tile_rows.reshape(1, slots),
-            tile_cols.reshape(1, slots),
-            tile_count,
-            index,
-        ),
-        [VM] * 3 + [SM] * 2,
+        (sample_ids, rows, tile_cols.reshape(1, slots), index),
+        [VM] * 3 + [SM],
         [grid, picks((slots, LANES), BF16), grid, f32(slots, LANES)]
         + [picks((4 * SHORT, slots), BF16)] * short,
     )

time: 56.5 us -> 55.8 us (0.988)
  Pallas kernels: 9.77 us -> 8.82 us
    pallas_call x15 -> x16, Pallas kernels: 9.77 us -> 8.82 us  [call(): pl.pallas_call(kernel, in_specs=in_specs, out_shape=outs, out_specs=out_s...]
where the time goes in v5:
time: 55.8 us; the launch traced here: 55.6 us
  starting transfers between devices  26.7 us (48%)
  waiting for transfers between devices  18.4 us (33%)
  Pallas kernels  8.82 us (16%)
  between operations  1.58 us (3%)
    ppermute x21, starting transfers between devices, exchange(): lax.ppermute(x, axis, [(i, i ^ k) for i in range(size)])  22.2 us
    ppermute x21, waiting for transfers between devices, exchange(): lax.ppermute(x, axis, [(i, i ^ k) for i in range(size)])  16.9 us
    pallas_call x16, Pallas kernels, call(): pl.pallas_call(kernel, in_specs=in_specs, out_shape=outs, out_specs=out_s...  8.82 us
    ppermute x3, starting transfers between devices, exchange_each(): lax.ppermute(x, axis, [(i, i ^ k) for i in range(4)])  4.45 us
    ppermute x3, waiting for transfers between devices, exchange_each(): lax.ppermute(x, axis, [(i, i ^ k) for i in range(4)])  1.5 us
  transfers between devices with their start and end apart: 24, of which 18 were waited for; matrix products, arithmetic and copies ran while one was open for 0% of the time, Pallas kernels for 3%

profile of v5, /device:TPU:0, one launch (start us, length us, event | category | flops | bytes accessed | tf_op | source)
XLA Modules:
  0.0 55.6 jit_solution(8730752592642969277)
XLA Ops:
  1.4 1.0 %shard_map.86 = (f32[64,128]{1,0:T(8,128)S(1)}, s32[64,128]{1,0:T(8,128)S(1)}, s32[1,64]{1,0:T(1,128)S(4)}) custom-call(s32[1,64]{1,0:T(1,128)} %bitcast.23, s32[1,64]{1,0:T(1,128)} %bitcast.19), custom_call_target="tpu_custom_call" | custom-call | flops 1073741824 | bytes 1048576 | tf_op jit(solution)/shard_map/pallas_call | solution.py:30
  2.4 0.0 copy-start.3
  2.5 0.0 copy-start.4
  2.5 0.0 copy-start.2
  2.5 0.1 copy-done
  2.6 0.8 %shard_map.88 = (f32[16,128]{1,0:T(8,128)S(1)}, f32[512,128]{1,0:T(8,128)S(1)}) custom-call(s32[1,64]{1,0:T(1,128)S(4)} %get-tuple-element.42.cols, f32[64,128]{1,0:T(8,128)S(1)} %compare_select_fusion.rows, bf16[64,128,128]{2,1,0:T(8,128)(2,1)S(1)} %bitcast.10, f32[2048,128]{1,0:T(8,128)S(1)} %bitcast.16), custom_call_target="tpu_custom_call" | custom-call | flops 2097152 | bytes 1048576 | tf_op jit(solution)/shard_map/pallas_call | solution.py:30
  3.3 2.4 %collective-permute-start.2 = (f32[16,128]{1,0:T(8,128)S(1)}, f32[16,128]{1,0:T(8,128)S(1)}, u32[]{:S(2)}, u32[]{:S(2)}) collective-permute-start(f32[16,128]{1,0:T(8,128)S(1)} %get-tuple-element.43.refs_0_), channel_id=1, source_target_pairs={{0,3},{1,2},{2,1},{3,0},{4,7},{5,6},{6,5},{7,4},{8,11},{9,10},{10,... | collective-permute-start | bytes 24584 | tf_op jit(solution)/shard_map/ppermute | solution.py:446
  5.8 0.6 %collective-permute-start.1 = (f32[16,128]{1,0:T(8,128)S(1)}, f32[16,128]{1,0:T(8,128)S(1)}, u32[]{:S(2)}, u32[]{:S(2)}) collective-permute-start(f32[16,128]{1,0:T(8,128)S(1)} %get-tuple-element.43.refs_0_), channel_id=1, source_target_pairs={{0,2},{1,3},{2,0},{3,1},{4,6},{5,7},{6,4},{7,5},{8,10},{9,11},{10,... | collective-permute-start | bytes 24584 | tf_op jit(solution)/shard_map/ppermute | solution.py:446
  6.4 0.0 collective-permute-start
  6.5 0.2 shard_map.87
  6.7 0.5 collective-permute-done.2.refs_3_
  7.1 2.3 %collective-permute-done.1.refs_2_ = f32[16,128]{1,0:T(8,128)S(1)} collective-permute-done((f32[16,128]{1,0:T(8,128)S(1)}, f32[16,128]{1,0:T(8,128)S(1)}, u32[]{:S(2)}, u32[]{:S(2)}) %collective-permute-start.1) | collective-permute-done | bytes 8224 | tf_op jit(solution)/shard_map/ppermute | solution.py:446
  9.4 0.0 collective-permute-done.refs_1_
  9.4 0.5 shard_map.89
  10.0 3.7 %collective-permute-start.5 = (f32[72,128]{1,0:T(8,128)S(1)}, f32[72,128]{1,0:T(8,128)S(1)}, u32[]{:S(2)}, u32[]{:S(2)}) collective-permute-start(f32[72,128]{1,0:T(8,128)S(1)} %get-tuple-element.50.refs_0_), channel_id=1, source_target_pairs={{0,12},{4,8},{8,4},{12,0},{1,13},{5,9},{9,5},{13,1},{2,14},{6,10},... | collective-permute-start | bytes 110600 | tf_op jit(solution)/shard_map/ppermute | solution.py:446
  13.6 0.8 %collective-permute-start.3 = (f32[72,128]{1,0:T(8,128)S(1)}, f32[72,128]{1,0:T(8,128)S(1)}, u32[]{:S(2)}, u32[]{:S(2)}) collective-permute-start(f32[72,128]{1,0:T(8,128)S(1)} %get-tuple-element.50.refs_0_), channel_id=1, source_target_pairs={{0,4},{4,0},{8,12},{12,8},{1,5},{5,1},{9,13},{13,9},{2,6},{6,2},{1... | collective-permute-start | bytes 110600 | tf_op jit(solution)/shard_map/ppermute | solution.py:446
  14.4 0.6 %shard_map.90.turned = bf16[64,128,128]{2,1,0:T(8,128)(2,1)S(1)} custom-call(bf16[64,128,128]{2,1,0:T(8,128)(2,1)S(1)} %bitcast.12), custom_call_target="tpu_custom_call" | custom-call | flops 2097152 | bytes 1048576 | tf_op jit(solution)/shard_map/pallas_call | solution.py:30
  15.0 1.2 %collective-permute-done.5.refs_3_ = f32[72,128]{1,0:T(8,128)S(1)} collective-permute-done((f32[72,128]{1,0:T(8,128)S(1)}, f32[72,128]{1,0:T(8,128)S(1)}, u32[]{:S(2)}, u32[]{:S(2)}) %collective-permute-start.5) | collective-permute-done | bytes 36896 | tf_op jit(solution)/shard_map/ppermute | solution.py:446
  16.2 2.3 %collective-permute-done.4.refs_2_ = f32[72,128]{1,0:T(8,128)S(1)} collective-permute-done((f32[72,128]{1,0:T(8,128)S(1)}, f32[72,128]{1,0:T(8,128)S(1)}, u32[]{:S(2)}, u32[]{:S(2)}) %collective-permute-start.4) | collective-permute-done | bytes 36896 | tf_op jit(solution)/shard_map/ppermute | solution.py:446
  18.5 0.6 %shard_map.92.refs_0_ = f32[8,128]{1,0:T(8,128)S(1)} custom-call(bf16[64,128,128]{2,1,0:T(8,128)(2,1)S(1)} %shard_map.90.turned, f32[512,128]{1,0:T(8,128)S(1)} %get-tuple-element.48.row_mask, bf16[64,256]{1,0:T(8,128)(2,1)S(1)} %shard_map.91.match, f32[72,128]{1,0:T(8,128)S(1)} %get-tuple-element.50.refs_0_, f32[72,128]{1,0:T(8,128)S(1)} %collective-permute-done.3.refs_1_, ...), custom_call_target="tpu_custom_call" | custom-call | flops 2097152 | bytes 1048576 | tf_op jit(solution)/shard_map/pallas_call | solution.py:30
  19.1 0.1 collective-permute-start.8
  19.2 0.7 %collective-permute-start.7 = (f32[8,128]{1,0:T(8,128)S(1)}, f32[8,128]{1,0:T(8,128)S(1)}, u32[]{:S(2)}, u32[]{:S(2)}) collective-permute-start(f32[8,128]{1,0:T(8,128)S(1)} %shard_map.92.refs_0_), channel_id=1, source_target_pairs={{0,2},{1,3},{2,0},{3,1},{4,6},{5,7},{6,4},{7,5},{8,10},{9,11},{10,... | collective-permute-start | bytes 12296 | tf_op jit(solution)/shard_map/ppermute | solution.py:446
  19.9 1.1 %collective-permute-start.6 = (f32[8,128]{1,0:T(8,128)S(1)}, f32[8,128]{1,0:T(8,128)S(1)}, u32[]{:S(2)}, u32[]{:S(2)}) collective-permute-start(f32[8,128]{1,0:T(8,128)S(1)} %shard_map.92.refs_0_), channel_id=1, source_target_pairs={{0,1},{1,0},{2,3},{3,2},{4,5},{5,4},{6,7},{7,6},{8,9},{9,8},{10,11... | collective-permute-start | bytes 12296 | tf_op jit(solution)/shard_map/ppermute | solution.py:446
  21.0 1.2 %collective-permute-done.8.refs_3_ = f32[8,128]{1,0:T(8,128)S(1)} collective-permute-done((f32[8,128]{1,0:T(8,128)S(1)}, f32[8,128]{1,0:T(8,128)S(1)}, u32[]{:S(2)}, u32[]{:S(2)}) %collective-permute-start.8) | collective-permute-done | bytes 4128 | tf_op jit(solution)/shard_map/ppermute | solution.py:446
  22.2 0.7 %collective-permute-done.7.refs_2_ = f32[8,128]{1,0:T(8,128)S(1)} collective-permute-done((f32[8,128]{1,0:T(8,128)S(1)}, f32[8,128]{1,0:T(8,128)S(1)}, u32[]{:S(2)}, u32[]{:S(2)}) %collective-permute-start.7) | collective-permute-done | bytes 4128 | tf_op jit(solution)/shard_map/ppermute | solution.py:446
  22.9 0.0 collective-permute-done.6.refs_1_
  22.9 0.5 shard_map.93
  23.4 1.5 %collective-permute-start.11 = (f32[72,128]{1,0:T(8,128)S(1)}, f32[72,128]{1,0:T(8,128)S(1)}, u32[]{:S(2)}, u32[]{:S(2)}) collective-permute-start(f32[72,128]{1,0:T(8,128)S(1)} %get-tuple-element.51.refs_0_.refs_4_), channel_id=1, source_target_pairs={{0,12},{4,8},{8,4},{12,0},{1,13},{5,9},{9,5},{13,1},{2,14},{6,10},... | collective-permute-start | bytes 110600 | tf_op jit(solution)/shard_map/ppermute | solution.py:446
  24.9 0.6 %collective-permute-start.10 = (f32[72,128]{1,0:T(8,128)S(1)}, f32[72,128]{1,0:T(8,128)S(1)}, u32[]{:S(2)}, u32[]{:S(2)}) collective-permute-start(f32[72,128]{1,0:T(8,128)S(1)} %get-tuple-element.51.refs_0_.refs_4_), channel_id=1, source_target_pairs={{0,8},{4,12},{8,0},{12,4},{1,9},{5,13},{9,1},{13,5},{2,10},{6,14},... | collective-permute-start | bytes 110600 | tf_op jit(solution)/shard_map/ppermute | solution.py:446
  25.6 2.3 %collective-permute-start.9 = (f32[72,128]{1,0:T(8,128)S(1)}, f32[72,128]{1,0:T(8,128)S(1)}, u32[]{:S(2)}, u32[]{:S(2)}) collective-permute-start(f32[72,128]{1,0:T(8,128)S(1)} %get-tuple-element.51.refs_0_.refs_4_), channel_id=1, source_target_pairs={{0,4},{4,0},{8,12},{12,8},{1,5},{5,1},{9,13},{13,9},{2,6},{6,2},{1... | collective-permute-start | bytes 110600 | tf_op jit(solution)/shard_map/ppermute | solution.py:446
  27.9 1.8 %collective-permute-done.11.refs_3_.refs_7_ = f32[72,128]{1,0:T(8,128)S(1)} collective-permute-done((f32[72,128]{1,0:T(8,128)S(1)}, f32[72,128]{1,0:T(8,128)S(1)}, u32[]{:S(2)}, u32[]{:S(2)}) %collective-permute-start.11) | collective-permute-done | bytes 36896 | tf_op jit(solution)/shard_map/ppermute | solution.py:446
  29.6 0.3 collective-permute-done.10.refs_2_.refs_6_
  29.9 0.3 collective-permute-done.9.refs_1_.refs_5_
  30.3 0.6 %shard_map.95.refs_0_ = f32[8,128]{1,0:T(8,128)S(1)} custom-call(bf16[64,128,128]{2,1,0:T(8,128)(2,1)S(1)} %shard_map.90.turned, f32[512,128]{1,0:T(8,128)S(1)} %get-tuple-element.48.row_mask, bf16[64,256]{1,0:T(8,128)(2,1)S(1)} %shard_map.91.match, f32[72,128]{1,0:T(8,128)S(1)} %get-tuple-element.51.refs_0_.refs_4_, ...), custom_call_target="tpu_custom_call" | custom-call | flops 2097152 | bytes 1048576 | tf_op jit(solution)/shard_map/pallas_call | solution.py:30
  30.9 0.3 collective-permute-start.14
  31.2 0.7 %collective-permute-start.13 = (f32[8,128]{1,0:T(8,128)S(1)}, f32[8,128]{1,0:T(8,128)S(1)}, u32[]{:S(2)}, u32[]{:S(2)}) collective-permute-start(f32[8,128]{1,0:T(8,128)S(1)} %shard_map.95.refs_0_), channel_id=1, source_target_pairs={{0,2},{1,3},{2,0},{3,1},{4,6},{5,7},{6,4},{7,5},{8,10},{9,11},{10,... | collective-permute-start | bytes 12296 | tf_op jit(solution)/shard_map/ppermute | solution.py:446
  31.9 0.9 %collective-permute-start.12 = (f32[8,128]{1,0:T(8,128)S(1)}, f32[8,128]{1,0:T(8,128)S(1)}, u32[]{:S(2)}, u32[]{:S(2)}) collective-permute-start(f32[8,128]{1,0:T(8,128)S(1)} %shard_map.95.refs_0_), channel_id=1, source_target_pairs={{0,1},{1,0},{2,3},{3,2},{4,5},{5,4},{6,7},{7,6},{8,9},{9,8},{10,11... | collective-permute-start | bytes 12296 | tf_op jit(solution)/shard_map/ppermute | solution.py:446
  32.8 0.1 shard_map.94
  32.9 1.0 %collective-permute-done.14.refs_3_ = f32[8,128]{1,0:T(8,128)S(1)} collective-permute-done((f32[8,128]{1,0:T(8,128)S(1)}, f32[8,128]{1,0:T(8,128)S(1)}, u32[]{:S(2)}, u32[]{:S(2)}) %collective-permute-start.14) | collective-permute-done | bytes 4128 | tf_op jit(solution)/shard_map/ppermute | solution.py:446
  34.0 0.9 %collective-permute-done.13.refs_2_ = f32[8,128]{1,0:T(8,128)S(1)} collective-permute-done((f32[8,128]{1,0:T(8,128)S(1)}, f32[8,128]{1,0:T(8,128)S(1)}, u32[]{:S(2)}, u32[]{:S(2)}) %collective-permute-start.13) | collective-permute-done | bytes 4128 | tf_op jit(solution)/shard_map/ppermute | solution.py:446
  34.8 0.0 collective-permute-done.12.refs_1_
  34.8 0.6 shard_map.96
  35.4 2.1 %collective-permute-start.17 = (f32[72,128]{1,0:T(8,128)S(1)}, f32[72,128]{1,0:T(8,128)S(1)}, u32[]{:S(2)}, u32[]{:S(2)}) collective-permute-start(f32[72,128]{1,0:T(8,128)S(1)} %get-tuple-element.55.refs_0_.refs_8_), channel_id=1, source_target_pairs={{0,12},{4,8},{8,4},{12,0},{1,13},{5,9},{9,5},{13,1},{2,14},{6,10},... | collective-permute-start | bytes 110600 | tf_op jit(solution)/shard_map/ppermute | solution.py:446
  37.5 0.7 %collective-permute-start.16 = (f32[72,128]{1,0:T(8,128)S(1)}, f32[72,128]{1,0:T(8,128)S(1)}, u32[]{:S(2)}, u32[]{:S(2)}) collective-permute-start(f32[72,128]{1,0:T(8,128)S(1)} %get-tuple-element.55.refs_0_.refs_8_), channel_id=1, source_target_pairs={{0,8},{4,12},{8,0},{12,4},{1,9},{5,13},{9,1},{13,5},{2,10},{6,14},... | collective-permute-start | bytes 110600 | tf_op jit(solution)/shard_map/ppermute | solution.py:446
  38.2 1.6 %collective-permute-start.15 = (f32[72,128]{1,0:T(8,128)S(1)}, f32[72,128]{1,0:T(8,128)S(1)}, u32[]{:S(2)}, u32[]{:S(2)}) collective-permute-start(f32[72,128]{1,0:T(8,128)S(1)} %get-tuple-element.55.refs_0_.refs_8_), channel_id=1, source_target_pairs={{0,4},{4,0},{8,12},{12,8},{1,5},{5,1},{9,13},{13,9},{2,6},{6,2},{1... | collective-permute-start | bytes 110600 | tf_op jit(solution)/shard_map/ppermute | solution.py:446
  39.8 1.4 %collective-permute-done.17.refs_3_.refs_11_ = f32[72,128]{1,0:T(8,128)S(1)} collective-permute-done((f32[72,128]{1,0:T(8,128)S(1)}, f32[72,128]{1,0:T(8,128)S(1)}, u32[]{:S(2)}, u32[]{:S(2)}) %collective-permute-start.17) | collective-permute-done | bytes 36896 | tf_op jit(solution)/shard_map/ppermute | solution.py:446
  41.2 1.2 %collective-permute-done.16.refs_2_.refs_10_ = f32[72,128]{1,0:T(8,128)S(1)} collective-permute-done((f32[72,128]{1,0:T(8,128)S(1)}, f32[72,128]{1,0:T(8,128)S(1)}, u32[]{:S(2)}, u32[]{:S(2)}) %collective-permute-start.16) | collective-permute-done | bytes 36896 | tf_op jit(solution)/shard_map/ppermute | solution.py:446
  42.5 0.3 collective-permute-done.15.refs_1_.refs_9_
  42.8 0.6 %shard_map.99.refs_0_ = f32[8,128]{1,0:T(8,128)S(1)} custom-call(bf16[64,128,128]{2,1,0:T(8,128)(2,1)S(1)} %shard_map.90.turned, f32[512,128]{1,0:T(8,128)S(1)} %get-tuple-element.48.row_mask, bf16[64,256]{1,0:T(8,128)(2,1)S(1)} %shard_map.91.match, f32[72,128]{1,0:T(8,128)S(1)} %get-tuple-element.55.refs_0_.refs_8_, ...), custom_call_target="tpu_custom_call" | custom-call | flops 2097152 | bytes 1048576 | tf_op jit(solution)/shard_map/pallas_call | solution.py:30
  43.4 0.1 collective-permute-start.20
  43.5 0.8 %collective-permute-start.19 = (f32[8,128]{1,0:T(8,128)S(1)}, f32[8,128]{1,0:T(8,128)S(1)}, u32[]{:S(2)}, u32[]{:S(2)}) collective-permute-start(f32[8,128]{1,0:T(8,128)S(1)} %shard_map.99.refs_0_), channel_id=1, source_target_pairs={{0,2},{1,3},{2,0},{3,1},{4,6},{5,7},{6,4},{7,5},{8,10},{9,11},{10,... | collective-permute-start | bytes 12296 | tf_op jit(solution)/shard_map/ppermute | solution.py:446
  44.3 1.0 %collective-permute-start.18 = (f32[8,128]{1,0:T(8,128)S(1)}, f32[8,128]{1,0:T(8,128)S(1)}, u32[]{:S(2)}, u32[]{:S(2)}) collective-permute-start(f32[8,128]{1,0:T(8,128)S(1)} %shard_map.99.refs_0_), channel_id=1, source_target_pairs={{0,1},{1,0},{2,3},{3,2},{4,5},{5,4},{6,7},{7,6},{8,9},{9,8},{10,11... | collective-permute-start | bytes 12296 | tf_op jit(solution)/shard_map/ppermute | solution.py:446
  45.3 0.2 shard_map.97
  45.5 0.9 %collective-permute-done.20.refs_3_ = f32[8,128]{1,0:T(8,128)S(1)} collective-permute-done((f32[8,128]{1,0:T(8,128)S(1)}, f32[8,128]{1,0:T(8,128)S(1)}, u32[]{:S(2)}, u32[]{:S(2)}) %collective-permute-start.20) | collective-permute-done | bytes 4128 | tf_op jit(solution)/shard_map/ppermute | solution.py:446
  46.5 0.7 %collective-permute-done.19.refs_2_ = f32[8,128]{1,0:T(8,128)S(1)} collective-permute-done((f32[8,128]{1,0:T(8,128)S(1)}, f32[8,128]{1,0:T(8,128)S(1)}, u32[]{:S(2)}, u32[]{:S(2)}) %collective-permute-start.19) | collective-permute-done | bytes 4128 | tf_op jit(solution)/shard_map/ppermute | solution.py:446
  47.1 0.7 %shard_map.100 = (f32[24,128]{1,0:T(8,128)S(1)}, f32[24,128]{1,0:T(8,128)S(1)}, f32[24,128]{1,0:T(8,128)S(1)}, f32[24,128]{1,0:T(8,128)S(1)}) custom-call(bf16[64,128,128]{2,1,0:T(8,128)(2,1)S(1)} %bitcast.15, bf16[64,128]{1,0:T(8,128)(2,1)S(1)} %get-tuple-element.39.row_pick, f32[8,128]{1,0:T(8,128)S(1)} %get-tuple-element.46.c, ...), custom_call_target="tpu_custom_call" | custom-call | flops 2097152 | bytes 1048576 | tf_op jit(solution)/shard_map/pallas_call | solution.py:30
  47.8 2.1 %collective-permute-start.21 = (f32[24,128]{1,0:T(8,128)S(1)}, f32[24,128]{1,0:T(8,128)S(1)}, u32[]{:S(2)}, u32[]{:S(2)}) collective-permute-start(f32[24,128]{1,0:T(8,128)S(1)} %get-tuple-element.67), channel_id=1, source_target_pairs={{0,12},{4,8},{8,4},{12,0},{1,13},{5,9},{9,5},{13,1},{2,14},{6,10},... | collective-permute-start | bytes 36872 | tf_op jit(solution)/shard_map/ppermute | solution.py:452
  49.9 0.5 collective-permute-start.22
  50.4 1.9 %collective-permute-start.23 = (f32[24,128]{1,0:T(8,128)S(1)}, f32[24,128]{1,0:T(8,128)S(1)}, u32[]{:S(2)}, u32[]{:S(2)}) collective-permute-start(f32[24,128]{1,0:T(8,128)S(1)} %get-tuple-element.69), channel_id=1, source_target_pairs={{0,4},{4,0},{8,12},{12,8},{1,5},{5,1},{9,13},{13,9},{2,6},{6,2},{1... | collective-permute-start | bytes 36872 | tf_op jit(solution)/shard_map/ppermute | solution.py:452
  52.3 0.7 %shard_map.98 = (f32[512,128]{1,0:T(8,128)S(1)}, f32[512,128]{1,0:T(8,128)S(1)}, f32[512,128]{1,0:T(8,128)S(1)}, f32[512,128]{1,0:T(8,128)S(1)}, bf16[512,128]{1,0:T(8,128)(2,1)S(1)}) custom-call(f32[2048,128]{1,0:T(8,128)S(1)} %bitcast.17, s32[1]{0:T(128)} %bitcast.4.index, f32[72,128]{1,0:T(8,128)S(1)} %get-tuple-element.50.refs_0_, ...), custom_call_target="tpu_custom_call" | custom-call | flops 2097152 | bytes 1048576 | tf_op jit(solution)/shard_map/pallas_call | solution.py:30
  53.0 0.4 collective-permute-done.21.refs_1_
  53.4 1.1 %collective-permute-done.22.refs_2_ = f32[24,128]{1,0:T(8,128)S(1)} collective-permute-done((f32[24,128]{1,0:T(8,128)S(1)}, f32[24,128]{1,0:T(8,128)S(1)}, u32[]{:S(2)}, u32[]{:S(2)}) %collective-permute-start.22) | collective-permute-done | bytes 12320 | tf_op jit(solution)/shard_map/ppermute | solution.py:452
  54.5 0.0 collective-permute-done.23.refs_3_
  54.5 1.1 %shard_map.101 = (f32[512,128]{1,0:T(8,128)}, f32[512,128]{1,0:T(8,128)}) custom-call(f32[8,128]{1,0:T(8,128)S(1)} %get-tuple-element.44.ww, f32[8,128]{1,0:T(8,128)S(1)} %get-tuple-element.58.refs_13_.num, f32[512,128]{1,0:T(8,128)S(1)} %get-tuple-element.59.res, f32[512,128]{1,0:T(8,128)S(1)} %get-tuple-element.60.direction, ...), custom_call_target="tpu_custom_call" | custom-call | flops 2097152 | bytes 1048576 | tf_op jit(solution)/shard_map/pallas_call | solution.py:30
  (11 shorter events, 0.0 us)
Async XLA Ops:
  0.6 1.9 %copy-start.1 = (f32[1,262144]{1,0:T(1,128)S(1)}, f32[1,262144]{1,0:T(1,128)}, u32[]{:S(2)}) copy-start(f32[1,262144]{1,0:T(1,128)} %param.13) | copy-start | bytes 3145732
  0.6 1.9 %copy-start = (bf16[1,1,64,128,128]{4,3,2,1,0:T(8,128)(2,1)S(1)}, bf16[1,1,64,128,128]{4,3,2,1,0:T(8,128)(2,1)}, u32[]{:S(2)}) copy-start(bf16[1,1,64,128,128]{4,3,2,1,0:T(8,128)(2,1)} %param.7) | copy-start | bytes 6291460
  2.4 4.0 %copy-start.3 = (s32[1,512]{1,0:T(1,128)S(1)}, s32[1,512]{1,0:T(1,128)}, u32[]{:S(2)}) copy-start(s32[1,512]{1,0:T(1,128)} %ids.1) | copy-start | bytes 6148
  2.5 4.0 %copy-start.4 = (s32[1,1,64]{2,1,0:T(1,128)S(1)}, s32[1,1,64]{2,1,0:T(1,128)}, u32[]{:S(2)}) copy-start(s32[1,1,64]{2,1,0:T(1,128)} %param.9) | copy-start | bytes 772
  2.5 7.0 %copy-start.2 = (s32[1,1024]{1,0:T(1,128)S(1)}, s32[1,1024]{1,0:T(1,128)}, u32[]{:S(2)}) copy-start(s32[1,1024]{1,0:T(1,128)} %param.12) | copy-start | bytes 12292
  3.3 3.8 %collective-permute-start.2 = (f32[16,128]{1,0:T(8,128)S(1)}, f32[16,128]{1,0:T(8,128)S(1)}, u32[]{:S(2)}, u32[]{:S(2)}) collective-permute-start(f32[16,128]{1,0:T(8,128)S(1)} %get-tuple-element.43.refs_0_), channel_id=1, source_target_pairs={{0,3},{1,2},{2,1},{3,0},{4,7},{5,6},{6,5},{7,4},{8,11},{9,10},{10,... | collective-permute-start | bytes 24584 | tf_op jit(solution)/shard_map/ppermute | solution.py:446
  5.8 3.7 %collective-permute-start.1 = (f32[16,128]{1,0:T(8,128)S(1)}, f32[16,128]{1,0:T(8,128)S(1)}, u32[]{:S(2)}, u32[]{:S(2)}) collective-permute-start(f32[16,128]{1,0:T(8,128)S(1)} %get-tuple-element.43.refs_0_), channel_id=1, source_target_pairs={{0,2},{1,3},{2,0},{3,1},{4,6},{5,7},{6,4},{7,5},{8,10},{9,11},{10,... | collective-permute-start | bytes 24584 | tf_op jit(solution)/shard_map/ppermute | solution.py:446
  6.4 3.0 %collective-permute-start = (f32[16,128]{1,0:T(8,128)S(1)}, f32[16,128]{1,0:T(8,128)S(1)}, u32[]{:S(2)}, u32[]{:S(2)}) collective-permute-start(f32[16,128]{1,0:T(8,128)S(1)} %get-tuple-element.43.refs_0_), channel_id=1, source_target_pairs={{0,1},{1,0},{2,3},{3,2},{4,5},{5,4},{6,7},{7,6},{8,9},{9,8},{10,11... | collective-permute-start | bytes 24584 | tf_op jit(solution)/shard_map/ppermute | solution.py:446
  10.0 6.3 %collective-permute-start.5 = (f32[72,128]{1,0:T(8,128)S(1)}, f32[72,128]{1,0:T(8,128)S(1)}, u32[]{:S(2)}, u32[]{:S(2)}) collective-permute-start(f32[72,128]{1,0:T(8,128)S(1)} %get-tuple-element.50.refs_0_), channel_id=1, source_target_pairs={{0,12},{4,8},{8,4},{12,0},{1,13},{5,9},{9,5},{13,1},{2,14},{6,10},... | collective-permute-start | bytes 110600 | tf_op jit(solution)/shard_map/ppermute | solution.py:446
  13.6 4.9 %collective-permute-start.4 = (f32[72,128]{1,0:T(8,128)S(1)}, f32[72,128]{1,0:T(8,128)S(1)}, u32[]{:S(2)}, u32[]{:S(2)}) collective-permute-start(f32[72,128]{1,0:T(8,128)S(1)} %get-tuple-element.50.refs_0_), channel_id=1, source_target_pairs={{0,8},{4,12},{8,0},{12,4},{1,9},{5,13},{9,1},{13,5},{2,10},{6,14},... | collective-permute-start | bytes 110600 | tf_op jit(solution)/shard_map/ppermute | solution.py:446
  13.6 4.9 %collective-permute-start.3 = (f32[72,128]{1,0:T(8,128)S(1)}, f32[72,128]{1,0:T(8,128)S(1)}, u32[]{:S(2)}, u32[]{:S(2)}) collective-permute-start(f32[72,128]{1,0:T(8,128)S(1)} %get-tuple-element.50.refs_0_), channel_id=1, source_target_pairs={{0,4},{4,0},{8,12},{12,8},{1,5},{5,1},{9,13},{13,9},{2,6},{6,2},{1... | collective-permute-start | bytes 110600 | tf_op jit(solution)/shard_map/ppermute | solution.py:446
  19.1 3.1 %collective-permute-start.8 = (f32[8,128]{1,0:T(8,128)S(1)}, f32[8,128]{1,0:T(8,128)S(1)}, u32[]{:S(2)}, u32[]{:S(2)}) collective-permute-start(f32[8,128]{1,0:T(8,128)S(1)} %shard_map.92.refs_0_), channel_id=1, source_target_pairs={{0,3},{1,2},{2,1},{3,0},{4,7},{5,6},{6,5},{7,4},{8,11},{9,10},{10,... | collective-permute-start | bytes 12296 | tf_op jit(solution)/shard_map/ppermute | solution.py:446
  19.2 3.7 %collective-permute-start.7 = (f32[8,128]{1,0:T(8,128)S(1)}, f32[8,128]{1,0:T(8,128)S(1)}, u32[]{:S(2)}, u32[]{:S(2)}) collective-permute-start(f32[8,128]{1,0:T(8,128)S(1)} %shard_map.92.refs_0_), channel_id=1, source_target_pairs={{0,2},{1,3},{2,0},{3,1},{4,6},{5,7},{6,4},{7,5},{8,10},{9,11},{10,... | collective-permute-start | bytes 12296 | tf_op jit(solution)/shard_map/ppermute | solution.py:446
  19.9 3.0 %collective-permute-start.6 = (f32[8,128]{1,0:T(8,128)S(1)}, f32[8,128]{1,0:T(8,128)S(1)}, u32[]{:S(2)}, u32[]{:S(2)}) collective-permute-start(f32[8,128]{1,0:T(8,128)S(1)} %shard_map.92.refs_0_), channel_id=1, source_target_pairs={{0,1},{1,0},{2,3},{3,2},{4,5},{5,4},{6,7},{7,6},{8,9},{9,8},{10,11... | collective-permute-start | bytes 12296 | tf_op jit(solution)/shard_map/ppermute | solution.py:446
  23.4 6.2 %collective-permute-start.11 = (f32[72,128]{1,0:T(8,128)S(1)}, f32[72,128]{1,0:T(8,128)S(1)}, u32[]{:S(2)}, u32[]{:S(2)}) collective-permute-start(f32[72,128]{1,0:T(8,128)S(1)} %get-tuple-element.51.refs_0_.refs_4_), channel_id=1, source_target_pairs={{0,12},{4,8},{8,4},{12,0},{1,13},{5,9},{9,5},{13,1},{2,14},{6,10},... | collective-permute-start | bytes 110600 | tf_op jit(solution)/shard_map/ppermute | solution.py:446
  24.9 5.0 %collective-permute-start.10 = (f32[72,128]{1,0:T(8,128)S(1)}, f32[72,128]{1,0:T(8,128)S(1)}, u32[]{:S(2)}, u32[]{:S(2)}) collective-permute-start(f32[72,128]{1,0:T(8,128)S(1)} %get-tuple-element.51.refs_0_.refs_4_), channel_id=1, source_target_pairs={{0,8},{4,12},{8,0},{12,4},{1,9},{5,13},{9,1},{13,5},{2,10},{6,14},... | collective-permute-start | bytes 110600 | tf_op jit(solution)/shard_map/ppermute | solution.py:446
  25.6 4.7 %collective-permute-start.9 = (f32[72,128]{1,0:T(8,128)S(1)}, f32[72,128]{1,0:T(8,128)S(1)}, u32[]{:S(2)}, u32[]{:S(2)}) collective-permute-start(f32[72,128]{1,0:T(8,128)S(1)} %get-tuple-element.51.refs_0_.refs_4_), channel_id=1, source_target_pairs={{0,4},{4,0},{8,12},{12,8},{1,5},{5,1},{9,13},{13,9},{2,6},{6,2},{1... | collective-permute-start | bytes 110600 | tf_op jit(solution)/shard_map/ppermute | solution.py:446
  30.9 3.1 %collective-permute-start.14 = (f32[8,128]{1,0:T(8,128)S(1)}, f32[8,128]{1,0:T(8,128)S(1)}, u32[]{:S(2)}, u32[]{:S(2)}) collective-permute-start(f32[8,128]{1,0:T(8,128)S(1)} %shard_map.95.refs_0_), channel_id=1, source_target_pairs={{0,3},{1,2},{2,1},{3,0},{4,7},{5,6},{6,5},{7,4},{8,11},{9,10},{10,... | collective-permute-start | bytes 12296 | tf_op jit(solution)/shard_map/ppermute | solution.py:446
  31.2 3.6 %collective-permute-start.13 = (f32[8,128]{1,0:T(8,128)S(1)}, f32[8,128]{1,0:T(8,128)S(1)}, u32[]{:S(2)}, u32[]{:S(2)}) collective-permute-start(f32[8,128]{1,0:T(8,128)S(1)} %shard_map.95.refs_0_), channel_id=1, source_target_pairs={{0,2},{1,3},{2,0},{3,1},{4,6},{5,7},{6,4},{7,5},{8,10},{9,11},{10,... | collective-permute-start | bytes 12296 | tf_op jit(solution)/shard_map/ppermute | solution.py:446
  31.9 2.9 %collective-permute-start.12 = (f32[8,128]{1,0:T(8,128)S(1)}, f32[8,128]{1,0:T(8,128)S(1)}, u32[]{:S(2)}, u32[]{:S(2)}) collective-permute-start(f32[8,128]{1,0:T(8,128)S(1)} %shard_map.95.refs_0_), channel_id=1, source_target_pairs={{0,1},{1,0},{2,3},{3,2},{4,5},{5,4},{6,7},{7,6},{8,9},{9,8},{10,11... | collective-permute-start | bytes 12296 | tf_op jit(solution)/shard_map/ppermute | solution.py:446
  35.4 5.9 %collective-permute-start.17 = (f32[72,128]{1,0:T(8,128)S(1)}, f32[72,128]{1,0:T(8,128)S(1)}, u32[]{:S(2)}, u32[]{:S(2)}) collective-permute-start(f32[72,128]{1,0:T(8,128)S(1)} %get-tuple-element.55.refs_0_.refs_8_), channel_id=1, source_target_pairs={{0,12},{4,8},{8,4},{12,0},{1,13},{5,9},{9,5},{13,1},{2,14},{6,10},... | collective-permute-start | bytes 110600 | tf_op jit(solution)/shard_map/ppermute | solution.py:446
  37.5 4.9 %collective-permute-start.16 = (f32[72,128]{1,0:T(8,128)S(1)}, f32[72,128]{1,0:T(8,128)S(1)}, u32[]{:S(2)}, u32[]{:S(2)}) collective-permute-start(f32[72,128]{1,0:T(8,128)S(1)} %get-tuple-element.55.refs_0_.refs_8_), channel_id=1, source_target_pairs={{0,8},{4,12},{8,0},{12,4},{1,9},{5,13},{9,1},{13,5},{2,10},{6,14},... | collective-permute-start | bytes 110600 | tf_op jit(solution)/shard_map/ppermute | solution.py:446
  38.2 4.5 %collective-permute-start.15 = (f32[72,128]{1,0:T(8,128)S(1)}, f32[72,128]{1,0:T(8,128)S(1)}, u32[]{:S(2)}, u32[]{:S(2)}) collective-permute-start(f32[72,128]{1,0:T(8,128)S(1)} %get-tuple-element.55.refs_0_.refs_8_), channel_id=1, source_target_pairs={{0,4},{4,0},{8,12},{12,8},{1,5},{5,1},{9,13},{13,9},{2,6},{6,2},{1... | collective-permute-start | bytes 110600 | tf_op jit(solution)/shard_map/ppermute | solution.py:446
  43.4 3.1 %collective-permute-start.20 = (f32[8,128]{1,0:T(8,128)S(1)}, f32[8,128]{1,0:T(8,128)S(1)}, u32[]{:S(2)}, u32[]{:S(2)}) collective-permute-start(f32[8,128]{1,0:T(8,128)S(1)} %shard_map.99.refs_0_), channel_id=1, source_target_pairs={{0,3},{1,2},{2,1},{3,0},{4,7},{5,6},{6,5},{7,4},{8,11},{9,10},{10,... | collective-permute-start | bytes 12296 | tf_op jit(solution)/shard_map/ppermute | solution.py:446
  43.5 3.7 %collective-permute-start.19 = (f32[8,128]{1,0:T(8,128)S(1)}, f32[8,128]{1,0:T(8,128)S(1)}, u32[]{:S(2)}, u32[]{:S(2)}) collective-permute-start(f32[8,128]{1,0:T(8,128)S(1)} %shard_map.99.refs_0_), channel_id=1, source_target_pairs={{0,2},{1,3},{2,0},{3,1},{4,6},{5,7},{6,4},{7,5},{8,10},{9,11},{10,... | collective-permute-start | bytes 12296 | tf_op jit(solution)/shard_map/ppermute | solution.py:446
  44.3 2.8 %collective-permute-start.18 = (f32[8,128]{1,0:T(8,128)S(1)}, f32[8,128]{1,0:T(8,128)S(1)}, u32[]{:S(2)}, u32[]{:S(2)}) collective-permute-start(f32[8,128]{1,0:T(8,128)S(1)} %shard_map.99.refs_0_), channel_id=1, source_target_pairs={{0,1},{1,0},{2,3},{3,2},{4,5},{5,4},{6,7},{7,6},{8,9},{9,8},{10,11... | collective-permute-start | bytes 12296 | tf_op jit(solution)/shard_map/ppermute | solution.py:446
  47.8 5.6 %collective-permute-start.21 = (f32[24,128]{1,0:T(8,128)S(1)}, f32[24,128]{1,0:T(8,128)S(1)}, u32[]{:S(2)}, u32[]{:S(2)}) collective-permute-start(f32[24,128]{1,0:T(8,128)S(1)} %get-tuple-element.67), channel_id=1, source_target_pairs={{0,12},{4,8},{8,4},{12,0},{1,13},{5,9},{9,5},{13,1},{2,14},{6,10},... | collective-permute-start | bytes 36872 | tf_op jit(solution)/shard_map/ppermute | solution.py:452
  49.9 4.6 %collective-permute-start.22 = (f32[24,128]{1,0:T(8,128)S(1)}, f32[24,128]{1,0:T(8,128)S(1)}, u32[]{:S(2)}, u32[]{:S(2)}) collective-permute-start(f32[24,128]{1,0:T(8,128)S(1)} %get-tuple-element.68), channel_id=1, source_target_pairs={{0,8},{4,12},{8,0},{12,4},{1,9},{5,13},{9,1},{13,5},{2,10},{6,14},... | collective-permute-start | bytes 36872 | tf_op jit(solution)/shard_map/ppermute | solution.py:452
  50.4 4.1 %collective-permute-start.23 = (f32[24,128]{1,0:T(8,128)S(1)}, f32[24,128]{1,0:T(8,128)S(1)}, u32[]{:S(2)}, u32[]{:S(2)}) collective-permute-start(f32[24,128]{1,0:T(8,128)S(1)} %get-tuple-element.69), channel_id=1, source_target_pairs={{0,4},{4,0},{8,12},{12,8},{1,5},{5,1},{9,13},{13,9},{2,6},{6,2},{1... | collective-permute-start | bytes 36872 | tf_op jit(solution)/shard_map/ppermute | solution.py:452

commit v6 on v5

--- a/solution.py
+++ b/solution.py
@@ -100,15 +100,16 @@
     return fold3(acc)
 
 
-def by_cols(tiles, row_pick, vec, msg):
+def by_cols(tiles, rows, vec, msg):
     slots = tiles.shape[0]
-    pieces = jnp.concatenate(split3(vec), axis=1)
-    pad = jnp.zeros((LANES - SUB, 3 * LANES), F32)
-    stacked = jnp.concatenate([pieces, pad], axis=0).astype(BF16)
-    lines = jnp.dot(row_pick[...], stacked, preferred_element_type=F32)
+    blocks = [jnp.broadcast_to(vec[r : r + 1, :], (SUB, LANES)) for r in range(SUB)]
     sub = iota((SUB, LANES), 0)
     for g in range(0, slots, SUB):
-        group = [lines[g : g + SUB, p * LANES : (p + 1) * LANES] for p in range(3)]
+        row = rows[g : g + SUB, :]
+        lines = jnp.zeros((SUB, LANES), F32)
+        for r in range(SUB):
+            lines = jnp.where(row == float(r), blocks[r], lines)
+        group = split3(lines)
         acc = jnp.zeros((4 * SUB, LANES), F32)
         for s in range(0, SUB, 2):
             left = [left_of([jnp.where(sub == t, piece, 0.0) for piece in group]) for t in (s, s + 1)]
@@ -182,7 +183,7 @@
     return jnp.broadcast_to(jnp.sum(own, axis=1, keepdims=True), (rows, LANES))
 
 
-def prep_kernel(ids, rows, cols_line, index, mask_out, pick_out, cols_out, own_out, *send_out):
+def prep_kernel(ids, rows, cols_line, index, mask_out, cols_out, own_out, *send_out):
     n = ids.shape[1]
     left = ((ids[...] >> 7) == iota((SUB, n), 0)).astype(F32).astype(BF16)
     right = ((ids[...] & (LANES - 1)) == iota((LANES, n), 0)).astype(F32).astype(BF16)
@@ -196,7 +197,6 @@
     line = jnp.sum(jnp.where(sub == (lane & (slots - 1)), own, 0.0), axis=0, keepdims=True)
     cols_out[...] = jnp.broadcast_to(line, (SUB, LANES))
     own_out[...] = own
-    pick_out[...] = (rows[...] == lane.astype(F32)).astype(F32).astype(BF16)
     for out in send_out:
         run, rank = ranks(line, own, 1)
         row = iota((SHORT, LANES), 0)
@@ -250,14 +250,14 @@
     return jnp.sum(x, axis=0, keepdims=True)
 
 
-def margin_kernel(n_f, scale, tiles, row_pick, mask, labels, cols, *refs):
+def margin_kernel(n_f, scale, tiles, rows, mask, labels, cols, *refs):
     got, (msg, m_out, c_out, e_out, ww_out) = refs[:n_f], refs[n_f:]
     slots = tiles.shape[0]
     pieces = [(ref, 2 * SUB) for ref in got]
     m = feat_sum(pieces)
     chance = jax.nn.sigmoid(m)
     e = chance - labels[...].astype(F32)
-    by_cols(tiles, row_pick, e, msg)
+    by_cols(tiles, rows, e, msg)
     zero = jnp.zeros((1, LANES), F32)
     write_tail(msg, slots, [zero, zero, zero, cols[0:1, :]])
     ww_out[...] = feat_sum(pieces, SUB)
@@ -282,13 +282,13 @@
     out[...] = by_rows(turned, pieces, row_mask)
 
 
-def first_kernel(n_f, tiles, row_pick, m, c, e, *refs):
+def first_kernel(n_f, tiles, rows, m, c, e, *refs):
     got, (msg, v_out) = refs[:n_f], refs[n_f:]
     slots = tiles.shape[0]
     v = -(LAMBDA * m[...] + feat_sum([(ref, SUB) for ref in got]))
     v_out[...] = v
     u = c[...] * v
-    by_cols(tiles, row_pick, u, msg)
+    by_cols(tiles, rows, u, msg)
     s = -e[...]
     write_tail(msg, slots, [line_of(-LAMBDA * m[...] * s + s * v), line_of(u * v)])
 
@@ -354,7 +354,7 @@
     save_numbers(num_out, new)
 
 
-def next_kernel(n_f, short, tiles, row_pick, c, vec, num, *refs):
+def next_kernel(n_f, short, tiles, rows, c, vec, num, *refs):
     got, (msg, *kept) = refs[:n_f], refs[n_f:]
     slots = tiles.shape[0]
     if short:
@@ -362,7 +362,7 @@
     gram = feat_sum([(ref, SUB) for ref in got])
     v = at(vec, 0) - numbers_of(num)["alpha"] * gram
     u = c[...] * v
-    by_cols(tiles, row_pick, u, msg)
+    by_cols(tiles, rows, u, msg)
     lines = [line_of(at(vec, 4) + at(vec, 2) * v), line_of(u * v), line_of(u * at(vec, 1))]
     if short:
         chosen = exact_pick(send[...], msg[...])
@@ -498,11 +498,11 @@
         [f32(2 * SUB, LANES), f32(slots * SUB, LANES)],
         scratch=[pltpu.VMEM((slots, LANES), F32), pltpu.VMEM((3 * slots, LANES), F32)],
     )
-    mask, row_pick, cols_line, own, *send = call(
+    mask, cols_line, own, *send = call(
         prep_kernel,
         (sample_ids, rows, tile_cols.reshape(1, slots), index),
         [VM] * 3 + [SM],
-        [grid, picks((slots, LANES), BF16), grid, f32(slots, LANES)]
+        [grid, grid, f32(slots, LANES)]
         + [picks((4 * SHORT, slots), BF16)] * short,
     )
     (turned,) = call(turn_kernel, (tiles,), [VM], [tile_shape])
@@ -510,7 +510,7 @@
     n_f = len(got)
     msg, m, c, e, ww = call(
         functools.partial(margin_kernel, n_f, scale),
-        (tiles, row_pick, mask, labels.reshape(SUB, LANES), cols_line, *got),
+        (tiles, rows, mask, labels.reshape(SUB, LANES), cols_line, *got),
         [VM] * (5 + n_f),
         [msg_shape, grid, grid, grid, grid],
     )
@@ -536,7 +536,7 @@
     got = forward(msgs, ORDERS[0])
     msg, v = call(
         functools.partial(first_kernel, n_f),
-        (tiles, row_pick, m, c, e, *got),
+        (tiles, rows, m, c, e, *got),
         [VM] * (5 + n_f),
         [msg_shape, grid],
     )
@@ -553,7 +553,7 @@
         if short and k == ITERS - 2:
             to_each = call(
                 functools.partial(next_kernel, n_f, True),
-                (tiles, row_pick, c, vec, num, *got, *send),
+                (tiles, rows, c, vec, num, *got, *send),
                 [VM] * (6 + n_f),
                 [f32(SHORT, LANES)] * 4,
                 scratch=[pltpu.VMEM((slots, LANES), F32)],
@@ -563,7 +563,7 @@
             break
         msg, *kept = call(
             functools.partial(next_kernel, n_f, False),
-            (tiles, row_pick, c, vec, num, *got),
+            (tiles, rows, c, vec, num, *got),
             [VM] * (5 + n_f),
             [msg_shape] + [grid, grid] * (k < ITERS - 2),
         )

time: 55.8 us -> 55.3 us (level)
  no operation moved by 1% of the time
where the time goes in v6:
time: 55.3 us; the launch traced here: 55.2 us
  starting transfers between devices  26.7 us (48%)
  waiting for transfers between devices  18.4 us (33%)
  Pallas kernels  8.36 us (15%)
  between operations  1.58 us (3%)
    ppermute x21, starting transfers between devices, exchange(): lax.ppermute(x, axis, [(i, i ^ k) for i in range(size)])  22.2 us
    ppermute x21, waiting for transfers between devices, exchange(): lax.ppermute(x, axis, [(i, i ^ k) for i in range(size)])  16.9 us
    pallas_call x16, Pallas kernels, call(): pl.pallas_call(kernel, in_specs=in_specs, out_shape=outs, out_specs=out_s...  8.36 us
    ppermute x3, starting transfers between devices, exchange_each(): lax.ppermute(x, axis, [(i, i ^ k) for i in range(4)])  4.45 us
    ppermute x3, waiting for transfers between devices, exchange_each(): lax.ppermute(x, axis, [(i, i ^ k) for i in range(4)])  1.5 us
  transfers between devices with their start and end apart: 24, of which 18 were waited for; matrix products, arithmetic and copies ran while one was open for 0% of the time, Pallas kernels for 3%

profile of v6, /device:TPU:0, one launch (start us, length us, event | category | flops | bytes accessed | tf_op | source)
XLA Modules:
  0.0 55.2 jit_solution(12950002108228450281)
XLA Ops:
  1.4 1.0 %shard_map.86 = (f32[64,128]{1,0:T(8,128)S(1)}, s32[64,128]{1,0:T(8,128)S(1)}, s32[1,64]{1,0:T(1,128)S(4)}) custom-call(s32[1,64]{1,0:T(1,128)} %bitcast.23, s32[1,64]{1,0:T(1,128)} %bitcast.19), custom_call_target="tpu_custom_call" | custom-call | flops 1073741824 | bytes 1048576 | tf_op jit(solution)/shard_map/pallas_call | solution.py:30
  2.4 0.0 copy-start.3
  2.5 0.0 copy-start.4
  2.5 0.0 copy-start.2
  2.5 0.1 copy-done
  2.6 0.8 %shard_map.88 = (f32[16,128]{1,0:T(8,128)S(1)}, f32[512,128]{1,0:T(8,128)S(1)}) custom-call(s32[1,64]{1,0:T(1,128)S(4)} %get-tuple-element.40.cols, f32[64,128]{1,0:T(8,128)S(1)} %compare_select_fusion.rows, bf16[64,128,128]{2,1,0:T(8,128)(2,1)S(1)} %bitcast.10, f32[2048,128]{1,0:T(8,128)S(1)} %bitcast.16), custom_call_target="tpu_custom_call" | custom-call | flops 2097152 | bytes 1048576 | tf_op jit(solution)/shard_map/pallas_call | solution.py:30
  3.3 2.4 %collective-permute-start.2 = (f32[16,128]{1,0:T(8,128)S(1)}, f32[16,128]{1,0:T(8,128)S(1)}, u32[]{:S(2)}, u32[]{:S(2)}) collective-permute-start(f32[16,128]{1,0:T(8,128)S(1)} %get-tuple-element.41.refs_0_), channel_id=1, source_target_pairs={{0,3},{1,2},{2,1},{3,0},{4,7},{5,6},{6,5},{7,4},{8,11},{9,10},{10,... | collective-permute-start | bytes 24584 | tf_op jit(solution)/shard_map/ppermute | solution.py:446
  5.8 0.6 %collective-permute-start.1 = (f32[16,128]{1,0:T(8,128)S(1)}, f32[16,128]{1,0:T(8,128)S(1)}, u32[]{:S(2)}, u32[]{:S(2)}) collective-permute-start(f32[16,128]{1,0:T(8,128)S(1)} %get-tuple-element.41.refs_0_), channel_id=1, source_target_pairs={{0,2},{1,3},{2,0},{3,1},{4,6},{5,7},{6,4},{7,5},{8,10},{9,11},{10,... | collective-permute-start | bytes 24584 | tf_op jit(solution)/shard_map/ppermute | solution.py:446
  6.4 0.0 collective-permute-start
  6.5 0.2 shard_map.87
  6.7 0.5 collective-permute-done.2.refs_3_
  7.1 2.3 %collective-permute-done.1.refs_2_ = f32[16,128]{1,0:T(8,128)S(1)} collective-permute-done((f32[16,128]{1,0:T(8,128)S(1)}, f32[16,128]{1,0:T(8,128)S(1)}, u32[]{:S(2)}, u32[]{:S(2)}) %collective-permute-start.1) | collective-permute-done | bytes 8224 | tf_op jit(solution)/shard_map/ppermute | solution.py:446
  9.4 0.0 collective-permute-done.refs_1_
  9.4 0.4 shard_map.89
  9.9 3.7 %collective-permute-start.5 = (f32[72,128]{1,0:T(8,128)S(1)}, f32[72,128]{1,0:T(8,128)S(1)}, u32[]{:S(2)}, u32[]{:S(2)}) collective-permute-start(f32[72,128]{1,0:T(8,128)S(1)} %get-tuple-element.48.refs_0_), channel_id=1, source_target_pairs={{0,12},{4,8},{8,4},{12,0},{1,13},{5,9},{9,5},{13,1},{2,14},{6,10},... | collective-permute-start | bytes 110600 | tf_op jit(solution)/shard_map/ppermute | solution.py:446
  13.5 0.0 collective-permute-start.4
  13.5 0.8 %collective-permute-start.3 = (f32[72,128]{1,0:T(8,128)S(1)}, f32[72,128]{1,0:T(8,128)S(1)}, u32[]{:S(2)}, u32[]{:S(2)}) collective-permute-start(f32[72,128]{1,0:T(8,128)S(1)} %get-tuple-element.48.refs_0_), channel_id=1, source_target_pairs={{0,4},{4,0},{8,12},{12,8},{1,5},{5,1},{9,13},{13,9},{2,6},{6,2},{1... | collective-permute-start | bytes 110600 | tf_op jit(solution)/shard_map/ppermute | solution.py:446
  14.3 0.6 %shard_map.90.turned = bf16[64,128,128]{2,1,0:T(8,128)(2,1)S(1)} custom-call(bf16[64,128,128]{2,1,0:T(8,128)(2,1)S(1)} %bitcast.12), custom_call_target="tpu_custom_call" | custom-call | flops 2097152 | bytes 1048576 | tf_op jit(solution)/shard_map/pallas_call | solution.py:30
  14.9 1.2 %collective-permute-done.5.refs_3_ = f32[72,128]{1,0:T(8,128)S(1)} collective-permute-done((f32[72,128]{1,0:T(8,128)S(1)}, f32[72,128]{1,0:T(8,128)S(1)}, u32[]{:S(2)}, u32[]{:S(2)}) %collective-permute-start.5) | collective-permute-done | bytes 36896 | tf_op jit(solution)/shard_map/ppermute | solution.py:446
  16.1 2.3 %collective-permute-done.4.refs_2_ = f32[72,128]{1,0:T(8,128)S(1)} collective-permute-done((f32[72,128]{1,0:T(8,128)S(1)}, f32[72,128]{1,0:T(8,128)S(1)}, u32[]{:S(2)}, u32[]{:S(2)}) %collective-permute-start.4) | collective-permute-done | bytes 36896 | tf_op jit(solution)/shard_map/ppermute | solution.py:446
  18.4 0.6 %shard_map.92.refs_0_ = f32[8,128]{1,0:T(8,128)S(1)} custom-call(bf16[64,128,128]{2,1,0:T(8,128)(2,1)S(1)} %shard_map.90.turned, f32[512,128]{1,0:T(8,128)S(1)} %get-tuple-element.46.row_mask, bf16[64,256]{1,0:T(8,128)(2,1)S(1)} %shard_map.91.match, f32[72,128]{1,0:T(8,128)S(1)} %get-tuple-element.48.refs_0_, f32[72,128]{1,0:T(8,128)S(1)} %collective-permute-done.3.refs_1_, ...), custom_call_target="tpu_custom_call" | custom-call | flops 2097152 | bytes 1048576 | tf_op jit(solution)/shard_map/pallas_call | solution.py:30
  19.0 0.1 collective-permute-start.8
  19.1 0.7 %collective-permute-start.7 = (f32[8,128]{1,0:T(8,128)S(1)}, f32[8,128]{1,0:T(8,128)S(1)}, u32[]{:S(2)}, u32[]{:S(2)}) collective-permute-start(f32[8,128]{1,0:T(8,128)S(1)} %shard_map.92.refs_0_), channel_id=1, source_target_pairs={{0,2},{1,3},{2,0},{3,1},{4,6},{5,7},{6,4},{7,5},{8,10},{9,11},{10,... | collective-permute-start | bytes 12296 | tf_op jit(solution)/shard_map/ppermute | solution.py:446
  19.8 1.1 %collective-permute-start.6 = (f32[8,128]{1,0:T(8,128)S(1)}, f32[8,128]{1,0:T(8,128)S(1)}, u32[]{:S(2)}, u32[]{:S(2)}) collective-permute-start(f32[8,128]{1,0:T(8,128)S(1)} %shard_map.92.refs_0_), channel_id=1, source_target_pairs={{0,1},{1,0},{2,3},{3,2},{4,5},{5,4},{6,7},{7,6},{8,9},{9,8},{10,11... | collective-permute-start | bytes 12296 | tf_op jit(solution)/shard_map/ppermute | solution.py:446
  20.9 1.2 %collective-permute-done.8.refs_3_ = f32[8,128]{1,0:T(8,128)S(1)} collective-permute-done((f32[8,128]{1,0:T(8,128)S(1)}, f32[8,128]{1,0:T(8,128)S(1)}, u32[]{:S(2)}, u32[]{:S(2)}) %collective-permute-start.8) | collective-permute-done | bytes 4128 | tf_op jit(solution)/shard_map/ppermute | solution.py:446
  22.1 0.7 %collective-permute-done.7.refs_2_ = f32[8,128]{1,0:T(8,128)S(1)} collective-permute-done((f32[8,128]{1,0:T(8,128)S(1)}, f32[8,128]{1,0:T(8,128)S(1)}, u32[]{:S(2)}, u32[]{:S(2)}) %collective-permute-start.7) | collective-permute-done | bytes 4128 | tf_op jit(solution)/shard_map/ppermute | solution.py:446
  22.7 0.4 shard_map.93
  23.2 1.5 %collective-permute-start.11 = (f32[72,128]{1,0:T(8,128)S(1)}, f32[72,128]{1,0:T(8,128)S(1)}, u32[]{:S(2)}, u32[]{:S(2)}) collective-permute-start(f32[72,128]{1,0:T(8,128)S(1)} %get-tuple-element.49.refs_0_.refs_4_), channel_id=1, source_target_pairs={{0,12},{4,8},{8,4},{12,0},{1,13},{5,9},{9,5},{13,1},{2,14},{6,10},... | collective-permute-start | bytes 110600 | tf_op jit(solution)/shard_map/ppermute | solution.py:446
  24.7 0.6 %collective-permute-start.10 = (f32[72,128]{1,0:T(8,128)S(1)}, f32[72,128]{1,0:T(8,128)S(1)}, u32[]{:S(2)}, u32[]{:S(2)}) collective-permute-start(f32[72,128]{1,0:T(8,128)S(1)} %get-tuple-element.49.refs_0_.refs_4_), channel_id=1, source_target_pairs={{0,8},{4,12},{8,0},{12,4},{1,9},{5,13},{9,1},{13,5},{2,10},{6,14},... | collective-permute-start | bytes 110600 | tf_op jit(solution)/shard_map/ppermute | solution.py:446
  25.3 2.3 %collective-permute-start.9 = (f32[72,128]{1,0:T(8,128)S(1)}, f32[72,128]{1,0:T(8,128)S(1)}, u32[]{:S(2)}, u32[]{:S(2)}) collective-permute-start(f32[72,128]{1,0:T(8,128)S(1)} %get-tuple-element.49.refs_0_.refs_4_), channel_id=1, source_target_pairs={{0,4},{4,0},{8,12},{12,8},{1,5},{5,1},{9,13},{13,9},{2,6},{6,2},{1... | collective-permute-start | bytes 110600 | tf_op jit(solution)/shard_map/ppermute | solution.py:446
  27.6 1.8 %collective-permute-done.11.refs_3_.refs_7_ = f32[72,128]{1,0:T(8,128)S(1)} collective-permute-done((f32[72,128]{1,0:T(8,128)S(1)}, f32[72,128]{1,0:T(8,128)S(1)}, u32[]{:S(2)}, u32[]{:S(2)}) %collective-permute-start.11) | collective-permute-done | bytes 36896 | tf_op jit(solution)/shard_map/ppermute | solution.py:446
  29.4 0.3 collective-permute-done.10.refs_2_.refs_6_
  29.7 0.3 collective-permute-done.9.refs_1_.refs_5_
  30.0 0.6 %shard_map.95.refs_0_ = f32[8,128]{1,0:T(8,128)S(1)} custom-call(bf16[64,128,128]{2,1,0:T(8,128)(2,1)S(1)} %shard_map.90.turned, f32[512,128]{1,0:T(8,128)S(1)} %get-tuple-element.46.row_mask, bf16[64,256]{1,0:T(8,128)(2,1)S(1)} %shard_map.91.match, f32[72,128]{1,0:T(8,128)S(1)} %get-tuple-element.49.refs_0_.refs_4_, ...), custom_call_target="tpu_custom_call" | custom-call | flops 2097152 | bytes 1048576 | tf_op jit(solution)/shard_map/pallas_call | solution.py:30
  30.6 0.3 collective-permute-start.14
  31.0 0.7 %collective-permute-start.13 = (f32[8,128]{1,0:T(8,128)S(1)}, f32[8,128]{1,0:T(8,128)S(1)}, u32[]{:S(2)}, u32[]{:S(2)}) collective-permute-start(f32[8,128]{1,0:T(8,128)S(1)} %shard_map.95.refs_0_), channel_id=1, source_target_pairs={{0,2},{1,3},{2,0},{3,1},{4,6},{5,7},{6,4},{7,5},{8,10},{9,11},{10,... | collective-permute-start | bytes 12296 | tf_op jit(solution)/shard_map/ppermute | solution.py:446
  31.6 0.9 %collective-permute-start.12 = (f32[8,128]{1,0:T(8,128)S(1)}, f32[8,128]{1,0:T(8,128)S(1)}, u32[]{:S(2)}, u32[]{:S(2)}) collective-permute-start(f32[8,128]{1,0:T(8,128)S(1)} %shard_map.95.refs_0_), channel_id=1, source_target_pairs={{0,1},{1,0},{2,3},{3,2},{4,5},{5,4},{6,7},{7,6},{8,9},{9,8},{10,11... | collective-permute-start | bytes 12296 | tf_op jit(solution)/shard_map/ppermute | solution.py:446
  32.6 0.1 shard_map.94
  32.7 1.0 %collective-permute-done.14.refs_3_ = f32[8,128]{1,0:T(8,128)S(1)} collective-permute-done((f32[8,128]{1,0:T(8,128)S(1)}, f32[8,128]{1,0:T(8,128)S(1)}, u32[]{:S(2)}, u32[]{:S(2)}) %collective-permute-start.14) | collective-permute-done | bytes 4128 | tf_op jit(solution)/shard_map/ppermute | solution.py:446
  33.7 0.9 %collective-permute-done.13.refs_2_ = f32[8,128]{1,0:T(8,128)S(1)} collective-permute-done((f32[8,128]{1,0:T(8,128)S(1)}, f32[8,128]{1,0:T(8,128)S(1)}, u32[]{:S(2)}, u32[]{:S(2)}) %collective-permute-start.13) | collective-permute-done | bytes 4128 | tf_op jit(solution)/shard_map/ppermute | solution.py:446
  34.6 0.0 collective-permute-done.12.refs_1_
  34.6 0.4 shard_map.96
  35.0 2.1 %collective-permute-start.17 = (f32[72,128]{1,0:T(8,128)S(1)}, f32[72,128]{1,0:T(8,128)S(1)}, u32[]{:S(2)}, u32[]{:S(2)}) collective-permute-start(f32[72,128]{1,0:T(8,128)S(1)} %get-tuple-element.53.refs_0_.refs_8_), channel_id=1, source_target_pairs={{0,12},{4,8},{8,4},{12,0},{1,13},{5,9},{9,5},{13,1},{2,14},{6,10},... | collective-permute-start | bytes 110600 | tf_op jit(solution)/shard_map/ppermute | solution.py:446
  37.2 0.7 %collective-permute-start.16 = (f32[72,128]{1,0:T(8,128)S(1)}, f32[72,128]{1,0:T(8,128)S(1)}, u32[]{:S(2)}, u32[]{:S(2)}) collective-permute-start(f32[72,128]{1,0:T(8,128)S(1)} %get-tuple-element.53.refs_0_.refs_8_), channel_id=1, source_target_pairs={{0,8},{4,12},{8,0},{12,4},{1,9},{5,13},{9,1},{13,5},{2,10},{6,14},... | collective-permute-start | bytes 110600 | tf_op jit(solution)/shard_map/ppermute | solution.py:446
  37.9 1.6 %collective-permute-start.15 = (f32[72,128]{1,0:T(8,128)S(1)}, f32[72,128]{1,0:T(8,128)S(1)}, u32[]{:S(2)}, u32[]{:S(2)}) collective-permute-start(f32[72,128]{1,0:T(8,128)S(1)} %get-tuple-element.53.refs_0_.refs_8_), channel_id=1, source_target_pairs={{0,4},{4,0},{8,12},{12,8},{1,5},{5,1},{9,13},{13,9},{2,6},{6,2},{1... | collective-permute-start | bytes 110600 | tf_op jit(solution)/shard_map/ppermute | solution.py:446
  39.5 1.4 %collective-permute-done.17.refs_3_.refs_11_ = f32[72,128]{1,0:T(8,128)S(1)} collective-permute-done((f32[72,128]{1,0:T(8,128)S(1)}, f32[72,128]{1,0:T(8,128)S(1)}, u32[]{:S(2)}, u32[]{:S(2)}) %collective-permute-start.17) | collective-permute-done | bytes 36896 | tf_op jit(solution)/shard_map/ppermute | solution.py:446
  40.9 1.2 %collective-permute-done.16.refs_2_.refs_10_ = f32[72,128]{1,0:T(8,128)S(1)} collective-permute-done((f32[72,128]{1,0:T(8,128)S(1)}, f32[72,128]{1,0:T(8,128)S(1)}, u32[]{:S(2)}, u32[]{:S(2)}) %collective-permute-start.16) | collective-permute-done | bytes 36896 | tf_op jit(solution)/shard_map/ppermute | solution.py:446
  42.1 0.3 collective-permute-done.15.refs_1_.refs_9_
  42.4 0.6 %shard_map.99.refs_0_ = f32[8,128]{1,0:T(8,128)S(1)} custom-call(bf16[64,128,128]{2,1,0:T(8,128)(2,1)S(1)} %shard_map.90.turned, f32[512,128]{1,0:T(8,128)S(1)} %get-tuple-element.46.row_mask, bf16[64,256]{1,0:T(8,128)(2,1)S(1)} %shard_map.91.match, f32[72,128]{1,0:T(8,128)S(1)} %get-tuple-element.53.refs_0_.refs_8_, ...), custom_call_target="tpu_custom_call" | custom-call | flops 2097152 | bytes 1048576 | tf_op jit(solution)/shard_map/pallas_call | solution.py:30
  43.0 0.1 collective-permute-start.20
  43.1 0.8 %collective-permute-start.19 = (f32[8,128]{1,0:T(8,128)S(1)}, f32[8,128]{1,0:T(8,128)S(1)}, u32[]{:S(2)}, u32[]{:S(2)}) collective-permute-start(f32[8,128]{1,0:T(8,128)S(1)} %shard_map.99.refs_0_), channel_id=1, source_target_pairs={{0,2},{1,3},{2,0},{3,1},{4,6},{5,7},{6,4},{7,5},{8,10},{9,11},{10,... | collective-permute-start | bytes 12296 | tf_op jit(solution)/shard_map/ppermute | solution.py:446
  44.0 1.0 %collective-permute-start.18 = (f32[8,128]{1,0:T(8,128)S(1)}, f32[8,128]{1,0:T(8,128)S(1)}, u32[]{:S(2)}, u32[]{:S(2)}) collective-permute-start(f32[8,128]{1,0:T(8,128)S(1)} %shard_map.99.refs_0_), channel_id=1, source_target_pairs={{0,1},{1,0},{2,3},{3,2},{4,5},{5,4},{6,7},{7,6},{8,9},{9,8},{10,11... | collective-permute-start | bytes 12296 | tf_op jit(solution)/shard_map/ppermute | solution.py:446
  45.0 0.2 shard_map.97
  45.2 0.9 %collective-permute-done.20.refs_3_ = f32[8,128]{1,0:T(8,128)S(1)} collective-permute-done((f32[8,128]{1,0:T(8,128)S(1)}, f32[8,128]{1,0:T(8,128)S(1)}, u32[]{:S(2)}, u32[]{:S(2)}) %collective-permute-start.20) | collective-permute-done | bytes 4128 | tf_op jit(solution)/shard_map/ppermute | solution.py:446
  46.1 0.7 %collective-permute-done.19.refs_2_ = f32[8,128]{1,0:T(8,128)S(1)} collective-permute-done((f32[8,128]{1,0:T(8,128)S(1)}, f32[8,128]{1,0:T(8,128)S(1)}, u32[]{:S(2)}, u32[]{:S(2)}) %collective-permute-start.19) | collective-permute-done | bytes 4128 | tf_op jit(solution)/shard_map/ppermute | solution.py:446
  46.8 0.6 %shard_map.100 = (f32[24,128]{1,0:T(8,128)S(1)}, f32[24,128]{1,0:T(8,128)S(1)}, f32[24,128]{1,0:T(8,128)S(1)}, f32[24,128]{1,0:T(8,128)S(1)}) custom-call(bf16[64,128,128]{2,1,0:T(8,128)(2,1)S(1)} %bitcast.15, f32[64,128]{1,0:T(8,128)S(1)} %compare_select_fusion.rows, f32[8,128]{1,0:T(8,128)S(1)} %get-tuple-element.44.c, ...), custom_call_target="tpu_custom_call" | custom-call | flops 2097152 | bytes 1048576 | tf_op jit(solution)/shard_map/pallas_call | solution.py:30
  47.4 2.1 %collective-permute-start.21 = (f32[24,128]{1,0:T(8,128)S(1)}, f32[24,128]{1,0:T(8,128)S(1)}, u32[]{:S(2)}, u32[]{:S(2)}) collective-permute-start(f32[24,128]{1,0:T(8,128)S(1)} %get-tuple-element.65), channel_id=1, source_target_pairs={{0,12},{4,8},{8,4},{12,0},{1,13},{5,9},{9,5},{13,1},{2,14},{6,10},... | collective-permute-start | bytes 36872 | tf_op jit(solution)/shard_map/ppermute | solution.py:452
  49.5 0.5 collective-permute-start.22
  49.9 1.9 %collective-permute-start.23 = (f32[24,128]{1,0:T(8,128)S(1)}, f32[24,128]{1,0:T(8,128)S(1)}, u32[]{:S(2)}, u32[]{:S(2)}) collective-permute-start(f32[24,128]{1,0:T(8,128)S(1)} %get-tuple-element.67), channel_id=1, source_target_pairs={{0,4},{4,0},{8,12},{12,8},{1,5},{5,1},{9,13},{13,9},{2,6},{6,2},{1... | collective-permute-start | bytes 36872 | tf_op jit(solution)/shard_map/ppermute | solution.py:452
  51.8 0.7 %shard_map.98 = (f32[512,128]{1,0:T(8,128)S(1)}, f32[512,128]{1,0:T(8,128)S(1)}, f32[512,128]{1,0:T(8,128)S(1)}, f32[512,128]{1,0:T(8,128)S(1)}, bf16[512,128]{1,0:T(8,128)(2,1)S(1)}) custom-call(f32[2048,128]{1,0:T(8,128)S(1)} %bitcast.17, s32[1]{0:T(128)} %bitcast.4.index, f32[72,128]{1,0:T(8,128)S(1)} %get-tuple-element.48.refs_0_, ...), custom_call_target="tpu_custom_call" | custom-call | flops 2097152 | bytes 1048576 | tf_op jit(solution)/shard_map/pallas_call | solution.py:30
  52.6 0.4 collective-permute-done.21.refs_1_
  52.9 1.1 %collective-permute-done.22.refs_2_ = f32[24,128]{1,0:T(8,128)S(1)} collective-permute-done((f32[24,128]{1,0:T(8,128)S(1)}, f32[24,128]{1,0:T(8,128)S(1)}, u32[]{:S(2)}, u32[]{:S(2)}) %collective-permute-start.22) | collective-permute-done | bytes 12320 | tf_op jit(solution)/shard_map/ppermute | solution.py:452
  54.1 0.0 collective-permute-done.23.refs_3_
  54.1 1.1 %shard_map.101 = (f32[512,128]{1,0:T(8,128)}, f32[512,128]{1,0:T(8,128)}) custom-call(f32[8,128]{1,0:T(8,128)S(1)} %get-tuple-element.42.ww, f32[8,128]{1,0:T(8,128)S(1)} %get-tuple-element.56.refs_13_.num, f32[512,128]{1,0:T(8,128)S(1)} %get-tuple-element.57.res, f32[512,128]{1,0:T(8,128)S(1)} %get-tuple-element.58.direction, ...), custom_call_target="tpu_custom_call" | custom-call | flops 2097152 | bytes 1048576 | tf_op jit(solution)/shard_map/pallas_call | solution.py:30
  (11 shorter events, 0.0 us)
Async XLA Ops:
  0.6 1.9 %copy-start.1 = (f32[1,262144]{1,0:T(1,128)S(1)}, f32[1,262144]{1,0:T(1,128)}, u32[]{:S(2)}) copy-start(f32[1,262144]{1,0:T(1,128)} %param.13) | copy-start | bytes 3145732
  0.6 1.9 %copy-start = (bf16[1,1,64,128,128]{4,3,2,1,0:T(8,128)(2,1)S(1)}, bf16[1,1,64,128,128]{4,3,2,1,0:T(8,128)(2,1)}, u32[]{:S(2)}) copy-start(bf16[1,1,64,128,128]{4,3,2,1,0:T(8,128)(2,1)} %param.7) | copy-start | bytes 6291460
  2.4 4.0 %copy-start.3 = (s32[1,512]{1,0:T(1,128)S(1)}, s32[1,512]{1,0:T(1,128)}, u32[]{:S(2)}) copy-start(s32[1,512]{1,0:T(1,128)} %ids.1) | copy-start | bytes 6148
  2.5 4.0 %copy-start.4 = (s32[1,1,64]{2,1,0:T(1,128)S(1)}, s32[1,1,64]{2,1,0:T(1,128)}, u32[]{:S(2)}) copy-start(s32[1,1,64]{2,1,0:T(1,128)} %param.9) | copy-start | bytes 772
  2.5 7.0 %copy-start.2 = (s32[1,1024]{1,0:T(1,128)S(1)}, s32[1,1024]{1,0:T(1,128)}, u32[]{:S(2)}) copy-start(s32[1,1024]{1,0:T(1,128)} %param.12) | copy-start | bytes 12292
  3.3 3.8 %collective-permute-start.2 = (f32[16,128]{1,0:T(8,128)S(1)}, f32[16,128]{1,0:T(8,128)S(1)}, u32[]{:S(2)}, u32[]{:S(2)}) collective-permute-start(f32[16,128]{1,0:T(8,128)S(1)} %get-tuple-element.41.refs_0_), channel_id=1, source_target_pairs={{0,3},{1,2},{2,1},{3,0},{4,7},{5,6},{6,5},{7,4},{8,11},{9,10},{10,... | collective-permute-start | bytes 24584 | tf_op jit(solution)/shard_map/ppermute | solution.py:446
  5.8 3.7 %collective-permute-start.1 = (f32[16,128]{1,0:T(8,128)S(1)}, f32[16,128]{1,0:T(8,128)S(1)}, u32[]{:S(2)}, u32[]{:S(2)}) collective-permute-start(f32[16,128]{1,0:T(8,128)S(1)} %get-tuple-element.41.refs_0_), channel_id=1, source_target_pairs={{0,2},{1,3},{2,0},{3,1},{4,6},{5,7},{6,4},{7,5},{8,10},{9,11},{10,... | collective-permute-start | bytes 24584 | tf_op jit(solution)/shard_map/ppermute | solution.py:446
  6.4 3.0 %collective-permute-start = (f32[16,128]{1,0:T(8,128)S(1)}, f32[16,128]{1,0:T(8,128)S(1)}, u32[]{:S(2)}, u32[]{:S(2)}) collective-permute-start(f32[16,128]{1,0:T(8,128)S(1)} %get-tuple-element.41.refs_0_), channel_id=1, source_target_pairs={{0,1},{1,0},{2,3},{3,2},{4,5},{5,4},{6,7},{7,6},{8,9},{9,8},{10,11... | collective-permute-start | bytes 24584 | tf_op jit(solution)/shard_map/ppermute | solution.py:446
  9.9 6.3 %collective-permute-start.5 = (f32[72,128]{1,0:T(8,128)S(1)}, f32[72,128]{1,0:T(8,128)S(1)}, u32[]{:S(2)}, u32[]{:S(2)}) collective-permute-start(f32[72,128]{1,0:T(8,128)S(1)} %get-tuple-element.48.refs_0_), channel_id=1, source_target_pairs={{0,12},{4,8},{8,4},{12,0},{1,13},{5,9},{9,5},{13,1},{2,14},{6,10},... | collective-permute-start | bytes 110600 | tf_op jit(solution)/shard_map/ppermute | solution.py:446
  13.5 4.9 %collective-permute-start.4 = (f32[72,128]{1,0:T(8,128)S(1)}, f32[72,128]{1,0:T(8,128)S(1)}, u32[]{:S(2)}, u32[]{:S(2)}) collective-permute-start(f32[72,128]{1,0:T(8,128)S(1)} %get-tuple-element.48.refs_0_), channel_id=1, source_target_pairs={{0,8},{4,12},{8,0},{12,4},{1,9},{5,13},{9,1},{13,5},{2,10},{6,14},... | collective-permute-start | bytes 110600 | tf_op jit(solution)/shard_map/ppermute | solution.py:446
  13.5 4.9 %collective-permute-start.3 = (f32[72,128]{1,0:T(8,128)S(1)}, f32[72,128]{1,0:T(8,128)S(1)}, u32[]{:S(2)}, u32[]{:S(2)}) collective-permute-start(f32[72,128]{1,0:T(8,128)S(1)} %get-tuple-element.48.refs_0_), channel_id=1, source_target_pairs={{0,4},{4,0},{8,12},{12,8},{1,5},{5,1},{9,13},{13,9},{2,6},{6,2},{1... | collective-permute-start | bytes 110600 | tf_op jit(solution)/shard_map/ppermute | solution.py:446
  19.0 3.1 %collective-permute-start.8 = (f32[8,128]{1,0:T(8,128)S(1)}, f32[8,128]{1,0:T(8,128)S(1)}, u32[]{:S(2)}, u32[]{:S(2)}) collective-permute-start(f32[8,128]{1,0:T(8,128)S(1)} %shard_map.92.refs_0_), channel_id=1, source_target_pairs={{0,3},{1,2},{2,1},{3,0},{4,7},{5,6},{6,5},{7,4},{8,11},{9,10},{10,... | collective-permute-start | bytes 12296 | tf_op jit(solution)/shard_map/ppermute | solution.py:446
  19.1 3.7 %collective-permute-start.7 = (f32[8,128]{1,0:T(8,128)S(1)}, f32[8,128]{1,0:T(8,128)S(1)}, u32[]{:S(2)}, u32[]{:S(2)}) collective-permute-start(f32[8,128]{1,0:T(8,128)S(1)} %shard_map.92.refs_0_), channel_id=1, source_target_pairs={{0,2},{1,3},{2,0},{3,1},{4,6},{5,7},{6,4},{7,5},{8,10},{9,11},{10,... | collective-permute-start | bytes 12296 | tf_op jit(solution)/shard_map/ppermute | solution.py:446
  19.8 3.0 %collective-permute-start.6 = (f32[8,128]{1,0:T(8,128)S(1)}, f32[8,128]{1,0:T(8,128)S(1)}, u32[]{:S(2)}, u32[]{:S(2)}) collective-permute-start(f32[8,128]{1,0:T(8,128)S(1)} %shard_map.92.refs_0_), channel_id=1, source_target_pairs={{0,1},{1,0},{2,3},{3,2},{4,5},{5,4},{6,7},{7,6},{8,9},{9,8},{10,11... | collective-permute-start | bytes 12296 | tf_op jit(solution)/shard_map/ppermute | solution.py:446
  23.2 6.2 %collective-permute-start.11 = (f32[72,128]{1,0:T(8,128)S(1)}, f32[72,128]{1,0:T(8,128)S(1)}, u32[]{:S(2)}, u32[]{:S(2)}) collective-permute-start(f32[72,128]{1,0:T(8,128)S(1)} %get-tuple-element.49.refs_0_.refs_4_), channel_id=1, source_target_pairs={{0,12},{4,8},{8,4},{12,0},{1,13},{5,9},{9,5},{13,1},{2,14},{6,10},... | collective-permute-start | bytes 110600 | tf_op jit(solution)/shard_map/ppermute | solution.py:446
  24.7 5.0 %collective-permute-start.10 = (f32[72,128]{1,0:T(8,128)S(1)}, f32[72,128]{1,0:T(8,128)S(1)}, u32[]{:S(2)}, u32[]{:S(2)}) collective-permute-start(f32[72,128]{1,0:T(8,128)S(1)} %get-tuple-element.49.refs_0_.refs_4_), channel_id=1, source_target_pairs={{0,8},{4,12},{8,0},{12,4},{1,9},{5,13},{9,1},{13,5},{2,10},{6,14},... | collective-permute-start | bytes 110600 | tf_op jit(solution)/shard_map/ppermute | solution.py:446
  25.3 4.7 %collective-permute-start.9 = (f32[72,128]{1,0:T(8,128)S(1)}, f32[72,128]{1,0:T(8,128)S(1)}, u32[]{:S(2)}, u32[]{:S(2)}) collective-permute-start(f32[72,128]{1,0:T(8,128)S(1)} %get-tuple-element.49.refs_0_.refs_4_), channel_id=1, source_target_pairs={{0,4},{4,0},{8,12},{12,8},{1,5},{5,1},{9,13},{13,9},{2,6},{6,2},{1... | collective-permute-start | bytes 110600 | tf_op jit(solution)/shard_map/ppermute | solution.py:446
  30.6 3.1 %collective-permute-start.14 = (f32[8,128]{1,0:T(8,128)S(1)}, f32[8,128]{1,0:T(8,128)S(1)}, u32[]{:S(2)}, u32[]{:S(2)}) collective-permute-start(f32[8,128]{1,0:T(8,128)S(1)} %shard_map.95.refs_0_), channel_id=1, source_target_pairs={{0,3},{1,2},{2,1},{3,0},{4,7},{5,6},{6,5},{7,4},{8,11},{9,10},{10,... | collective-permute-start | bytes 12296 | tf_op jit(solution)/shard_map/ppermute | solution.py:446
  31.0 3.6 %collective-permute-start.13 = (f32[8,128]{1,0:T(8,128)S(1)}, f32[8,128]{1,0:T(8,128)S(1)}, u32[]{:S(2)}, u32[]{:S(2)}) collective-permute-start(f32[8,128]{1,0:T(8,128)S(1)} %shard_map.95.refs_0_), channel_id=1, source_target_pairs={{0,2},{1,3},{2,0},{3,1},{4,6},{5,7},{6,4},{7,5},{8,10},{9,11},{10,... | collective-permute-start | bytes 12296 | tf_op jit(solution)/shard_map/ppermute | solution.py:446
  31.6 2.9 %collective-permute-start.12 = (f32[8,128]{1,0:T(8,128)S(1)}, f32[8,128]{1,0:T(8,128)S(1)}, u32[]{:S(2)}, u32[]{:S(2)}) collective-permute-start(f32[8,128]{1,0:T(8,128)S(1)} %shard_map.95.refs_0_), channel_id=1, source_target_pairs={{0,1},{1,0},{2,3},{3,2},{4,5},{5,4},{6,7},{7,6},{8,9},{9,8},{10,11... | collective-permute-start | bytes 12296 | tf_op jit(solution)/shard_map/ppermute | solution.py:446
  35.0 5.9 %collective-permute-start.17 = (f32[72,128]{1,0:T(8,128)S(1)}, f32[72,128]{1,0:T(8,128)S(1)}, u32[]{:S(2)}, u32[]{:S(2)}) collective-permute-start(f32[72,128]{1,0:T(8,128)S(1)} %get-tuple-element.53.refs_0_.refs_8_), channel_id=1, source_target_pairs={{0,12},{4,8},{8,4},{12,0},{1,13},{5,9},{9,5},{13,1},{2,14},{6,10},... | collective-permute-start | bytes 110600 | tf_op jit(solution)/shard_map/ppermute | solution.py:446
  37.2 4.9 %collective-permute-start.16 = (f32[72,128]{1,0:T(8,128)S(1)}, f32[72,128]{1,0:T(8,128)S(1)}, u32[]{:S(2)}, u32[]{:S(2)}) collective-permute-start(f32[72,128]{1,0:T(8,128)S(1)} %get-tuple-element.53.refs_0_.refs_8_), channel_id=1, source_target_pairs={{0,8},{4,12},{8,0},{12,4},{1,9},{5,13},{9,1},{13,5},{2,10},{6,14},... | collective-permute-start | bytes 110600 | tf_op jit(solution)/shard_map/ppermute | solution.py:446
  37.9 4.5 %collective-permute-start.15 = (f32[72,128]{1,0:T(8,128)S(1)}, f32[72,128]{1,0:T(8,128)S(1)}, u32[]{:S(2)}, u32[]{:S(2)}) collective-permute-start(f32[72,128]{1,0:T(8,128)S(1)} %get-tuple-element.53.refs_0_.refs_8_), channel_id=1, source_target_pairs={{0,4},{4,0},{8,12},{12,8},{1,5},{5,1},{9,13},{13,9},{2,6},{6,2},{1... | collective-permute-start | bytes 110600 | tf_op jit(solution)/shard_map/ppermute | solution.py:446
  43.0 3.1 %collective-permute-start.20 = (f32[8,128]{1,0:T(8,128)S(1)}, f32[8,128]{1,0:T(8,128)S(1)}, u32[]{:S(2)}, u32[]{:S(2)}) collective-permute-start(f32[8,128]{1,0:T(8,128)S(1)} %shard_map.99.refs_0_), channel_id=1, source_target_pairs={{0,3},{1,2},{2,1},{3,0},{4,7},{5,6},{6,5},{7,4},{8,11},{9,10},{10,... | collective-permute-start | bytes 12296 | tf_op jit(solution)/shard_map/ppermute | solution.py:446
  43.1 3.7 %collective-permute-start.19 = (f32[8,128]{1,0:T(8,128)S(1)}, f32[8,128]{1,0:T(8,128)S(1)}, u32[]{:S(2)}, u32[]{:S(2)}) collective-permute-start(f32[8,128]{1,0:T(8,128)S(1)} %shard_map.99.refs_0_), channel_id=1, source_target_pairs={{0,2},{1,3},{2,0},{3,1},{4,6},{5,7},{6,4},{7,5},{8,10},{9,11},{10,... | collective-permute-start | bytes 12296 | tf_op jit(solution)/shard_map/ppermute | solution.py:446
  44.0 2.8 %collective-permute-start.18 = (f32[8,128]{1,0:T(8,128)S(1)}, f32[8,128]{1,0:T(8,128)S(1)}, u32[]{:S(2)}, u32[]{:S(2)}) collective-permute-start(f32[8,128]{1,0:T(8,128)S(1)} %shard_map.99.refs_0_), channel_id=1, source_target_pairs={{0,1},{1,0},{2,3},{3,2},{4,5},{5,4},{6,7},{7,6},{8,9},{9,8},{10,11... | collective-permute-start | bytes 12296 | tf_op jit(solution)/shard_map/ppermute | solution.py:446
  47.4 5.6 %collective-permute-start.21 = (f32[24,128]{1,0:T(8,128)S(1)}, f32[24,128]{1,0:T(8,128)S(1)}, u32[]{:S(2)}, u32[]{:S(2)}) collective-permute-start(f32[24,128]{1,0:T(8,128)S(1)} %get-tuple-element.65), channel_id=1, source_target_pairs={{0,12},{4,8},{8,4},{12,0},{1,13},{5,9},{9,5},{13,1},{2,14},{6,10},... | collective-permute-start | bytes 36872 | tf_op jit(solution)/shard_map/ppermute | solution.py:452
  49.5 4.6 %collective-permute-start.22 = (f32[24,128]{1,0:T(8,128)S(1)}, f32[24,128]{1,0:T(8,128)S(1)}, u32[]{:S(2)}, u32[]{:S(2)}) collective-permute-start(f32[24,128]{1,0:T(8,128)S(1)} %get-tuple-element.66), channel_id=1, source_target_pairs={{0,8},{4,12},{8,0},{12,4},{1,9},{5,13},{9,1},{13,5},{2,10},{6,14},... | collective-permute-start | bytes 36872 | tf_op jit(solution)/shard_map/ppermute | solution.py:452
  49.9 4.1 %collective-permute-start.23 = (f32[24,128]{1,0:T(8,128)S(1)}, f32[24,128]{1,0:T(8,128)S(1)}, u32[]{:S(2)}, u32[]{:S(2)}) collective-permute-start(f32[24,128]{1,0:T(8,128)S(1)} %get-tuple-element.67), channel_id=1, source_target_pairs={{0,4},{4,0},{8,12},{12,8},{1,5},{5,1},{9,13},{13,9},{2,6},{6,2},{1... | collective-permute-start | bytes 36872 | tf_op jit(solution)/shard_map/ppermute | solution.py:452

commit v7 on v6

--- a/solution.py
+++ b/solution.py
@@ -9,7 +9,7 @@
 
 ITERS = 3
 LAMBDA = 0.02
-ORDERS = ((1, 2, 3),) * ITERS + ((3, 2, 1),)
+ORDERS = ((1, 3, 2),) * ITERS + ((2, 3, 1),)
 FEAT_ORDER = (1, 2, 3)
 
 F32, BF16, I32 = jnp.float32, jnp.bfloat16, jnp.int32
@@ -446,11 +446,10 @@
     return [x] + [lax.ppermute(x, axis, [(i, i ^ k) for i in range(size)]) for k in order]
 
 
-def exchange_each(arrays, axis):
-    keys = (3, 2, 1)
+def exchange_each(arrays, axis, order):
+    to = dict(zip((3, 2, 1), arrays[1:], strict=True))
     return [arrays[0]] + [
-        lax.ppermute(x, axis, [(i, i ^ k) for i in range(4)])
-        for k, x in zip(keys, arrays[1:], strict=True)
+        lax.ppermute(to[k], axis, [(i, i ^ k) for i in range(4)]) for k in order
     ]
 
 
@@ -558,7 +557,7 @@
                 [f32(SHORT, LANES)] * 4,
                 scratch=[pltpu.VMEM((slots, LANES), F32)],
             )
-            history.append(exchange_each(to_each, "inst"))
+            history.append(exchange_each(to_each, "inst", ORDERS[ITERS]))
             nums.append(num)
             break
         msg, *kept = call(

time: 55.3 us -> 54.9 us (level)
  starting transfers between devices: 26.7 us -> 23.8 us
  waiting for transfers between devices: 18.4 us -> 20.9 us
    ppermute x21, starting transfers between devices: 22.2 us -> 20.2 us  [exchange(): lax.ppermute(x, axis, [(i, i ^ k) for i in range(size)])]
    ppermute x21, waiting for transfers between devices: 16.9 us -> 18.6 us  [exchange(): lax.ppermute(x, axis, [(i, i ^ k) for i in range(size)])]
    ppermute x3, starting transfers between devices: 4.45 us -> 3.55 us  [exchange_each(): lax.ppermute(to[k], axis, [(i, i ^ k) for i in range(4)])]
    ppermute x3, waiting for transfers between devices: 1.5 us -> 2.24 us  [exchange_each(): lax.ppermute(to[k], axis, [(i, i ^ k) for i in range(4)])]
where the time goes in v7:
time: 54.9 us; the launch traced here: 54.7 us
  starting transfers between devices  23.8 us (43%)
  waiting for transfers between devices  20.9 us (38%)
  Pallas kernels  8.37 us (15%)
  between operations  1.59 us (3%)
    ppermute x21, starting transfers between devices, exchange(): lax.ppermute(x, axis, [(i, i ^ k) for i in range(size)])  20.2 us
    ppermute x21, waiting for transfers between devices, exchange(): lax.ppermute(x, axis, [(i, i ^ k) for i in range(size)])  18.6 us
    pallas_call x16, Pallas kernels, call(): pl.pallas_call(kernel, in_specs=in_specs, out_shape=outs, out_specs=out_s...  8.37 us
    ppermute x3, starting transfers between devices, exchange_each(): lax.ppermute(to[k], axis, [(i, i ^ k) for i in range(4)])  3.55 us
    ppermute x3, waiting for transfers between devices, exchange_each(): lax.ppermute(to[k], axis, [(i, i ^ k) for i in range(4)])  2.24 us
  transfers between devices with their start and end apart: 24, of which 18 were waited for; matrix products, arithmetic and copies ran while one was open for 0% of the time, Pallas kernels for 3%

profile of v7, /device:TPU:0, one launch (start us, length us, event | category | flops | bytes accessed | tf_op | source)
XLA Modules:
  0.0 54.7 jit_solution(248892869804388442)
XLA Ops:
  1.4 1.0 %shard_map.86 = (f32[64,128]{1,0:T(8,128)S(1)}, s32[64,128]{1,0:T(8,128)S(1)}, s32[1,64]{1,0:T(1,128)S(4)}) custom-call(s32[1,64]{1,0:T(1,128)} %bitcast.23, s32[1,64]{1,0:T(1,128)} %bitcast.19), custom_call_target="tpu_custom_call" | custom-call | flops 1073741824 | bytes 1048576 | tf_op jit(solution)/shard_map/pallas_call | solution.py:30
  2.4 0.0 copy-start.3
  2.5 0.0 copy-start.4
  2.5 0.0 copy-start.2
  2.5 0.1 copy-done
  2.6 0.8 %shard_map.88 = (f32[16,128]{1,0:T(8,128)S(1)}, f32[512,128]{1,0:T(8,128)S(1)}) custom-call(s32[1,64]{1,0:T(1,128)S(4)} %get-tuple-element.40.cols, f32[64,128]{1,0:T(8,128)S(1)} %compare_select_fusion.rows, bf16[64,128,128]{2,1,0:T(8,128)(2,1)S(1)} %bitcast.10, f32[2048,128]{1,0:T(8,128)S(1)} %bitcast.16), custom_call_target="tpu_custom_call" | custom-call | flops 2097152 | bytes 1048576 | tf_op jit(solution)/shard_map/pallas_call | solution.py:30
  3.3 2.4 %collective-permute-start.2 = (f32[16,128]{1,0:T(8,128)S(1)}, f32[16,128]{1,0:T(8,128)S(1)}, u32[]{:S(2)}, u32[]{:S(2)}) collective-permute-start(f32[16,128]{1,0:T(8,128)S(1)} %get-tuple-element.41.refs_0_), channel_id=1, source_target_pairs={{0,3},{1,2},{2,1},{3,0},{4,7},{5,6},{6,5},{7,4},{8,11},{9,10},{10,... | collective-permute-start | bytes 24584 | tf_op jit(solution)/shard_map/ppermute | solution.py:446
  5.8 0.6 %collective-permute-start.1 = (f32[16,128]{1,0:T(8,128)S(1)}, f32[16,128]{1,0:T(8,128)S(1)}, u32[]{:S(2)}, u32[]{:S(2)}) collective-permute-start(f32[16,128]{1,0:T(8,128)S(1)} %get-tuple-element.41.refs_0_), channel_id=1, source_target_pairs={{0,2},{1,3},{2,0},{3,1},{4,6},{5,7},{6,4},{7,5},{8,10},{9,11},{10,... | collective-permute-start | bytes 24584 | tf_op jit(solution)/shard_map/ppermute | solution.py:446
  6.4 0.0 collective-permute-start
  6.5 0.2 shard_map.87
  6.7 0.5 collective-permute-done.2.refs_3_
  7.1 2.3 %collective-permute-done.1.refs_2_ = f32[16,128]{1,0:T(8,128)S(1)} collective-permute-done((f32[16,128]{1,0:T(8,128)S(1)}, f32[16,128]{1,0:T(8,128)S(1)}, u32[]{:S(2)}, u32[]{:S(2)}) %collective-permute-start.1) | collective-permute-done | bytes 8224 | tf_op jit(solution)/shard_map/ppermute | solution.py:446
  9.4 0.0 collective-permute-done.refs_1_
  9.4 0.4 shard_map.89
  9.9 2.6 %collective-permute-start.5 = (f32[72,128]{1,0:T(8,128)S(1)}, f32[72,128]{1,0:T(8,128)S(1)}, u32[]{:S(2)}, u32[]{:S(2)}) collective-permute-start(f32[72,128]{1,0:T(8,128)S(1)} %get-tuple-element.48.refs_0_), channel_id=1, source_target_pairs={{0,8},{4,12},{8,0},{12,4},{1,9},{5,13},{9,1},{13,5},{2,10},{6,14},... | collective-permute-start | bytes 110600 | tf_op jit(solution)/shard_map/ppermute | solution.py:446
  12.5 1.3 %collective-permute-start.4 = (f32[72,128]{1,0:T(8,128)S(1)}, f32[72,128]{1,0:T(8,128)S(1)}, u32[]{:S(2)}, u32[]{:S(2)}) collective-permute-start(f32[72,128]{1,0:T(8,128)S(1)} %get-tuple-element.48.refs_0_), channel_id=1, source_target_pairs={{0,12},{4,8},{8,4},{12,0},{1,13},{5,9},{9,5},{13,1},{2,14},{6,10},... | collective-permute-start | bytes 110600 | tf_op jit(solution)/shard_map/ppermute | solution.py:446
  13.9 0.2 collective-permute-start.3
  14.1 0.6 %shard_map.90.turned = bf16[64,128,128]{2,1,0:T(8,128)(2,1)S(1)} custom-call(bf16[64,128,128]{2,1,0:T(8,128)(2,1)S(1)} %bitcast.12), custom_call_target="tpu_custom_call" | custom-call | flops 2097152 | bytes 1048576 | tf_op jit(solution)/shard_map/pallas_call | solution.py:30
  14.7 0.1 collective-permute-done.5.refs_3_
  14.8 3.5 %collective-permute-done.4.refs_2_ = f32[72,128]{1,0:T(8,128)S(1)} collective-permute-done((f32[72,128]{1,0:T(8,128)S(1)}, f32[72,128]{1,0:T(8,128)S(1)}, u32[]{:S(2)}, u32[]{:S(2)}) %collective-permute-start.4) | collective-permute-done | bytes 36896 | tf_op jit(solution)/shard_map/ppermute | solution.py:446
  18.3 0.0 collective-permute-done.3.refs_1_
  18.3 0.6 %shard_map.92.refs_0_ = f32[8,128]{1,0:T(8,128)S(1)} custom-call(bf16[64,128,128]{2,1,0:T(8,128)(2,1)S(1)} %shard_map.90.turned, f32[512,128]{1,0:T(8,128)S(1)} %get-tuple-element.46.row_mask, bf16[64,256]{1,0:T(8,128)(2,1)S(1)} %shard_map.91.match, f32[72,128]{1,0:T(8,128)S(1)} %get-tuple-element.48.refs_0_, f32[72,128]{1,0:T(8,128)S(1)} %collective-permute-done.3.refs_1_, ...), custom_call_target="tpu_custom_call" | custom-call | flops 2097152 | bytes 1048576 | tf_op jit(solution)/shard_map/pallas_call | solution.py:30
  18.9 0.1 collective-permute-start.8
  19.0 0.7 %collective-permute-start.7 = (f32[8,128]{1,0:T(8,128)S(1)}, f32[8,128]{1,0:T(8,128)S(1)}, u32[]{:S(2)}, u32[]{:S(2)}) collective-permute-start(f32[8,128]{1,0:T(8,128)S(1)} %shard_map.92.refs_0_), channel_id=1, source_target_pairs={{0,2},{1,3},{2,0},{3,1},{4,6},{5,7},{6,4},{7,5},{8,10},{9,11},{10,... | collective-permute-start | bytes 12296 | tf_op jit(solution)/shard_map/ppermute | solution.py:446
  19.7 1.1 %collective-permute-start.6 = (f32[8,128]{1,0:T(8,128)S(1)}, f32[8,128]{1,0:T(8,128)S(1)}, u32[]{:S(2)}, u32[]{:S(2)}) collective-permute-start(f32[8,128]{1,0:T(8,128)S(1)} %shard_map.92.refs_0_), channel_id=1, source_target_pairs={{0,1},{1,0},{2,3},{3,2},{4,5},{5,4},{6,7},{7,6},{8,9},{9,8},{10,11... | collective-permute-start | bytes 12296 | tf_op jit(solution)/shard_map/ppermute | solution.py:446
  20.8 1.2 %collective-permute-done.8.refs_3_ = f32[8,128]{1,0:T(8,128)S(1)} collective-permute-done((f32[8,128]{1,0:T(8,128)S(1)}, f32[8,128]{1,0:T(8,128)S(1)}, u32[]{:S(2)}, u32[]{:S(2)}) %collective-permute-start.8) | collective-permute-done | bytes 4128 | tf_op jit(solution)/shard_map/ppermute | solution.py:446
  22.0 0.7 %collective-permute-done.7.refs_2_ = f32[8,128]{1,0:T(8,128)S(1)} collective-permute-done((f32[8,128]{1,0:T(8,128)S(1)}, f32[8,128]{1,0:T(8,128)S(1)}, u32[]{:S(2)}, u32[]{:S(2)}) %collective-permute-start.7) | collective-permute-done | bytes 4128 | tf_op jit(solution)/shard_map/ppermute | solution.py:446
  22.6 0.0 collective-permute-done.6.refs_1_
  22.6 0.4 shard_map.93
  23.1 1.3 %collective-permute-start.11 = (f32[72,128]{1,0:T(8,128)S(1)}, f32[72,128]{1,0:T(8,128)S(1)}, u32[]{:S(2)}, u32[]{:S(2)}) collective-permute-start(f32[72,128]{1,0:T(8,128)S(1)} %get-tuple-element.49.refs_0_.refs_4_), channel_id=1, source_target_pairs={{0,8},{4,12},{8,0},{12,4},{1,9},{5,13},{9,1},{13,5},{2,10},{6,14},... | collective-permute-start | bytes 110600 | tf_op jit(solution)/shard_map/ppermute | solution.py:446
  24.4 1.1 %collective-permute-start.10 = (f32[72,128]{1,0:T(8,128)S(1)}, f32[72,128]{1,0:T(8,128)S(1)}, u32[]{:S(2)}, u32[]{:S(2)}) collective-permute-start(f32[72,128]{1,0:T(8,128)S(1)} %get-tuple-element.49.refs_0_.refs_4_), channel_id=1, source_target_pairs={{0,12},{4,8},{8,4},{12,0},{1,13},{5,9},{9,5},{13,1},{2,14},{6,10},... | collective-permute-start | bytes 110600 | tf_op jit(solution)/shard_map/ppermute | solution.py:446
  25.4 1.2 %collective-permute-start.9 = (f32[72,128]{1,0:T(8,128)S(1)}, f32[72,128]{1,0:T(8,128)S(1)}, u32[]{:S(2)}, u32[]{:S(2)}) collective-permute-start(f32[72,128]{1,0:T(8,128)S(1)} %get-tuple-element.49.refs_0_.refs_4_), channel_id=1, source_target_pairs={{0,4},{4,0},{8,12},{12,8},{1,5},{5,1},{9,13},{13,9},{2,6},{6,2},{1... | collective-permute-start | bytes 110600 | tf_op jit(solution)/shard_map/ppermute | solution.py:446
  26.6 1.9 %collective-permute-done.11.refs_3_.refs_7_ = f32[72,128]{1,0:T(8,128)S(1)} collective-permute-done((f32[72,128]{1,0:T(8,128)S(1)}, f32[72,128]{1,0:T(8,128)S(1)}, u32[]{:S(2)}, u32[]{:S(2)}) %collective-permute-start.11) | collective-permute-done | bytes 36896 | tf_op jit(solution)/shard_map/ppermute | solution.py:446
  28.5 1.6 %collective-permute-done.10.refs_2_.refs_6_ = f32[72,128]{1,0:T(8,128)S(1)} collective-permute-done((f32[72,128]{1,0:T(8,128)S(1)}, f32[72,128]{1,0:T(8,128)S(1)}, u32[]{:S(2)}, u32[]{:S(2)}) %collective-permute-start.10) | collective-permute-done | bytes 36896 | tf_op jit(solution)/shard_map/ppermute | solution.py:446
  30.1 0.6 %shard_map.95.refs_0_ = f32[8,128]{1,0:T(8,128)S(1)} custom-call(bf16[64,128,128]{2,1,0:T(8,128)(2,1)S(1)} %shard_map.90.turned, f32[512,128]{1,0:T(8,128)S(1)} %get-tuple-element.46.row_mask, bf16[64,256]{1,0:T(8,128)(2,1)S(1)} %shard_map.91.match, f32[72,128]{1,0:T(8,128)S(1)} %get-tuple-element.49.refs_0_.refs_4_, ...), custom_call_target="tpu_custom_call" | custom-call | flops 2097152 | bytes 1048576 | tf_op jit(solution)/shard_map/pallas_call | solution.py:30
  30.7 0.1 collective-permute-start.14
  30.8 0.7 %collective-permute-start.13 = (f32[8,128]{1,0:T(8,128)S(1)}, f32[8,128]{1,0:T(8,128)S(1)}, u32[]{:S(2)}, u32[]{:S(2)}) collective-permute-start(f32[8,128]{1,0:T(8,128)S(1)} %shard_map.95.refs_0_), channel_id=1, source_target_pairs={{0,2},{1,3},{2,0},{3,1},{4,6},{5,7},{6,4},{7,5},{8,10},{9,11},{10,... | collective-permute-start | bytes 12296 | tf_op jit(solution)/shard_map/ppermute | solution.py:446
  31.5 1.1 %collective-permute-start.12 = (f32[8,128]{1,0:T(8,128)S(1)}, f32[8,128]{1,0:T(8,128)S(1)}, u32[]{:S(2)}, u32[]{:S(2)}) collective-permute-start(f32[8,128]{1,0:T(8,128)S(1)} %shard_map.95.refs_0_), channel_id=1, source_target_pairs={{0,1},{1,0},{2,3},{3,2},{4,5},{5,4},{6,7},{7,6},{8,9},{9,8},{10,11... | collective-permute-start | bytes 12296 | tf_op jit(solution)/shard_map/ppermute | solution.py:446
  32.6 0.1 shard_map.94
  32.8 1.0 %collective-permute-done.14.refs_3_ = f32[8,128]{1,0:T(8,128)S(1)} collective-permute-done((f32[8,128]{1,0:T(8,128)S(1)}, f32[8,128]{1,0:T(8,128)S(1)}, u32[]{:S(2)}, u32[]{:S(2)}) %collective-permute-start.14) | collective-permute-done | bytes 4128 | tf_op jit(solution)/shard_map/ppermute | solution.py:446
  33.8 0.7 %collective-permute-done.13.refs_2_ = f32[8,128]{1,0:T(8,128)S(1)} collective-permute-done((f32[8,128]{1,0:T(8,128)S(1)}, f32[8,128]{1,0:T(8,128)S(1)}, u32[]{:S(2)}, u32[]{:S(2)}) %collective-permute-start.13) | collective-permute-done | bytes 4128 | tf_op jit(solution)/shard_map/ppermute | solution.py:446
  34.5 0.4 shard_map.96
  34.9 1.1 %collective-permute-start.17 = (f32[72,128]{1,0:T(8,128)S(1)}, f32[72,128]{1,0:T(8,128)S(1)}, u32[]{:S(2)}, u32[]{:S(2)}) collective-permute-start(f32[72,128]{1,0:T(8,128)S(1)} %get-tuple-element.53.refs_0_.refs_8_), channel_id=1, source_target_pairs={{0,8},{4,12},{8,0},{12,4},{1,9},{5,13},{9,1},{13,5},{2,10},{6,14},... | collective-permute-start | bytes 110600 | tf_op jit(solution)/shard_map/ppermute | solution.py:446
  36.0 1.8 %collective-permute-start.16 = (f32[72,128]{1,0:T(8,128)S(1)}, f32[72,128]{1,0:T(8,128)S(1)}, u32[]{:S(2)}, u32[]{:S(2)}) collective-permute-start(f32[72,128]{1,0:T(8,128)S(1)} %get-tuple-element.53.refs_0_.refs_8_), channel_id=1, source_target_pairs={{0,12},{4,8},{8,4},{12,0},{1,13},{5,9},{9,5},{13,1},{2,14},{6,10},... | collective-permute-start | bytes 110600 | tf_op jit(solution)/shard_map/ppermute | solution.py:446
  37.8 0.7 %collective-permute-start.15 = (f32[72,128]{1,0:T(8,128)S(1)}, f32[72,128]{1,0:T(8,128)S(1)}, u32[]{:S(2)}, u32[]{:S(2)}) collective-permute-start(f32[72,128]{1,0:T(8,128)S(1)} %get-tuple-element.53.refs_0_.refs_8_), channel_id=1, source_target_pairs={{0,4},{4,0},{8,12},{12,8},{1,5},{5,1},{9,13},{13,9},{2,6},{6,2},{1... | collective-permute-start | bytes 110600 | tf_op jit(solution)/shard_map/ppermute | solution.py:446
  38.5 2.1 %collective-permute-done.17.refs_3_.refs_11_ = f32[72,128]{1,0:T(8,128)S(1)} collective-permute-done((f32[72,128]{1,0:T(8,128)S(1)}, f32[72,128]{1,0:T(8,128)S(1)}, u32[]{:S(2)}, u32[]{:S(2)}) %collective-permute-start.17) | collective-permute-done | bytes 36896 | tf_op jit(solution)/shard_map/ppermute | solution.py:446
  40.5 1.3 %collective-permute-done.16.refs_2_.refs_10_ = f32[72,128]{1,0:T(8,128)S(1)} collective-permute-done((f32[72,128]{1,0:T(8,128)S(1)}, f32[72,128]{1,0:T(8,128)S(1)}, u32[]{:S(2)}, u32[]{:S(2)}) %collective-permute-start.16) | collective-permute-done | bytes 36896 | tf_op jit(solution)/shard_map/ppermute | solution.py:446
  41.9 0.3 collective-permute-done.15.refs_1_.refs_9_
  42.1 0.6 %shard_map.99.refs_0_ = f32[8,128]{1,0:T(8,128)S(1)} custom-call(bf16[64,128,128]{2,1,0:T(8,128)(2,1)S(1)} %shard_map.90.turned, f32[512,128]{1,0:T(8,128)S(1)} %get-tuple-element.46.row_mask, bf16[64,256]{1,0:T(8,128)(2,1)S(1)} %shard_map.91.match, f32[72,128]{1,0:T(8,128)S(1)} %get-tuple-element.53.refs_0_.refs_8_, ...), custom_call_target="tpu_custom_call" | custom-call | flops 2097152 | bytes 1048576 | tf_op jit(solution)/shard_map/pallas_call | solution.py:30
  42.7 0.1 collective-permute-start.20
  42.8 0.7 %collective-permute-start.19 = (f32[8,128]{1,0:T(8,128)S(1)}, f32[8,128]{1,0:T(8,128)S(1)}, u32[]{:S(2)}, u32[]{:S(2)}) collective-permute-start(f32[8,128]{1,0:T(8,128)S(1)} %shard_map.99.refs_0_), channel_id=1, source_target_pairs={{0,2},{1,3},{2,0},{3,1},{4,6},{5,7},{6,4},{7,5},{8,10},{9,11},{10,... | collective-permute-start | bytes 12296 | tf_op jit(solution)/shard_map/ppermute | solution.py:446
  43.5 1.1 %collective-permute-start.18 = (f32[8,128]{1,0:T(8,128)S(1)}, f32[8,128]{1,0:T(8,128)S(1)}, u32[]{:S(2)}, u32[]{:S(2)}) collective-permute-start(f32[8,128]{1,0:T(8,128)S(1)} %shard_map.99.refs_0_), channel_id=1, source_target_pairs={{0,1},{1,0},{2,3},{3,2},{4,5},{5,4},{6,7},{7,6},{8,9},{9,8},{10,11... | collective-permute-start | bytes 12296 | tf_op jit(solution)/shard_map/ppermute | solution.py:446
  44.7 0.2 shard_map.97
  44.9 0.9 %collective-permute-done.20.refs_3_ = f32[8,128]{1,0:T(8,128)S(1)} collective-permute-done((f32[8,128]{1,0:T(8,128)S(1)}, f32[8,128]{1,0:T(8,128)S(1)}, u32[]{:S(2)}, u32[]{:S(2)}) %collective-permute-start.20) | collective-permute-done | bytes 4128 | tf_op jit(solution)/shard_map/ppermute | solution.py:446
  45.8 0.7 %collective-permute-done.19.refs_2_ = f32[8,128]{1,0:T(8,128)S(1)} collective-permute-done((f32[8,128]{1,0:T(8,128)S(1)}, f32[8,128]{1,0:T(8,128)S(1)}, u32[]{:S(2)}, u32[]{:S(2)}) %collective-permute-start.19) | collective-permute-done | bytes 4128 | tf_op jit(solution)/shard_map/ppermute | solution.py:446
  46.5 0.6 %shard_map.100 = (f32[24,128]{1,0:T(8,128)S(1)}, f32[24,128]{1,0:T(8,128)S(1)}, f32[24,128]{1,0:T(8,128)S(1)}, f32[24,128]{1,0:T(8,128)S(1)}) custom-call(bf16[64,128,128]{2,1,0:T(8,128)(2,1)S(1)} %bitcast.15, f32[64,128]{1,0:T(8,128)S(1)} %compare_select_fusion.rows, f32[8,128]{1,0:T(8,128)S(1)} %get-tuple-element.44.c, ...), custom_call_target="tpu_custom_call" | custom-call | flops 2097152 | bytes 1048576 | tf_op jit(solution)/shard_map/pallas_call | solution.py:30
  47.1 0.9 %collective-permute-start.21 = (f32[24,128]{1,0:T(8,128)S(1)}, f32[24,128]{1,0:T(8,128)S(1)}, u32[]{:S(2)}, u32[]{:S(2)}) collective-permute-start(f32[24,128]{1,0:T(8,128)S(1)} %get-tuple-element.65), channel_id=1, source_target_pairs={{0,8},{4,12},{8,0},{12,4},{1,9},{5,13},{9,1},{13,5},{2,10},{6,14},... | collective-permute-start | bytes 36872 | tf_op jit(solution)/shard_map/ppermute | solution.py:452
  48.0 1.8 %collective-permute-start.22 = (f32[24,128]{1,0:T(8,128)S(1)}, f32[24,128]{1,0:T(8,128)S(1)}, u32[]{:S(2)}, u32[]{:S(2)}) collective-permute-start(f32[24,128]{1,0:T(8,128)S(1)} %get-tuple-element.66), channel_id=1, source_target_pairs={{0,12},{4,8},{8,4},{12,0},{1,13},{5,9},{9,5},{13,1},{2,14},{6,10},... | collective-permute-start | bytes 36872 | tf_op jit(solution)/shard_map/ppermute | solution.py:452
  49.8 0.8 %collective-permute-start.23 = (f32[24,128]{1,0:T(8,128)S(1)}, f32[24,128]{1,0:T(8,128)S(1)}, u32[]{:S(2)}, u32[]{:S(2)}) collective-permute-start(f32[24,128]{1,0:T(8,128)S(1)} %get-tuple-element.67), channel_id=1, source_target_pairs={{0,4},{4,0},{8,12},{12,8},{1,5},{5,1},{9,13},{13,9},{2,6},{6,2},{1... | collective-permute-start | bytes 36872 | tf_op jit(solution)/shard_map/ppermute | solution.py:452
  50.7 0.7 %shard_map.98 = (f32[512,128]{1,0:T(8,128)S(1)}, f32[512,128]{1,0:T(8,128)S(1)}, f32[512,128]{1,0:T(8,128)S(1)}, f32[512,128]{1,0:T(8,128)S(1)}, bf16[512,128]{1,0:T(8,128)(2,1)S(1)}) custom-call(f32[2048,128]{1,0:T(8,128)S(1)} %bitcast.17, s32[1]{0:T(128)} %bitcast.4.index, f32[72,128]{1,0:T(8,128)S(1)} %get-tuple-element.48.refs_0_, ...), custom_call_target="tpu_custom_call" | custom-call | flops 2097152 | bytes 1048576 | tf_op jit(solution)/shard_map/pallas_call | solution.py:30
  51.4 0.5 collective-permute-done.21.refs_1_
  51.9 1.6 %collective-permute-done.22.refs_2_ = f32[24,128]{1,0:T(8,128)S(1)} collective-permute-done((f32[24,128]{1,0:T(8,128)S(1)}, f32[24,128]{1,0:T(8,128)S(1)}, u32[]{:S(2)}, u32[]{:S(2)}) %collective-permute-start.22) | collective-permute-done | bytes 12320 | tf_op jit(solution)/shard_map/ppermute | solution.py:452
  53.5 0.1 collective-permute-done.23.refs_3_
  53.6 1.1 %shard_map.101 = (f32[512,128]{1,0:T(8,128)}, f32[512,128]{1,0:T(8,128)}) custom-call(f32[8,128]{1,0:T(8,128)S(1)} %get-tuple-element.42.ww, f32[8,128]{1,0:T(8,128)S(1)} %get-tuple-element.56.refs_13_.num, f32[512,128]{1,0:T(8,128)S(1)} %get-tuple-element.57.res, f32[512,128]{1,0:T(8,128)S(1)} %get-tuple-element.58.direction, ...), custom_call_target="tpu_custom_call" | custom-call | flops 2097152 | bytes 1048576 | tf_op jit(solution)/shard_map/pallas_call | solution.py:30
  (11 shorter events, 0.0 us)
Async XLA Ops:
  0.6 1.9 %copy-start.1 = (f32[1,262144]{1,0:T(1,128)S(1)}, f32[1,262144]{1,0:T(1,128)}, u32[]{:S(2)}) copy-start(f32[1,262144]{1,0:T(1,128)} %param.13) | copy-start | bytes 3145732
  0.6 1.9 %copy-start = (bf16[1,1,64,128,128]{4,3,2,1,0:T(8,128)(2,1)S(1)}, bf16[1,1,64,128,128]{4,3,2,1,0:T(8,128)(2,1)}, u32[]{:S(2)}) copy-start(bf16[1,1,64,128,128]{4,3,2,1,0:T(8,128)(2,1)} %param.7) | copy-start | bytes 6291460
  2.4 4.0 %copy-start.3 = (s32[1,512]{1,0:T(1,128)S(1)}, s32[1,512]{1,0:T(1,128)}, u32[]{:S(2)}) copy-start(s32[1,512]{1,0:T(1,128)} %ids.1) | copy-start | bytes 6148
  2.5 4.0 %copy-start.4 = (s32[1,1,64]{2,1,0:T(1,128)S(1)}, s32[1,1,64]{2,1,0:T(1,128)}, u32[]{:S(2)}) copy-start(s32[1,1,64]{2,1,0:T(1,128)} %param.9) | copy-start | bytes 772
  2.5 7.0 %copy-start.2 = (s32[1,1024]{1,0:T(1,128)S(1)}, s32[1,1024]{1,0:T(1,128)}, u32[]{:S(2)}) copy-start(s32[1,1024]{1,0:T(1,128)} %param.12) | copy-start | bytes 12292
  3.3 3.8 %collective-permute-start.2 = (f32[16,128]{1,0:T(8,128)S(1)}, f32[16,128]{1,0:T(8,128)S(1)}, u32[]{:S(2)}, u32[]{:S(2)}) collective-permute-start(f32[16,128]{1,0:T(8,128)S(1)} %get-tuple-element.41.refs_0_), channel_id=1, source_target_pairs={{0,3},{1,2},{2,1},{3,0},{4,7},{5,6},{6,5},{7,4},{8,11},{9,10},{10,... | collective-permute-start | bytes 24584 | tf_op jit(solution)/shard_map/ppermute | solution.py:446
  5.8 3.7 %collective-permute-start.1 = (f32[16,128]{1,0:T(8,128)S(1)}, f32[16,128]{1,0:T(8,128)S(1)}, u32[]{:S(2)}, u32[]{:S(2)}) collective-permute-start(f32[16,128]{1,0:T(8,128)S(1)} %get-tuple-element.41.refs_0_), channel_id=1, source_target_pairs={{0,2},{1,3},{2,0},{3,1},{4,6},{5,7},{6,4},{7,5},{8,10},{9,11},{10,... | collective-permute-start | bytes 24584 | tf_op jit(solution)/shard_map/ppermute | solution.py:446
  6.4 3.0 %collective-permute-start = (f32[16,128]{1,0:T(8,128)S(1)}, f32[16,128]{1,0:T(8,128)S(1)}, u32[]{:S(2)}, u32[]{:S(2)}) collective-permute-start(f32[16,128]{1,0:T(8,128)S(1)} %get-tuple-element.41.refs_0_), channel_id=1, source_target_pairs={{0,1},{1,0},{2,3},{3,2},{4,5},{5,4},{6,7},{7,6},{8,9},{9,8},{10,11... | collective-permute-start | bytes 24584 | tf_op jit(solution)/shard_map/ppermute | solution.py:446
  9.9 4.9 %collective-permute-start.5 = (f32[72,128]{1,0:T(8,128)S(1)}, f32[72,128]{1,0:T(8,128)S(1)}, u32[]{:S(2)}, u32[]{:S(2)}) collective-permute-start(f32[72,128]{1,0:T(8,128)S(1)} %get-tuple-element.48.refs_0_), channel_id=1, source_target_pairs={{0,8},{4,12},{8,0},{12,4},{1,9},{5,13},{9,1},{13,5},{2,10},{6,14},... | collective-permute-start | bytes 110600 | tf_op jit(solution)/shard_map/ppermute | solution.py:446
  12.5 5.8 %collective-permute-start.4 = (f32[72,128]{1,0:T(8,128)S(1)}, f32[72,128]{1,0:T(8,128)S(1)}, u32[]{:S(2)}, u32[]{:S(2)}) collective-permute-start(f32[72,128]{1,0:T(8,128)S(1)} %get-tuple-element.48.refs_0_), channel_id=1, source_target_pairs={{0,12},{4,8},{8,4},{12,0},{1,13},{5,9},{9,5},{13,1},{2,14},{6,10},... | collective-permute-start | bytes 110600 | tf_op jit(solution)/shard_map/ppermute | solution.py:446
  13.9 4.4 %collective-permute-start.3 = (f32[72,128]{1,0:T(8,128)S(1)}, f32[72,128]{1,0:T(8,128)S(1)}, u32[]{:S(2)}, u32[]{:S(2)}) collective-permute-start(f32[72,128]{1,0:T(8,128)S(1)} %get-tuple-element.48.refs_0_), channel_id=1, source_target_pairs={{0,4},{4,0},{8,12},{12,8},{1,5},{5,1},{9,13},{13,9},{2,6},{6,2},{1... | collective-permute-start | bytes 110600 | tf_op jit(solution)/shard_map/ppermute | solution.py:446
  18.9 3.1 %collective-permute-start.8 = (f32[8,128]{1,0:T(8,128)S(1)}, f32[8,128]{1,0:T(8,128)S(1)}, u32[]{:S(2)}, u32[]{:S(2)}) collective-permute-start(f32[8,128]{1,0:T(8,128)S(1)} %shard_map.92.refs_0_), channel_id=1, source_target_pairs={{0,3},{1,2},{2,1},{3,0},{4,7},{5,6},{6,5},{7,4},{8,11},{9,10},{10,... | collective-permute-start | bytes 12296 | tf_op jit(solution)/shard_map/ppermute | solution.py:446
  19.0 3.7 %collective-permute-start.7 = (f32[8,128]{1,0:T(8,128)S(1)}, f32[8,128]{1,0:T(8,128)S(1)}, u32[]{:S(2)}, u32[]{:S(2)}) collective-permute-start(f32[8,128]{1,0:T(8,128)S(1)} %shard_map.92.refs_0_), channel_id=1, source_target_pairs={{0,2},{1,3},{2,0},{3,1},{4,6},{5,7},{6,4},{7,5},{8,10},{9,11},{10,... | collective-permute-start | bytes 12296 | tf_op jit(solution)/shard_map/ppermute | solution.py:446
  19.7 3.0 %collective-permute-start.6 = (f32[8,128]{1,0:T(8,128)S(1)}, f32[8,128]{1,0:T(8,128)S(1)}, u32[]{:S(2)}, u32[]{:S(2)}) collective-permute-start(f32[8,128]{1,0:T(8,128)S(1)} %shard_map.92.refs_0_), channel_id=1, source_target_pairs={{0,1},{1,0},{2,3},{3,2},{4,5},{5,4},{6,7},{7,6},{8,9},{9,8},{10,11... | collective-permute-start | bytes 12296 | tf_op jit(solution)/shard_map/ppermute | solution.py:446
  23.1 5.5 %collective-permute-start.11 = (f32[72,128]{1,0:T(8,128)S(1)}, f32[72,128]{1,0:T(8,128)S(1)}, u32[]{:S(2)}, u32[]{:S(2)}) collective-permute-start(f32[72,128]{1,0:T(8,128)S(1)} %get-tuple-element.49.refs_0_.refs_4_), channel_id=1, source_target_pairs={{0,8},{4,12},{8,0},{12,4},{1,9},{5,13},{9,1},{13,5},{2,10},{6,14},... | collective-permute-start | bytes 110600 | tf_op jit(solution)/shard_map/ppermute | solution.py:446
  24.4 5.8 %collective-permute-start.10 = (f32[72,128]{1,0:T(8,128)S(1)}, f32[72,128]{1,0:T(8,128)S(1)}, u32[]{:S(2)}, u32[]{:S(2)}) collective-permute-start(f32[72,128]{1,0:T(8,128)S(1)} %get-tuple-element.49.refs_0_.refs_4_), channel_id=1, source_target_pairs={{0,12},{4,8},{8,4},{12,0},{1,13},{5,9},{9,5},{13,1},{2,14},{6,10},... | collective-permute-start | bytes 110600 | tf_op jit(solution)/shard_map/ppermute | solution.py:446
  25.4 4.7 %collective-permute-start.9 = (f32[72,128]{1,0:T(8,128)S(1)}, f32[72,128]{1,0:T(8,128)S(1)}, u32[]{:S(2)}, u32[]{:S(2)}) collective-permute-start(f32[72,128]{1,0:T(8,128)S(1)} %get-tuple-element.49.refs_0_.refs_4_), channel_id=1, source_target_pairs={{0,4},{4,0},{8,12},{12,8},{1,5},{5,1},{9,13},{13,9},{2,6},{6,2},{1... | collective-permute-start | bytes 110600 | tf_op jit(solution)/shard_map/ppermute | solution.py:446
  30.7 3.1 %collective-permute-start.14 = (f32[8,128]{1,0:T(8,128)S(1)}, f32[8,128]{1,0:T(8,128)S(1)}, u32[]{:S(2)}, u32[]{:S(2)}) collective-permute-start(f32[8,128]{1,0:T(8,128)S(1)} %shard_map.95.refs_0_), channel_id=1, source_target_pairs={{0,3},{1,2},{2,1},{3,0},{4,7},{5,6},{6,5},{7,4},{8,11},{9,10},{10,... | collective-permute-start | bytes 12296 | tf_op jit(solution)/shard_map/ppermute | solution.py:446
  30.8 3.7 %collective-permute-start.13 = (f32[8,128]{1,0:T(8,128)S(1)}, f32[8,128]{1,0:T(8,128)S(1)}, u32[]{:S(2)}, u32[]{:S(2)}) collective-permute-start(f32[8,128]{1,0:T(8,128)S(1)} %shard_map.95.refs_0_), channel_id=1, source_target_pairs={{0,2},{1,3},{2,0},{3,1},{4,6},{5,7},{6,4},{7,5},{8,10},{9,11},{10,... | collective-permute-start | bytes 12296 | tf_op jit(solution)/shard_map/ppermute | solution.py:446
  31.5 3.0 %collective-permute-start.12 = (f32[8,128]{1,0:T(8,128)S(1)}, f32[8,128]{1,0:T(8,128)S(1)}, u32[]{:S(2)}, u32[]{:S(2)}) collective-permute-start(f32[8,128]{1,0:T(8,128)S(1)} %shard_map.95.refs_0_), channel_id=1, source_target_pairs={{0,1},{1,0},{2,3},{3,2},{4,5},{5,4},{6,7},{7,6},{8,9},{9,8},{10,11... | collective-permute-start | bytes 12296 | tf_op jit(solution)/shard_map/ppermute | solution.py:446
  34.9 5.6 %collective-permute-start.17 = (f32[72,128]{1,0:T(8,128)S(1)}, f32[72,128]{1,0:T(8,128)S(1)}, u32[]{:S(2)}, u32[]{:S(2)}) collective-permute-start(f32[72,128]{1,0:T(8,128)S(1)} %get-tuple-element.53.refs_0_.refs_8_), channel_id=1, source_target_pairs={{0,8},{4,12},{8,0},{12,4},{1,9},{5,13},{9,1},{13,5},{2,10},{6,14},... | collective-permute-start | bytes 110600 | tf_op jit(solution)/shard_map/ppermute | solution.py:446
  36.0 5.9 %collective-permute-start.16 = (f32[72,128]{1,0:T(8,128)S(1)}, f32[72,128]{1,0:T(8,128)S(1)}, u32[]{:S(2)}, u32[]{:S(2)}) collective-permute-start(f32[72,128]{1,0:T(8,128)S(1)} %get-tuple-element.53.refs_0_.refs_8_), channel_id=1, source_target_pairs={{0,12},{4,8},{8,4},{12,0},{1,13},{5,9},{9,5},{13,1},{2,14},{6,10},... | collective-permute-start | bytes 110600 | tf_op jit(solution)/shard_map/ppermute | solution.py:446
  37.8 4.4 %collective-permute-start.15 = (f32[72,128]{1,0:T(8,128)S(1)}, f32[72,128]{1,0:T(8,128)S(1)}, u32[]{:S(2)}, u32[]{:S(2)}) collective-permute-start(f32[72,128]{1,0:T(8,128)S(1)} %get-tuple-element.53.refs_0_.refs_8_), channel_id=1, source_target_pairs={{0,4},{4,0},{8,12},{12,8},{1,5},{5,1},{9,13},{13,9},{2,6},{6,2},{1... | collective-permute-start | bytes 110600 | tf_op jit(solution)/shard_map/ppermute | solution.py:446
  42.7 3.1 %collective-permute-start.20 = (f32[8,128]{1,0:T(8,128)S(1)}, f32[8,128]{1,0:T(8,128)S(1)}, u32[]{:S(2)}, u32[]{:S(2)}) collective-permute-start(f32[8,128]{1,0:T(8,128)S(1)} %shard_map.99.refs_0_), channel_id=1, source_target_pairs={{0,3},{1,2},{2,1},{3,0},{4,7},{5,6},{6,5},{7,4},{8,11},{9,10},{10,... | collective-permute-start | bytes 12296 | tf_op jit(solution)/shard_map/ppermute | solution.py:446
  42.8 3.7 %collective-permute-start.19 = (f32[8,128]{1,0:T(8,128)S(1)}, f32[8,128]{1,0:T(8,128)S(1)}, u32[]{:S(2)}, u32[]{:S(2)}) collective-permute-start(f32[8,128]{1,0:T(8,128)S(1)} %shard_map.99.refs_0_), channel_id=1, source_target_pairs={{0,2},{1,3},{2,0},{3,1},{4,6},{5,7},{6,4},{7,5},{8,10},{9,11},{10,... | collective-permute-start | bytes 12296 | tf_op jit(solution)/shard_map/ppermute | solution.py:446
  43.5 3.0 %collective-permute-start.18 = (f32[8,128]{1,0:T(8,128)S(1)}, f32[8,128]{1,0:T(8,128)S(1)}, u32[]{:S(2)}, u32[]{:S(2)}) collective-permute-start(f32[8,128]{1,0:T(8,128)S(1)} %shard_map.99.refs_0_), channel_id=1, source_target_pairs={{0,1},{1,0},{2,3},{3,2},{4,5},{5,4},{6,7},{7,6},{8,9},{9,8},{10,11... | collective-permute-start | bytes 12296 | tf_op jit(solution)/shard_map/ppermute | solution.py:446
  47.1 4.8 %collective-permute-start.21 = (f32[24,128]{1,0:T(8,128)S(1)}, f32[24,128]{1,0:T(8,128)S(1)}, u32[]{:S(2)}, u32[]{:S(2)}) collective-permute-start(f32[24,128]{1,0:T(8,128)S(1)} %get-tuple-element.65), channel_id=1, source_target_pairs={{0,8},{4,12},{8,0},{12,4},{1,9},{5,13},{9,1},{13,5},{2,10},{6,14},... | collective-permute-start | bytes 36872 | tf_op jit(solution)/shard_map/ppermute | solution.py:452
  48.0 5.5 %collective-permute-start.22 = (f32[24,128]{1,0:T(8,128)S(1)}, f32[24,128]{1,0:T(8,128)S(1)}, u32[]{:S(2)}, u32[]{:S(2)}) collective-permute-start(f32[24,128]{1,0:T(8,128)S(1)} %get-tuple-element.66), channel_id=1, source_target_pairs={{0,12},{4,8},{8,4},{12,0},{1,13},{5,9},{9,5},{13,1},{2,14},{6,10},... | collective-permute-start | bytes 36872 | tf_op jit(solution)/shard_map/ppermute | solution.py:452
  49.8 3.8 %collective-permute-start.23 = (f32[24,128]{1,0:T(8,128)S(1)}, f32[24,128]{1,0:T(8,128)S(1)}, u32[]{:S(2)}, u32[]{:S(2)}) collective-permute-start(f32[24,128]{1,0:T(8,128)S(1)} %get-tuple-element.67), channel_id=1, source_target_pairs={{0,4},{4,0},{8,12},{12,8},{1,5},{5,1},{9,13},{13,9},{2,6},{6,2},{1... | collective-permute-start | bytes 36872 | tf_op jit(solution)/shard_map/ppermute | solution.py:452

commit v8 on v7

--- a/solution.py
+++ b/solution.py
@@ -54,7 +54,7 @@
     hi = x.astype(BF16).astype(F32)
     rest = x - hi
     mid = rest.astype(BF16).astype(F32)
-    return hi, mid, (rest - mid).astype(BF16).astype(F32)
+    return hi, mid, rest - mid
 
 
 def exact_pick(pick, values):
@@ -200,9 +200,8 @@
     for out in send_out:
         run, rank = ranks(line, own, 1)
         row = iota((SHORT, LANES), 0)
-        for j, k in enumerate((0, 3, 2, 1)):
-            sent = (row == rank) & (run == (index[0] ^ k))
-            out[j * SHORT : (j + 1) * SHORT, :] = sent.astype(F32)[:, :slots].astype(BF16)
+        sent = [((row == rank) & (run == (index[0] ^ k))).astype(F32) for k in (0, 3, 2, 1)]
+        out[...] = jnp.concatenate(sent, axis=0)[:, :slots].astype(BF16)
 
 
 def feat_sum(refs, first=0):

time: 54.9 us -> 54.9 us (level)
  no operation moved by 1% of the time
where the time goes in v8:
time: 54.9 us; the launch traced here: 54.7 us
  starting transfers between devices  23.8 us (43%)
  waiting for transfers between devices  20.9 us (38%)
  Pallas kernels  8.37 us (15%)
  between operations  1.59 us (3%)
    ppermute x21, starting transfers between devices, exchange(): lax.ppermute(x, axis, [(i, i ^ k) for i in range(size)])  20.2 us
    ppermute x21, waiting for transfers between devices, exchange(): lax.ppermute(x, axis, [(i, i ^ k) for i in range(size)])  18.6 us
    pallas_call x16, Pallas kernels, call(): pl.pallas_call(kernel, in_specs=in_specs, out_shape=outs, out_specs=out_s...  8.37 us
    ppermute x3, starting transfers between devices, exchange_each(): lax.ppermute(to[k], axis, [(i, i ^ k) for i in range(4)])  3.55 us
    ppermute x3, waiting for transfers between devices, exchange_each(): lax.ppermute(to[k], axis, [(i, i ^ k) for i in range(4)])  2.24 us
  transfers between devices with their start and end apart: 24, of which 18 were waited for; matrix products, arithmetic and copies ran while one was open for 0% of the time, Pallas kernels for 3%

profile of v8, /device:TPU:0, one launch (start us, length us, event | category | flops | bytes accessed | tf_op | source)
XLA Modules:
  0.0 54.7 jit_solution(6404097369304783609)
XLA Ops:
  1.4 1.0 %shard_map.86 = (f32[64,128]{1,0:T(8,128)S(1)}, s32[64,128]{1,0:T(8,128)S(1)}, s32[1,64]{1,0:T(1,128)S(4)}) custom-call(s32[1,64]{1,0:T(1,128)} %bitcast.23, s32[1,64]{1,0:T(1,128)} %bitcast.19), custom_call_target="tpu_custom_call" | custom-call | flops 1073741824 | bytes 1048576 | tf_op jit(solution)/shard_map/pallas_call | solution.py:30
  2.4 0.0 copy-start.3
  2.5 0.0 copy-start.4
  2.5 0.0 copy-start.2
  2.5 0.1 copy-done
  2.6 0.8 %shard_map.88 = (f32[16,128]{1,0:T(8,128)S(1)}, f32[512,128]{1,0:T(8,128)S(1)}) custom-call(s32[1,64]{1,0:T(1,128)S(4)} %get-tuple-element.40.cols, f32[64,128]{1,0:T(8,128)S(1)} %compare_select_fusion.rows, bf16[64,128,128]{2,1,0:T(8,128)(2,1)S(1)} %bitcast.10, f32[2048,128]{1,0:T(8,128)S(1)} %bitcast.16), custom_call_target="tpu_custom_call" | custom-call | flops 2097152 | bytes 1048576 | tf_op jit(solution)/shard_map/pallas_call | solution.py:30
  3.3 2.4 %collective-permute-start.2 = (f32[16,128]{1,0:T(8,128)S(1)}, f32[16,128]{1,0:T(8,128)S(1)}, u32[]{:S(2)}, u32[]{:S(2)}) collective-permute-start(f32[16,128]{1,0:T(8,128)S(1)} %get-tuple-element.41.refs_0_), channel_id=1, source_target_pairs={{0,3},{1,2},{2,1},{3,0},{4,7},{5,6},{6,5},{7,4},{8,11},{9,10},{10,... | collective-permute-start | bytes 24584 | tf_op jit(solution)/shard_map/ppermute | solution.py:445
  5.8 0.6 %collective-permute-start.1 = (f32[16,128]{1,0:T(8,128)S(1)}, f32[16,128]{1,0:T(8,128)S(1)}, u32[]{:S(2)}, u32[]{:S(2)}) collective-permute-start(f32[16,128]{1,0:T(8,128)S(1)} %get-tuple-element.41.refs_0_), channel_id=1, source_target_pairs={{0,2},{1,3},{2,0},{3,1},{4,6},{5,7},{6,4},{7,5},{8,10},{9,11},{10,... | collective-permute-start | bytes 24584 | tf_op jit(solution)/shard_map/ppermute | solution.py:445
  6.4 0.0 collective-permute-start
  6.5 0.2 shard_map.87
  6.7 0.5 collective-permute-done.2.refs_3_
  7.1 2.3 %collective-permute-done.1.refs_2_ = f32[16,128]{1,0:T(8,128)S(1)} collective-permute-done((f32[16,128]{1,0:T(8,128)S(1)}, f32[16,128]{1,0:T(8,128)S(1)}, u32[]{:S(2)}, u32[]{:S(2)}) %collective-permute-start.1) | collective-permute-done | bytes 8224 | tf_op jit(solution)/shard_map/ppermute | solution.py:445
  9.4 0.0 collective-permute-done.refs_1_
  9.4 0.4 shard_map.89
  9.8 2.7 %collective-permute-start.5 = (f32[72,128]{1,0:T(8,128)S(1)}, f32[72,128]{1,0:T(8,128)S(1)}, u32[]{:S(2)}, u32[]{:S(2)}) collective-permute-start(f32[72,128]{1,0:T(8,128)S(1)} %get-tuple-element.48.refs_0_), channel_id=1, source_target_pairs={{0,8},{4,12},{8,0},{12,4},{1,9},{5,13},{9,1},{13,5},{2,10},{6,14},... | collective-permute-start | bytes 110600 | tf_op jit(solution)/shard_map/ppermute | solution.py:445
  12.5 1.3 %collective-permute-start.4 = (f32[72,128]{1,0:T(8,128)S(1)}, f32[72,128]{1,0:T(8,128)S(1)}, u32[]{:S(2)}, u32[]{:S(2)}) collective-permute-start(f32[72,128]{1,0:T(8,128)S(1)} %get-tuple-element.48.refs_0_), channel_id=1, source_target_pairs={{0,12},{4,8},{8,4},{12,0},{1,13},{5,9},{9,5},{13,1},{2,14},{6,10},... | collective-permute-start | bytes 110600 | tf_op jit(solution)/shard_map/ppermute | solution.py:445
  13.9 0.2 collective-permute-start.3
  14.1 0.6 %shard_map.90.turned = bf16[64,128,128]{2,1,0:T(8,128)(2,1)S(1)} custom-call(bf16[64,128,128]{2,1,0:T(8,128)(2,1)S(1)} %bitcast.12), custom_call_target="tpu_custom_call" | custom-call | flops 2097152 | bytes 1048576 | tf_op jit(solution)/shard_map/pallas_call | solution.py:30
  14.7 0.1 collective-permute-done.5.refs_3_
  14.8 3.5 %collective-permute-done.4.refs_2_ = f32[72,128]{1,0:T(8,128)S(1)} collective-permute-done((f32[72,128]{1,0:T(8,128)S(1)}, f32[72,128]{1,0:T(8,128)S(1)}, u32[]{:S(2)}, u32[]{:S(2)}) %collective-permute-start.4) | collective-permute-done | bytes 36896 | tf_op jit(solution)/shard_map/ppermute | solution.py:445
  18.3 0.0 collective-permute-done.3.refs_1_
  18.3 0.6 %shard_map.92.refs_0_ = f32[8,128]{1,0:T(8,128)S(1)} custom-call(bf16[64,128,128]{2,1,0:T(8,128)(2,1)S(1)} %shard_map.90.turned, f32[512,128]{1,0:T(8,128)S(1)} %get-tuple-element.46.row_mask, bf16[64,256]{1,0:T(8,128)(2,1)S(1)} %shard_map.91.match, f32[72,128]{1,0:T(8,128)S(1)} %get-tuple-element.48.refs_0_, f32[72,128]{1,0:T(8,128)S(1)} %collective-permute-done.3.refs_1_, ...), custom_call_target="tpu_custom_call" | custom-call | flops 2097152 | bytes 1048576 | tf_op jit(solution)/shard_map/pallas_call | solution.py:30
  18.9 0.1 collective-permute-start.8
  19.0 0.7 %collective-permute-start.7 = (f32[8,128]{1,0:T(8,128)S(1)}, f32[8,128]{1,0:T(8,128)S(1)}, u32[]{:S(2)}, u32[]{:S(2)}) collective-permute-start(f32[8,128]{1,0:T(8,128)S(1)} %shard_map.92.refs_0_), channel_id=1, source_target_pairs={{0,2},{1,3},{2,0},{3,1},{4,6},{5,7},{6,4},{7,5},{8,10},{9,11},{10,... | collective-permute-start | bytes 12296 | tf_op jit(solution)/shard_map/ppermute | solution.py:445
  19.7 1.1 %collective-permute-start.6 = (f32[8,128]{1,0:T(8,128)S(1)}, f32[8,128]{1,0:T(8,128)S(1)}, u32[]{:S(2)}, u32[]{:S(2)}) collective-permute-start(f32[8,128]{1,0:T(8,128)S(1)} %shard_map.92.refs_0_), channel_id=1, source_target_pairs={{0,1},{1,0},{2,3},{3,2},{4,5},{5,4},{6,7},{7,6},{8,9},{9,8},{10,11... | collective-permute-start | bytes 12296 | tf_op jit(solution)/shard_map/ppermute | solution.py:445
  20.8 1.2 %collective-permute-done.8.refs_3_ = f32[8,128]{1,0:T(8,128)S(1)} collective-permute-done((f32[8,128]{1,0:T(8,128)S(1)}, f32[8,128]{1,0:T(8,128)S(1)}, u32[]{:S(2)}, u32[]{:S(2)}) %collective-permute-start.8) | collective-permute-done | bytes 4128 | tf_op jit(solution)/shard_map/ppermute | solution.py:445
  22.0 0.7 %collective-permute-done.7.refs_2_ = f32[8,128]{1,0:T(8,128)S(1)} collective-permute-done((f32[8,128]{1,0:T(8,128)S(1)}, f32[8,128]{1,0:T(8,128)S(1)}, u32[]{:S(2)}, u32[]{:S(2)}) %collective-permute-start.7) | collective-permute-done | bytes 4128 | tf_op jit(solution)/shard_map/ppermute | solution.py:445
  22.6 0.4 shard_map.93
  23.1 1.3 %collective-permute-start.11 = (f32[72,128]{1,0:T(8,128)S(1)}, f32[72,128]{1,0:T(8,128)S(1)}, u32[]{:S(2)}, u32[]{:S(2)}) collective-permute-start(f32[72,128]{1,0:T(8,128)S(1)} %get-tuple-element.49.refs_0_.refs_4_), channel_id=1, source_target_pairs={{0,8},{4,12},{8,0},{12,4},{1,9},{5,13},{9,1},{13,5},{2,10},{6,14},... | collective-permute-start | bytes 110600 | tf_op jit(solution)/shard_map/ppermute | solution.py:445
  24.4 1.1 %collective-permute-start.10 = (f32[72,128]{1,0:T(8,128)S(1)}, f32[72,128]{1,0:T(8,128)S(1)}, u32[]{:S(2)}, u32[]{:S(2)}) collective-permute-start(f32[72,128]{1,0:T(8,128)S(1)} %get-tuple-element.49.refs_0_.refs_4_), channel_id=1, source_target_pairs={{0,12},{4,8},{8,4},{12,0},{1,13},{5,9},{9,5},{13,1},{2,14},{6,10},... | collective-permute-start | bytes 110600 | tf_op jit(solution)/shard_map/ppermute | solution.py:445
  25.4 1.2 %collective-permute-start.9 = (f32[72,128]{1,0:T(8,128)S(1)}, f32[72,128]{1,0:T(8,128)S(1)}, u32[]{:S(2)}, u32[]{:S(2)}) collective-permute-start(f32[72,128]{1,0:T(8,128)S(1)} %get-tuple-element.49.refs_0_.refs_4_), channel_id=1, source_target_pairs={{0,4},{4,0},{8,12},{12,8},{1,5},{5,1},{9,13},{13,9},{2,6},{6,2},{1... | collective-permute-start | bytes 110600 | tf_op jit(solution)/shard_map/ppermute | solution.py:445
  26.6 1.9 %collective-permute-done.11.refs_3_.refs_7_ = f32[72,128]{1,0:T(8,128)S(1)} collective-permute-done((f32[72,128]{1,0:T(8,128)S(1)}, f32[72,128]{1,0:T(8,128)S(1)}, u32[]{:S(2)}, u32[]{:S(2)}) %collective-permute-start.11) | collective-permute-done | bytes 36896 | tf_op jit(solution)/shard_map/ppermute | solution.py:445
  28.5 1.6 %collective-permute-done.10.refs_2_.refs_6_ = f32[72,128]{1,0:T(8,128)S(1)} collective-permute-done((f32[72,128]{1,0:T(8,128)S(1)}, f32[72,128]{1,0:T(8,128)S(1)}, u32[]{:S(2)}, u32[]{:S(2)}) %collective-permute-start.10) | collective-permute-done | bytes 36896 | tf_op jit(solution)/shard_map/ppermute | solution.py:445
  30.1 0.6 %shard_map.95.refs_0_ = f32[8,128]{1,0:T(8,128)S(1)} custom-call(bf16[64,128,128]{2,1,0:T(8,128)(2,1)S(1)} %shard_map.90.turned, f32[512,128]{1,0:T(8,128)S(1)} %get-tuple-element.46.row_mask, bf16[64,256]{1,0:T(8,128)(2,1)S(1)} %shard_map.91.match, f32[72,128]{1,0:T(8,128)S(1)} %get-tuple-element.49.refs_0_.refs_4_, ...), custom_call_target="tpu_custom_call" | custom-call | flops 2097152 | bytes 1048576 | tf_op jit(solution)/shard_map/pallas_call | solution.py:30
  30.7 0.1 collective-permute-start.14
  30.8 0.7 %collective-permute-start.13 = (f32[8,128]{1,0:T(8,128)S(1)}, f32[8,128]{1,0:T(8,128)S(1)}, u32[]{:S(2)}, u32[]{:S(2)}) collective-permute-start(f32[8,128]{1,0:T(8,128)S(1)} %shard_map.95.refs_0_), channel_id=1, source_target_pairs={{0,2},{1,3},{2,0},{3,1},{4,6},{5,7},{6,4},{7,5},{8,10},{9,11},{10,... | collective-permute-start | bytes 12296 | tf_op jit(solution)/shard_map/ppermute | solution.py:445
  31.5 1.1 %collective-permute-start.12 = (f32[8,128]{1,0:T(8,128)S(1)}, f32[8,128]{1,0:T(8,128)S(1)}, u32[]{:S(2)}, u32[]{:S(2)}) collective-permute-start(f32[8,128]{1,0:T(8,128)S(1)} %shard_map.95.refs_0_), channel_id=1, source_target_pairs={{0,1},{1,0},{2,3},{3,2},{4,5},{5,4},{6,7},{7,6},{8,9},{9,8},{10,11... | collective-permute-start | bytes 12296 | tf_op jit(solution)/shard_map/ppermute | solution.py:445
  32.6 0.1 shard_map.94
  32.8 1.0 %collective-permute-done.14.refs_3_ = f32[8,128]{1,0:T(8,128)S(1)} collective-permute-done((f32[8,128]{1,0:T(8,128)S(1)}, f32[8,128]{1,0:T(8,128)S(1)}, u32[]{:S(2)}, u32[]{:S(2)}) %collective-permute-start.14) | collective-permute-done | bytes 4128 | tf_op jit(solution)/shard_map/ppermute | solution.py:445
  33.8 0.7 %collective-permute-done.13.refs_2_ = f32[8,128]{1,0:T(8,128)S(1)} collective-permute-done((f32[8,128]{1,0:T(8,128)S(1)}, f32[8,128]{1,0:T(8,128)S(1)}, u32[]{:S(2)}, u32[]{:S(2)}) %collective-permute-start.13) | collective-permute-done | bytes 4128 | tf_op jit(solution)/shard_map/ppermute | solution.py:445
  34.5 0.0 collective-permute-done.12.refs_1_
  34.5 0.4 shard_map.96
  34.9 1.1 %collective-permute-start.17 = (f32[72,128]{1,0:T(8,128)S(1)}, f32[72,128]{1,0:T(8,128)S(1)}, u32[]{:S(2)}, u32[]{:S(2)}) collective-permute-start(f32[72,128]{1,0:T(8,128)S(1)} %get-tuple-element.53.refs_0_.refs_8_), channel_id=1, source_target_pairs={{0,8},{4,12},{8,0},{12,4},{1,9},{5,13},{9,1},{13,5},{2,10},{6,14},... | collective-permute-start | bytes 110600 | tf_op jit(solution)/shard_map/ppermute | solution.py:445
  36.0 1.8 %collective-permute-start.16 = (f32[72,128]{1,0:T(8,128)S(1)}, f32[72,128]{1,0:T(8,128)S(1)}, u32[]{:S(2)}, u32[]{:S(2)}) collective-permute-start(f32[72,128]{1,0:T(8,128)S(1)} %get-tuple-element.53.refs_0_.refs_8_), channel_id=1, source_target_pairs={{0,12},{4,8},{8,4},{12,0},{1,13},{5,9},{9,5},{13,1},{2,14},{6,10},... | collective-permute-start | bytes 110600 | tf_op jit(solution)/shard_map/ppermute | solution.py:445
  37.8 0.7 %collective-permute-start.15 = (f32[72,128]{1,0:T(8,128)S(1)}, f32[72,128]{1,0:T(8,128)S(1)}, u32[]{:S(2)}, u32[]{:S(2)}) collective-permute-start(f32[72,128]{1,0:T(8,128)S(1)} %get-tuple-element.53.refs_0_.refs_8_), channel_id=1, source_target_pairs={{0,4},{4,0},{8,12},{12,8},{1,5},{5,1},{9,13},{13,9},{2,6},{6,2},{1... | collective-permute-start | bytes 110600 | tf_op jit(solution)/shard_map/ppermute | solution.py:445
  38.5 2.1 %collective-permute-done.17.refs_3_.refs_11_ = f32[72,128]{1,0:T(8,128)S(1)} collective-permute-done((f32[72,128]{1,0:T(8,128)S(1)}, f32[72,128]{1,0:T(8,128)S(1)}, u32[]{:S(2)}, u32[]{:S(2)}) %collective-permute-start.17) | collective-permute-done | bytes 36896 | tf_op jit(solution)/shard_map/ppermute | solution.py:445
  40.5 1.3 %collective-permute-done.16.refs_2_.refs_10_ = f32[72,128]{1,0:T(8,128)S(1)} collective-permute-done((f32[72,128]{1,0:T(8,128)S(1)}, f32[72,128]{1,0:T(8,128)S(1)}, u32[]{:S(2)}, u32[]{:S(2)}) %collective-permute-start.16) | collective-permute-done | bytes 36896 | tf_op jit(solution)/shard_map/ppermute | solution.py:445
  41.9 0.3 collective-permute-done.15.refs_1_.refs_9_
  42.1 0.6 %shard_map.99.refs_0_ = f32[8,128]{1,0:T(8,128)S(1)} custom-call(bf16[64,128,128]{2,1,0:T(8,128)(2,1)S(1)} %shard_map.90.turned, f32[512,128]{1,0:T(8,128)S(1)} %get-tuple-element.46.row_mask, bf16[64,256]{1,0:T(8,128)(2,1)S(1)} %shard_map.91.match, f32[72,128]{1,0:T(8,128)S(1)} %get-tuple-element.53.refs_0_.refs_8_, ...), custom_call_target="tpu_custom_call" | custom-call | flops 2097152 | bytes 1048576 | tf_op jit(solution)/shard_map/pallas_call | solution.py:30
  42.7 0.1 collective-permute-start.20
  42.8 0.7 %collective-permute-start.19 = (f32[8,128]{1,0:T(8,128)S(1)}, f32[8,128]{1,0:T(8,128)S(1)}, u32[]{:S(2)}, u32[]{:S(2)}) collective-permute-start(f32[8,128]{1,0:T(8,128)S(1)} %shard_map.99.refs_0_), channel_id=1, source_target_pairs={{0,2},{1,3},{2,0},{3,1},{4,6},{5,7},{6,4},{7,5},{8,10},{9,11},{10,... | collective-permute-start | bytes 12296 | tf_op jit(solution)/shard_map/ppermute | solution.py:445
  43.5 1.1 %collective-permute-start.18 = (f32[8,128]{1,0:T(8,128)S(1)}, f32[8,128]{1,0:T(8,128)S(1)}, u32[]{:S(2)}, u32[]{:S(2)}) collective-permute-start(f32[8,128]{1,0:T(8,128)S(1)} %shard_map.99.refs_0_), channel_id=1, source_target_pairs={{0,1},{1,0},{2,3},{3,2},{4,5},{5,4},{6,7},{7,6},{8,9},{9,8},{10,11... | collective-permute-start | bytes 12296 | tf_op jit(solution)/shard_map/ppermute | solution.py:445
  44.7 0.2 shard_map.97
  44.9 0.9 %collective-permute-done.20.refs_3_ = f32[8,128]{1,0:T(8,128)S(1)} collective-permute-done((f32[8,128]{1,0:T(8,128)S(1)}, f32[8,128]{1,0:T(8,128)S(1)}, u32[]{:S(2)}, u32[]{:S(2)}) %collective-permute-start.20) | collective-permute-done | bytes 4128 | tf_op jit(solution)/shard_map/ppermute | solution.py:445
  45.8 0.7 %collective-permute-done.19.refs_2_ = f32[8,128]{1,0:T(8,128)S(1)} collective-permute-done((f32[8,128]{1,0:T(8,128)S(1)}, f32[8,128]{1,0:T(8,128)S(1)}, u32[]{:S(2)}, u32[]{:S(2)}) %collective-permute-start.19) | collective-permute-done | bytes 4128 | tf_op jit(solution)/shard_map/ppermute | solution.py:445
  46.5 0.6 %shard_map.100 = (f32[24,128]{1,0:T(8,128)S(1)}, f32[24,128]{1,0:T(8,128)S(1)}, f32[24,128]{1,0:T(8,128)S(1)}, f32[24,128]{1,0:T(8,128)S(1)}) custom-call(bf16[64,128,128]{2,1,0:T(8,128)(2,1)S(1)} %bitcast.15, f32[64,128]{1,0:T(8,128)S(1)} %compare_select_fusion.rows, f32[8,128]{1,0:T(8,128)S(1)} %get-tuple-element.44.c, ...), custom_call_target="tpu_custom_call" | custom-call | flops 2097152 | bytes 1048576 | tf_op jit(solution)/shard_map/pallas_call | solution.py:30
  47.1 0.9 %collective-permute-start.21 = (f32[24,128]{1,0:T(8,128)S(1)}, f32[24,128]{1,0:T(8,128)S(1)}, u32[]{:S(2)}, u32[]{:S(2)}) collective-permute-start(f32[24,128]{1,0:T(8,128)S(1)} %get-tuple-element.65), channel_id=1, source_target_pairs={{0,8},{4,12},{8,0},{12,4},{1,9},{5,13},{9,1},{13,5},{2,10},{6,14},... | collective-permute-start | bytes 36872 | tf_op jit(solution)/shard_map/ppermute | solution.py:451
  48.0 1.8 %collective-permute-start.22 = (f32[24,128]{1,0:T(8,128)S(1)}, f32[24,128]{1,0:T(8,128)S(1)}, u32[]{:S(2)}, u32[]{:S(2)}) collective-permute-start(f32[24,128]{1,0:T(8,128)S(1)} %get-tuple-element.66), channel_id=1, source_target_pairs={{0,12},{4,8},{8,4},{12,0},{1,13},{5,9},{9,5},{13,1},{2,14},{6,10},... | collective-permute-start | bytes 36872 | tf_op jit(solution)/shard_map/ppermute | solution.py:451
  49.8 0.8 %collective-permute-start.23 = (f32[24,128]{1,0:T(8,128)S(1)}, f32[24,128]{1,0:T(8,128)S(1)}, u32[]{:S(2)}, u32[]{:S(2)}) collective-permute-start(f32[24,128]{1,0:T(8,128)S(1)} %get-tuple-element.67), channel_id=1, source_target_pairs={{0,4},{4,0},{8,12},{12,8},{1,5},{5,1},{9,13},{13,9},{2,6},{6,2},{1... | collective-permute-start | bytes 36872 | tf_op jit(solution)/shard_map/ppermute | solution.py:451
  50.7 0.7 %shard_map.98 = (f32[512,128]{1,0:T(8,128)S(1)}, f32[512,128]{1,0:T(8,128)S(1)}, f32[512,128]{1,0:T(8,128)S(1)}, f32[512,128]{1,0:T(8,128)S(1)}, bf16[512,128]{1,0:T(8,128)(2,1)S(1)}) custom-call(f32[2048,128]{1,0:T(8,128)S(1)} %bitcast.17, s32[1]{0:T(128)} %bitcast.4.index, f32[72,128]{1,0:T(8,128)S(1)} %get-tuple-element.48.refs_0_, ...), custom_call_target="tpu_custom_call" | custom-call | flops 2097152 | bytes 1048576 | tf_op jit(solution)/shard_map/pallas_call | solution.py:30
  51.4 0.5 collective-permute-done.21.refs_1_
  51.9 1.6 %collective-permute-done.22.refs_2_ = f32[24,128]{1,0:T(8,128)S(1)} collective-permute-done((f32[24,128]{1,0:T(8,128)S(1)}, f32[24,128]{1,0:T(8,128)S(1)}, u32[]{:S(2)}, u32[]{:S(2)}) %collective-permute-start.22) | collective-permute-done | bytes 12320 | tf_op jit(solution)/shard_map/ppermute | solution.py:451
  53.5 0.1 collective-permute-done.23.refs_3_
  53.6 1.1 %shard_map.101 = (f32[512,128]{1,0:T(8,128)}, f32[512,128]{1,0:T(8,128)}) custom-call(f32[8,128]{1,0:T(8,128)S(1)} %get-tuple-element.42.ww, f32[8,128]{1,0:T(8,128)S(1)} %get-tuple-element.56.refs_13_.num, f32[512,128]{1,0:T(8,128)S(1)} %get-tuple-element.57.res, f32[512,128]{1,0:T(8,128)S(1)} %get-tuple-element.58.direction, ...), custom_call_target="tpu_custom_call" | custom-call | flops 2097152 | bytes 1048576 | tf_op jit(solution)/shard_map/pallas_call | solution.py:30
  (11 shorter events, 0.0 us)
Async XLA Ops:
  0.6 1.9 %copy-start.1 = (f32[1,262144]{1,0:T(1,128)S(1)}, f32[1,262144]{1,0:T(1,128)}, u32[]{:S(2)}) copy-start(f32[1,262144]{1,0:T(1,128)} %param.13) | copy-start | bytes 3145732
  0.6 1.9 %copy-start = (bf16[1,1,64,128,128]{4,3,2,1,0:T(8,128)(2,1)S(1)}, bf16[1,1,64,128,128]{4,3,2,1,0:T(8,128)(2,1)}, u32[]{:S(2)}) copy-start(bf16[1,1,64,128,128]{4,3,2,1,0:T(8,128)(2,1)} %param.7) | copy-start | bytes 6291460
  2.4 4.0 %copy-start.3 = (s32[1,512]{1,0:T(1,128)S(1)}, s32[1,512]{1,0:T(1,128)}, u32[]{:S(2)}) copy-start(s32[1,512]{1,0:T(1,128)} %ids.1) | copy-start | bytes 6148
  2.5 4.0 %copy-start.4 = (s32[1,1,64]{2,1,0:T(1,128)S(1)}, s32[1,1,64]{2,1,0:T(1,128)}, u32[]{:S(2)}) copy-start(s32[1,1,64]{2,1,0:T(1,128)} %param.9) | copy-start | bytes 772
  2.5 7.0 %copy-start.2 = (s32[1,1024]{1,0:T(1,128)S(1)}, s32[1,1024]{1,0:T(1,128)}, u32[]{:S(2)}) copy-start(s32[1,1024]{1,0:T(1,128)} %param.12) | copy-start | bytes 12292
  3.3 3.8 %collective-permute-start.2 = (f32[16,128]{1,0:T(8,128)S(1)}, f32[16,128]{1,0:T(8,128)S(1)}, u32[]{:S(2)}, u32[]{:S(2)}) collective-permute-start(f32[16,128]{1,0:T(8,128)S(1)} %get-tuple-element.41.refs_0_), channel_id=1, source_target_pairs={{0,3},{1,2},{2,1},{3,0},{4,7},{5,6},{6,5},{7,4},{8,11},{9,10},{10,... | collective-permute-start | bytes 24584 | tf_op jit(solution)/shard_map/ppermute | solution.py:445
  5.8 3.7 %collective-permute-start.1 = (f32[16,128]{1,0:T(8,128)S(1)}, f32[16,128]{1,0:T(8,128)S(1)}, u32[]{:S(2)}, u32[]{:S(2)}) collective-permute-start(f32[16,128]{1,0:T(8,128)S(1)} %get-tuple-element.41.refs_0_), channel_id=1, source_target_pairs={{0,2},{1,3},{2,0},{3,1},{4,6},{5,7},{6,4},{7,5},{8,10},{9,11},{10,... | collective-permute-start | bytes 24584 | tf_op jit(solution)/shard_map/ppermute | solution.py:445
  6.4 3.0 %collective-permute-start = (f32[16,128]{1,0:T(8,128)S(1)}, f32[16,128]{1,0:T(8,128)S(1)}, u32[]{:S(2)}, u32[]{:S(2)}) collective-permute-start(f32[16,128]{1,0:T(8,128)S(1)} %get-tuple-element.41.refs_0_), channel_id=1, source_target_pairs={{0,1},{1,0},{2,3},{3,2},{4,5},{5,4},{6,7},{7,6},{8,9},{9,8},{10,11... | collective-permute-start | bytes 24584 | tf_op jit(solution)/shard_map/ppermute | solution.py:445
  9.8 4.9 %collective-permute-start.5 = (f32[72,128]{1,0:T(8,128)S(1)}, f32[72,128]{1,0:T(8,128)S(1)}, u32[]{:S(2)}, u32[]{:S(2)}) collective-permute-start(f32[72,128]{1,0:T(8,128)S(1)} %get-tuple-element.48.refs_0_), channel_id=1, source_target_pairs={{0,8},{4,12},{8,0},{12,4},{1,9},{5,13},{9,1},{13,5},{2,10},{6,14},... | collective-permute-start | bytes 110600 | tf_op jit(solution)/shard_map/ppermute | solution.py:445
  12.5 5.8 %collective-permute-start.4 = (f32[72,128]{1,0:T(8,128)S(1)}, f32[72,128]{1,0:T(8,128)S(1)}, u32[]{:S(2)}, u32[]{:S(2)}) collective-permute-start(f32[72,128]{1,0:T(8,128)S(1)} %get-tuple-element.48.refs_0_), channel_id=1, source_target_pairs={{0,12},{4,8},{8,4},{12,0},{1,13},{5,9},{9,5},{13,1},{2,14},{6,10},... | collective-permute-start | bytes 110600 | tf_op jit(solution)/shard_map/ppermute | solution.py:445
  13.9 4.4 %collective-permute-start.3 = (f32[72,128]{1,0:T(8,128)S(1)}, f32[72,128]{1,0:T(8,128)S(1)}, u32[]{:S(2)}, u32[]{:S(2)}) collective-permute-start(f32[72,128]{1,0:T(8,128)S(1)} %get-tuple-element.48.refs_0_), channel_id=1, source_target_pairs={{0,4},{4,0},{8,12},{12,8},{1,5},{5,1},{9,13},{13,9},{2,6},{6,2},{1... | collective-permute-start | bytes 110600 | tf_op jit(solution)/shard_map/ppermute | solution.py:445
  18.9 3.1 %collective-permute-start.8 = (f32[8,128]{1,0:T(8,128)S(1)}, f32[8,128]{1,0:T(8,128)S(1)}, u32[]{:S(2)}, u32[]{:S(2)}) collective-permute-start(f32[8,128]{1,0:T(8,128)S(1)} %shard_map.92.refs_0_), channel_id=1, source_target_pairs={{0,3},{1,2},{2,1},{3,0},{4,7},{5,6},{6,5},{7,4},{8,11},{9,10},{10,... | collective-permute-start | bytes 12296 | tf_op jit(solution)/shard_map/ppermute | solution.py:445
  19.0 3.7 %collective-permute-start.7 = (f32[8,128]{1,0:T(8,128)S(1)}, f32[8,128]{1,0:T(8,128)S(1)}, u32[]{:S(2)}, u32[]{:S(2)}) collective-permute-start(f32[8,128]{1,0:T(8,128)S(1)} %shard_map.92.refs_0_), channel_id=1, source_target_pairs={{0,2},{1,3},{2,0},{3,1},{4,6},{5,7},{6,4},{7,5},{8,10},{9,11},{10,... | collective-permute-start | bytes 12296 | tf_op jit(solution)/shard_map/ppermute | solution.py:445
  19.7 3.0 %collective-permute-start.6 = (f32[8,128]{1,0:T(8,128)S(1)}, f32[8,128]{1,0:T(8,128)S(1)}, u32[]{:S(2)}, u32[]{:S(2)}) collective-permute-start(f32[8,128]{1,0:T(8,128)S(1)} %shard_map.92.refs_0_), channel_id=1, source_target_pairs={{0,1},{1,0},{2,3},{3,2},{4,5},{5,4},{6,7},{7,6},{8,9},{9,8},{10,11... | collective-permute-start | bytes 12296 | tf_op jit(solution)/shard_map/ppermute | solution.py:445
  23.1 5.5 %collective-permute-start.11 = (f32[72,128]{1,0:T(8,128)S(1)}, f32[72,128]{1,0:T(8,128)S(1)}, u32[]{:S(2)}, u32[]{:S(2)}) collective-permute-start(f32[72,128]{1,0:T(8,128)S(1)} %get-tuple-element.49.refs_0_.refs_4_), channel_id=1, source_target_pairs={{0,8},{4,12},{8,0},{12,4},{1,9},{5,13},{9,1},{13,5},{2,10},{6,14},... | collective-permute-start | bytes 110600 | tf_op jit(solution)/shard_map/ppermute | solution.py:445
  24.4 5.8 %collective-permute-start.10 = (f32[72,128]{1,0:T(8,128)S(1)}, f32[72,128]{1,0:T(8,128)S(1)}, u32[]{:S(2)}, u32[]{:S(2)}) collective-permute-start(f32[72,128]{1,0:T(8,128)S(1)} %get-tuple-element.49.refs_0_.refs_4_), channel_id=1, source_target_pairs={{0,12},{4,8},{8,4},{12,0},{1,13},{5,9},{9,5},{13,1},{2,14},{6,10},... | collective-permute-start | bytes 110600 | tf_op jit(solution)/shard_map/ppermute | solution.py:445
  25.4 4.7 %collective-permute-start.9 = (f32[72,128]{1,0:T(8,128)S(1)}, f32[72,128]{1,0:T(8,128)S(1)}, u32[]{:S(2)}, u32[]{:S(2)}) collective-permute-start(f32[72,128]{1,0:T(8,128)S(1)} %get-tuple-element.49.refs_0_.refs_4_), channel_id=1, source_target_pairs={{0,4},{4,0},{8,12},{12,8},{1,5},{5,1},{9,13},{13,9},{2,6},{6,2},{1... | collective-permute-start | bytes 110600 | tf_op jit(solution)/shard_map/ppermute | solution.py:445
  30.7 3.1 %collective-permute-start.14 = (f32[8,128]{1,0:T(8,128)S(1)}, f32[8,128]{1,0:T(8,128)S(1)}, u32[]{:S(2)}, u32[]{:S(2)}) collective-permute-start(f32[8,128]{1,0:T(8,128)S(1)} %shard_map.95.refs_0_), channel_id=1, source_target_pairs={{0,3},{1,2},{2,1},{3,0},{4,7},{5,6},{6,5},{7,4},{8,11},{9,10},{10,... | collective-permute-start | bytes 12296 | tf_op jit(solution)/shard_map/ppermute | solution.py:445
  30.8 3.7 %collective-permute-start.13 = (f32[8,128]{1,0:T(8,128)S(1)}, f32[8,128]{1,0:T(8,128)S(1)}, u32[]{:S(2)}, u32[]{:S(2)}) collective-permute-start(f32[8,128]{1,0:T(8,128)S(1)} %shard_map.95.refs_0_), channel_id=1, source_target_pairs={{0,2},{1,3},{2,0},{3,1},{4,6},{5,7},{6,4},{7,5},{8,10},{9,11},{10,... | collective-permute-start | bytes 12296 | tf_op jit(solution)/shard_map/ppermute | solution.py:445
  31.5 3.0 %collective-permute-start.12 = (f32[8,128]{1,0:T(8,128)S(1)}, f32[8,128]{1,0:T(8,128)S(1)}, u32[]{:S(2)}, u32[]{:S(2)}) collective-permute-start(f32[8,128]{1,0:T(8,128)S(1)} %shard_map.95.refs_0_), channel_id=1, source_target_pairs={{0,1},{1,0},{2,3},{3,2},{4,5},{5,4},{6,7},{7,6},{8,9},{9,8},{10,11... | collective-permute-start | bytes 12296 | tf_op jit(solution)/shard_map/ppermute | solution.py:445
  34.9 5.6 %collective-permute-start.17 = (f32[72,128]{1,0:T(8,128)S(1)}, f32[72,128]{1,0:T(8,128)S(1)}, u32[]{:S(2)}, u32[]{:S(2)}) collective-permute-start(f32[72,128]{1,0:T(8,128)S(1)} %get-tuple-element.53.refs_0_.refs_8_), channel_id=1, source_target_pairs={{0,8},{4,12},{8,0},{12,4},{1,9},{5,13},{9,1},{13,5},{2,10},{6,14},... | collective-permute-start | bytes 110600 | tf_op jit(solution)/shard_map/ppermute | solution.py:445
  36.0 5.9 %collective-permute-start.16 = (f32[72,128]{1,0:T(8,128)S(1)}, f32[72,128]{1,0:T(8,128)S(1)}, u32[]{:S(2)}, u32[]{:S(2)}) collective-permute-start(f32[72,128]{1,0:T(8,128)S(1)} %get-tuple-element.53.refs_0_.refs_8_), channel_id=1, source_target_pairs={{0,12},{4,8},{8,4},{12,0},{1,13},{5,9},{9,5},{13,1},{2,14},{6,10},... | collective-permute-start | bytes 110600 | tf_op jit(solution)/shard_map/ppermute | solution.py:445
  37.8 4.4 %collective-permute-start.15 = (f32[72,128]{1,0:T(8,128)S(1)}, f32[72,128]{1,0:T(8,128)S(1)}, u32[]{:S(2)}, u32[]{:S(2)}) collective-permute-start(f32[72,128]{1,0:T(8,128)S(1)} %get-tuple-element.53.refs_0_.refs_8_), channel_id=1, source_target_pairs={{0,4},{4,0},{8,12},{12,8},{1,5},{5,1},{9,13},{13,9},{2,6},{6,2},{1... | collective-permute-start | bytes 110600 | tf_op jit(solution)/shard_map/ppermute | solution.py:445
  42.7 3.1 %collective-permute-start.20 = (f32[8,128]{1,0:T(8,128)S(1)}, f32[8,128]{1,0:T(8,128)S(1)}, u32[]{:S(2)}, u32[]{:S(2)}) collective-permute-start(f32[8,128]{1,0:T(8,128)S(1)} %shard_map.99.refs_0_), channel_id=1, source_target_pairs={{0,3},{1,2},{2,1},{3,0},{4,7},{5,6},{6,5},{7,4},{8,11},{9,10},{10,... | collective-permute-start | bytes 12296 | tf_op jit(solution)/shard_map/ppermute | solution.py:445
  42.8 3.7 %collective-permute-start.19 = (f32[8,128]{1,0:T(8,128)S(1)}, f32[8,128]{1,0:T(8,128)S(1)}, u32[]{:S(2)}, u32[]{:S(2)}) collective-permute-start(f32[8,128]{1,0:T(8,128)S(1)} %shard_map.99.refs_0_), channel_id=1, source_target_pairs={{0,2},{1,3},{2,0},{3,1},{4,6},{5,7},{6,4},{7,5},{8,10},{9,11},{10,... | collective-permute-start | bytes 12296 | tf_op jit(solution)/shard_map/ppermute | solution.py:445
  43.5 3.0 %collective-permute-start.18 = (f32[8,128]{1,0:T(8,128)S(1)}, f32[8,128]{1,0:T(8,128)S(1)}, u32[]{:S(2)}, u32[]{:S(2)}) collective-permute-start(f32[8,128]{1,0:T(8,128)S(1)} %shard_map.99.refs_0_), channel_id=1, source_target_pairs={{0,1},{1,0},{2,3},{3,2},{4,5},{5,4},{6,7},{7,6},{8,9},{9,8},{10,11... | collective-permute-start | bytes 12296 | tf_op jit(solution)/shard_map/ppermute | solution.py:445
  47.1 4.8 %collective-permute-start.21 = (f32[24,128]{1,0:T(8,128)S(1)}, f32[24,128]{1,0:T(8,128)S(1)}, u32[]{:S(2)}, u32[]{:S(2)}) collective-permute-start(f32[24,128]{1,0:T(8,128)S(1)} %get-tuple-element.65), channel_id=1, source_target_pairs={{0,8},{4,12},{8,0},{12,4},{1,9},{5,13},{9,1},{13,5},{2,10},{6,14},... | collective-permute-start | bytes 36872 | tf_op jit(solution)/shard_map/ppermute | solution.py:451
  48.0 5.5 %collective-permute-start.22 = (f32[24,128]{1,0:T(8,128)S(1)}, f32[24,128]{1,0:T(8,128)S(1)}, u32[]{:S(2)}, u32[]{:S(2)}) collective-permute-start(f32[24,128]{1,0:T(8,128)S(1)} %get-tuple-element.66), channel_id=1, source_target_pairs={{0,12},{4,8},{8,4},{12,0},{1,13},{5,9},{9,5},{13,1},{2,14},{6,10},... | collective-permute-start | bytes 36872 | tf_op jit(solution)/shard_map/ppermute | solution.py:451
  49.8 3.8 %collective-permute-start.23 = (f32[24,128]{1,0:T(8,128)S(1)}, f32[24,128]{1,0:T(8,128)S(1)}, u32[]{:S(2)}, u32[]{:S(2)}) collective-permute-start(f32[24,128]{1,0:T(8,128)S(1)} %get-tuple-element.67), channel_id=1, source_target_pairs={{0,4},{4,0},{8,12},{12,8},{1,5},{5,1},{9,13},{13,9},{2,6},{6,2},{1... | collective-permute-start | bytes 36872 | tf_op jit(solution)/shard_map/ppermute | solution.py:451

commit v9 on v8

--- a/solution.py
+++ b/solution.py
@@ -59,6 +59,9 @@
 
 def exact_pick(pick, values):
     wide = values.shape[1]
+    if values.shape[0] % LANES == 0:
+        pieces = jnp.concatenate(split3(values), axis=0).astype(BF16)
+        return jnp.dot(jnp.concatenate([pick] * 3, axis=1), pieces, preferred_element_type=F32)
     pieces = jnp.concatenate(split3(values), axis=1).astype(BF16)
     out = jnp.dot(pick, pieces, preferred_element_type=F32)
     return out[:, :wide] + out[:, wide : 2 * wide] + out[:, 2 * wide :]

time: 54.9 us -> 54.9 us (level)
  transfers between devices with their start and end apart: 24 -> 24, of which waited for: 18 -> 18; matrix products, arithmetic and copies ran while one was open for 0% -> 0% of each run, Pallas kernels for 3% -> 4%
where the time goes in v9:
time: 54.9 us; the launch traced here: 54.7 us
  starting transfers between devices  23.8 us (43%)
  waiting for transfers between devices  20.7 us (38%)
  Pallas kernels  8.52 us (16%)
  between operations  1.6 us (3%)
    ppermute x21, starting transfers between devices, exchange(): lax.ppermute(x, axis, [(i, i ^ k) for i in range(size)])  20.2 us
    ppermute x21, waiting for transfers between devices, exchange(): lax.ppermute(x, axis, [(i, i ^ k) for i in range(size)])  18.7 us
    pallas_call x16, Pallas kernels, call(): pl.pallas_call(kernel, in_specs=in_specs, out_shape=outs, out_specs=out_s...  8.52 us
    ppermute x3, starting transfers between devices, exchange_each(): lax.ppermute(to[k], axis, [(i, i ^ k) for i in range(4)])  3.55 us
    ppermute x3, waiting for transfers between devices, exchange_each(): lax.ppermute(to[k], axis, [(i, i ^ k) for i in range(4)])  2.09 us
  transfers between devices with their start and end apart: 24, of which 18 were waited for; matrix products, arithmetic and copies ran while one was open for 0% of the time, Pallas kernels for 4%

profile of v9, /device:TPU:0, one launch (start us, length us, event | category | flops | bytes accessed | tf_op | source)
XLA Modules:
  0.0 54.7 jit_solution(5474444852775306574)
XLA Ops:
  1.4 1.0 %shard_map.86 = (f32[64,128]{1,0:T(8,128)S(1)}, s32[64,128]{1,0:T(8,128)S(1)}, s32[1,64]{1,0:T(1,128)S(4)}) custom-call(s32[1,64]{1,0:T(1,128)} %bitcast.23, s32[1,64]{1,0:T(1,128)} %bitcast.19), custom_call_target="tpu_custom_call" | custom-call | flops 1073741824 | bytes 1048576 | tf_op jit(solution)/shard_map/pallas_call | solution.py:30
  2.4 0.0 copy-start.3
  2.5 0.0 copy-start.4
  2.5 0.0 copy-start.2
  2.5 0.1 copy-done
  2.6 0.8 %shard_map.88 = (f32[16,128]{1,0:T(8,128)S(1)}, f32[512,128]{1,0:T(8,128)S(1)}) custom-call(s32[1,64]{1,0:T(1,128)S(4)} %get-tuple-element.40.cols, f32[64,128]{1,0:T(8,128)S(1)} %compare_select_fusion.rows, bf16[64,128,128]{2,1,0:T(8,128)(2,1)S(1)} %bitcast.10, f32[2048,128]{1,0:T(8,128)S(1)} %bitcast.16), custom_call_target="tpu_custom_call" | custom-call | flops 2097152 | bytes 1048576 | tf_op jit(solution)/shard_map/pallas_call | solution.py:30
  3.3 2.4 %collective-permute-start.2 = (f32[16,128]{1,0:T(8,128)S(1)}, f32[16,128]{1,0:T(8,128)S(1)}, u32[]{:S(2)}, u32[]{:S(2)}) collective-permute-start(f32[16,128]{1,0:T(8,128)S(1)} %get-tuple-element.41.refs_0_), channel_id=1, source_target_pairs={{0,3},{1,2},{2,1},{3,0},{4,7},{5,6},{6,5},{7,4},{8,11},{9,10},{10,... | collective-permute-start | bytes 24584 | tf_op jit(solution)/shard_map/ppermute | solution.py:448
  5.8 0.6 %collective-permute-start.1 = (f32[16,128]{1,0:T(8,128)S(1)}, f32[16,128]{1,0:T(8,128)S(1)}, u32[]{:S(2)}, u32[]{:S(2)}) collective-permute-start(f32[16,128]{1,0:T(8,128)S(1)} %get-tuple-element.41.refs_0_), channel_id=1, source_target_pairs={{0,2},{1,3},{2,0},{3,1},{4,6},{5,7},{6,4},{7,5},{8,10},{9,11},{10,... | collective-permute-start | bytes 24584 | tf_op jit(solution)/shard_map/ppermute | solution.py:448
  6.4 0.0 collective-permute-start
  6.5 0.2 shard_map.87
  6.7 0.5 collective-permute-done.2.refs_3_
  7.1 2.3 %collective-permute-done.1.refs_2_ = f32[16,128]{1,0:T(8,128)S(1)} collective-permute-done((f32[16,128]{1,0:T(8,128)S(1)}, f32[16,128]{1,0:T(8,128)S(1)}, u32[]{:S(2)}, u32[]{:S(2)}) %collective-permute-start.1) | collective-permute-done | bytes 8224 | tf_op jit(solution)/shard_map/ppermute | solution.py:448
  9.4 0.0 collective-permute-done.refs_1_
  9.4 0.4 shard_map.89
  9.8 2.7 %collective-permute-start.5 = (f32[72,128]{1,0:T(8,128)S(1)}, f32[72,128]{1,0:T(8,128)S(1)}, u32[]{:S(2)}, u32[]{:S(2)}) collective-permute-start(f32[72,128]{1,0:T(8,128)S(1)} %get-tuple-element.48.refs_0_), channel_id=1, source_target_pairs={{0,8},{4,12},{8,0},{12,4},{1,9},{5,13},{9,1},{13,5},{2,10},{6,14},... | collective-permute-start | bytes 110600 | tf_op jit(solution)/shard_map/ppermute | solution.py:448
  12.5 1.3 %collective-permute-start.4 = (f32[72,128]{1,0:T(8,128)S(1)}, f32[72,128]{1,0:T(8,128)S(1)}, u32[]{:S(2)}, u32[]{:S(2)}) collective-permute-start(f32[72,128]{1,0:T(8,128)S(1)} %get-tuple-element.48.refs_0_), channel_id=1, source_target_pairs={{0,12},{4,8},{8,4},{12,0},{1,13},{5,9},{9,5},{13,1},{2,14},{6,10},... | collective-permute-start | bytes 110600 | tf_op jit(solution)/shard_map/ppermute | solution.py:448
  13.9 0.2 collective-permute-start.3
  14.1 0.6 %shard_map.90.turned = bf16[64,128,128]{2,1,0:T(8,128)(2,1)S(1)} custom-call(bf16[64,128,128]{2,1,0:T(8,128)(2,1)S(1)} %bitcast.12), custom_call_target="tpu_custom_call" | custom-call | flops 2097152 | bytes 1048576 | tf_op jit(solution)/shard_map/pallas_call | solution.py:30
  14.7 0.1 collective-permute-done.5.refs_3_
  14.8 3.5 %collective-permute-done.4.refs_2_ = f32[72,128]{1,0:T(8,128)S(1)} collective-permute-done((f32[72,128]{1,0:T(8,128)S(1)}, f32[72,128]{1,0:T(8,128)S(1)}, u32[]{:S(2)}, u32[]{:S(2)}) %collective-permute-start.4) | collective-permute-done | bytes 36896 | tf_op jit(solution)/shard_map/ppermute | solution.py:448
  18.3 0.0 collective-permute-done.3.refs_1_
  18.3 0.6 %shard_map.92.refs_0_ = f32[8,128]{1,0:T(8,128)S(1)} custom-call(bf16[64,128,128]{2,1,0:T(8,128)(2,1)S(1)} %shard_map.90.turned, f32[512,128]{1,0:T(8,128)S(1)} %get-tuple-element.46.row_mask, bf16[64,256]{1,0:T(8,128)(2,1)S(1)} %shard_map.91.match, f32[72,128]{1,0:T(8,128)S(1)} %get-tuple-element.48.refs_0_, f32[72,128]{1,0:T(8,128)S(1)} %collective-permute-done.3.refs_1_, ...), custom_call_target="tpu_custom_call" | custom-call | flops 2097152 | bytes 1048576 | tf_op jit(solution)/shard_map/pallas_call | solution.py:30
  18.9 0.1 collective-permute-start.8
  19.0 0.7 %collective-permute-start.7 = (f32[8,128]{1,0:T(8,128)S(1)}, f32[8,128]{1,0:T(8,128)S(1)}, u32[]{:S(2)}, u32[]{:S(2)}) collective-permute-start(f32[8,128]{1,0:T(8,128)S(1)} %shard_map.92.refs_0_), channel_id=1, source_target_pairs={{0,2},{1,3},{2,0},{3,1},{4,6},{5,7},{6,4},{7,5},{8,10},{9,11},{10,... | collective-permute-start | bytes 12296 | tf_op jit(solution)/shard_map/ppermute | solution.py:448
  19.7 1.1 %collective-permute-start.6 = (f32[8,128]{1,0:T(8,128)S(1)}, f32[8,128]{1,0:T(8,128)S(1)}, u32[]{:S(2)}, u32[]{:S(2)}) collective-permute-start(f32[8,128]{1,0:T(8,128)S(1)} %shard_map.92.refs_0_), channel_id=1, source_target_pairs={{0,1},{1,0},{2,3},{3,2},{4,5},{5,4},{6,7},{7,6},{8,9},{9,8},{10,11... | collective-permute-start | bytes 12296 | tf_op jit(solution)/shard_map/ppermute | solution.py:448
  20.8 1.2 %collective-permute-done.8.refs_3_ = f32[8,128]{1,0:T(8,128)S(1)} collective-permute-done((f32[8,128]{1,0:T(8,128)S(1)}, f32[8,128]{1,0:T(8,128)S(1)}, u32[]{:S(2)}, u32[]{:S(2)}) %collective-permute-start.8) | collective-permute-done | bytes 4128 | tf_op jit(solution)/shard_map/ppermute | solution.py:448
  22.0 0.7 %collective-permute-done.7.refs_2_ = f32[8,128]{1,0:T(8,128)S(1)} collective-permute-done((f32[8,128]{1,0:T(8,128)S(1)}, f32[8,128]{1,0:T(8,128)S(1)}, u32[]{:S(2)}, u32[]{:S(2)}) %collective-permute-start.7) | collective-permute-done | bytes 4128 | tf_op jit(solution)/shard_map/ppermute | solution.py:448
  22.6 0.0 collective-permute-done.6.refs_1_
  22.7 0.4 shard_map.93
  23.1 1.3 %collective-permute-start.11 = (f32[72,128]{1,0:T(8,128)S(1)}, f32[72,128]{1,0:T(8,128)S(1)}, u32[]{:S(2)}, u32[]{:S(2)}) collective-permute-start(f32[72,128]{1,0:T(8,128)S(1)} %get-tuple-element.49.refs_0_.refs_4_), channel_id=1, source_target_pairs={{0,8},{4,12},{8,0},{12,4},{1,9},{5,13},{9,1},{13,5},{2,10},{6,14},... | collective-permute-start | bytes 110600 | tf_op jit(solution)/shard_map/ppermute | solution.py:448
  24.4 1.1 %collective-permute-start.10 = (f32[72,128]{1,0:T(8,128)S(1)}, f32[72,128]{1,0:T(8,128)S(1)}, u32[]{:S(2)}, u32[]{:S(2)}) collective-permute-start(f32[72,128]{1,0:T(8,128)S(1)} %get-tuple-element.49.refs_0_.refs_4_), channel_id=1, source_target_pairs={{0,12},{4,8},{8,4},{12,0},{1,13},{5,9},{9,5},{13,1},{2,14},{6,10},... | collective-permute-start | bytes 110600 | tf_op jit(solution)/shard_map/ppermute | solution.py:448
  25.4 1.2 %collective-permute-start.9 = (f32[72,128]{1,0:T(8,128)S(1)}, f32[72,128]{1,0:T(8,128)S(1)}, u32[]{:S(2)}, u32[]{:S(2)}) collective-permute-start(f32[72,128]{1,0:T(8,128)S(1)} %get-tuple-element.49.refs_0_.refs_4_), channel_id=1, source_target_pairs={{0,4},{4,0},{8,12},{12,8},{1,5},{5,1},{9,13},{13,9},{2,6},{6,2},{1... | collective-permute-start | bytes 110600 | tf_op jit(solution)/shard_map/ppermute | solution.py:448
  26.6 1.9 %collective-permute-done.11.refs_3_.refs_7_ = f32[72,128]{1,0:T(8,128)S(1)} collective-permute-done((f32[72,128]{1,0:T(8,128)S(1)}, f32[72,128]{1,0:T(8,128)S(1)}, u32[]{:S(2)}, u32[]{:S(2)}) %collective-permute-start.11) | collective-permute-done | bytes 36896 | tf_op jit(solution)/shard_map/ppermute | solution.py:448
  28.6 1.6 %collective-permute-done.10.refs_2_.refs_6_ = f32[72,128]{1,0:T(8,128)S(1)} collective-permute-done((f32[72,128]{1,0:T(8,128)S(1)}, f32[72,128]{1,0:T(8,128)S(1)}, u32[]{:S(2)}, u32[]{:S(2)}) %collective-permute-start.10) | collective-permute-done | bytes 36896 | tf_op jit(solution)/shard_map/ppermute | solution.py:448
  30.1 0.6 %shard_map.95.refs_0_ = f32[8,128]{1,0:T(8,128)S(1)} custom-call(bf16[64,128,128]{2,1,0:T(8,128)(2,1)S(1)} %shard_map.90.turned, f32[512,128]{1,0:T(8,128)S(1)} %get-tuple-element.46.row_mask, bf16[64,256]{1,0:T(8,128)(2,1)S(1)} %shard_map.91.match, f32[72,128]{1,0:T(8,128)S(1)} %get-tuple-element.49.refs_0_.refs_4_, ...), custom_call_target="tpu_custom_call" | custom-call | flops 2097152 | bytes 1048576 | tf_op jit(solution)/shard_map/pallas_call | solution.py:30
  30.7 0.1 collective-permute-start.14
  30.8 0.7 %collective-permute-start.13 = (f32[8,128]{1,0:T(8,128)S(1)}, f32[8,128]{1,0:T(8,128)S(1)}, u32[]{:S(2)}, u32[]{:S(2)}) collective-permute-start(f32[8,128]{1,0:T(8,128)S(1)} %shard_map.95.refs_0_), channel_id=1, source_target_pairs={{0,2},{1,3},{2,0},{3,1},{4,6},{5,7},{6,4},{7,5},{8,10},{9,11},{10,... | collective-permute-start | bytes 12296 | tf_op jit(solution)/shard_map/ppermute | solution.py:448
  31.5 1.1 %collective-permute-start.12 = (f32[8,128]{1,0:T(8,128)S(1)}, f32[8,128]{1,0:T(8,128)S(1)}, u32[]{:S(2)}, u32[]{:S(2)}) collective-permute-start(f32[8,128]{1,0:T(8,128)S(1)} %shard_map.95.refs_0_), channel_id=1, source_target_pairs={{0,1},{1,0},{2,3},{3,2},{4,5},{5,4},{6,7},{7,6},{8,9},{9,8},{10,11... | collective-permute-start | bytes 12296 | tf_op jit(solution)/shard_map/ppermute | solution.py:448
  32.7 0.1 shard_map.94
  32.8 1.0 %collective-permute-done.14.refs_3_ = f32[8,128]{1,0:T(8,128)S(1)} collective-permute-done((f32[8,128]{1,0:T(8,128)S(1)}, f32[8,128]{1,0:T(8,128)S(1)}, u32[]{:S(2)}, u32[]{:S(2)}) %collective-permute-start.14) | collective-permute-done | bytes 4128 | tf_op jit(solution)/shard_map/ppermute | solution.py:448
  33.8 0.7 %collective-permute-done.13.refs_2_ = f32[8,128]{1,0:T(8,128)S(1)} collective-permute-done((f32[8,128]{1,0:T(8,128)S(1)}, f32[8,128]{1,0:T(8,128)S(1)}, u32[]{:S(2)}, u32[]{:S(2)}) %collective-permute-start.13) | collective-permute-done | bytes 4128 | tf_op jit(solution)/shard_map/ppermute | solution.py:448
  34.5 0.4 shard_map.96
  34.9 1.1 %collective-permute-start.17 = (f32[72,128]{1,0:T(8,128)S(1)}, f32[72,128]{1,0:T(8,128)S(1)}, u32[]{:S(2)}, u32[]{:S(2)}) collective-permute-start(f32[72,128]{1,0:T(8,128)S(1)} %get-tuple-element.53.refs_0_.refs_8_), channel_id=1, source_target_pairs={{0,8},{4,12},{8,0},{12,4},{1,9},{5,13},{9,1},{13,5},{2,10},{6,14},... | collective-permute-start | bytes 110600 | tf_op jit(solution)/shard_map/ppermute | solution.py:448
  36.0 1.8 %collective-permute-start.16 = (f32[72,128]{1,0:T(8,128)S(1)}, f32[72,128]{1,0:T(8,128)S(1)}, u32[]{:S(2)}, u32[]{:S(2)}) collective-permute-start(f32[72,128]{1,0:T(8,128)S(1)} %get-tuple-element.53.refs_0_.refs_8_), channel_id=1, source_target_pairs={{0,12},{4,8},{8,4},{12,0},{1,13},{5,9},{9,5},{13,1},{2,14},{6,10},... | collective-permute-start | bytes 110600 | tf_op jit(solution)/shard_map/ppermute | solution.py:448
  37.8 0.7 %collective-permute-start.15 = (f32[72,128]{1,0:T(8,128)S(1)}, f32[72,128]{1,0:T(8,128)S(1)}, u32[]{:S(2)}, u32[]{:S(2)}) collective-permute-start(f32[72,128]{1,0:T(8,128)S(1)} %get-tuple-element.53.refs_0_.refs_8_), channel_id=1, source_target_pairs={{0,4},{4,0},{8,12},{12,8},{1,5},{5,1},{9,13},{13,9},{2,6},{6,2},{1... | collective-permute-start | bytes 110600 | tf_op jit(solution)/shard_map/ppermute | solution.py:448
  38.5 2.1 %collective-permute-done.17.refs_3_.refs_11_ = f32[72,128]{1,0:T(8,128)S(1)} collective-permute-done((f32[72,128]{1,0:T(8,128)S(1)}, f32[72,128]{1,0:T(8,128)S(1)}, u32[]{:S(2)}, u32[]{:S(2)}) %collective-permute-start.17) | collective-permute-done | bytes 36896 | tf_op jit(solution)/shard_map/ppermute | solution.py:448
  40.6 1.4 %collective-permute-done.16.refs_2_.refs_10_ = f32[72,128]{1,0:T(8,128)S(1)} collective-permute-done((f32[72,128]{1,0:T(8,128)S(1)}, f32[72,128]{1,0:T(8,128)S(1)}, u32[]{:S(2)}, u32[]{:S(2)}) %collective-permute-start.16) | collective-permute-done | bytes 36896 | tf_op jit(solution)/shard_map/ppermute | solution.py:448
  41.9 0.3 collective-permute-done.15.refs_1_.refs_9_
  42.2 0.6 %shard_map.99.refs_0_ = f32[8,128]{1,0:T(8,128)S(1)} custom-call(bf16[64,128,128]{2,1,0:T(8,128)(2,1)S(1)} %shard_map.90.turned, f32[512,128]{1,0:T(8,128)S(1)} %get-tuple-element.46.row_mask, bf16[64,256]{1,0:T(8,128)(2,1)S(1)} %shard_map.91.match, f32[72,128]{1,0:T(8,128)S(1)} %get-tuple-element.53.refs_0_.refs_8_, ...), custom_call_target="tpu_custom_call" | custom-call | flops 2097152 | bytes 1048576 | tf_op jit(solution)/shard_map/pallas_call | solution.py:30
  42.8 0.1 collective-permute-start.20
  42.9 0.7 %collective-permute-start.19 = (f32[8,128]{1,0:T(8,128)S(1)}, f32[8,128]{1,0:T(8,128)S(1)}, u32[]{:S(2)}, u32[]{:S(2)}) collective-permute-start(f32[8,128]{1,0:T(8,128)S(1)} %shard_map.99.refs_0_), channel_id=1, source_target_pairs={{0,2},{1,3},{2,0},{3,1},{4,6},{5,7},{6,4},{7,5},{8,10},{9,11},{10,... | collective-permute-start | bytes 12296 | tf_op jit(solution)/shard_map/ppermute | solution.py:448
  43.6 1.2 %collective-permute-start.18 = (f32[8,128]{1,0:T(8,128)S(1)}, f32[8,128]{1,0:T(8,128)S(1)}, u32[]{:S(2)}, u32[]{:S(2)}) collective-permute-start(f32[8,128]{1,0:T(8,128)S(1)} %shard_map.99.refs_0_), channel_id=1, source_target_pairs={{0,1},{1,0},{2,3},{3,2},{4,5},{5,4},{6,7},{7,6},{8,9},{9,8},{10,11... | collective-permute-start | bytes 12296 | tf_op jit(solution)/shard_map/ppermute | solution.py:448
  44.7 0.2 shard_map.97
  44.9 0.9 %collective-permute-done.20.refs_3_ = f32[8,128]{1,0:T(8,128)S(1)} collective-permute-done((f32[8,128]{1,0:T(8,128)S(1)}, f32[8,128]{1,0:T(8,128)S(1)}, u32[]{:S(2)}, u32[]{:S(2)}) %collective-permute-start.20) | collective-permute-done | bytes 4128 | tf_op jit(solution)/shard_map/ppermute | solution.py:448
  45.9 0.7 %collective-permute-done.19.refs_2_ = f32[8,128]{1,0:T(8,128)S(1)} collective-permute-done((f32[8,128]{1,0:T(8,128)S(1)}, f32[8,128]{1,0:T(8,128)S(1)}, u32[]{:S(2)}, u32[]{:S(2)}) %collective-permute-start.19) | collective-permute-done | bytes 4128 | tf_op jit(solution)/shard_map/ppermute | solution.py:448
  46.5 0.6 %shard_map.100 = (f32[24,128]{1,0:T(8,128)S(1)}, f32[24,128]{1,0:T(8,128)S(1)}, f32[24,128]{1,0:T(8,128)S(1)}, f32[24,128]{1,0:T(8,128)S(1)}) custom-call(bf16[64,128,128]{2,1,0:T(8,128)(2,1)S(1)} %bitcast.15, f32[64,128]{1,0:T(8,128)S(1)} %compare_select_fusion.rows, f32[8,128]{1,0:T(8,128)S(1)} %get-tuple-element.44.c, ...), custom_call_target="tpu_custom_call" | custom-call | flops 2097152 | bytes 1048576 | tf_op jit(solution)/shard_map/pallas_call | solution.py:30
  47.1 0.9 %collective-permute-start.21 = (f32[24,128]{1,0:T(8,128)S(1)}, f32[24,128]{1,0:T(8,128)S(1)}, u32[]{:S(2)}, u32[]{:S(2)}) collective-permute-start(f32[24,128]{1,0:T(8,128)S(1)} %get-tuple-element.65), channel_id=1, source_target_pairs={{0,8},{4,12},{8,0},{12,4},{1,9},{5,13},{9,1},{13,5},{2,10},{6,14},... | collective-permute-start | bytes 36872 | tf_op jit(solution)/shard_map/ppermute | solution.py:454
  48.0 1.8 %collective-permute-start.22 = (f32[24,128]{1,0:T(8,128)S(1)}, f32[24,128]{1,0:T(8,128)S(1)}, u32[]{:S(2)}, u32[]{:S(2)}) collective-permute-start(f32[24,128]{1,0:T(8,128)S(1)} %get-tuple-element.66), channel_id=1, source_target_pairs={{0,12},{4,8},{8,4},{12,0},{1,13},{5,9},{9,5},{13,1},{2,14},{6,10},... | collective-permute-start | bytes 36872 | tf_op jit(solution)/shard_map/ppermute | solution.py:454
  49.8 0.8 %collective-permute-start.23 = (f32[24,128]{1,0:T(8,128)S(1)}, f32[24,128]{1,0:T(8,128)S(1)}, u32[]{:S(2)}, u32[]{:S(2)}) collective-permute-start(f32[24,128]{1,0:T(8,128)S(1)} %get-tuple-element.67), channel_id=1, source_target_pairs={{0,4},{4,0},{8,12},{12,8},{1,5},{5,1},{9,13},{13,9},{2,6},{6,2},{1... | collective-permute-start | bytes 36872 | tf_op jit(solution)/shard_map/ppermute | solution.py:454
  50.7 0.9 %shard_map.98 = (f32[512,128]{1,0:T(8,128)S(1)}, f32[512,128]{1,0:T(8,128)S(1)}, f32[512,128]{1,0:T(8,128)S(1)}, f32[512,128]{1,0:T(8,128)S(1)}, bf16[512,128]{1,0:T(8,128)(2,1)S(1)}) custom-call(f32[2048,128]{1,0:T(8,128)S(1)} %bitcast.17, s32[1]{0:T(128)} %bitcast.4.index, f32[72,128]{1,0:T(8,128)S(1)} %get-tuple-element.48.refs_0_, ...), custom_call_target="tpu_custom_call" | custom-call | flops 2097152 | bytes 1048576 | tf_op jit(solution)/shard_map/pallas_call | solution.py:30
  51.6 0.4 collective-permute-done.21.refs_1_
  51.9 1.6 %collective-permute-done.22.refs_2_ = f32[24,128]{1,0:T(8,128)S(1)} collective-permute-done((f32[24,128]{1,0:T(8,128)S(1)}, f32[24,128]{1,0:T(8,128)S(1)}, u32[]{:S(2)}, u32[]{:S(2)}) %collective-permute-start.22) | collective-permute-done | bytes 12320 | tf_op jit(solution)/shard_map/ppermute | solution.py:454
  53.5 0.1 collective-permute-done.23.refs_3_
  53.7 1.1 %shard_map.101 = (f32[512,128]{1,0:T(8,128)}, f32[512,128]{1,0:T(8,128)}) custom-call(f32[8,128]{1,0:T(8,128)S(1)} %get-tuple-element.42.ww, f32[8,128]{1,0:T(8,128)S(1)} %get-tuple-element.56.refs_13_.num, f32[512,128]{1,0:T(8,128)S(1)} %get-tuple-element.57.res, f32[512,128]{1,0:T(8,128)S(1)} %get-tuple-element.58.direction, ...), custom_call_target="tpu_custom_call" | custom-call | flops 2097152 | bytes 1048576 | tf_op jit(solution)/shard_map/pallas_call | solution.py:30
  (11 shorter events, 0.0 us)
Async XLA Ops:
  0.6 1.9 %copy-start.1 = (f32[1,262144]{1,0:T(1,128)S(1)}, f32[1,262144]{1,0:T(1,128)}, u32[]{:S(2)}) copy-start(f32[1,262144]{1,0:T(1,128)} %param.13) | copy-start | bytes 3145732
  0.6 1.9 %copy-start = (bf16[1,1,64,128,128]{4,3,2,1,0:T(8,128)(2,1)S(1)}, bf16[1,1,64,128,128]{4,3,2,1,0:T(8,128)(2,1)}, u32[]{:S(2)}) copy-start(bf16[1,1,64,128,128]{4,3,2,1,0:T(8,128)(2,1)} %param.7) | copy-start | bytes 6291460
  2.4 4.0 %copy-start.3 = (s32[1,512]{1,0:T(1,128)S(1)}, s32[1,512]{1,0:T(1,128)}, u32[]{:S(2)}) copy-start(s32[1,512]{1,0:T(1,128)} %ids.1) | copy-start | bytes 6148
  2.5 4.0 %copy-start.4 = (s32[1,1,64]{2,1,0:T(1,128)S(1)}, s32[1,1,64]{2,1,0:T(1,128)}, u32[]{:S(2)}) copy-start(s32[1,1,64]{2,1,0:T(1,128)} %param.9) | copy-start | bytes 772
  2.5 7.0 %copy-start.2 = (s32[1,1024]{1,0:T(1,128)S(1)}, s32[1,1024]{1,0:T(1,128)}, u32[]{:S(2)}) copy-start(s32[1,1024]{1,0:T(1,128)} %param.12) | copy-start | bytes 12292
  3.3 3.8 %collective-permute-start.2 = (f32[16,128]{1,0:T(8,128)S(1)}, f32[16,128]{1,0:T(8,128)S(1)}, u32[]{:S(2)}, u32[]{:S(2)}) collective-permute-start(f32[16,128]{1,0:T(8,128)S(1)} %get-tuple-element.41.refs_0_), channel_id=1, source_target_pairs={{0,3},{1,2},{2,1},{3,0},{4,7},{5,6},{6,5},{7,4},{8,11},{9,10},{10,... | collective-permute-start | bytes 24584 | tf_op jit(solution)/shard_map/ppermute | solution.py:448
  5.8 3.7 %collective-permute-start.1 = (f32[16,128]{1,0:T(8,128)S(1)}, f32[16,128]{1,0:T(8,128)S(1)}, u32[]{:S(2)}, u32[]{:S(2)}) collective-permute-start(f32[16,128]{1,0:T(8,128)S(1)} %get-tuple-element.41.refs_0_), channel_id=1, source_target_pairs={{0,2},{1,3},{2,0},{3,1},{4,6},{5,7},{6,4},{7,5},{8,10},{9,11},{10,... | collective-permute-start | bytes 24584 | tf_op jit(solution)/shard_map/ppermute | solution.py:448
  6.4 3.0 %collective-permute-start = (f32[16,128]{1,0:T(8,128)S(1)}, f32[16,128]{1,0:T(8,128)S(1)}, u32[]{:S(2)}, u32[]{:S(2)}) collective-permute-start(f32[16,128]{1,0:T(8,128)S(1)} %get-tuple-element.41.refs_0_), channel_id=1, source_target_pairs={{0,1},{1,0},{2,3},{3,2},{4,5},{5,4},{6,7},{7,6},{8,9},{9,8},{10,11... | collective-permute-start | bytes 24584 | tf_op jit(solution)/shard_map/ppermute | solution.py:448
  9.8 4.9 %collective-permute-start.5 = (f32[72,128]{1,0:T(8,128)S(1)}, f32[72,128]{1,0:T(8,128)S(1)}, u32[]{:S(2)}, u32[]{:S(2)}) collective-permute-start(f32[72,128]{1,0:T(8,128)S(1)} %get-tuple-element.48.refs_0_), channel_id=1, source_target_pairs={{0,8},{4,12},{8,0},{12,4},{1,9},{5,13},{9,1},{13,5},{2,10},{6,14},... | collective-permute-start | bytes 110600 | tf_op jit(solution)/shard_map/ppermute | solution.py:448
  12.5 5.8 %collective-permute-start.4 = (f32[72,128]{1,0:T(8,128)S(1)}, f32[72,128]{1,0:T(8,128)S(1)}, u32[]{:S(2)}, u32[]{:S(2)}) collective-permute-start(f32[72,128]{1,0:T(8,128)S(1)} %get-tuple-element.48.refs_0_), channel_id=1, source_target_pairs={{0,12},{4,8},{8,4},{12,0},{1,13},{5,9},{9,5},{13,1},{2,14},{6,10},... | collective-permute-start | bytes 110600 | tf_op jit(solution)/shard_map/ppermute | solution.py:448
  13.9 4.4 %collective-permute-start.3 = (f32[72,128]{1,0:T(8,128)S(1)}, f32[72,128]{1,0:T(8,128)S(1)}, u32[]{:S(2)}, u32[]{:S(2)}) collective-permute-start(f32[72,128]{1,0:T(8,128)S(1)} %get-tuple-element.48.refs_0_), channel_id=1, source_target_pairs={{0,4},{4,0},{8,12},{12,8},{1,5},{5,1},{9,13},{13,9},{2,6},{6,2},{1... | collective-permute-start | bytes 110600 | tf_op jit(solution)/shard_map/ppermute | solution.py:448
  18.9 3.1 %collective-permute-start.8 = (f32[8,128]{1,0:T(8,128)S(1)}, f32[8,128]{1,0:T(8,128)S(1)}, u32[]{:S(2)}, u32[]{:S(2)}) collective-permute-start(f32[8,128]{1,0:T(8,128)S(1)} %shard_map.92.refs_0_), channel_id=1, source_target_pairs={{0,3},{1,2},{2,1},{3,0},{4,7},{5,6},{6,5},{7,4},{8,11},{9,10},{10,... | collective-permute-start | bytes 12296 | tf_op jit(solution)/shard_map/ppermute | solution.py:448
  19.0 3.7 %collective-permute-start.7 = (f32[8,128]{1,0:T(8,128)S(1)}, f32[8,128]{1,0:T(8,128)S(1)}, u32[]{:S(2)}, u32[]{:S(2)}) collective-permute-start(f32[8,128]{1,0:T(8,128)S(1)} %shard_map.92.refs_0_), channel_id=1, source_target_pairs={{0,2},{1,3},{2,0},{3,1},{4,6},{5,7},{6,4},{7,5},{8,10},{9,11},{10,... | collective-permute-start | bytes 12296 | tf_op jit(solution)/shard_map/ppermute | solution.py:448
  19.7 3.0 %collective-permute-start.6 = (f32[8,128]{1,0:T(8,128)S(1)}, f32[8,128]{1,0:T(8,128)S(1)}, u32[]{:S(2)}, u32[]{:S(2)}) collective-permute-start(f32[8,128]{1,0:T(8,128)S(1)} %shard_map.92.refs_0_), channel_id=1, source_target_pairs={{0,1},{1,0},{2,3},{3,2},{4,5},{5,4},{6,7},{7,6},{8,9},{9,8},{10,11... | collective-permute-start | bytes 12296 | tf_op jit(solution)/shard_map/ppermute | solution.py:448
  23.1 5.5 %collective-permute-start.11 = (f32[72,128]{1,0:T(8,128)S(1)}, f32[72,128]{1,0:T(8,128)S(1)}, u32[]{:S(2)}, u32[]{:S(2)}) collective-permute-start(f32[72,128]{1,0:T(8,128)S(1)} %get-tuple-element.49.refs_0_.refs_4_), channel_id=1, source_target_pairs={{0,8},{4,12},{8,0},{12,4},{1,9},{5,13},{9,1},{13,5},{2,10},{6,14},... | collective-permute-start | bytes 110600 | tf_op jit(solution)/shard_map/ppermute | solution.py:448
  24.4 5.8 %collective-permute-start.10 = (f32[72,128]{1,0:T(8,128)S(1)}, f32[72,128]{1,0:T(8,128)S(1)}, u32[]{:S(2)}, u32[]{:S(2)}) collective-permute-start(f32[72,128]{1,0:T(8,128)S(1)} %get-tuple-element.49.refs_0_.refs_4_), channel_id=1, source_target_pairs={{0,12},{4,8},{8,4},{12,0},{1,13},{5,9},{9,5},{13,1},{2,14},{6,10},... | collective-permute-start | bytes 110600 | tf_op jit(solution)/shard_map/ppermute | solution.py:448
  25.4 4.7 %collective-permute-start.9 = (f32[72,128]{1,0:T(8,128)S(1)}, f32[72,128]{1,0:T(8,128)S(1)}, u32[]{:S(2)}, u32[]{:S(2)}) collective-permute-start(f32[72,128]{1,0:T(8,128)S(1)} %get-tuple-element.49.refs_0_.refs_4_), channel_id=1, source_target_pairs={{0,4},{4,0},{8,12},{12,8},{1,5},{5,1},{9,13},{13,9},{2,6},{6,2},{1... | collective-permute-start | bytes 110600 | tf_op jit(solution)/shard_map/ppermute | solution.py:448
  30.7 3.1 %collective-permute-start.14 = (f32[8,128]{1,0:T(8,128)S(1)}, f32[8,128]{1,0:T(8,128)S(1)}, u32[]{:S(2)}, u32[]{:S(2)}) collective-permute-start(f32[8,128]{1,0:T(8,128)S(1)} %shard_map.95.refs_0_), channel_id=1, source_target_pairs={{0,3},{1,2},{2,1},{3,0},{4,7},{5,6},{6,5},{7,4},{8,11},{9,10},{10,... | collective-permute-start | bytes 12296 | tf_op jit(solution)/shard_map/ppermute | solution.py:448
  30.8 3.7 %collective-permute-start.13 = (f32[8,128]{1,0:T(8,128)S(1)}, f32[8,128]{1,0:T(8,128)S(1)}, u32[]{:S(2)}, u32[]{:S(2)}) collective-permute-start(f32[8,128]{1,0:T(8,128)S(1)} %shard_map.95.refs_0_), channel_id=1, source_target_pairs={{0,2},{1,3},{2,0},{3,1},{4,6},{5,7},{6,4},{7,5},{8,10},{9,11},{10,... | collective-permute-start | bytes 12296 | tf_op jit(solution)/shard_map/ppermute | solution.py:448
  31.5 3.0 %collective-permute-start.12 = (f32[8,128]{1,0:T(8,128)S(1)}, f32[8,128]{1,0:T(8,128)S(1)}, u32[]{:S(2)}, u32[]{:S(2)}) collective-permute-start(f32[8,128]{1,0:T(8,128)S(1)} %shard_map.95.refs_0_), channel_id=1, source_target_pairs={{0,1},{1,0},{2,3},{3,2},{4,5},{5,4},{6,7},{7,6},{8,9},{9,8},{10,11... | collective-permute-start | bytes 12296 | tf_op jit(solution)/shard_map/ppermute | solution.py:448
  34.9 5.6 %collective-permute-start.17 = (f32[72,128]{1,0:T(8,128)S(1)}, f32[72,128]{1,0:T(8,128)S(1)}, u32[]{:S(2)}, u32[]{:S(2)}) collective-permute-start(f32[72,128]{1,0:T(8,128)S(1)} %get-tuple-element.53.refs_0_.refs_8_), channel_id=1, source_target_pairs={{0,8},{4,12},{8,0},{12,4},{1,9},{5,13},{9,1},{13,5},{2,10},{6,14},... | collective-permute-start | bytes 110600 | tf_op jit(solution)/shard_map/ppermute | solution.py:448
  36.0 5.9 %collective-permute-start.16 = (f32[72,128]{1,0:T(8,128)S(1)}, f32[72,128]{1,0:T(8,128)S(1)}, u32[]{:S(2)}, u32[]{:S(2)}) collective-permute-start(f32[72,128]{1,0:T(8,128)S(1)} %get-tuple-element.53.refs_0_.refs_8_), channel_id=1, source_target_pairs={{0,12},{4,8},{8,4},{12,0},{1,13},{5,9},{9,5},{13,1},{2,14},{6,10},... | collective-permute-start | bytes 110600 | tf_op jit(solution)/shard_map/ppermute | solution.py:448
  37.8 4.4 %collective-permute-start.15 = (f32[72,128]{1,0:T(8,128)S(1)}, f32[72,128]{1,0:T(8,128)S(1)}, u32[]{:S(2)}, u32[]{:S(2)}) collective-permute-start(f32[72,128]{1,0:T(8,128)S(1)} %get-tuple-element.53.refs_0_.refs_8_), channel_id=1, source_target_pairs={{0,4},{4,0},{8,12},{12,8},{1,5},{5,1},{9,13},{13,9},{2,6},{6,2},{1... | collective-permute-start | bytes 110600 | tf_op jit(solution)/shard_map/ppermute | solution.py:448
  42.8 3.1 %collective-permute-start.20 = (f32[8,128]{1,0:T(8,128)S(1)}, f32[8,128]{1,0:T(8,128)S(1)}, u32[]{:S(2)}, u32[]{:S(2)}) collective-permute-start(f32[8,128]{1,0:T(8,128)S(1)} %shard_map.99.refs_0_), channel_id=1, source_target_pairs={{0,3},{1,2},{2,1},{3,0},{4,7},{5,6},{6,5},{7,4},{8,11},{9,10},{10,... | collective-permute-start | bytes 12296 | tf_op jit(solution)/shard_map/ppermute | solution.py:448
  42.9 3.7 %collective-permute-start.19 = (f32[8,128]{1,0:T(8,128)S(1)}, f32[8,128]{1,0:T(8,128)S(1)}, u32[]{:S(2)}, u32[]{:S(2)}) collective-permute-start(f32[8,128]{1,0:T(8,128)S(1)} %shard_map.99.refs_0_), channel_id=1, source_target_pairs={{0,2},{1,3},{2,0},{3,1},{4,6},{5,7},{6,4},{7,5},{8,10},{9,11},{10,... | collective-permute-start | bytes 12296 | tf_op jit(solution)/shard_map/ppermute | solution.py:448
  43.6 3.0 %collective-permute-start.18 = (f32[8,128]{1,0:T(8,128)S(1)}, f32[8,128]{1,0:T(8,128)S(1)}, u32[]{:S(2)}, u32[]{:S(2)}) collective-permute-start(f32[8,128]{1,0:T(8,128)S(1)} %shard_map.99.refs_0_), channel_id=1, source_target_pairs={{0,1},{1,0},{2,3},{3,2},{4,5},{5,4},{6,7},{7,6},{8,9},{9,8},{10,11... | collective-permute-start | bytes 12296 | tf_op jit(solution)/shard_map/ppermute | solution.py:448
  47.1 4.8 %collective-permute-start.21 = (f32[24,128]{1,0:T(8,128)S(1)}, f32[24,128]{1,0:T(8,128)S(1)}, u32[]{:S(2)}, u32[]{:S(2)}) collective-permute-start(f32[24,128]{1,0:T(8,128)S(1)} %get-tuple-element.65), channel_id=1, source_target_pairs={{0,8},{4,12},{8,0},{12,4},{1,9},{5,13},{9,1},{13,5},{2,10},{6,14},... | collective-permute-start | bytes 36872 | tf_op jit(solution)/shard_map/ppermute | solution.py:454
  48.0 5.5 %collective-permute-start.22 = (f32[24,128]{1,0:T(8,128)S(1)}, f32[24,128]{1,0:T(8,128)S(1)}, u32[]{:S(2)}, u32[]{:S(2)}) collective-permute-start(f32[24,128]{1,0:T(8,128)S(1)} %get-tuple-element.66), channel_id=1, source_target_pairs={{0,12},{4,8},{8,4},{12,0},{1,13},{5,9},{9,5},{13,1},{2,14},{6,10},... | collective-permute-start | bytes 36872 | tf_op jit(solution)/shard_map/ppermute | solution.py:454
  49.8 3.8 %collective-permute-start.23 = (f32[24,128]{1,0:T(8,128)S(1)}, f32[24,128]{1,0:T(8,128)S(1)}, u32[]{:S(2)}, u32[]{:S(2)}) collective-permute-start(f32[24,128]{1,0:T(8,128)S(1)} %get-tuple-element.67), channel_id=1, source_target_pairs={{0,4},{4,0},{8,12},{12,8},{1,5},{5,1},{9,13},{13,9},{2,6},{6,2},{1... | collective-permute-start | bytes 36872 | tf_op jit(solution)/shard_map/ppermute | solution.py:454
